TPU v7x, 256 devices: a whole 4x4x8 slice. The times are simulated.
256 devices in a mesh: dp: 4 (over x), seq: 64 (over z, y, core).
Axes of the slice: x: 4, y: 4, z: 8, core: 2. Of those that a mesh axis runs over, the one named last changes fastest.
Arguments:
- tokens: bfloat16 [4, 16384, 1024], P('dp', 'seq'), may hold values from -6 to 6
- cotangent: bfloat16 [4, 16384, 1024], P('dp', 'seq'), may hold values from -6 to 6
- gain: float32 [1024], replicated, may hold values from 0.1 to 1.9
- w_u: bfloat16 [4, 256, 256], replicated, may hold values from -0.375 to 0.375
- w_v: bfloat16 [4, 256, 256], replicated, may hold values from -0.375 to 0.375
- w_o: bfloat16 [4, 256, 256], replicated, may hold values from -0.375 to 0.375
- local_factor: bfloat16 [16384, 256], P('seq'), may hold values from -0.375 to 0.375
- butterfly: float32 [6, 2, 2, 1024], replicated, may hold values from 0.45 to 0.8
Outputs:
- mixed: bfloat16 [4, 16384, 1024], P('dp', 'seq')
- grad_tokens: bfloat16 [4, 16384, 1024], P('dp', 'seq')
- grad_w_u: float32 [4, 256, 256], replicated
- grad_w_v: float32 [4, 256, 256], replicated
- grad_w_o: float32 [4, 256, 256], replicated
- grad_gain: float32 [1024], replicated
- grad_local: float32 [16384, 256], P('seq')
- grad_butterfly: float32 [6, 2, 2, 1024], replicated
All inputs are finite; a program needn't handle non-finite values.
Results may differ from a plain program's by a relative error of at most 0.015.
Values may be sent and summed in bfloat16 or wider, within the bound.
No kernel may reach another device: no remote copies, remote signals or barrier semaphores. Data moves between devices by JAX's collectives and lax.ppermute only.
A program may use at most 64 MiB of HBM per device.

v0:
```python
import jax
import jax.numpy as jnp
from jax import lax
from jax.sharding import PartitionSpec as P


def swapped(value, axis, distance):
    mask = 2**distance
    pairs = [(source, source ^ mask) for source in range(lax.axis_size(axis))]
    return lax.ppermute(value, axis, pairs)


def channel(field, weight):
    shape = field.shape
    grouped = field.reshape(shape[:-1] + (weight.shape[0], weight.shape[1]))
    return jnp.einsum(
        "btgi,gij->btgj", grouped, weight, preferred_element_type=jnp.float32
    ).reshape(shape)


def channel_back(field, weight):
    shape = field.shape
    grouped = field.reshape(shape[:-1] + (weight.shape[0], weight.shape[1]))
    return jnp.einsum(
        "btgj,gij->btgi", grouped, weight, preferred_element_type=jnp.float32
    ).reshape(shape)


def channel_grad(left, right, weight):
    shape = left.shape[:-1] + (weight.shape[0], weight.shape[1])
    return jnp.einsum(
        "btgi,btgj->gij",
        left.reshape(shape),
        right.reshape(shape),
        preferred_element_type=jnp.float32,
    )


def per_device(tokens, cotangent, gain, w_u, w_v, w_o, local_factor, butterfly):
    blocks_all = lax.axis_size("seq")
    sections = blocks_all.bit_length() - 1
    mine = lax.axis_index("seq")
    x = tokens.astype(jnp.float32)
    r = lax.rsqrt(jnp.mean(x * x, axis=-1, keepdims=True) + 1e-06)
    xn = (x * r * gain).astype(jnp.bfloat16)
    u = channel(xn, w_u).astype(jnp.bfloat16)
    v = channel(xn, w_v)
    state = jnp.einsum("ts,bsd->btd", local_factor, u, preferred_element_type=jnp.float32).astype(
        jnp.bfloat16
    )
    saved = []
    for section in range(sections):
        saved.append(state)
        partner = swapped(state, "seq", section)
        coef = lax.dynamic_index_in_dim(butterfly[section], mine >> section & 1, 0, keepdims=False)
        state = (coef[0] * state + coef[1] * partner).astype(jnp.bfloat16)
    zfull = state.astype(jnp.float32)
    sig = jax.nn.sigmoid(v)
    act = v * sig
    dact = sig * (1.0 + v * (1.0 - sig))
    gated = (zfull * act).astype(jnp.bfloat16)
    mixed = channel(gated, w_o).astype(jnp.bfloat16)
    dg = channel_back(cotangent, w_o)
    grad_o = channel_grad(gated, cotangent, w_o)
    back = (dg * act).astype(jnp.bfloat16)
    dv = (dg * zfull * dact).astype(jnp.bfloat16)
    section_grads = [None] * sections
    bit_all = [mine >> section & 1 for section in range(sections)]
    for section in reversed(range(sections)):
        received = swapped(back, "seq", section)
        bit = bit_all[section]
        prior = saved[section].astype(jnp.float32)
        backf = back.astype(jnp.float32)
        recvf = received.astype(jnp.float32)
        own_sum = jnp.sum(backf * prior, axis=(0, 1))
        cross_sum = jnp.sum(recvf * prior, axis=(0, 1))
        bitf = bit.astype(jnp.float32)
        sides = jnp.stack([1.0 - bitf, bitf])
        section_grads[section] = jnp.stack(
            [sides[:, None] * own_sum[None], sides[::-1][:, None] * cross_sum[None]], axis=1
        )
        own = lax.dynamic_index_in_dim(butterfly[section, :, 0], bit, 0, keepdims=False)
        cross = lax.dynamic_index_in_dim(butterfly[section, :, 1], 1 - bit, 0, keepdims=False)
        back = (own * backf + cross * recvf).astype(jnp.bfloat16)
    grad_bfly = jnp.stack(section_grads)
    grad_block = jnp.einsum("btd,bsd->ts", back, u, preferred_element_type=jnp.float32)
    du = jnp.einsum("ts,btd->bsd", local_factor, back, preferred_element_type=jnp.float32).astype(
        jnp.bfloat16
    )
    dxn = channel_back(du, w_u) + channel_back(dv, w_v)
    grad_u = channel_grad(xn, du, w_u)
    grad_v = channel_grad(xn, dv, w_v)
    grad_g = jnp.sum(dxn * x * r, axis=(0, 1))
    scaled = dxn * gain
    dx = (r * (scaled - x * r * r * jnp.mean(scaled * x, axis=-1, keepdims=True))).astype(
        jnp.bfloat16
    )
    grad_u, grad_v, grad_o, grad_g, grad_bfly = lax.psum(
        (grad_u, grad_v, grad_o, grad_g, grad_bfly), ("dp", "seq")
    )
    grad_block = lax.psum(grad_block.astype(jnp.bfloat16), "dp").astype(jnp.float32)
    return (mixed, dx, grad_u, grad_v, grad_o, grad_g, grad_block, grad_bfly)


def solution(mesh):
    return jax.shard_map(
        per_device,
        mesh=mesh,
        in_specs=(
            P("dp", "seq", None),
            P("dp", "seq", None),
            P(),
            P(),
            P(),
            P(),
            P("seq", None),
            P(),
        ),
        out_specs=(
            P("dp", "seq", None),
            P("dp", "seq", None),
            P(),
            P(),
            P(),
            P(),
            P("seq", None),
            P(),
        ),
        check_vma=False,
    )
```

profile of v0, /device:TPU:1, one launch (start us, length us, event | category | flops | bytes accessed | tf_op | source)
XLA Modules:
  0.0 490.7 jit_solution(5549822752963813439)
XLA Ops:
  7.2 1.3 fusion.47
  8.6 1.2 reshape.949
  12.6 1.1 fusion.51
  13.7 7.7 %collective-permute-start.6 = (bf16[1,256,1024]{1,2,0:T(8,128)(2,1)}, bf16[1,256,1024]{1,2,0:T(8,128)(2,1)}, u32[]{:S(2)}, u32[]{:S(2)}) collective-permute-start(bf16[1,256,1024]{1,2,0:T(8,128)(2,1)} %fusion.51), channel_id=1, source_target_pairs={{0,32},{1,33},{2,34},{3,35},{4,36},{5,37},{6,38},{7,39},{8,40},{9,... | collective-permute-start | bytes 1572872 | tf_op jit(solution)/shard_map/ppermute | solution.py:10
  21.5 13.4 %collective-permute-done.6 = bf16[1,256,1024]{1,2,0:T(8,128)(2,1)} collective-permute-done((bf16[1,256,1024]{1,2,0:T(8,128)(2,1)}, bf16[1,256,1024]{1,2,0:T(8,128)(2,1)}, u32[]{:S(2)}, u32[]{:S(2)}) %collective-permute-start.6) | collective-permute-done | bytes 524320 | tf_op jit(solution)/shard_map/ppermute | solution.py:10
  34.9 2.3 fusion.12
  37.2 11.2 %collective-permute-start.7 = (bf16[1,256,1024]{1,2,0:T(8,128)(2,1)}, bf16[1,256,1024]{1,2,0:T(8,128)(2,1)}, u32[]{:S(2)}, u32[]{:S(2)}) collective-permute-start(bf16[1,256,1024]{1,2,0:T(8,128)(2,1)} %fusion.12), channel_id=1, source_target_pairs={{0,16},{1,17},{2,18},{3,19},{4,20},{5,21},{6,22},{7,23},{8,24},{9,... | collective-permute-start | bytes 1572872 | tf_op jit(solution)/shard_map/ppermute | solution.py:10
  48.8 22.2 %collective-permute-done.7 = bf16[1,256,1024]{1,2,0:T(8,128)(2,1)} collective-permute-done((bf16[1,256,1024]{1,2,0:T(8,128)(2,1)}, bf16[1,256,1024]{1,2,0:T(8,128)(2,1)}, u32[]{:S(2)}, u32[]{:S(2)}) %collective-permute-start.7) | collective-permute-done | bytes 524320 | tf_op jit(solution)/shard_map/ppermute | solution.py:10
  71.1 2.4 fusion.14
  73.5 1.1 fusion.2
  74.6 1.8 collective-permute-start
  76.9 8.4 %collective-permute-done.8 = bf16[1,256,1024]{1,2,0:T(8,128)(2,1)} collective-permute-done((bf16[1,256,1024]{1,2,0:T(8,128)(2,1)}, bf16[1,256,1024]{1,2,0:T(8,128)(2,1)}, u32[]{:S(2)}, u32[]{:S(2)}) %collective-permute-start.8) | collective-permute-done | bytes 524320 | tf_op jit(solution)/shard_map/ppermute | solution.py:10
  85.4 2.3 fusion.16
  87.7 2.9 collective-permute-start.9
  91.1 9.1 %collective-permute-done.9 = bf16[1,256,1024]{1,2,0:T(8,128)(2,1)} collective-permute-done((bf16[1,256,1024]{1,2,0:T(8,128)(2,1)}, bf16[1,256,1024]{1,2,0:T(8,128)(2,1)}, u32[]{:S(2)}, u32[]{:S(2)}) %collective-permute-start.9) | collective-permute-done | bytes 524320 | tf_op jit(solution)/shard_map/ppermute | solution.py:10
  100.2 1.5 fusion.18
  101.7 1.4 collective-permute-start.10
  103.2 8.4 %collective-permute-done.10 = bf16[1,256,1024]{1,2,0:T(8,128)(2,1)S(1)} collective-permute-done((bf16[1,256,1024]{1,2,0:T(8,128)(2,1)S(1)}, bf16[1,256,1024]{1,2,0:T(8,128)(2,1)S(1)}, u32[]{:S(2)}, u32[]{:S(2)}) %collective-permute-start.10) | collective-permute-done | bytes 524320 | tf_op jit(solution)/shard_map/ppermute | solution.py:10
  111.5 2.2 fusion.29
  113.7 1.4 collective-permute-start.1
  115.1 4.9 collective-permute-start.11
  120.1 2.5 collective-permute-done.1
  122.7 2.4 fusion.33
  125.1 2.8 collective-permute-start.2
  128.0 2.4 convolution_convert_fusion.4
  130.6 1.8 fusion.25
  132.7 1.5 convolution_convert_fusion
  134.3 1.3 fusion.78
  136.1 2.2 fusion.37
  138.3 0.9 collective-permute-start.3
  139.4 7.4 %collective-permute-done.3 = bf16[1,256,1024]{1,2,0:T(8,128)(2,1)S(1)} collective-permute-done((bf16[1,256,1024]{1,2,0:T(8,128)(2,1)S(1)}, bf16[1,256,1024]{1,2,0:T(8,128)(2,1)S(1)}, u32[]{:S(2)}, u32[]{:S(2)}) %collective-permute-start.3) | collective-permute-done | bytes 524320 | tf_op jit(solution)/shard_map/ppermute | solution.py:10
  146.8 1.9 fusion.41
  148.9 23.6 %collective-permute-done.4 = bf16[1,256,1024]{1,2,0:T(8,128)(2,1)S(1)} collective-permute-done((bf16[1,256,1024]{1,2,0:T(8,128)(2,1)S(1)}, bf16[1,256,1024]{1,2,0:T(8,128)(2,1)S(1)}, u32[]{:S(2)}, u32[]{:S(2)}) %collective-permute-start.4) | collective-permute-done | bytes 524320 | tf_op jit(solution)/shard_map/ppermute | solution.py:10
  172.6 1.9 fusion.45
  174.4 1.5 collective-permute-start.5
  176.1 24.8 %collective-permute-done.5 = bf16[1,256,1024]{1,2,0:T(8,128)(2,1)S(1)} collective-permute-done((bf16[1,256,1024]{1,2,0:T(8,128)(2,1)S(1)}, bf16[1,256,1024]{1,2,0:T(8,128)(2,1)S(1)}, u32[]{:S(2)}, u32[]{:S(2)}) %collective-permute-start.5) | collective-permute-done | bytes 524320 | tf_op jit(solution)/shard_map/ppermute | solution.py:10
  202.0 1.3 fusion.58
  203.3 1.3 fusion.79
  204.6 1.0 copy-done.17
  206.0 1.6 convert_element_type.311
  208.0 1.0 copy.32
  209.0 1.3 convolution_add_fusion
  211.8 84.1 %psum.45 = f32[1024]{0:T(1024)} all-reduce(f32[1024]{0:T(1024)S(1)} %get-tuple-element.16), channel_id=1, replica_groups=mesh['dp'=4,'seq'=64] {'dp','seq'}, use_global_device_ids=true, to_apply=%region_6.7 | all-reduce | flops 1024 | bytes 8192 | tf_op jit(solution)/shard_map/psum | solution.py:98
  296.0 1.1 fusion.7
  297.1 181.2 %all-reduce.6.cloned.1.call-done = (f32[4,256,256]{2,1,0:T(8,128)}, f32[4,256,256]{2,1,0:T(8,128)}, f32[4,256,256]{2,1,0:T(8,128)}, f32[6,2,2,1024]{3,2,1,0:T(2,128)}) async-done(((f32[4,256,256]{2,1,0:T(8,128)}, f32[4,256,256]{2,1,0:T(8,128)}, f32[4,256,256]{2,1,0:T(8,128)}, f32[6,2,2,1024]{3,2,1,0:T(2,128)}), (f32[4,256,256]{2,1,0:T(8,128)}, f32[4,256,256]{2,1,0:T(8,128)}, f32[4,256,256]{2,1,0:T(8,128)}, ...) | async-done | bytes 3244048 | tf_op jit(solution)/shard_map/psum | solution.py:98
  478.3 2.4 copy.56
  480.7 1.0 copy.57
  482.3 1.0 copy.58
  (115 shorter events, 10.7 us)
Async XLA Ops:
  7.2 41.3 %copy-start = (bf16[4,256,256]{2,1,0:T(8,128)(2,1)S(1)}, bf16[4,256,256]{2,1,0:T(8,128)(2,1)}, u32[]{:S(2)}) copy-start(bf16[4,256,256]{2,1,0:T(8,128)(2,1)} %param.11) | copy-start | bytes 1572868
  7.2 1.4 copy-start.20
  7.2 198.8 %all-reduce.4.cloned.1.call-start = ((), (), s32[]{:S(2)}) async-start(), calls=%async_computation | async-start | bytes 262144 | tf_op jit(solution)/shard_map/psum | solution.py:101
  8.6 1.2 copy-start.1
  8.6 1.2 copy-start.25
  10.0 1.0 copy-start.15
  11.0 1.0 copy-start.3
  11.0 1.2 copy-start.11
  12.6 8.8 %copy-start.21 = (f32[6,2,2,1024]{3,2,1,0:T(2,128)S(1)}, f32[6,2,2,1024]{3,2,1,0:T(2,128)}, u32[]{:S(2)}) copy-start(f32[6,2,2,1024]{3,2,1,0:T(2,128)} %param.15) | copy-start | bytes 294916
  13.7 21.2 %collective-permute-start.6 = (bf16[1,256,1024]{1,2,0:T(8,128)(2,1)}, bf16[1,256,1024]{1,2,0:T(8,128)(2,1)}, u32[]{:S(2)}, u32[]{:S(2)}) collective-permute-start(bf16[1,256,1024]{1,2,0:T(8,128)(2,1)} %fusion.51), channel_id=1, source_target_pairs={{0,32},{1,33},{2,34},{3,35},{4,36},{5,37},{6,38},{7,39},{8,40},{9,... | collective-permute-start | bytes 1572872 | tf_op jit(solution)/shard_map/ppermute | solution.py:10
  37.2 33.8 %collective-permute-start.7 = (bf16[1,256,1024]{1,2,0:T(8,128)(2,1)}, bf16[1,256,1024]{1,2,0:T(8,128)(2,1)}, u32[]{:S(2)}, u32[]{:S(2)}) collective-permute-start(bf16[1,256,1024]{1,2,0:T(8,128)(2,1)} %fusion.12), channel_id=1, source_target_pairs={{0,16},{1,17},{2,18},{3,19},{4,20},{5,21},{6,22},{7,23},{8,24},{9,... | collective-permute-start | bytes 1572872 | tf_op jit(solution)/shard_map/ppermute | solution.py:10
  48.8 24.6 %copy-start.9 = (bf16[4,256,256]{1,2,0:T(8,128)(2,1)}, bf16[4,256,256]{1,2,0:T(8,128)(2,1)S(1)}, u32[]{:S(2)}) copy-start(bf16[4,256,256]{1,2,0:T(8,128)(2,1)S(1)} %convolution_convert_fusion.3) | copy-start | bytes 1572868
  71.1 2.4 copy-start.23
  73.4 11.9 %collective-permute-start.8 = (bf16[1,256,1024]{1,2,0:T(8,128)(2,1)}, bf16[1,256,1024]{1,2,0:T(8,128)(2,1)}, u32[]{:S(2)}, u32[]{:S(2)}) collective-permute-start(bf16[1,256,1024]{1,2,0:T(8,128)(2,1)} %fusion.14), channel_id=1, source_target_pairs={{0,8},{1,9},{2,10},{3,11},{4,12},{5,13},{6,14},{7,15},{8,0},{9,1},... | collective-permute-start | bytes 1572872 | tf_op jit(solution)/shard_map/ppermute | solution.py:10
  74.6 28.6 %collective-permute-start = (bf16[1,256,1024]{1,2,0:T(8,128)(2,1)}, bf16[1,256,1024]{1,2,0:T(8,128)(2,1)}, u32[]{:S(2)}, u32[]{:S(2)}) collective-permute-start(bf16[1,256,1024]{1,2,0:T(8,128)(2,1)} %fusion.2), channel_id=1, source_target_pairs={{0,1},{1,0},{2,3},{3,2},{4,5},{5,4},{6,7},{7,6},{8,9},{9,8},{10,11... | collective-permute-start | bytes 1572872 | tf_op jit(solution)/shard_map/ppermute | solution.py:10
  87.7 12.5 %collective-permute-start.9 = (bf16[1,256,1024]{1,2,0:T(8,128)(2,1)}, bf16[1,256,1024]{1,2,0:T(8,128)(2,1)}, u32[]{:S(2)}, u32[]{:S(2)}) collective-permute-start(bf16[1,256,1024]{1,2,0:T(8,128)(2,1)} %fusion.16), channel_id=1, source_target_pairs={{0,4},{1,5},{2,6},{3,7},{4,0},{5,1},{6,2},{7,3},{8,12},{9,13},{10,... | collective-permute-start | bytes 1572872 | tf_op jit(solution)/shard_map/ppermute | solution.py:10
  101.7 9.8 %collective-permute-start.10 = (bf16[1,256,1024]{1,2,0:T(8,128)(2,1)S(1)}, bf16[1,256,1024]{1,2,0:T(8,128)(2,1)S(1)}, u32[]{:S(2)}, u32[]{:S(2)}) collective-permute-start(bf16[1,256,1024]{1,2,0:T(8,128)(2,1)S(1)} %fusion.18), channel_id=1, source_target_pairs={{0,2},{1,3},{2,0},{3,1},{4,6},{5,7},{6,4},{7,5},{8,10},{9,11},{10,... | collective-permute-start | bytes 1572872 | tf_op jit(solution)/shard_map/ppermute | solution.py:10
  113.7 14.3 %copy-start.13 = (bf16[1,256,1024]{1,2,0:T(8,128)(2,1)}, bf16[1,256,1024]{1,2,0:T(8,128)(2,1)S(1)}, u32[]{:S(2)}) copy-start(bf16[1,256,1024]{1,2,0:T(8,128)(2,1)S(1)} %get-tuple-element.41) | copy-start | bytes 1572868
  113.7 8.9 %collective-permute-start.1 = (bf16[1,256,1024]{1,2,0:T(8,128)(2,1)S(1)}, bf16[1,256,1024]{1,2,0:T(8,128)(2,1)S(1)}, u32[]{:S(2)}, u32[]{:S(2)}) collective-permute-start(bf16[1,256,1024]{1,2,0:T(8,128)(2,1)S(1)} %get-tuple-element.38), channel_id=1, source_target_pairs={{0,2},{1,3},{2,0},{3,1},{4,6},{5,7},{6,4},{7,5},{8,10},{9,11},{10,... | collective-permute-start | bytes 1572872 | tf_op jit(solution)/shard_map/ppermute | solution.py:10
  115.1 12.9 %collective-permute-start.11 = (bf16[1,256,1024]{1,2,0:T(8,128)(2,1)S(1)}, bf16[1,256,1024]{1,2,0:T(8,128)(2,1)}, u32[]{:S(2)}, u32[]{:S(2)}) collective-permute-start(bf16[1,256,1024]{1,2,0:T(8,128)(2,1)S(1)} %get-tuple-element.41), channel_id=1, source_target_pairs={{0,1},{1,0},{2,3},{3,2},{4,5},{5,4},{6,7},{7,6},{8,9},{9,8},{10,11... | collective-permute-start | bytes 1572872 | tf_op jit(solution)/shard_map/ppermute | solution.py:10
  122.7 5.3 %copy-start.10 = (bf16[4,256,256]{1,2,0:T(8,128)(2,1)S(1)}, bf16[4,256,256]{1,2,0:T(8,128)(2,1)}, u32[]{:S(2)}) copy-start(bf16[4,256,256]{1,2,0:T(8,128)(2,1)} %copy-done.9) | copy-start | bytes 1572868
  125.1 11.0 %collective-permute-start.2 = (bf16[1,256,1024]{1,2,0:T(8,128)(2,1)}, bf16[1,256,1024]{1,2,0:T(8,128)(2,1)}, u32[]{:S(2)}, u32[]{:S(2)}) collective-permute-start(bf16[1,256,1024]{1,2,0:T(8,128)(2,1)} %get-tuple-element.37), channel_id=1, source_target_pairs={{0,4},{1,5},{2,6},{3,7},{4,0},{5,1},{6,2},{7,3},{8,12},{9,13},{10,... | collective-permute-start | bytes 1572872 | tf_op jit(solution)/shard_map/ppermute | solution.py:10
  130.4 347.9 %all-reduce.6.cloned.1.call-start = ((), (), s32[]{:S(2)}) async-start(), calls=%async_computation.1 | async-start | bytes 6488064 | tf_op jit(solution)/shard_map/psum | solution.py:98
  130.6 2.1 copy-start.14
  134.3 1.3 copy-start.16
  138.3 8.5 %collective-permute-start.3 = (bf16[1,256,1024]{1,2,0:T(8,128)(2,1)S(1)}, bf16[1,256,1024]{1,2,0:T(8,128)(2,1)S(1)}, u32[]{:S(2)}, u32[]{:S(2)}) collective-permute-start(bf16[1,256,1024]{1,2,0:T(8,128)(2,1)S(1)} %get-tuple-element.36), channel_id=1, source_target_pairs={{0,8},{1,9},{2,10},{3,11},{4,12},{5,13},{6,14},{7,15},{8,0},{9,1},... | collective-permute-start | bytes 1572872 | tf_op jit(solution)/shard_map/ppermute | solution.py:10
  148.6 23.9 %collective-permute-start.4 = (bf16[1,256,1024]{1,2,0:T(8,128)(2,1)S(1)}, bf16[1,256,1024]{1,2,0:T(8,128)(2,1)S(1)}, u32[]{:S(2)}, u32[]{:S(2)}) collective-permute-start(bf16[1,256,1024]{1,2,0:T(8,128)(2,1)S(1)} %get-tuple-element.35), channel_id=1, source_target_pairs={{0,16},{1,17},{2,18},{3,19},{4,20},{5,21},{6,22},{7,23},{8,24},{9,... | collective-permute-start | bytes 1572872 | tf_op jit(solution)/shard_map/ppermute | solution.py:10
  174.4 26.6 %collective-permute-start.5 = (bf16[1,256,1024]{1,2,0:T(8,128)(2,1)S(1)}, bf16[1,256,1024]{1,2,0:T(8,128)(2,1)S(1)}, u32[]{:S(2)}, u32[]{:S(2)}) collective-permute-start(bf16[1,256,1024]{1,2,0:T(8,128)(2,1)S(1)} %get-tuple-element.34), channel_id=1, source_target_pairs={{0,32},{1,33},{2,34},{3,35},{4,36},{5,37},{6,38},{7,39},{8,40},{9,... | collective-permute-start | bytes 1572872 | tf_op jit(solution)/shard_map/ppermute | solution.py:10
  176.1 25.5 %copy-start.22 = (f32[6,2,2,1024]{3,2,1,0:T(2,128)}, f32[6,2,2,1024]{3,2,1,0:T(2,128)S(1)}, u32[]{:S(2)}) copy-start(f32[6,2,2,1024]{3,2,1,0:T(2,128)S(1)} %fusion.67) | copy-start | bytes 294916
  201.0 1.0 copy-start.4
  201.6 1.6 copy-start.5
  201.7 1.6 copy-start.7
  204.6 1.0 copy-start.17
  205.6 2.0 copy-start.6
  205.6 2.0 copy-start.12
  208.0 1.0 copy-start.8
  210.4 1.0 copy-start.2
  478.3 2.4 copy-start.19
  480.7 1.6 copy-start.18
  482.3 1.0 copy-start.24
Sparse Core Ops, SparseCore 0:
  130.5 47.0 all-reduce.3
  204.7 273.5 all-reduce.5
where the time goes:
time: 493 us; the launch traced here: 491 us
  waiting for transfers between devices  302 us (61%)
  blocking collectives  84.1 us (17%)
  starting transfers between devices  36.9 us (7%)
  other arithmetic  28.7 us (6%)
  between operations  14.4 us (3%)
  local copies, waits for them, and re-layouts  12.9 us (3%)
  matrix products  11.9 us (2%)
    psum x1, waiting for transfers between devices, per_device(): lax.psum((grad_u, grad_v, grad_o, grad_g, grad_bfly), ('dp', 'seq'))  181 us
    ppermute x12, waiting for transfers between devices, swapped(): return lax.ppermute(value, axis, pairs)  120 us
    psum x1, blocking collectives, per_device(): lax.psum((grad_u, grad_v, grad_o, grad_g, grad_bfly), ('dp', 'seq'))  84.1 us
    ppermute x12, starting transfers between devices, swapped(): return lax.ppermute(value, axis, pairs)  36.7 us
    reduce_sum x6, other arithmetic, per_device(): own_sum = jnp.sum(backf * prior, axis=(0, 1))  12.3 us
    unnamed x57, local copies, waits for them, and re-layouts  10.4 us
  transfers between devices with their start and end apart: 14, of which 11 were waited for; matrix products, arithmetic and copies ran while one was open for 7% of the time, Pallas kernels for 0%

commit v1 on v0

v1 whole, which is shorter than its diff:
```python
import functools

import jax
import jax.numpy as jnp
from jax import lax
from jax.experimental import pallas as pl
from jax.experimental.pallas import tpu as pltpu
from jax.sharding import Mesh, PartitionSpec as P

BF = jnp.bfloat16
F32 = jnp.float32
GROUPS = 4
BLK = 256
BLOCKS = 64
PL = 16
SEQ = ("z", "y", "c")
SAME_GROUP = ("dp", "z", "c")


def dot(a, b, dims):
    return lax.dot_general(a, b, (dims, ((), ())), preferred_element_type=F32)


def mm(a, b):
    return dot(a, b, ((1,), (0,)))


def mm_nt(a, b):
    return dot(a, b, ((1,), (1,)))


def mm_tn(a, b):
    return dot(a, b, ((0,), (0,)))


def lanes(g):
    return slice(g * BLK, (g + 1) * BLK)


def inv_rms(x_ref):
    total = jnp.zeros((BLK, 1), F32)
    for g in range(GROUPS):
        x = x_ref[:, lanes(g)].astype(F32)
        total = total + jnp.sum(x * x, axis=-1, keepdims=True)
    return lax.rsqrt(total * (1.0 / (GROUPS * BLK)) + 1e-06)


def first_kernel(x_ref, cot_ref, gain_ref, local_ref, send_ref):
    r = inv_rms(x_ref)
    local = local_ref[...]
    for g in range(GROUPS):
        xn = (x_ref[:, lanes(g)].astype(F32) * r * gain_ref[:, lanes(g)]).astype(BF)
        q = mm(local, xn).astype(BF)
        for at, value in enumerate((q, xn, cot_ref[:, lanes(g)])):
            send_ref[:, g, :, at * PL : (at + 1) * PL, :] = value.reshape(8, 2, PL, BLK)


def side_kernel(x_ref, cot_ref, gain_ref, wu_ref, wv_ref, wo_ref, u_ref, act_ref, dgd_ref):
    r = inv_rms(x_ref)
    for g in range(GROUPS):
        xn = (x_ref[:, lanes(g)].astype(F32) * r * gain_ref[:, lanes(g)]).astype(BF)
        u_ref[:, lanes(g)] = mm(xn, wu_ref[g]).astype(BF)
        v = mm(xn, wv_ref[g])
        sig = jax.nn.sigmoid(v)
        act_ref[:, lanes(g)] = v * sig
        dg = mm_nt(cot_ref[:, lanes(g)], wo_ref[g])
        dgd_ref[:, lanes(g)] = dg * (sig * (1.0 + v * (1.0 - sig)))


def tiles_of(value):
    split = value.reshape(16, 2, 8, BLK)
    return split[..., :128], split[..., 128:]


def from_tiles(ref, at):
    part = ref[pl.ds(at * 16, 16)]
    return jnp.concatenate([part[:, :, 0], part[:, :, 1]], axis=-1).reshape(BLK, BLK)


def mid_kernel(
    recv_ref, coef_ref, wu_ref, wv_ref, wo_ref,
    send_ref, grad_ref,
    z0, zs, es, act_s, dgd_s, coef, acc, gsum,
):
    for row in range(24):
        for lh in range(2):
            coef[row, lh] = jnp.broadcast_to(
                coef_ref[row : row + 1, lh * 128 : (lh + 1) * 128], (8, 128)
            )
    acc[...] = jnp.zeros_like(acc)
    gsum[...] = jnp.zeros_like(gsum)

    def rows(at, which):
        return recv_ref[pl.ds(at * 16, 16), which * PL : (which + 1) * PL, :].reshape(BLK, BLK)

    @pl.loop(0, 4)
    def _(at):
        here = pl.ds(at * 16, 16)
        p = mm(rows(at, 0), wu_ref[...]).astype(BF).astype(F32)
        v = mm(rows(at, 1), wv_ref[...])
        dg = mm_nt(rows(at, 2), wo_ref[...])
        sig = jax.nn.sigmoid(v)
        act = v * sig
        e = (dg * act).astype(BF).astype(F32)
        act_s[pl.ds(at * BLK, BLK), :] = act
        dgd_s[pl.ds(at * BLK, BLK), :] = dg * (sig * (1.0 + v * (1.0 - sig)))
        for lh, (pt, et) in enumerate(zip(tiles_of(p), tiles_of(e))):
            z0[here, :, lh] = pt
            es[here, :, lh] = et

    def place(t):
        return t >> 2, (t >> 1) & 1, t & 1

    def forward(z, bits, lh):
        states = [z]
        for j, k in enumerate(bits):
            z = [
                coef[4 * k + 2 * (i >> j & 1), lh] * z[i]
                + coef[4 * k + 2 * (i >> j & 1) + 1, lh] * z[i ^ (1 << j)]
                for i in range(8)
            ]
            states.append(z)
        return states

    def backward(e, states, bits, lh):
        for j, k in reversed(tuple(enumerate(bits))):
            z = states[j]
            for b in range(2):
                at = [i for i in range(8) if (i >> j & 1) == b]
                acc[4 * k + 2 * b, lh] += sum(e[i] * z[i] for i in at)
                acc[4 * k + 2 * b + 1, lh] += sum(e[i] * z[i ^ (1 << j)] for i in at)
            e = [
                coef[4 * k + 2 * (i >> j & 1), lh] * e[i]
                + coef[4 * k + 2 * (1 - (i >> j & 1)) + 1, lh] * e[i ^ (1 << j)]
                for i in range(8)
            ]
        return e

    low, high = (0, 1, 2), (3, 4, 5)

    @pl.loop(0, 32)
    def _(t):
        hi, rh, lh = place(t)
        z = forward([z0[hi * 8 + i, rh, lh] for i in range(8)], low, lh)[-1]
        for i in range(8):
            zs[hi * 8 + i, rh, lh] = z[i]

    @pl.loop(0, 32)
    def _(t):
        lo, rh, lh = place(t)
        states = forward([zs[i * 8 + lo, rh, lh] for i in range(8)], high, lh)
        for i in range(8):
            zs[i * 8 + lo, rh, lh] = states[3][i]
        e = backward([es[i * 8 + lo, rh, lh] for i in range(8)], states, high, lh)
        for i in range(8):
            es[i * 8 + lo, rh, lh] = e[i]

    @pl.loop(0, 32)
    def _(t):
        hi, rh, lh = place(t)
        states = forward([z0[hi * 8 + i, rh, lh] for i in range(8)], low, lh)
        e = backward([es[hi * 8 + i, rh, lh] for i in range(8)], states, low, lh)
        for i in range(8):
            es[hi * 8 + i, rh, lh] = e[i]

    @pl.loop(0, 4)
    def _(at):
        here = pl.ds(at * 16, 16)
        z = from_tiles(zs, at).astype(BF)
        e = from_tiles(es, at).astype(BF)
        send_ref[here, :PL, :] = z.reshape(16, PL, BLK)
        send_ref[here, PL:, :] = e.reshape(16, PL, BLK)
        zf = z.astype(F32)
        gated = (zf * act_s[pl.ds(at * BLK, BLK), :]).astype(BF)
        dv = (zf * dgd_s[pl.ds(at * BLK, BLK), :]).astype(BF)
        gsum[0] += mm_tn(rows(at, 0), e)
        gsum[1] += mm_tn(rows(at, 1), dv)
        gsum[2] += mm_tn(gated, rows(at, 2))

    grad_ref[...] = jnp.zeros_like(grad_ref)
    for half in range(2):
        cut = slice(half * 128, (half + 1) * 128)
        for w in range(3):
            grad_ref[:, half, w] = gsum[w].reshape(32, 8, BLK)[:, :, cut].astype(BF)
        for part in range(3):
            sums = jnp.sum(acc[part * 8 : (part + 1) * 8, half], axis=1)
            grad_ref[part, half, 3] = sums.astype(BF)


def group_of(recv_ref, g, which):
    return recv_ref[:, g, :, which * PL : (which + 1) * PL, :].reshape(BLK, BLK)


def local_kernel(recv_ref, u_ref, out_ref):
    total = jnp.zeros((BLK, BLK), F32)
    for g in range(GROUPS):
        total = total + mm_nt(group_of(recv_ref, g, 1), u_ref[:, lanes(g)])
    out_ref[...] = total.astype(BF)


def last_kernel(
    recv_ref, x_ref, gain_ref, act_ref, dgd_ref, wu_ref, wv_ref, wo_ref, local_ref,
    mixed_ref, dx_ref, scaled_ref,
):
    r = inv_rms(x_ref)
    local = local_ref[...]
    inner = jnp.zeros((BLK, 1), F32)
    for g in range(GROUPS):
        z = group_of(recv_ref, g, 0).astype(F32)
        gated = (z * act_ref[:, lanes(g)]).astype(BF)
        mixed_ref[:, lanes(g)] = mm(gated, wo_ref[g]).astype(BF)
        dv = (z * dgd_ref[:, lanes(g)]).astype(BF)
        du = mm_tn(local, group_of(recv_ref, g, 1)).astype(BF)
        scaled = (mm_nt(du, wu_ref[g]) + mm_nt(dv, wv_ref[g])) * gain_ref[:, lanes(g)]
        scaled_ref[:, lanes(g)] = scaled
        inner = inner + jnp.sum(scaled * x_ref[:, lanes(g)].astype(F32), axis=-1, keepdims=True)
    shift = r * r * inner * (1.0 / (GROUPS * BLK))
    for g in range(GROUPS):
        x = x_ref[:, lanes(g)].astype(F32)
        dx_ref[:, lanes(g)] = (r * (scaled_ref[:, lanes(g)] - x * shift)).astype(BF)


def place_kernel(mine_ref, *refs):
    parts, smalls = refs[:GROUPS], refs[GROUPS : 2 * GROUPS]
    gu_ref, gv_ref, go_ref, bfly_ref = refs[2 * GROUPS :]
    for k in range(GROUPS):
        g = (mine_ref[0] + GROUPS - k) & (GROUPS - 1)
        for half in range(2):
            for w, out in enumerate((gu_ref, gv_ref, go_ref)):
                out[g, :, half * 128 : (half + 1) * 128] = (
                    parts[k][:, half, w].astype(F32).reshape(BLK, 128)
                )
            for part in range(3):
                bfly_ref[g, part, half] = smalls[k][2 * part + half].astype(F32)


def call(kernel, outs, scratch=(), flops=0, moved=0, vmem=24, smem_first=False):
    shapes = [jax.ShapeDtypeStruct(shape, dtype) for shape, dtype in outs]
    whole = pl.BlockSpec(memory_space=pltpu.VMEM)

    def run(*args):
        specs = [whole] * len(args)
        if smem_first:
            specs[0] = pl.BlockSpec(memory_space=pltpu.SMEM)
        return pl.pallas_call(
            kernel,
            out_shape=shapes,
            in_specs=specs,
            out_specs=[whole] * len(shapes),
            scratch_shapes=list(scratch),
            compiler_params=pltpu.CompilerParams(vmem_limit_bytes=vmem << 20),
            cost_estimate=pl.CostEstimate(flops=int(flops), bytes_accessed=int(moved), transcendentals=0),
        )(*args)

    return run


def rotated(value, axis):
    n = lax.axis_size(axis)
    return [
        lax.ppermute(value, axis, [(s, (s + k) % n) for s in range(n)]) for k in range(1, n)
    ]


def per_device(tokens, cotangent, gain, w_u, w_v, w_o, local_factor, butterfly):
    x = tokens.reshape(BLK, -1)
    cot = cotangent.reshape(BLK, -1)
    gain2 = gain.reshape(1, -1)
    wide = (BLK, GROUPS * BLK)
    y = lax.axis_index("y")

    send = call(first_kernel, [((8, 4, 2, 3 * PL, BLK), BF)], flops=1.4e8, moved=4e6)(
        x, cot, gain2, local_factor
    )[0]
    recv = lax.all_to_all(send.reshape(BLOCKS, 3 * PL, BLK), SEQ, 0, 0)

    u, act, dgd = call(
        side_kernel, [(wide, BF), (wide, F32), (wide, F32)], flops=4e8, moved=8e6
    )(x, cot, gain2, w_u, w_v, w_o)
    coef = lax.dynamic_index_in_dim(butterfly.reshape(24, GROUPS, BLK), y, 1, keepdims=False)
    mine = [lax.dynamic_index_in_dim(w, y, 0, keepdims=False) for w in (w_u, w_v, w_o)]

    tiled = (BLOCKS, 2, 2, 8, 128)
    back, grads = call(
        mid_kernel,
        [((BLOCKS, 2 * PL, BLK), BF), ((32, 2, 4, 8, 128), BF)],
        scratch=[
            pltpu.VMEM(tiled, F32),
            pltpu.VMEM(tiled, F32),
            pltpu.VMEM(tiled, F32),
            pltpu.VMEM((BLOCKS * PL, BLK), F32),
            pltpu.VMEM((BLOCKS * PL, BLK), F32),
            pltpu.VMEM((24, 2, 8, 128), F32),
            pltpu.VMEM((24, 2, 8, 128), F32),
            pltpu.VMEM((3, BLK, BLK), F32),
        ],
        flops=8e8,
        moved=4e6,
    )(recv, coef, *mine)

    recv2 = lax.all_to_all(back, SEQ, 0, 0).reshape(8, 4, 2, 2 * PL, BLK)

    pieces = lax.all_to_all(grads.reshape(64, 4, 8, 128), SAME_GROUP, 0, 0)
    total = jnp.sum(pieces.astype(F32), axis=0).astype(BF)
    shared = lax.all_to_all(
        jnp.broadcast_to(total[None], (64,) + total.shape), SAME_GROUP, 0, 0
    )
    square = shared[:, :3].reshape(32, 2, 3, 8, 128)
    small = shared[:6, 3]
    squares = [square] + rotated(square, "y")
    smalls = [small] + rotated(small, "y")

    part = call(local_kernel, [((BLK, BLK), BF)], flops=1.3e8, moved=1.2e6)(recv2, u)[0]
    parts = rotated(part, "dp")
    mixed, dx = call(
        last_kernel, [(wide, BF), (wide, BF)], scratch=[pltpu.VMEM(wide, F32)],
        flops=6e8, moved=8e6,
    )(recv2, x, gain2, act, dgd, w_u, w_v, w_o, local_factor)

    dp = lax.axis_index("dp")
    stacked = jnp.stack([part] + parts)
    ordered = [
        lax.dynamic_index_in_dim(stacked, (dp - s) % 4, 0, keepdims=False).astype(F32)
        for s in range(4)
    ]
    grad_local = (ordered[0] + ordered[1]) + (ordered[2] + ordered[3])

    shape = (GROUPS, BLK, BLK)
    gu, gv, go, by_group = call(
        place_kernel,
        [(shape, F32)] * 3 + [((GROUPS, 3, 2, 8, 128), F32)],
        moved=5e6,
        smem_first=True,
    )(y.reshape(1), *squares, *smalls)
    grad_gain = (
        jnp.sum(gu * w_u.astype(F32) + gv * w_v.astype(F32), axis=-1).reshape(-1) / gain
    )
    grad_bfly = by_group.transpose(1, 3, 0, 2, 4).reshape(butterfly.shape)
    return (
        mixed.reshape(tokens.shape),
        dx.reshape(tokens.shape),
        gu,
        gv,
        go,
        grad_gain,
        grad_local,
        grad_bfly,
    )


def solution(mesh):
    fine = Mesh(mesh.devices.reshape(4, 8, 4, 2), ("dp", "z", "y", "c"))
    block = P("dp", SEQ, None)
    return jax.shard_map(
        per_device,
        mesh=fine,
        in_specs=(block, block, P(), P(), P(), P(), P(SEQ, None), P()),
        out_specs=(block, block, P(), P(), P(), P(), P(SEQ, None), P()),
        check_vma=False,
    )
```

time: 493 us -> 182 us (0.37)
  waiting for transfers between devices: 302 us -> 83.2 us
  blocking collectives: 84.1 us -> 25.2 us
  other arithmetic: 28.7 us -> 4.45 us
  Pallas kernels: 0 us -> 13.6 us
  between operations: 14.4 us -> 0.85 us
  matrix products: 11.9 us -> 0 us
    psum x2 -> x0, waiting for transfers between devices: 181 us -> none  [the longest x1 181 us: per_device(): lax.psum((grad_u, grad_v, grad_o, grad_g, grad_bfly), ('dp', 'seq'))]
    ppermute x12 -> x9, waiting for transfers between devices: 120 us -> 8.05 us  [rotated(): lax.ppermute(value, axis, [(s, (s + k) % n) for s in range(n)])]
    psum x1 -> x0, blocking collectives: 84.1 us -> none  [per_device(): lax.psum((grad_u, grad_v, grad_o, grad_g, grad_bfly), ('dp', 'seq'))]
    all_to_all x0 -> x3, waiting for transfers between devices: none -> 75.1 us  [the longest x1 38.1 us: per_device(): recv = lax.all_to_all(send.reshape(BLOCKS, 3 * PL, BLK), SEQ, 0, 0)]
    all_to_all x0 -> x3, starting transfers between devices: none -> 26.8 us  [the longest x1 13.5 us: per_device(): recv = lax.all_to_all(send.reshape(BLOCKS, 3 * PL, BLK), SEQ, 0, 0)]
    all_to_all x0 -> x1, blocking collectives: none -> 25.2 us  [per_device(): pieces = lax.all_to_all(grads.reshape(64, 4, 8, 128), SAME_GROUP, 0, 0)]
    ppermute x12 -> x9, starting transfers between devices: 36.7 us -> 11.8 us  [rotated(): lax.ppermute(value, axis, [(s, (s + k) % n) for s in range(n)])]
    pallas_call x0 -> x6, Pallas kernels: none -> 13.6 us  [run(): pl.pallas_call(kernel, out_shape=shapes, in_specs=specs, out_specs=[whole...]
  transfers between devices with their start and end apart: 14 -> 12, of which waited for: 11 -> 6; matrix products, arithmetic and copies ran while one was open for 7% -> 3% of each run, Pallas kernels for 0% -> 2%
where the time goes in v1:
time: 182 us; the launch traced here: 180 us
  waiting for transfers between devices  83.2 us (46%)
  starting transfers between devices  38.6 us (21%)
  blocking collectives  25.2 us (14%)
  local copies, waits for them, and re-layouts  14 us (8%)
  Pallas kernels  13.6 us (7%)
  other arithmetic  4.45 us (2%)
    all_to_all x1, waiting for transfers between devices, per_device(): recv = lax.all_to_all(send.reshape(BLOCKS, 3 * PL, BLK), SEQ, 0, 0)  38.1 us
    all_to_all x1, waiting for transfers between devices, per_device(): recv2 = lax.all_to_all(back, SEQ, 0, 0).reshape(8, 4, 2, 2 * PL, BLK)  26.8 us
    all_to_all x1, blocking collectives, per_device(): pieces = lax.all_to_all(grads.reshape(64, 4, 8, 128), SAME_GROUP, 0, 0)  25.2 us
    pallas_call x6, Pallas kernels, run(): pl.pallas_call(kernel, out_shape=shapes, in_specs=specs, out_specs=[whole...  13.6 us
    all_to_all x1, starting transfers between devices, per_device(): recv = lax.all_to_all(send.reshape(BLOCKS, 3 * PL, BLK), SEQ, 0, 0)  13.5 us
    ppermute x9, starting transfers between devices, rotated(): lax.ppermute(value, axis, [(s, (s + k) % n) for s in range(n)])  11.8 us
    unnamed x38, local copies, waits for them, and re-layouts  10.5 us
    all_to_all x1, waiting for transfers between devices, per_device(): lax.all_to_all(jnp.broadcast_to(total[None], (64,) + total.shape), SAME_G...  10.2 us
  transfers between devices with their start and end apart: 12, of which 6 were waited for; matrix products, arithmetic and copies ran while one was open for 3% of the time, Pallas kernels for 2%

profile of v1, /device:TPU:1, one launch (start us, length us, event | category | flops | bytes accessed | tf_op | source)
XLA Modules:
  0.0 180.0 jit_solution(3354514022849927523)
XLA Ops:
  0.6 0.0 copy-start.2
  0.6 1.0 copy-done.2
  1.7 1.0 copy-done.5
  2.7 0.9 copy-done.12
  3.6 0.7 copy-done.14
  4.3 1.6 shard_map.143
  6.0 13.5 %all-to-all-start = ((bf16[64,48,256]{2,1,0:T(8,128)(2,1)}), bf16[64,48,256]{2,1,0:T(8,128)(2,1)}, u32[]{:S(2)}, u32[]{:S(2)}) async-start(bf16[64,48,256]{2,1,0:T(8,128)(2,1)} %bitcast.3), calls=%async_computation | async-start | bytes 3145728 | tf_op jit(solution)/shard_map/all_to_all | solution.py:275
  19.5 0.1 reshape.67
  19.6 0.6 copy.34
  20.3 38.1 %all-to-all-done.recv_ref = bf16[64,48,256]{2,1,0:T(8,128)(2,1)} async-done(((bf16[64,48,256]{2,1,0:T(8,128)(2,1)}), bf16[64,48,256]{2,1,0:T(8,128)(2,1)}, u32[]{:S(2)}, u32[]{:S(2)}) %all-to-all-start) | async-done | bytes 1572896 | tf_op jit(solution)/shard_map/all_to_all | solution.py:275
  58.4 0.7 copy-done.16
  59.1 7.2 %shard_map.144 = (bf16[64,32,256]{2,1,0:T(8,128)(2,1)S(1)}, bf16[32,2,4,8,128]{4,3,2,1,0:T(8,128)(2,1)S(1)}) custom-call(bf16[64,48,256]{2,1,0:T(8,128)(2,1)} %all-to-all-done.recv_ref, f32[24,256]{1,0:T(8,128)S(1)} %bitcast.49, bf16[256,256]{1,0:T(8,128)(2,1)S(1)} %dynamic-slice_bitcast_fusion.2.wu_ref, bf16[256,256]{1,0:T(8,128)(2,1)S(1)} %get-tuple-element.31.wv_ref, ...), custom_call_target="tpu_custom_call" | custom-call | flops 800000000 | bytes 4000000 | tf_op jit(solution)/shard_map/pallas_call | solution.py:245
  66.3 25.2 %all_to_all.20 = bf16[64,4,8,128]{3,2,1,0:T(8,128)(2,1)} all-to-all(bf16[64,4,8,128]{3,2,1,0:T(8,128)(2,1)S(1)} %bitcast.43), channel_id=1, replica_groups=mesh['dp'=4,'z'=8,'y'=4,'c'=2] {'dp','z','c'}, dimensions={0} | all-to-all | bytes 1048576 | tf_op jit(solution)/shard_map/all_to_all | solution.py:303
  91.5 6.2 %all-to-all-start.1 = ((bf16[64,32,256]{2,1,0:T(8,128)(2,1)}), bf16[64,32,256]{2,1,0:T(8,128)(2,1)S(1)}, u32[]{:S(2)}, u32[]{:S(2)}) async-start(bf16[64,32,256]{2,1,0:T(8,128)(2,1)} %copy-done.7), calls=%async_computation.1 | async-start | bytes 2097152 | tf_op jit(solution)/shard_map/all_to_all | solution.py:301
  97.7 1.2 reduce_sum.21
  98.9 26.8 %all-to-all-done.1 = bf16[64,32,256]{2,1,0:T(8,128)(2,1)S(1)} async-done(((bf16[64,32,256]{2,1,0:T(8,128)(2,1)}), bf16[64,32,256]{2,1,0:T(8,128)(2,1)S(1)}, u32[]{:S(2)}, u32[]{:S(2)}) %all-to-all-start.1) | async-done | bytes 1048608 | tf_op jit(solution)/shard_map/all_to_all | solution.py:301
  125.7 0.9 broadcast_in_dim.2
  126.6 7.1 %all-to-all-start.3 = ((bf16[64,4,8,128]{3,2,1,0:T(8,128)(2,1)}), bf16[64,4,8,128]{3,2,1,0:T(8,128)(2,1)}, u32[]{:S(2)}, u32[]{:S(2)}) async-start(bf16[64,4,8,128]{3,2,1,0:T(8,128)(2,1)} %broadcast_in_dim.2), calls=%async_computation.3 | async-start | bytes 1048576 | tf_op jit(solution)/shard_map/all_to_all | solution.py:305
  133.7 1.0 copy-done.6
  134.8 0.7 shard_map.145
  135.5 1.0 copy-done.8
  136.5 1.0 copy-done.10
  137.5 0.3 shard_map.148
  137.8 2.9 %collective-permute-start.8 = (bf16[256,256]{1,0:T(8,128)(2,1)S(1)}, bf16[256,256]{1,0:T(8,128)(2,1)S(1)}, u32[]{:S(2)}, u32[]{:S(2)}) collective-permute-start(bf16[256,256]{1,0:T(8,128)(2,1)S(1)} %shard_map.148), channel_id=1, source_target_pairs={{0,192},{64,0},{128,64},{192,128},{1,193},{65,1},{129,65},{193,129... | collective-permute-start | bytes 393224 | tf_op jit(solution)/shard_map/ppermute | solution.py:261
  140.7 10.2 %all-to-all-done.3 = bf16[64,4,8,128]{3,2,1,0:T(8,128)(2,1)} async-done(((bf16[64,4,8,128]{3,2,1,0:T(8,128)(2,1)}), bf16[64,4,8,128]{3,2,1,0:T(8,128)(2,1)}, u32[]{:S(2)}, u32[]{:S(2)}) %all-to-all-start.3) | async-done | bytes 524320 | tf_op jit(solution)/shard_map/all_to_all | solution.py:305
  150.9 1.0 slice.8
  152.0 0.4 collective-permute-start
  152.4 2.4 %collective-permute-start.1 = (bf16[32,2,3,8,128]{4,3,2,1,0:T(8,128)(2,1)S(1)}, bf16[32,2,3,8,128]{4,3,2,1,0:T(8,128)(2,1)S(1)}, u32[]{:S(2)}, u32[]{:S(2)}) collective-permute-start(bf16[32,2,3,8,128]{4,3,2,1,0:T(8,128)(2,1)S(1)} %bitcast.40), channel_id=1, source_target_pairs={{0,4},{2,6},{4,0},{6,2},{1,5},{3,7},{5,1},{7,3},{8,12},{10,14},{12... | collective-permute-start | bytes 1179656 | tf_op jit(solution)/shard_map/ppermute | solution.py:261
  154.8 1.2 collective-permute-start.2
  155.9 2.9 %collective-permute-start.7 = (bf16[256,256]{1,0:T(8,128)(2,1)S(1)}, bf16[256,256]{1,0:T(8,128)(2,1)S(1)}, u32[]{:S(2)}, u32[]{:S(2)}) collective-permute-start(bf16[256,256]{1,0:T(8,128)(2,1)S(1)} %shard_map.148), channel_id=1, source_target_pairs={{0,128},{64,192},{128,0},{192,64},{1,129},{65,193},{129,1},{193,65... | collective-permute-start | bytes 393224 | tf_op jit(solution)/shard_map/ppermute | solution.py:261
  158.9 0.4 collective-permute-start.6
  159.3 0.7 slice_bitcast_fusion.refs_4_
  160.0 1.2 copy-done.9
  161.2 1.2 copy-done.11
  162.4 1.9 %shard_map.146 = (bf16[256,1024]{1,0:T(8,128)(2,1)}, bf16[256,1024]{1,0:T(8,128)(2,1)}) custom-call(bf16[8,4,2,32,256]{4,3,2,1,0:T(8,128)(2,1)S(1)} %bitcast.33, bf16[256,1024]{1,0:T(8,128)(2,1)S(1)} %bitcast.36, f32[1,1024]{1,0:T(1,128)S(1)} %bitcast.48, f32[256,1024]{1,0:T(8,128)S(1)} %copy-done.9, f32[256,1024]{1,0:T(8,128)S(1)} %copy-done.11, ...), custom_call_target="tpu_custom_call" | custom-call | flops 600000000 | bytes 8000000 | tf_op jit(solution)/shard_map/pallas_call | solution.py:245
  164.3 0.3 collective-permute-start.3
  164.6 1.0 collective-permute-done.6
  165.6 1.1 collective-permute-start.4
  166.7 0.1 pad_maximum_fusion
  166.8 5.6 %collective-permute-done.3.refs_5_ = bf16[6,8,128]{2,1,0:T(8,128)(2,1)S(1)} collective-permute-done((bf16[6,8,128]{2,1,0:T(8,128)(2,1)S(1)}, bf16[6,8,128]{2,1,0:T(8,128)(2,1)S(1)}, u32[]{:S(2)}, u32[]{:S(2)}) %collective-permute-start.3) | collective-permute-done | bytes 12320 | tf_op jit(solution)/shard_map/ppermute | solution.py:261
  172.3 0.3 collective-permute-start.5
  172.6 0.8 add_bitcast_fusion
  173.4 1.5 collective-permute-done.5.refs_7_
  174.9 1.8 %shard_map.147 = (f32[4,256,256]{2,1,0:T(8,128)}, f32[4,256,256]{2,1,0:T(8,128)}, f32[4,256,256]{2,1,0:T(8,128)}, f32[4,3,2,8,128]{4,3,2,1,0:T(8,128)S(1)}) custom-call(s32[1]{0:T(128)} %bitcast.11.mine_ref, bf16[32,2,3,8,128]{4,3,2,1,0:T(8,128)(2,1)S(1)} %bitcast.42, bf16[32,2,3,8,128]{4,3,2,1,0:T(8,128)(2,1)S(1)} %collective-permute-done.refs_1_, ...), custom_call_target="tpu_custom_call" | custom-call | bytes 5000000 | tf_op jit(solution)/shard_map/pallas_call | solution.py:245
  176.7 1.8 %add_reduce_fusion = f32[4,256]{1,0:T(4,128)S(1)} fusion(f32[4,256,256]{2,1,0:T(8,128)} %get-tuple-element.14, bf16[4,256,256]{2,1,0:T(8,128)(2,1)S(1)} %copy-done.1, f32[4,256,256]{2,1,0:T(8,128)} %get-tuple-element.13, bf16[4,256,256]{2,1,0:T(8,128)(2,1)S(1)} %copy-done), kind=kLoop, calls=%fused_computation | loop fusion | flops 1571840 | bytes 3149824 | tf_op jit(solution)/shard_map/reduce_sum | solution.py:336
  178.6 0.6 div.3
  179.2 0.1 copy.29
  179.2 0.8 reshape.75
  (35 shorter events, 0.1 us)
Async XLA Ops:
  0.6 1.0 copy-start.2
  1.7 1.0 copy-start.5
  2.7 0.9 copy-start.12
  3.6 0.7 copy-start.14
  6.0 13.5 %copy-start.17 = (f32[6,2,2,1024]{3,2,1,0:T(2,128)S(1)}, f32[6,2,2,1024]{3,2,1,0:T(2,128)}, u32[]{:S(2)}) copy-start(f32[6,2,2,1024]{3,2,1,0:T(2,128)} %param.15) | copy-start | bytes 294916
  6.0 14.3 %copy-start = (bf16[4,256,256]{2,1,0:T(8,128)(2,1)S(1)}, bf16[4,256,256]{2,1,0:T(8,128)(2,1)}, u32[]{:S(2)}) copy-start(bf16[4,256,256]{2,1,0:T(8,128)(2,1)} %wu_ref.3) | copy-start | bytes 1572868
  6.0 14.3 %copy-start.1 = (bf16[4,256,256]{2,1,0:T(8,128)(2,1)S(1)}, bf16[4,256,256]{2,1,0:T(8,128)(2,1)}, u32[]{:S(2)}) copy-start(bf16[4,256,256]{2,1,0:T(8,128)(2,1)} %wv_ref.3) | copy-start | bytes 1572868
  6.0 14.3 %copy-start.4 = (bf16[4,256,256]{2,1,0:T(8,128)(2,1)S(1)}, bf16[4,256,256]{2,1,0:T(8,128)(2,1)}, u32[]{:S(2)}) copy-start(bf16[4,256,256]{2,1,0:T(8,128)(2,1)} %wo_ref.3) | copy-start | bytes 1572868
  6.0 52.4 %all-to-all-start = ((bf16[64,48,256]{2,1,0:T(8,128)(2,1)}), bf16[64,48,256]{2,1,0:T(8,128)(2,1)}, u32[]{:S(2)}, u32[]{:S(2)}) async-start(bf16[64,48,256]{2,1,0:T(8,128)(2,1)} %bitcast.3), calls=%async_computation | async-start | bytes 3145728 | tf_op jit(solution)/shard_map/all_to_all | solution.py:275
  58.4 0.7 copy-start.16
  66.3 25.2 %copy-start.7 = (bf16[64,32,256]{2,1,0:T(8,128)(2,1)}, bf16[64,32,256]{2,1,0:T(8,128)(2,1)S(1)}, u32[]{:S(2)}) copy-start(bf16[64,32,256]{2,1,0:T(8,128)(2,1)S(1)} %get-tuple-element.19) | copy-start | bytes 3145732
  91.5 34.2 %all-to-all-start.1 = ((bf16[64,32,256]{2,1,0:T(8,128)(2,1)}), bf16[64,32,256]{2,1,0:T(8,128)(2,1)S(1)}, u32[]{:S(2)}, u32[]{:S(2)}) async-start(bf16[64,32,256]{2,1,0:T(8,128)(2,1)} %copy-done.7), calls=%async_computation.1 | async-start | bytes 2097152 | tf_op jit(solution)/shard_map/all_to_all | solution.py:301
  97.7 36.0 %copy-start.3 = (bf16[1,256,1024]{2,1,0:T(8,128)(2,1)S(1)}, bf16[1,256,1024]{2,1,0:T(8,128)(2,1)}, u32[]{:S(2)}) copy-start(bf16[1,256,1024]{2,1,0:T(8,128)(2,1)} %param.8) | copy-start | bytes 1572868
  97.7 36.0 %copy-start.15 = (f32[1024]{0:T(1024)S(1)}, f32[1024]{0:T(1024)}, u32[]{:S(2)}) copy-start(f32[1024]{0:T(1024)} %param.10) | copy-start | bytes 12292
  126.6 24.4 %all-to-all-start.3 = ((bf16[64,4,8,128]{3,2,1,0:T(8,128)(2,1)}), bf16[64,4,8,128]{3,2,1,0:T(8,128)(2,1)}, u32[]{:S(2)}, u32[]{:S(2)}) async-start(bf16[64,4,8,128]{3,2,1,0:T(8,128)(2,1)} %broadcast_in_dim.2), calls=%async_computation.3 | async-start | bytes 1048576 | tf_op jit(solution)/shard_map/all_to_all | solution.py:305
  133.7 1.0 copy-start.6
  135.5 1.0 copy-start.8
  136.5 1.0 copy-start.10
  137.5 22.5 %copy-start.13 = (bf16[256,256]{1,0:T(8,128)(2,1)S(1)}, bf16[256,256]{1,0:T(8,128)(2,1)}, u32[]{:S(2)}) copy-start(bf16[256,256]{1,0:T(8,128)(2,1)} %local_ref.3) | copy-start | bytes 393220
  137.8 21.1 %collective-permute-start.8 = (bf16[256,256]{1,0:T(8,128)(2,1)S(1)}, bf16[256,256]{1,0:T(8,128)(2,1)S(1)}, u32[]{:S(2)}, u32[]{:S(2)}) collective-permute-start(bf16[256,256]{1,0:T(8,128)(2,1)S(1)} %shard_map.148), channel_id=1, source_target_pairs={{0,192},{64,0},{128,64},{192,128},{1,193},{65,1},{129,65},{193,129... | collective-permute-start | bytes 393224 | tf_op jit(solution)/shard_map/ppermute | solution.py:261
  152.0 22.9 %collective-permute-start = (bf16[32,2,3,8,128]{4,3,2,1,0:T(8,128)(2,1)S(1)}, bf16[32,2,3,8,128]{4,3,2,1,0:T(8,128)(2,1)S(1)}, u32[]{:S(2)}, u32[]{:S(2)}) collective-permute-start(bf16[32,2,3,8,128]{4,3,2,1,0:T(8,128)(2,1)S(1)} %bitcast.39), channel_id=1, source_target_pairs={{0,2},{2,4},{4,6},{6,0},{1,3},{3,5},{5,7},{7,1},{8,10},{10,12},{12... | collective-permute-start | bytes 1179656 | tf_op jit(solution)/shard_map/ppermute | solution.py:261
  152.4 22.5 %collective-permute-start.1 = (bf16[32,2,3,8,128]{4,3,2,1,0:T(8,128)(2,1)S(1)}, bf16[32,2,3,8,128]{4,3,2,1,0:T(8,128)(2,1)S(1)}, u32[]{:S(2)}, u32[]{:S(2)}) collective-permute-start(bf16[32,2,3,8,128]{4,3,2,1,0:T(8,128)(2,1)S(1)} %bitcast.40), channel_id=1, source_target_pairs={{0,4},{2,6},{4,0},{6,2},{1,5},{3,7},{5,1},{7,3},{8,12},{10,14},{12... | collective-permute-start | bytes 1179656 | tf_op jit(solution)/shard_map/ppermute | solution.py:261
  154.8 20.1 %collective-permute-start.2 = (bf16[32,2,3,8,128]{4,3,2,1,0:T(8,128)(2,1)S(1)}, bf16[32,2,3,8,128]{4,3,2,1,0:T(8,128)(2,1)S(1)}, u32[]{:S(2)}, u32[]{:S(2)}) collective-permute-start(bf16[32,2,3,8,128]{4,3,2,1,0:T(8,128)(2,1)S(1)} %bitcast.41), channel_id=1, source_target_pairs={{0,6},{2,0},{4,2},{6,4},{1,7},{3,1},{5,3},{7,5},{8,14},{10,8},{12,... | collective-permute-start | bytes 1179656 | tf_op jit(solution)/shard_map/ppermute | solution.py:261
  155.9 8.4 %collective-permute-start.7 = (bf16[256,256]{1,0:T(8,128)(2,1)S(1)}, bf16[256,256]{1,0:T(8,128)(2,1)S(1)}, u32[]{:S(2)}, u32[]{:S(2)}) collective-permute-start(bf16[256,256]{1,0:T(8,128)(2,1)S(1)} %shard_map.148), channel_id=1, source_target_pairs={{0,128},{64,192},{128,0},{192,64},{1,129},{65,193},{129,1},{193,65... | collective-permute-start | bytes 393224 | tf_op jit(solution)/shard_map/ppermute | solution.py:261
  158.9 6.8 %collective-permute-start.6 = (bf16[256,256]{1,0:T(8,128)(2,1)S(1)}, bf16[256,256]{1,0:T(8,128)(2,1)S(1)}, u32[]{:S(2)}, u32[]{:S(2)}) collective-permute-start(bf16[256,256]{1,0:T(8,128)(2,1)S(1)} %shard_map.148), channel_id=1, source_target_pairs={{0,64},{64,128},{128,192},{192,0},{1,65},{65,129},{129,193},{193,1... | collective-permute-start | bytes 393224 | tf_op jit(solution)/shard_map/ppermute | solution.py:261
  160.0 1.2 copy-start.9
  161.2 1.2 copy-start.11
  164.3 8.0 %collective-permute-start.3 = (bf16[6,8,128]{2,1,0:T(8,128)(2,1)S(1)}, bf16[6,8,128]{2,1,0:T(8,128)(2,1)S(1)}, u32[]{:S(2)}, u32[]{:S(2)}) collective-permute-start(bf16[6,8,128]{2,1,0:T(8,128)(2,1)S(1)} %slice_bitcast_fusion.refs_4_), channel_id=1, source_target_pairs={{0,2},{2,4},{4,6},{6,0},{1,3},{3,5},{5,7},{7,1},{8,10},{10,12},{12... | collective-permute-start | bytes 36872 | tf_op jit(solution)/shard_map/ppermute | solution.py:261
  165.6 7.8 %collective-permute-start.4 = (bf16[6,8,128]{2,1,0:T(8,128)(2,1)S(1)}, bf16[6,8,128]{2,1,0:T(8,128)(2,1)S(1)}, u32[]{:S(2)}, u32[]{:S(2)}) collective-permute-start(bf16[6,8,128]{2,1,0:T(8,128)(2,1)S(1)} %slice_bitcast_fusion.refs_4_), channel_id=1, source_target_pairs={{0,4},{2,6},{4,0},{6,2},{1,5},{3,7},{5,1},{7,3},{8,12},{10,14},{12... | collective-permute-start | bytes 36872 | tf_op jit(solution)/shard_map/ppermute | solution.py:261
  172.3 2.5 %collective-permute-start.5 = (bf16[6,8,128]{2,1,0:T(8,128)(2,1)S(1)}, bf16[6,8,128]{2,1,0:T(8,128)(2,1)S(1)}, u32[]{:S(2)}, u32[]{:S(2)}) collective-permute-start(bf16[6,8,128]{2,1,0:T(8,128)(2,1)S(1)} %slice_bitcast_fusion.refs_4_), channel_id=1, source_target_pairs={{0,6},{2,0},{4,2},{6,4},{1,7},{3,1},{5,3},{7,5},{8,14},{10,8},{12,... | collective-permute-start | bytes 36872 | tf_op jit(solution)/shard_map/ppermute | solution.py:261

commit v2 on v1

--- a/solution.py
+++ b/solution.py
@@ -45,14 +45,30 @@
     return lax.rsqrt(total * (1.0 / (GROUPS * BLK)) + 1e-06)
 
 
-def first_kernel(x_ref, cot_ref, gain_ref, local_ref, send_ref):
+def first_kernel(x_hbm, cot_hbm, gain_ref, local_hbm, send_ref, x_ref, cot_ref, local_ref, sems):
+    copies = [
+        pltpu.make_async_copy(src, dst, sems.at[at])
+        for at, (src, dst) in enumerate(
+            ((x_hbm, x_ref), (local_hbm, local_ref), (cot_hbm, cot_ref))
+        )
+    ]
+    for copy in copies:
+        copy.start()
+
+    def put(g, at, value):
+        send_ref[:, g, :, at * PL : (at + 1) * PL, :] = value.reshape(8, 2, PL, BLK)
+
+    copies[0].wait()
     r = inv_rms(x_ref)
+    copies[1].wait()
     local = local_ref[...]
     for g in range(GROUPS):
         xn = (x_ref[:, lanes(g)].astype(F32) * r * gain_ref[:, lanes(g)]).astype(BF)
-        q = mm(local, xn).astype(BF)
-        for at, value in enumerate((q, xn, cot_ref[:, lanes(g)])):
-            send_ref[:, g, :, at * PL : (at + 1) * PL, :] = value.reshape(8, 2, PL, BLK)
+        put(g, 1, xn)
+        put(g, 0, mm(local, xn).astype(BF))
+    copies[2].wait()
+    for g in range(GROUPS):
+        put(g, 2, cot_ref[:, lanes(g)])
 
 
 def side_kernel(x_ref, cot_ref, gain_ref, wu_ref, wv_ref, wo_ref, u_ref, act_ref, dgd_ref):
@@ -78,8 +94,8 @@
 
 
 def mid_kernel(
-    recv_ref, coef_ref, wu_ref, wv_ref, wo_ref,
-    send_ref, grad_ref,
+    place_ref, recv_ref, coef_ref, wu_ref, wv_ref, wo_ref,
+    send_ref, keep_ref, give_ref,
     z0, zs, es, act_s, dgd_s, coef, acc, gsum,
 ):
     for row in range(24):
@@ -177,14 +193,52 @@
         gsum[1] += mm_tn(rows(at, 1), dv)
         gsum[2] += mm_tn(gated, rows(at, 2))
 
-    grad_ref[...] = jnp.zeros_like(grad_ref)
-    for half in range(2):
-        cut = slice(half * 128, (half + 1) * 128)
+    own = place_ref[3]
+    for ref, half in ((keep_ref, own), (give_ref, 1 - own)):
+        cut = pl.ds(pl.multiple_of(half * 128, 128), 128)
         for w in range(3):
-            grad_ref[:, half, w] = gsum[w].reshape(32, 8, BLK)[:, :, cut].astype(BF)
+            ref[:, w * 8 : (w + 1) * 8] = (
+                gsum[w, :, cut].reshape(4, 8, 8, 128).astype(ref.dtype)
+            )
         for part in range(3):
             sums = jnp.sum(acc[part * 8 : (part + 1) * 8, half], axis=1)
-            grad_ref[part, half, 3] = sums.astype(BF)
+            ref[part, 24] = sums.astype(ref.dtype)
+        ref[3, 24] = jnp.zeros((8, 128), ref.dtype)
+
+
+def core_sum_kernel(place_ref, keep_ref, got_ref, own_ref, *give_refs):
+    def piece(k):
+        d = (place_ref[0] + k) & 3
+        return keep_ref[d] + got_ref[d].astype(F32)
+
+    own_ref[...] = piece(0)
+    for k, ref in enumerate(give_refs, 1):
+        ref[...] = piece(k).astype(BF)
+
+
+def dp_sum_kernel(own_ref, *refs):
+    *got, out_ref = refs
+    total = own_ref[...]
+    for ref in got:
+        total = total + ref[...].astype(F32)
+    out_ref[...] = total.astype(BF)
+
+
+def ordered_sum_kernel(axis, place_ref, *refs):
+    *parts, out_ref, held = refs
+    n = len(parts)
+    for k, ref in enumerate(parts):
+        held[(place_ref[axis] + n - k) & (n - 1)] = ref[...]
+    total = held[0].astype(F32)
+    for at in range(1, n):
+        total = total + held[at].astype(F32)
+    out_ref[...] = total.astype(out_ref.dtype)
+
+
+def gather_kernel(place_ref, *refs):
+    *parts, out_ref = refs
+    for k, ref in enumerate(parts):
+        out_ref[(place_ref[0] + 4 - k) & 3] = ref[...]
 
 
 def group_of(recv_ref, g, which):
@@ -220,28 +274,43 @@
         dx_ref[:, lanes(g)] = (r * (scaled_ref[:, lanes(g)] - x * shift)).astype(BF)
 
 
-def place_kernel(mine_ref, *refs):
-    parts, smalls = refs[:GROUPS], refs[GROUPS : 2 * GROUPS]
-    gu_ref, gv_ref, go_ref, bfly_ref = refs[2 * GROUPS :]
+def place_kernel(place_ref, wu_ref, wv_ref, gain_ref, *refs):
+    own, other = refs[:GROUPS], refs[GROUPS : 2 * GROUPS]
+    gu_ref, gv_ref, go_ref, gain_out, bfly_ref = refs[2 * GROUPS :]
     for k in range(GROUPS):
-        g = (mine_ref[0] + GROUPS - k) & (GROUPS - 1)
-        for half in range(2):
+        g = (place_ref[2] + GROUPS - k) & (GROUPS - 1)
+        for parts, half in ((own, place_ref[3]), (other, 1 - place_ref[3])):
+            cut = pl.ds(pl.multiple_of(half * 128, 128), 128)
             for w, out in enumerate((gu_ref, gv_ref, go_ref)):
-                out[g, :, half * 128 : (half + 1) * 128] = (
-                    parts[k][:, half, w].astype(F32).reshape(BLK, 128)
+                out[g, :, cut] = (
+                    parts[k][:, w * 8 : (w + 1) * 8].astype(F32).reshape(BLK, 128)
                 )
+            wide = pl.ds(pl.multiple_of(g * BLK + half * 128, 128), 128)
             for part in range(3):
-                bfly_ref[g, part, half] = smalls[k][2 * part + half].astype(F32)
-
-
-def call(kernel, outs, scratch=(), flops=0, moved=0, vmem=24, smem_first=False):
+                tile = parts[k][part, 24].astype(F32)
+                for s in range(8):
+                    row = part * 8 + s
+                    bfly_ref[row // 4, row // 2 % 2, row % 2 : row % 2 + 1, wide] = tile[s : s + 1]
+    ones = jnp.ones((8, BLK), F32)
+    for g in range(GROUPS):
+        product = gu_ref[g] * wu_ref[g].astype(F32) + gv_ref[g] * wv_ref[g].astype(F32)
+        sums = lax.dot_general(
+            ones, product, (((1,), (1,)), ((), ())),
+            precision=lax.Precision.HIGHEST, preferred_element_type=F32,
+        )
+        gain_out[:, lanes(g)] = sums[:1] / gain_ref[:, lanes(g)]
+
+
+def call(kernel, outs, scratch=(), flops=0, moved=0, vmem=24, smem=(), hbm=()):
     shapes = [jax.ShapeDtypeStruct(shape, dtype) for shape, dtype in outs]
     whole = pl.BlockSpec(memory_space=pltpu.VMEM)
 
     def run(*args):
         specs = [whole] * len(args)
-        if smem_first:
-            specs[0] = pl.BlockSpec(memory_space=pltpu.SMEM)
+        for at in smem:
+            specs[at] = pl.BlockSpec(memory_space=pltpu.SMEM)
+        for at in hbm:
+            specs[at] = pl.BlockSpec(memory_space=pltpu.HBM)
         return pl.pallas_call(
             kernel,
             out_shape=shapes,
@@ -249,17 +318,26 @@
             out_specs=[whole] * len(shapes),
             scratch_shapes=list(scratch),
             compiler_params=pltpu.CompilerParams(vmem_limit_bytes=vmem << 20),
-            cost_estimate=pl.CostEstimate(flops=int(flops), bytes_accessed=int(moved), transcendentals=0),
+            cost_estimate=pl.CostEstimate(
+                flops=int(flops), bytes_accessed=int(moved), transcendentals=0
+            ),
         )(*args)
 
     return run
 
 
-def rotated(value, axis):
+def rotated(values, axis):
     n = lax.axis_size(axis)
+    if not isinstance(values, (list, tuple)):
+        values = [values] * (n - 1)
     return [
-        lax.ppermute(value, axis, [(s, (s + k) % n) for s in range(n)]) for k in range(1, n)
+        lax.ppermute(value, axis, [(s, (s + k) % n) for s in range(n)])
+        for k, value in enumerate(values, 1)
     ]
+
+
+def swapped(value):
+    return lax.ppermute(value, "c", [(0, 1), (1, 0)])
 
 
 def per_device(tokens, cotangent, gain, w_u, w_v, w_o, local_factor, butterfly):
@@ -268,10 +346,22 @@
     gain2 = gain.reshape(1, -1)
     wide = (BLK, GROUPS * BLK)
     y = lax.axis_index("y")
-
-    send = call(first_kernel, [((8, 4, 2, 3 * PL, BLK), BF)], flops=1.4e8, moved=4e6)(
-        x, cot, gain2, local_factor
-    )[0]
+    place = jnp.stack([lax.axis_index(axis) for axis in ("dp", "z", "y", "c")]).astype(jnp.int32)
+
+    send = call(
+        first_kernel,
+        [((8, 4, 2, 3 * PL, BLK), BF)],
+        scratch=[
+            pltpu.VMEM(wide, BF),
+            pltpu.VMEM(wide, BF),
+            pltpu.VMEM((BLK, BLK), BF),
+            pltpu.SemaphoreType.DMA((3,)),
+        ],
+        flops=1.4e8,
+        moved=4e6,
+        hbm=(0, 1, 3),
+        vmem=58,
+    )(x, cot, gain2, local_factor)[0]
     recv = lax.all_to_all(send.reshape(BLOCKS, 3 * PL, BLK), SEQ, 0, 0)
 
     u, act, dgd = call(
@@ -281,9 +371,10 @@
     mine = [lax.dynamic_index_in_dim(w, y, 0, keepdims=False) for w in (w_u, w_v, w_o)]
 
     tiled = (BLOCKS, 2, 2, 8, 128)
-    back, grads = call(
+    quarter = (25, 8, 128)
+    back, keep, give = call(
         mid_kernel,
-        [((BLOCKS, 2 * PL, BLK), BF), ((32, 2, 4, 8, 128), BF)],
+        [((BLOCKS, 2 * PL, BLK), BF), ((4,) + quarter, F32), ((4,) + quarter, BF)],
         scratch=[
             pltpu.VMEM(tiled, F32),
             pltpu.VMEM(tiled, F32),
@@ -296,53 +387,55 @@
         ],
         flops=8e8,
         moved=4e6,
-    )(recv, coef, *mine)
+        smem=(0,),
+    )(place, recv, coef, *mine)
 
     recv2 = lax.all_to_all(back, SEQ, 0, 0).reshape(8, 4, 2, 2 * PL, BLK)
 
-    pieces = lax.all_to_all(grads.reshape(64, 4, 8, 128), SAME_GROUP, 0, 0)
-    total = jnp.sum(pieces.astype(F32), axis=0).astype(BF)
-    shared = lax.all_to_all(
-        jnp.broadcast_to(total[None], (64,) + total.shape), SAME_GROUP, 0, 0
-    )
-    square = shared[:, :3].reshape(32, 2, 3, 8, 128)
-    small = shared[:6, 3]
-    squares = [square] + rotated(square, "y")
-    smalls = [small] + rotated(small, "y")
+    own, *gives = call(
+        core_sum_kernel, [(quarter, F32)] + [(quarter, BF)] * 3, moved=1e6, smem=(0,)
+    )(place, keep, swapped(give))
+    part_z = call(dp_sum_kernel, [(quarter, BF)], moved=3e5)(own, *rotated(gives, "dp"))[0]
+    slice_ = call(
+        functools.partial(ordered_sum_kernel, 1),
+        [(quarter, BF)],
+        scratch=[pltpu.VMEM((8,) + quarter, BF)],
+        moved=5e5,
+        smem=(0,),
+    )(place, part_z, *rotated(part_z, "z"))[0]
+    mine_y = call(gather_kernel, [((4,) + quarter, BF)], moved=4e5, smem=(0,))(
+        place, slice_, *rotated(slice_, "dp")
+    )[0]
+    halves = [mine_y] + rotated(mine_y, "y")
+    others = [swapped(half) for half in halves]
+    shape = (GROUPS, BLK, BLK)
+    gu, gv, go, grad_gain, grad_bfly = call(
+        place_kernel,
+        [(shape, F32)] * 3 + [(gain2.shape, F32), (butterfly.shape, F32)],
+        moved=5e6,
+        smem=(0,),
+    )(place, w_u, w_v, gain2, *halves, *others)
 
     part = call(local_kernel, [((BLK, BLK), BF)], flops=1.3e8, moved=1.2e6)(recv2, u)[0]
-    parts = rotated(part, "dp")
+    grad_local = call(
+        functools.partial(ordered_sum_kernel, 0),
+        [((BLK, BLK), F32)],
+        scratch=[pltpu.VMEM((4, BLK, BLK), BF)],
+        moved=8e5,
+        smem=(0,),
+    )(place, part, *rotated(part, "dp"))[0]
     mixed, dx = call(
         last_kernel, [(wide, BF), (wide, BF)], scratch=[pltpu.VMEM(wide, F32)],
         flops=6e8, moved=8e6,
     )(recv2, x, gain2, act, dgd, w_u, w_v, w_o, local_factor)
 
-    dp = lax.axis_index("dp")
-    stacked = jnp.stack([part] + parts)
-    ordered = [
-        lax.dynamic_index_in_dim(stacked, (dp - s) % 4, 0, keepdims=False).astype(F32)
-        for s in range(4)
-    ]
-    grad_local = (ordered[0] + ordered[1]) + (ordered[2] + ordered[3])
-
-    shape = (GROUPS, BLK, BLK)
-    gu, gv, go, by_group = call(
-        place_kernel,
-        [(shape, F32)] * 3 + [((GROUPS, 3, 2, 8, 128), F32)],
-        moved=5e6,
-        smem_first=True,
-    )(y.reshape(1), *squares, *smalls)
-    grad_gain = (
-        jnp.sum(gu * w_u.astype(F32) + gv * w_v.astype(F32), axis=-1).reshape(-1) / gain
-    )
-    grad_bfly = by_group.transpose(1, 3, 0, 2, 4).reshape(butterfly.shape)
     return (
         mixed.reshape(tokens.shape),
         dx.reshape(tokens.shape),
         gu,
         gv,
         go,
-        grad_gain,
+        grad_gain.reshape(gain.shape),
         grad_local,
         grad_bfly,
     )

time: 182 us -> 151 us (0.83)
  waiting for transfers between devices: 83.2 us -> 53.6 us
  blocking collectives: 25.2 us -> 0 us
  starting transfers between devices: 38.6 us -> 62.2 us
  Pallas kernels: 13.6 us -> 20.5 us
  other arithmetic: 4.45 us -> 0.59 us
    all_to_all x1, waiting for transfers between devices: 26.8 us -> 0.01 us  [per_device(): recv2 = lax.all_to_all(back, SEQ, 0, 0).reshape(8, 4, 2, 2 * PL, BLK)]
    all_to_all x1 -> x0, blocking collectives: 25.2 us -> none  [per_device(): pieces = lax.all_to_all(grads.reshape(64, 4, 8, 128), SAME_GROUP, 0, 0)]
    ppermute x9 -> x19, starting transfers between devices: 11.8 us -> 32.2 us  [rotated(): lax.ppermute(value, axis, [(s, (s + k) % n) for s in range(n)])]
    all_to_all x1 -> x0, waiting for transfers between devices: 10.2 us -> none  [per_device(): lax.all_to_all(jnp.broadcast_to(total[None], (64,) + total.shape), SAME_G...]
    ppermute x0 -> x5, starting transfers between devices: none -> 9.87 us  [swapped(): return lax.ppermute(value, 'c', [(0, 1), (1, 0)])]
    ppermute x9 -> x19, waiting for transfers between devices: 8.05 us -> 16.1 us  [rotated(): lax.ppermute(value, axis, [(s, (s + k) % n) for s in range(n)])]
    all_to_all x1 -> x0, starting transfers between devices: 7.13 us -> none  [per_device(): lax.all_to_all(jnp.broadcast_to(total[None], (64,) + total.shape), SAME_G...]
    pallas_call x6 -> x11, Pallas kernels: 13.6 us -> 20.5 us  [run(): pl.pallas_call(kernel, out_shape=shapes, in_specs=specs, out_specs=[whole...]
  transfers between devices with their start and end apart: 12 -> 26, of which waited for: 6 -> 10; matrix products, arithmetic and copies ran while one was open for 3% -> 2% of each run, Pallas kernels for 2% -> 6%
where the time goes in v2:
time: 151 us; the launch traced here: 150 us
  starting transfers between devices  62.2 us (41%)
  waiting for transfers between devices  53.6 us (35%)
  Pallas kernels  20.5 us (14%)
  local copies, waits for them, and re-layouts  12.4 us (8%)
    all_to_all x1, waiting for transfers between devices, per_device(): recv = lax.all_to_all(send.reshape(BLOCKS, 3 * PL, BLK), SEQ, 0, 0)  36.2 us
    ppermute x19, starting transfers between devices, rotated(): lax.ppermute(value, axis, [(s, (s + k) % n) for s in range(n)])  32.2 us
    pallas_call x11, Pallas kernels, run(): pl.pallas_call(kernel, out_shape=shapes, in_specs=specs, out_specs=[whole...  20.5 us
    ppermute x19, waiting for transfers between devices, rotated(): lax.ppermute(value, axis, [(s, (s + k) % n) for s in range(n)])  16.1 us
    all_to_all x1, starting transfers between devices, per_device(): recv = lax.all_to_all(send.reshape(BLOCKS, 3 * PL, BLK), SEQ, 0, 0)  13.5 us
    unnamed x49, local copies, waits for them, and re-layouts  10.9 us
    ppermute x5, starting transfers between devices, swapped(): return lax.ppermute(value, 'c', [(0, 1), (1, 0)])  9.87 us
    all_to_all x1, starting transfers between devices, per_device(): recv2 = lax.all_to_all(back, SEQ, 0, 0).reshape(8, 4, 2, 2 * PL, BLK)  6.59 us
  transfers between devices with their start and end apart: 26, of which 10 were waited for; matrix products, arithmetic and copies ran while one was open for 2% of the time, Pallas kernels for 6%

profile of v2, /device:TPU:1, one launch (start us, length us, event | category | flops | bytes accessed | tf_op | source)
XLA Modules:
  0.0 150.2 jit_solution(8321395076841712584)
XLA Ops:
  0.6 3.5 %shard_map.143 = bf16[8,4,2,48,256]{4,3,2,1,0:T(8,128)(2,1)} custom-call(bf16[256,1024]{1,0:T(8,128)(2,1)} %bitcast.23, bf16[256,1024]{1,0:T(8,128)(2,1)} %bitcast.26, f32[1,1024]{1,0:T(1,128)} %bitcast.28, bf16[256,256]{1,0:T(8,128)(2,1)} %local_ref.1), custom_call_target="tpu_custom_call" | custom-call | flops 140000000 | bytes 4000000 | tf_op jit(solution)/shard_map/pallas_call | solution.py:314
  4.2 13.5 %all-to-all-start = ((bf16[64,48,256]{2,1,0:T(8,128)(2,1)}), bf16[64,48,256]{2,1,0:T(8,128)(2,1)}, u32[]{:S(2)}, u32[]{:S(2)}) async-start(bf16[64,48,256]{2,1,0:T(8,128)(2,1)} %bitcast.33), calls=%async_computation | async-start | bytes 3145728 | tf_op jit(solution)/shard_map/all_to_all | solution.py:365
  19.7 0.7 dynamic-slice_bitcast_fusion
  20.4 36.2 %all-to-all-done.recv_ref = bf16[64,48,256]{2,1,0:T(8,128)(2,1)} async-done(((bf16[64,48,256]{2,1,0:T(8,128)(2,1)}), bf16[64,48,256]{2,1,0:T(8,128)(2,1)}, u32[]{:S(2)}, u32[]{:S(2)}) %all-to-all-start) | async-done | bytes 1572896 | tf_op jit(solution)/shard_map/all_to_all | solution.py:365
  56.6 0.9 copy-done.13
  57.5 0.9 copy-done.14
  58.4 0.9 copy-done.15
  59.3 0.7 copy-done.18
  60.7 7.1 %shard_map.144 = (bf16[64,32,256]{2,1,0:T(8,128)(2,1)S(1)}, f32[4,25,8,128]{3,2,1,0:T(8,128)S(1)}, bf16[4,25,8,128]{3,2,1,0:T(8,128)(2,1)S(1)}) custom-call(s32[4]{0:T(128)S(1)} %copy-done.19, bf16[64,48,256]{2,1,0:T(8,128)(2,1)} %all-to-all-done.recv_ref, f32[24,256]{1,0:T(8,128)S(1)} %bitcast.32, bf16[256,256]{1,0:T(8,128)(2,1)S(1)} %copy-done.15, ...), custom_call_target="tpu_custom_call" | custom-call | flops 800000000 | bytes 4000000 | tf_op jit(solution)/shard_map/pallas_call | solution.py:314
  67.8 1.0 copy-done.5
  68.8 0.7 copy-done.22
  69.4 6.6 %all-to-all-start.1 = ((bf16[64,32,256]{2,1,0:T(8,128)(2,1)}), bf16[64,32,256]{2,1,0:T(8,128)(2,1)S(1)}, u32[]{:S(2)}, u32[]{:S(2)}) async-start(bf16[64,32,256]{2,1,0:T(8,128)(2,1)} %copy-done.5), calls=%async_computation.1 | async-start | bytes 2097152 | tf_op jit(solution)/shard_map/all_to_all | solution.py:393
  76.6 1.3 collective-permute-done.got_ref
  79.1 1.3 collective-permute-start.1
  80.4 2.4 %collective-permute-start.2 = (bf16[25,8,128]{2,1,0:T(8,128)(2,1)S(1)}, bf16[25,8,128]{2,1,0:T(8,128)(2,1)S(1)}, u32[]{:S(2)}, u32[]{:S(2)}) collective-permute-start(bf16[25,8,128]{2,1,0:T(8,128)(2,1)S(1)} %get-tuple-element.34), channel_id=1, source_target_pairs={{0,128},{64,192},{128,0},{192,64},{1,129},{65,193},{129,1},{193,65... | collective-permute-start | bytes 153608 | tf_op jit(solution)/shard_map/ppermute | solution.py:334
  82.9 1.2 collective-permute-start.3
  84.0 1.5 collective-permute-done.2.refs_1_
  86.2 1.4 collective-permute-start.4
  87.6 2.1 %collective-permute-start.5 = (bf16[25,8,128]{2,1,0:T(8,128)(2,1)S(1)}, bf16[25,8,128]{2,1,0:T(8,128)(2,1)S(1)}, u32[]{:S(2)}, u32[]{:S(2)}) collective-permute-start(bf16[25,8,128]{2,1,0:T(8,128)(2,1)S(1)} %shard_map.148.refs_0_), channel_id=1, source_target_pairs={{0,16},{8,24},{16,32},{24,40},{32,48},{40,56},{48,0},{56,8},{1,17}... | collective-permute-start | bytes 153608 | tf_op jit(solution)/shard_map/ppermute | solution.py:334
  89.7 2.6 %collective-permute-start.6 = (bf16[25,8,128]{2,1,0:T(8,128)(2,1)S(1)}, bf16[25,8,128]{2,1,0:T(8,128)(2,1)S(1)}, u32[]{:S(2)}, u32[]{:S(2)}) collective-permute-start(bf16[25,8,128]{2,1,0:T(8,128)(2,1)S(1)} %shard_map.148.refs_0_), channel_id=1, source_target_pairs={{0,24},{8,32},{16,40},{24,48},{32,56},{40,0},{48,8},{56,16},{1,25}... | collective-permute-start | bytes 153608 | tf_op jit(solution)/shard_map/ppermute | solution.py:334
  92.2 1.9 %collective-permute-start.7 = (bf16[25,8,128]{2,1,0:T(8,128)(2,1)S(1)}, bf16[25,8,128]{2,1,0:T(8,128)(2,1)S(1)}, u32[]{:S(2)}, u32[]{:S(2)}) collective-permute-start(bf16[25,8,128]{2,1,0:T(8,128)(2,1)S(1)} %shard_map.148.refs_0_), channel_id=1, source_target_pairs={{0,32},{8,40},{16,48},{24,56},{32,0},{40,8},{48,16},{56,24},{1,33}... | collective-permute-start | bytes 153608 | tf_op jit(solution)/shard_map/ppermute | solution.py:334
  94.1 2.6 %collective-permute-start.8 = (bf16[25,8,128]{2,1,0:T(8,128)(2,1)S(1)}, bf16[25,8,128]{2,1,0:T(8,128)(2,1)S(1)}, u32[]{:S(2)}, u32[]{:S(2)}) collective-permute-start(bf16[25,8,128]{2,1,0:T(8,128)(2,1)S(1)} %shard_map.148.refs_0_), channel_id=1, source_target_pairs={{0,40},{8,48},{16,56},{24,0},{32,8},{40,16},{48,24},{56,32},{1,41}... | collective-permute-start | bytes 153608 | tf_op jit(solution)/shard_map/ppermute | solution.py:334
  96.8 5.6 %collective-permute-done.4.refs_1_ = bf16[25,8,128]{2,1,0:T(8,128)(2,1)S(1)} collective-permute-done((bf16[25,8,128]{2,1,0:T(8,128)(2,1)S(1)}, bf16[25,8,128]{2,1,0:T(8,128)(2,1)S(1)}, u32[]{:S(2)}, u32[]{:S(2)}) %collective-permute-start.4) | collective-permute-done | bytes 51232 | tf_op jit(solution)/shard_map/ppermute | solution.py:334
  102.3 2.0 %collective-permute-start.9 = (bf16[25,8,128]{2,1,0:T(8,128)(2,1)S(1)}, bf16[25,8,128]{2,1,0:T(8,128)(2,1)S(1)}, u32[]{:S(2)}, u32[]{:S(2)}) collective-permute-start(bf16[25,8,128]{2,1,0:T(8,128)(2,1)S(1)} %shard_map.148.refs_0_), channel_id=1, source_target_pairs={{0,48},{8,56},{16,0},{24,8},{32,16},{40,24},{48,32},{56,40},{1,49}... | collective-permute-start | bytes 153608 | tf_op jit(solution)/shard_map/ppermute | solution.py:334
  104.3 0.9 collective-permute-done.5.refs_2_
  105.2 1.1 collective-permute-start.10
  106.3 1.6 %collective-permute-done.6.refs_3_ = bf16[25,8,128]{2,1,0:T(8,128)(2,1)S(1)} collective-permute-done((bf16[25,8,128]{2,1,0:T(8,128)(2,1)S(1)}, bf16[25,8,128]{2,1,0:T(8,128)(2,1)S(1)}, u32[]{:S(2)}, u32[]{:S(2)}) %collective-permute-start.6) | collective-permute-done | bytes 51232 | tf_op jit(solution)/shard_map/ppermute | solution.py:334
  107.9 3.8 %collective-permute-done.7.refs_4_ = bf16[25,8,128]{2,1,0:T(8,128)(2,1)S(1)} collective-permute-done((bf16[25,8,128]{2,1,0:T(8,128)(2,1)S(1)}, bf16[25,8,128]{2,1,0:T(8,128)(2,1)S(1)}, u32[]{:S(2)}, u32[]{:S(2)}) %collective-permute-start.7) | collective-permute-done | bytes 51232 | tf_op jit(solution)/shard_map/ppermute | solution.py:334
  112.4 1.5 collective-permute-start.11
  113.8 2.5 %collective-permute-start.12 = (bf16[25,8,128]{2,1,0:T(8,128)(2,1)S(1)}, bf16[25,8,128]{2,1,0:T(8,128)(2,1)S(1)}, u32[]{:S(2)}, u32[]{:S(2)}) collective-permute-start(bf16[25,8,128]{2,1,0:T(8,128)(2,1)S(1)} %shard_map.149.refs_0_), channel_id=1, source_target_pairs={{0,128},{64,192},{128,0},{192,64},{1,129},{65,193},{129,1},{193,65... | collective-permute-start | bytes 153608 | tf_op jit(solution)/shard_map/ppermute | solution.py:334
  116.3 1.2 collective-permute-start.13
  117.4 0.9 collective-permute-done.12.refs_2_
  118.3 1.2 collective-permute-done.13.refs_3_
  120.1 1.3 collective-permute-start.14
  121.4 2.5 %collective-permute-start.15 = (bf16[4,25,8,128]{3,2,1,0:T(8,128)(2,1)S(1)}, bf16[4,25,8,128]{3,2,1,0:T(8,128)(2,1)}, u32[]{:S(2)}, u32[]{:S(2)}) collective-permute-start(bf16[4,25,8,128]{3,2,1,0:T(8,128)(2,1)S(1)} %shard_map.150.refs_0_), channel_id=1, source_target_pairs={{0,4},{2,6},{4,0},{6,2},{1,5},{3,7},{5,1},{7,3},{8,12},{10,14},{12... | collective-permute-start | bytes 614408 | tf_op jit(solution)/shard_map/ppermute | solution.py:334
  123.9 1.2 collective-permute-start.16
  125.1 4.6 %collective-permute-start.17 = (bf16[4,25,8,128]{3,2,1,0:T(8,128)(2,1)S(1)}, bf16[4,25,8,128]{3,2,1,0:T(8,128)(2,1)}, u32[]{:S(2)}, u32[]{:S(2)}) collective-permute-start(bf16[4,25,8,128]{3,2,1,0:T(8,128)(2,1)S(1)} %shard_map.150.refs_0_), channel_id=1, source_target_pairs={{0,1},{1,0},{2,3},{3,2},{4,5},{5,4},{6,7},{7,6},{8,9},{9,8},{10,11... | collective-permute-start | bytes 614408 | tf_op jit(solution)/shard_map/ppermute | solution.py:340
  129.7 2.5 %collective-permute-start.18 = (bf16[4,25,8,128]{3,2,1,0:T(8,128)(2,1)S(1)}, bf16[4,25,8,128]{3,2,1,0:T(8,128)(2,1)}, u32[]{:S(2)}, u32[]{:S(2)}) collective-permute-start(bf16[4,25,8,128]{3,2,1,0:T(8,128)(2,1)S(1)} %collective-permute-done.14.refs_1_), channel_id=1, source_target_pairs={{0,1},{1,0},{2,3},{3,2},{4,5},{5,4},{6,7},{7,6},{8,9},{9,8},{10,11... | collective-permute-start | bytes 614408 | tf_op jit(solution)/shard_map/ppermute | solution.py:340
  132.2 2.3 %collective-permute-start.19 = (bf16[4,25,8,128]{3,2,1,0:T(8,128)(2,1)}, bf16[4,25,8,128]{3,2,1,0:T(8,128)(2,1)}, u32[]{:S(2)}, u32[]{:S(2)}) collective-permute-start(bf16[4,25,8,128]{3,2,1,0:T(8,128)(2,1)} %collective-permute-done.15.refs_2_), channel_id=1, source_target_pairs={{0,1},{1,0},{2,3},{3,2},{4,5},{5,4},{6,7},{7,6},{8,9},{9,8},{10,11... | collective-permute-start | bytes 614408 | tf_op jit(solution)/shard_map/ppermute | solution.py:340
  134.5 0.7 shard_map.145
  135.2 1.0 copy-done.6
  136.2 1.0 copy-done.8
  137.2 0.8 copy-done.10
  138.0 1.1 copy-done.11
  139.6 3.3 %collective-permute-start.22 = (bf16[256,256]{1,0:T(8,128)(2,1)S(1)}, bf16[256,256]{1,0:T(8,128)(2,1)S(1)}, u32[]{:S(2)}, u32[]{:S(2)}) collective-permute-start(bf16[256,256]{1,0:T(8,128)(2,1)S(1)} %shard_map.152.refs_0_), channel_id=1, source_target_pairs={{0,128},{64,192},{128,0},{192,64},{1,129},{65,193},{129,1},{193,65... | collective-permute-start | bytes 393224 | tf_op jit(solution)/shard_map/ppermute | solution.py:334
  143.1 3.8 %shard_map.151 = (f32[4,256,256]{2,1,0:T(8,128)}, f32[4,256,256]{2,1,0:T(8,128)}, f32[4,256,256]{2,1,0:T(8,128)}, f32[1,1024]{1,0:T(1,128)}, f32[6,2,2,1024]{3,2,1,0:T(2,128)}) custom-call(s32[4]{0:T(128)S(1)} %copy-done.21, bf16[4,256,256]{2,1,0:T(8,128)(2,1)S(1)} %copy-done, bf16[4,256,256]{2,1,0:T(8,128)(2,1)S(1)} %copy-done.1, f32[1,1024]{1,0:T(1,128)S(1)} %bitcast.30, ...), custom_call_target="tpu_custom_call" | custom-call | bytes 5000000 | tf_op jit(solution)/shard_map/pallas_call | solution.py:314
  146.8 1.9 %shard_map.146 = (bf16[256,1024]{1,0:T(8,128)(2,1)}, bf16[256,1024]{1,0:T(8,128)(2,1)}) custom-call(bf16[8,4,2,32,256]{4,3,2,1,0:T(8,128)(2,1)S(1)} %bitcast.22, bf16[256,1024]{1,0:T(8,128)(2,1)S(1)} %bitcast.25, f32[1,1024]{1,0:T(1,128)S(1)} %bitcast.31, f32[256,1024]{1,0:T(8,128)S(1)} %copy-done.7, f32[256,1024]{1,0:T(8,128)S(1)} %copy-done.9, ...), custom_call_target="tpu_custom_call" | custom-call | flops 600000000 | bytes 8000000 | tf_op jit(solution)/shard_map/pallas_call | solution.py:314
  148.8 1.4 shard_map.153
  (69 shorter events, 7.0 us)
Async XLA Ops:
  4.1 13.5 %copy-start.23 = (f32[6,2,2,1024]{3,2,1,0:T(2,128)S(1)}, f32[6,2,2,1024]{3,2,1,0:T(2,128)}, u32[]{:S(2)}) copy-start(f32[6,2,2,1024]{3,2,1,0:T(2,128)} %param.15) | copy-start | bytes 294916
  4.1 14.9 %copy-start = (bf16[4,256,256]{2,1,0:T(8,128)(2,1)S(1)}, bf16[4,256,256]{2,1,0:T(8,128)(2,1)}, u32[]{:S(2)}) copy-start(bf16[4,256,256]{2,1,0:T(8,128)(2,1)} %wu_ref.5) | copy-start | bytes 1572868
  4.2 15.5 %copy-start.1 = (bf16[4,256,256]{2,1,0:T(8,128)(2,1)S(1)}, bf16[4,256,256]{2,1,0:T(8,128)(2,1)}, u32[]{:S(2)}) copy-start(bf16[4,256,256]{2,1,0:T(8,128)(2,1)} %wv_ref.5) | copy-start | bytes 1572868
  4.2 15.5 %copy-start.3 = (bf16[4,256,256]{2,1,0:T(8,128)(2,1)S(1)}, bf16[4,256,256]{2,1,0:T(8,128)(2,1)}, u32[]{:S(2)}) copy-start(bf16[4,256,256]{2,1,0:T(8,128)(2,1)} %wo_ref.3) | copy-start | bytes 1572868
  4.2 52.4 %all-to-all-start = ((bf16[64,48,256]{2,1,0:T(8,128)(2,1)}), bf16[64,48,256]{2,1,0:T(8,128)(2,1)}, u32[]{:S(2)}, u32[]{:S(2)}) async-start(bf16[64,48,256]{2,1,0:T(8,128)(2,1)} %bitcast.33), calls=%async_computation | async-start | bytes 3145728 | tf_op jit(solution)/shard_map/all_to_all | solution.py:365
  56.6 0.9 copy-start.13
  57.5 0.9 copy-start.14
  58.4 0.9 copy-start.15
  59.3 0.7 copy-start.18
  67.8 1.0 copy-start.5
  68.8 0.7 copy-start.22
  69.4 65.0 %copy-start.2 = (bf16[1,256,1024]{2,1,0:T(8,128)(2,1)S(1)}, bf16[1,256,1024]{2,1,0:T(8,128)(2,1)}, u32[]{:S(2)}) copy-start(bf16[1,256,1024]{2,1,0:T(8,128)(2,1)} %param.8) | copy-start | bytes 1572868
  69.4 68.6 %all-to-all-start.1 = ((bf16[64,32,256]{2,1,0:T(8,128)(2,1)}), bf16[64,32,256]{2,1,0:T(8,128)(2,1)S(1)}, u32[]{:S(2)}, u32[]{:S(2)}) async-start(bf16[64,32,256]{2,1,0:T(8,128)(2,1)} %copy-done.5), calls=%async_computation.1 | async-start | bytes 2097152 | tf_op jit(solution)/shard_map/all_to_all | solution.py:393
  76.0 58.4 %copy-start.4 = (bf16[1,256,1024]{2,1,0:T(8,128)(2,1)S(1)}, bf16[1,256,1024]{2,1,0:T(8,128)(2,1)}, u32[]{:S(2)}) copy-start(bf16[1,256,1024]{2,1,0:T(8,128)(2,1)} %param.9) | copy-start | bytes 1572868
  76.0 58.4 %copy-start.16 = (f32[1024]{0:T(1024)S(1)}, f32[1024]{0:T(1024)}, u32[]{:S(2)}) copy-start(f32[1024]{0:T(1024)} %param.10) | copy-start | bytes 12292
  76.1 1.8 %collective-permute-start = (bf16[4,25,8,128]{3,2,1,0:T(8,128)(2,1)}, bf16[4,25,8,128]{3,2,1,0:T(8,128)(2,1)S(1)}, u32[]{:S(2)}, u32[]{:S(2)}) collective-permute-start(bf16[4,25,8,128]{3,2,1,0:T(8,128)(2,1)} %copy-done.22), channel_id=1, source_target_pairs={{0,1},{1,0},{2,3},{3,2},{4,5},{5,4},{6,7},{7,6},{8,9},{9,8},{10,11... | collective-permute-start | bytes 614408 | tf_op jit(solution)/shard_map/ppermute | solution.py:340
  79.1 4.9 %collective-permute-start.1 = (bf16[25,8,128]{2,1,0:T(8,128)(2,1)S(1)}, bf16[25,8,128]{2,1,0:T(8,128)(2,1)S(1)}, u32[]{:S(2)}, u32[]{:S(2)}) collective-permute-start(bf16[25,8,128]{2,1,0:T(8,128)(2,1)S(1)} %get-tuple-element.33), channel_id=1, source_target_pairs={{0,64},{64,128},{128,192},{192,0},{1,65},{65,129},{129,193},{193,1... | collective-permute-start | bytes 153608 | tf_op jit(solution)/shard_map/ppermute | solution.py:334
  80.4 5.1 %collective-permute-start.2 = (bf16[25,8,128]{2,1,0:T(8,128)(2,1)S(1)}, bf16[25,8,128]{2,1,0:T(8,128)(2,1)S(1)}, u32[]{:S(2)}, u32[]{:S(2)}) collective-permute-start(bf16[25,8,128]{2,1,0:T(8,128)(2,1)S(1)} %get-tuple-element.34), channel_id=1, source_target_pairs={{0,128},{64,192},{128,0},{192,64},{1,129},{65,193},{129,1},{193,65... | collective-permute-start | bytes 153608 | tf_op jit(solution)/shard_map/ppermute | solution.py:334
  82.9 3.3 %collective-permute-start.3 = (bf16[25,8,128]{2,1,0:T(8,128)(2,1)S(1)}, bf16[25,8,128]{2,1,0:T(8,128)(2,1)S(1)}, u32[]{:S(2)}, u32[]{:S(2)}) collective-permute-start(bf16[25,8,128]{2,1,0:T(8,128)(2,1)S(1)} %get-tuple-element.35), channel_id=1, source_target_pairs={{0,192},{64,0},{128,64},{192,128},{1,193},{65,1},{129,65},{193,129... | collective-permute-start | bytes 153608 | tf_op jit(solution)/shard_map/ppermute | solution.py:334
  86.2 16.1 %collective-permute-start.4 = (bf16[25,8,128]{2,1,0:T(8,128)(2,1)S(1)}, bf16[25,8,128]{2,1,0:T(8,128)(2,1)S(1)}, u32[]{:S(2)}, u32[]{:S(2)}) collective-permute-start(bf16[25,8,128]{2,1,0:T(8,128)(2,1)S(1)} %shard_map.148.refs_0_), channel_id=1, source_target_pairs={{0,8},{8,16},{16,24},{24,32},{32,40},{40,48},{48,56},{56,0},{1,9},... | collective-permute-start | bytes 153608 | tf_op jit(solution)/shard_map/ppermute | solution.py:334
  87.6 17.6 %collective-permute-start.5 = (bf16[25,8,128]{2,1,0:T(8,128)(2,1)S(1)}, bf16[25,8,128]{2,1,0:T(8,128)(2,1)S(1)}, u32[]{:S(2)}, u32[]{:S(2)}) collective-permute-start(bf16[25,8,128]{2,1,0:T(8,128)(2,1)S(1)} %shard_map.148.refs_0_), channel_id=1, source_target_pairs={{0,16},{8,24},{16,32},{24,40},{32,48},{40,56},{48,0},{56,8},{1,17}... | collective-permute-start | bytes 153608 | tf_op jit(solution)/shard_map/ppermute | solution.py:334
  89.7 18.2 %collective-permute-start.6 = (bf16[25,8,128]{2,1,0:T(8,128)(2,1)S(1)}, bf16[25,8,128]{2,1,0:T(8,128)(2,1)S(1)}, u32[]{:S(2)}, u32[]{:S(2)}) collective-permute-start(bf16[25,8,128]{2,1,0:T(8,128)(2,1)S(1)} %shard_map.148.refs_0_), channel_id=1, source_target_pairs={{0,24},{8,32},{16,40},{24,48},{32,56},{40,0},{48,8},{56,16},{1,25}... | collective-permute-start | bytes 153608 | tf_op jit(solution)/shard_map/ppermute | solution.py:334
  92.2 19.5 %collective-permute-start.7 = (bf16[25,8,128]{2,1,0:T(8,128)(2,1)S(1)}, bf16[25,8,128]{2,1,0:T(8,128)(2,1)S(1)}, u32[]{:S(2)}, u32[]{:S(2)}) collective-permute-start(bf16[25,8,128]{2,1,0:T(8,128)(2,1)S(1)} %shard_map.148.refs_0_), channel_id=1, source_target_pairs={{0,32},{8,40},{16,48},{24,56},{32,0},{40,8},{48,16},{56,24},{1,33}... | collective-permute-start | bytes 153608 | tf_op jit(solution)/shard_map/ppermute | solution.py:334
  94.1 17.6 %collective-permute-start.8 = (bf16[25,8,128]{2,1,0:T(8,128)(2,1)S(1)}, bf16[25,8,128]{2,1,0:T(8,128)(2,1)S(1)}, u32[]{:S(2)}, u32[]{:S(2)}) collective-permute-start(bf16[25,8,128]{2,1,0:T(8,128)(2,1)S(1)} %shard_map.148.refs_0_), channel_id=1, source_target_pairs={{0,40},{8,48},{16,56},{24,0},{32,8},{40,16},{48,24},{56,32},{1,41}... | collective-permute-start | bytes 153608 | tf_op jit(solution)/shard_map/ppermute | solution.py:334
  102.3 9.4 %collective-permute-start.9 = (bf16[25,8,128]{2,1,0:T(8,128)(2,1)S(1)}, bf16[25,8,128]{2,1,0:T(8,128)(2,1)S(1)}, u32[]{:S(2)}, u32[]{:S(2)}) collective-permute-start(bf16[25,8,128]{2,1,0:T(8,128)(2,1)S(1)} %shard_map.148.refs_0_), channel_id=1, source_target_pairs={{0,48},{8,56},{16,0},{24,8},{32,16},{40,24},{48,32},{56,40},{1,49}... | collective-permute-start | bytes 153608 | tf_op jit(solution)/shard_map/ppermute | solution.py:334
  105.2 6.6 %collective-permute-start.10 = (bf16[25,8,128]{2,1,0:T(8,128)(2,1)S(1)}, bf16[25,8,128]{2,1,0:T(8,128)(2,1)S(1)}, u32[]{:S(2)}, u32[]{:S(2)}) collective-permute-start(bf16[25,8,128]{2,1,0:T(8,128)(2,1)S(1)} %shard_map.148.refs_0_), channel_id=1, source_target_pairs={{0,56},{8,0},{16,8},{24,16},{32,24},{40,32},{48,40},{56,48},{1,57}... | collective-permute-start | bytes 153608 | tf_op jit(solution)/shard_map/ppermute | solution.py:334
  112.4 5.1 %collective-permute-start.11 = (bf16[25,8,128]{2,1,0:T(8,128)(2,1)S(1)}, bf16[25,8,128]{2,1,0:T(8,128)(2,1)S(1)}, u32[]{:S(2)}, u32[]{:S(2)}) collective-permute-start(bf16[25,8,128]{2,1,0:T(8,128)(2,1)S(1)} %shard_map.149.refs_0_), channel_id=1, source_target_pairs={{0,64},{64,128},{128,192},{192,0},{1,65},{65,129},{129,193},{193,1... | collective-permute-start | bytes 153608 | tf_op jit(solution)/shard_map/ppermute | solution.py:334
  113.8 4.5 %collective-permute-start.12 = (bf16[25,8,128]{2,1,0:T(8,128)(2,1)S(1)}, bf16[25,8,128]{2,1,0:T(8,128)(2,1)S(1)}, u32[]{:S(2)}, u32[]{:S(2)}) collective-permute-start(bf16[25,8,128]{2,1,0:T(8,128)(2,1)S(1)} %shard_map.149.refs_0_), channel_id=1, source_target_pairs={{0,128},{64,192},{128,0},{192,64},{1,129},{65,193},{129,1},{193,65... | collective-permute-start | bytes 153608 | tf_op jit(solution)/shard_map/ppermute | solution.py:334
  116.3 3.3 %collective-permute-start.13 = (bf16[25,8,128]{2,1,0:T(8,128)(2,1)S(1)}, bf16[25,8,128]{2,1,0:T(8,128)(2,1)S(1)}, u32[]{:S(2)}, u32[]{:S(2)}) collective-permute-start(bf16[25,8,128]{2,1,0:T(8,128)(2,1)S(1)} %shard_map.149.refs_0_), channel_id=1, source_target_pairs={{0,192},{64,0},{128,64},{192,128},{1,193},{65,1},{129,65},{193,129... | collective-permute-start | bytes 153608 | tf_op jit(solution)/shard_map/ppermute | solution.py:334
  120.1 9.6 %collective-permute-start.14 = (bf16[4,25,8,128]{3,2,1,0:T(8,128)(2,1)S(1)}, bf16[4,25,8,128]{3,2,1,0:T(8,128)(2,1)S(1)}, u32[]{:S(2)}, u32[]{:S(2)}) collective-permute-start(bf16[4,25,8,128]{3,2,1,0:T(8,128)(2,1)S(1)} %shard_map.150.refs_0_), channel_id=1, source_target_pairs={{0,2},{2,4},{4,6},{6,0},{1,3},{3,5},{5,7},{7,1},{8,10},{10,12},{12... | collective-permute-start | bytes 614408 | tf_op jit(solution)/shard_map/ppermute | solution.py:334
  121.4 10.7 %collective-permute-start.15 = (bf16[4,25,8,128]{3,2,1,0:T(8,128)(2,1)S(1)}, bf16[4,25,8,128]{3,2,1,0:T(8,128)(2,1)}, u32[]{:S(2)}, u32[]{:S(2)}) collective-permute-start(bf16[4,25,8,128]{3,2,1,0:T(8,128)(2,1)S(1)} %shard_map.150.refs_0_), channel_id=1, source_target_pairs={{0,4},{2,6},{4,0},{6,2},{1,5},{3,7},{5,1},{7,3},{8,12},{10,14},{12... | collective-permute-start | bytes 614408 | tf_op jit(solution)/shard_map/ppermute | solution.py:334
  123.9 10.5 %collective-permute-start.16 = (bf16[4,25,8,128]{3,2,1,0:T(8,128)(2,1)S(1)}, bf16[4,25,8,128]{3,2,1,0:T(8,128)(2,1)}, u32[]{:S(2)}, u32[]{:S(2)}) collective-permute-start(bf16[4,25,8,128]{3,2,1,0:T(8,128)(2,1)S(1)} %shard_map.150.refs_0_), channel_id=1, source_target_pairs={{0,6},{2,0},{4,2},{6,4},{1,7},{3,1},{5,3},{7,5},{8,14},{10,8},{12,... | collective-permute-start | bytes 614408 | tf_op jit(solution)/shard_map/ppermute | solution.py:334
  125.1 14.4 %collective-permute-start.17 = (bf16[4,25,8,128]{3,2,1,0:T(8,128)(2,1)S(1)}, bf16[4,25,8,128]{3,2,1,0:T(8,128)(2,1)}, u32[]{:S(2)}, u32[]{:S(2)}) collective-permute-start(bf16[4,25,8,128]{3,2,1,0:T(8,128)(2,1)S(1)} %shard_map.150.refs_0_), channel_id=1, source_target_pairs={{0,1},{1,0},{2,3},{3,2},{4,5},{5,4},{6,7},{7,6},{8,9},{9,8},{10,11... | collective-permute-start | bytes 614408 | tf_op jit(solution)/shard_map/ppermute | solution.py:340
  129.7 13.2 %collective-permute-start.18 = (bf16[4,25,8,128]{3,2,1,0:T(8,128)(2,1)S(1)}, bf16[4,25,8,128]{3,2,1,0:T(8,128)(2,1)}, u32[]{:S(2)}, u32[]{:S(2)}) collective-permute-start(bf16[4,25,8,128]{3,2,1,0:T(8,128)(2,1)S(1)} %collective-permute-done.14.refs_1_), channel_id=1, source_target_pairs={{0,1},{1,0},{2,3},{3,2},{4,5},{5,4},{6,7},{7,6},{8,9},{9,8},{10,11... | collective-permute-start | bytes 614408 | tf_op jit(solution)/shard_map/ppermute | solution.py:340
  132.2 10.9 %collective-permute-start.19 = (bf16[4,25,8,128]{3,2,1,0:T(8,128)(2,1)}, bf16[4,25,8,128]{3,2,1,0:T(8,128)(2,1)}, u32[]{:S(2)}, u32[]{:S(2)}) collective-permute-start(bf16[4,25,8,128]{3,2,1,0:T(8,128)(2,1)} %collective-permute-done.15.refs_2_), channel_id=1, source_target_pairs={{0,1},{1,0},{2,3},{3,2},{4,5},{5,4},{6,7},{7,6},{8,9},{9,8},{10,11... | collective-permute-start | bytes 614408 | tf_op jit(solution)/shard_map/ppermute | solution.py:340
  134.5 8.6 %collective-permute-start.20 = (bf16[4,25,8,128]{3,2,1,0:T(8,128)(2,1)}, bf16[4,25,8,128]{3,2,1,0:T(8,128)(2,1)}, u32[]{:S(2)}, u32[]{:S(2)}) collective-permute-start(bf16[4,25,8,128]{3,2,1,0:T(8,128)(2,1)} %collective-permute-done.16.refs_3_), channel_id=1, source_target_pairs={{0,1},{1,0},{2,3},{3,2},{4,5},{5,4},{6,7},{7,6},{8,9},{9,8},{10,11... | collective-permute-start | bytes 614408 | tf_op jit(solution)/shard_map/ppermute | solution.py:340
  135.2 1.0 copy-start.6
  136.2 1.0 copy-start.8
  137.2 0.8 copy-start.10
  138.0 5.0 %copy-start.21 = (s32[4]{0:T(128)S(1)}, s32[4]{0:T(128)}, u32[]{:S(2)}) copy-start(s32[4]{0:T(128)} %pad_add_fusion.place_ref) | copy-start | bytes 52
  138.0 1.1 copy-start.11
  139.1 4.0 %copy-start.17 = (f32[1024]{0:T(1024)S(1)}, f32[1024]{0:T(1024)}, u32[]{:S(2)}) copy-start(f32[1024]{0:T(1024)} %param.10) | copy-start | bytes 12292
  139.4 7.4 %copy-start.7 = (f32[256,1024]{1,0:T(8,128)S(1)}, f32[256,1024]{1,0:T(8,128)}, u32[]{:S(2)}) copy-start(f32[256,1024]{1,0:T(8,128)} %copy-done.6) | copy-start | bytes 3145732
  139.4 7.4 %copy-start.9 = (f32[256,1024]{1,0:T(8,128)S(1)}, f32[256,1024]{1,0:T(8,128)}, u32[]{:S(2)}) copy-start(f32[256,1024]{1,0:T(8,128)} %copy-done.8) | copy-start | bytes 3145732
  139.4 7.4 %copy-start.12 = (bf16[256,256]{1,0:T(8,128)(2,1)S(1)}, bf16[256,256]{1,0:T(8,128)(2,1)}, u32[]{:S(2)}) copy-start(bf16[256,256]{1,0:T(8,128)(2,1)} %local_ref.1) | copy-start | bytes 393220
  139.5 9.3 %collective-permute-start.21 = (bf16[256,256]{1,0:T(8,128)(2,1)S(1)}, bf16[256,256]{1,0:T(8,128)(2,1)S(1)}, u32[]{:S(2)}, u32[]{:S(2)}) collective-permute-start(bf16[256,256]{1,0:T(8,128)(2,1)S(1)} %shard_map.152.refs_0_), channel_id=1, source_target_pairs={{0,64},{64,128},{128,192},{192,0},{1,65},{65,129},{129,193},{193,1... | collective-permute-start | bytes 393224 | tf_op jit(solution)/shard_map/ppermute | solution.py:334
  139.6 9.2 %collective-permute-start.22 = (bf16[256,256]{1,0:T(8,128)(2,1)S(1)}, bf16[256,256]{1,0:T(8,128)(2,1)S(1)}, u32[]{:S(2)}, u32[]{:S(2)}) collective-permute-start(bf16[256,256]{1,0:T(8,128)(2,1)S(1)} %shard_map.152.refs_0_), channel_id=1, source_target_pairs={{0,128},{64,192},{128,0},{192,64},{1,129},{65,193},{129,1},{193,65... | collective-permute-start | bytes 393224 | tf_op jit(solution)/shard_map/ppermute | solution.py:334
  142.9 5.9 %collective-permute-start.23 = (bf16[256,256]{1,0:T(8,128)(2,1)S(1)}, bf16[256,256]{1,0:T(8,128)(2,1)S(1)}, u32[]{:S(2)}, u32[]{:S(2)}) collective-permute-start(bf16[256,256]{1,0:T(8,128)(2,1)S(1)} %shard_map.152.refs_0_), channel_id=1, source_target_pairs={{0,192},{64,0},{128,64},{192,128},{1,193},{65,1},{129,65},{193,129... | collective-permute-start | bytes 393224 | tf_op jit(solution)/shard_map/ppermute | solution.py:334
  (2 other events, 1.3 us)

commit v3 on v2

--- a/solution.py
+++ b/solution.py
@@ -94,23 +94,49 @@
 
 
 def mid_kernel(
-    place_ref, recv_ref, coef_ref, wu_ref, wv_ref, wo_ref,
-    send_ref, keep_ref, give_ref,
-    z0, zs, es, act_s, dgd_s, coef, acc, gsum,
+    place_ref, recv_hbm, coef_hbm, wu_hbm, wv_hbm, wo_hbm,
+    send_hbm, keep_ref, give_ref,
+    recv_ref, send_ref, coef_ref, wu_ref, wv_ref, wo_ref,
+    z0, zs, es, act_s, dgd_s, coef, acc, gsum, in_sems, out_sems, sems,
 ):
+    group = place_ref[2]
+
+    def fetch(at):
+        here = pl.ds(at * 16, 16)
+        return pltpu.make_async_copy(recv_hbm.at[here], recv_ref.at[here], in_sems.at[at])
+
+    def deliver(at):
+        here = pl.ds(at * 16, 16)
+        return pltpu.make_async_copy(send_ref.at[here], send_hbm.at[here], out_sems.at[at])
+
+    mine = pl.ds(pl.multiple_of(group * BLK, BLK), BLK)
+    weights = [
+        pltpu.make_async_copy(src.at[group], dst, sems.at[at])
+        for at, (src, dst) in enumerate(
+            ((wu_hbm, wu_ref), (wv_hbm, wv_ref), (wo_hbm, wo_ref))
+        )
+    ]
+    coefs = pltpu.make_async_copy(coef_hbm.at[:, :, :, mine], coef_ref, sems.at[3])
+    for copy in (fetch(0), *weights, coefs, fetch(1), fetch(2), fetch(3)):
+        copy.start()
+    acc[...] = jnp.zeros_like(acc)
+    gsum[...] = jnp.zeros_like(gsum)
+    coefs.wait()
     for row in range(24):
         for lh in range(2):
             coef[row, lh] = jnp.broadcast_to(
-                coef_ref[row : row + 1, lh * 128 : (lh + 1) * 128], (8, 128)
+                coef_ref[row // 4, row // 2 % 2, row % 2 : row % 2 + 1, lh * 128 : (lh + 1) * 128],
+                (8, 128),
             )
-    acc[...] = jnp.zeros_like(acc)
-    gsum[...] = jnp.zeros_like(gsum)
+    for copy in weights:
+        copy.wait()
 
     def rows(at, which):
         return recv_ref[pl.ds(at * 16, 16), which * PL : (which + 1) * PL, :].reshape(BLK, BLK)
 
     @pl.loop(0, 4)
     def _(at):
+        fetch(at).wait()
         here = pl.ds(at * 16, 16)
         p = mm(rows(at, 0), wu_ref[...]).astype(BF).astype(F32)
         v = mm(rows(at, 1), wv_ref[...])
@@ -186,6 +212,7 @@
         e = from_tiles(es, at).astype(BF)
         send_ref[here, :PL, :] = z.reshape(16, PL, BLK)
         send_ref[here, PL:, :] = e.reshape(16, PL, BLK)
+        deliver(at).start()
         zf = z.astype(F32)
         gated = (zf * act_s[pl.ds(at * BLK, BLK), :]).astype(BF)
         dv = (zf * dgd_s[pl.ds(at * BLK, BLK), :]).astype(BF)
@@ -204,6 +231,8 @@
             sums = jnp.sum(acc[part * 8 : (part + 1) * 8, half], axis=1)
             ref[part, 24] = sums.astype(ref.dtype)
         ref[3, 24] = jnp.zeros((8, 128), ref.dtype)
+    for at in range(4):
+        deliver(at).wait()
 
 
 def core_sum_kernel(place_ref, keep_ref, got_ref, own_ref, *give_refs):
@@ -224,15 +253,18 @@
     out_ref[...] = total.astype(BF)
 
 
-def ordered_sum_kernel(axis, place_ref, *refs):
+def pair_sum_kernel(a_ref, b_ref, out_ref):
+    out_ref[...] = (a_ref[...].astype(F32) + b_ref[...].astype(F32)).astype(out_ref.dtype)
+
+
+def ordered_sum_kernel(place_ref, *refs):
     *parts, out_ref, held = refs
-    n = len(parts)
     for k, ref in enumerate(parts):
-        held[(place_ref[axis] + n - k) & (n - 1)] = ref[...]
+        held[(place_ref[0] + 4 - k) & 3] = ref[...]
     total = held[0].astype(F32)
-    for at in range(1, n):
+    for at in range(1, 4):
         total = total + held[at].astype(F32)
-    out_ref[...] = total.astype(out_ref.dtype)
+    out_ref[...] = total
 
 
 def gather_kernel(place_ref, *refs):
@@ -301,7 +333,7 @@
         gain_out[:, lanes(g)] = sums[:1] / gain_ref[:, lanes(g)]
 
 
-def call(kernel, outs, scratch=(), flops=0, moved=0, vmem=24, smem=(), hbm=()):
+def call(kernel, outs, scratch=(), flops=0, moved=0, vmem=24, smem=(), hbm=(), hbm_out=(), free=()):
     shapes = [jax.ShapeDtypeStruct(shape, dtype) for shape, dtype in outs]
     whole = pl.BlockSpec(memory_space=pltpu.VMEM)
 
@@ -311,11 +343,16 @@
             specs[at] = pl.BlockSpec(memory_space=pltpu.SMEM)
         for at in hbm:
             specs[at] = pl.BlockSpec(memory_space=pltpu.HBM)
+        for at in free:
+            specs[at] = pl.BlockSpec(memory_space=pl.ANY)
         return pl.pallas_call(
             kernel,
             out_shape=shapes,
             in_specs=specs,
-            out_specs=[whole] * len(shapes),
+            out_specs=[
+                pl.BlockSpec(memory_space=pltpu.HBM) if at in hbm_out else whole
+                for at in range(len(shapes))
+            ],
             scratch_shapes=list(scratch),
             compiler_params=pltpu.CompilerParams(vmem_limit_bytes=vmem << 20),
             cost_estimate=pl.CostEstimate(
@@ -336,8 +373,8 @@
     ]
 
 
-def swapped(value):
-    return lax.ppermute(value, "c", [(0, 1), (1, 0)])
+def swapped(value, axis="c", bit=1):
+    return lax.ppermute(value, axis, [(s, s ^ bit) for s in range(lax.axis_size(axis))])
 
 
 def per_device(tokens, cotangent, gain, w_u, w_v, w_o, local_factor, butterfly):
@@ -345,7 +382,6 @@
     cot = cotangent.reshape(BLK, -1)
     gain2 = gain.reshape(1, -1)
     wide = (BLK, GROUPS * BLK)
-    y = lax.axis_index("y")
     place = jnp.stack([lax.axis_index(axis) for axis in ("dp", "z", "y", "c")]).astype(jnp.int32)
 
     send = call(
@@ -365,10 +401,9 @@
     recv = lax.all_to_all(send.reshape(BLOCKS, 3 * PL, BLK), SEQ, 0, 0)
 
     u, act, dgd = call(
-        side_kernel, [(wide, BF), (wide, F32), (wide, F32)], flops=4e8, moved=8e6
+        side_kernel, [(wide, BF), (wide, F32), (wide, F32)], flops=4e8, moved=8e6, vmem=63
     )(x, cot, gain2, w_u, w_v, w_o)
-    coef = lax.dynamic_index_in_dim(butterfly.reshape(24, GROUPS, BLK), y, 1, keepdims=False)
-    mine = [lax.dynamic_index_in_dim(w, y, 0, keepdims=False) for w in (w_u, w_v, w_o)]
+    recv, u, act, dgd = lax.optimization_barrier((recv, u, act, dgd))
 
     tiled = (BLOCKS, 2, 2, 8, 128)
     quarter = (25, 8, 128)
@@ -376,6 +411,12 @@
         mid_kernel,
         [((BLOCKS, 2 * PL, BLK), BF), ((4,) + quarter, F32), ((4,) + quarter, BF)],
         scratch=[
+            pltpu.VMEM((BLOCKS, 3 * PL, BLK), BF),
+            pltpu.VMEM((BLOCKS, 2 * PL, BLK), BF),
+            pltpu.VMEM(butterfly.shape[:3] + (BLK,), F32),
+            pltpu.VMEM((BLK, BLK), BF),
+            pltpu.VMEM((BLK, BLK), BF),
+            pltpu.VMEM((BLK, BLK), BF),
             pltpu.VMEM(tiled, F32),
             pltpu.VMEM(tiled, F32),
             pltpu.VMEM(tiled, F32),
@@ -384,30 +425,50 @@
             pltpu.VMEM((24, 2, 8, 128), F32),
             pltpu.VMEM((24, 2, 8, 128), F32),
             pltpu.VMEM((3, BLK, BLK), F32),
+            pltpu.SemaphoreType.DMA((4,)),
+            pltpu.SemaphoreType.DMA((4,)),
+            pltpu.SemaphoreType.DMA((4,)),
         ],
         flops=8e8,
         moved=4e6,
+        vmem=63,
         smem=(0,),
-    )(place, recv, coef, *mine)
+        hbm=(2, 3, 4, 5),
+        free=(1,),
+        hbm_out=(0,),
+    )(place, recv, butterfly, w_u, w_v, w_o)
 
     recv2 = lax.all_to_all(back, SEQ, 0, 0).reshape(8, 4, 2, 2 * PL, BLK)
 
     own, *gives = call(
         core_sum_kernel, [(quarter, F32)] + [(quarter, BF)] * 3, moved=1e6, smem=(0,)
     )(place, keep, swapped(give))
-    part_z = call(dp_sum_kernel, [(quarter, BF)], moved=3e5)(own, *rotated(gives, "dp"))[0]
-    slice_ = call(
-        functools.partial(ordered_sum_kernel, 1),
-        [(quarter, BF)],
-        scratch=[pltpu.VMEM((8,) + quarter, BF)],
-        moved=5e5,
-        smem=(0,),
-    )(place, part_z, *rotated(part_z, "z"))[0]
+    slice_ = call(dp_sum_kernel, [(quarter, BF)], moved=3e5)(own, *rotated(gives, "dp"))[0]
+    for bit in (1, 2, 4):
+        slice_ = call(pair_sum_kernel, [(quarter, BF)], moved=2e5)(
+            slice_, swapped(slice_, "z", bit)
+        )[0]
     mine_y = call(gather_kernel, [((4,) + quarter, BF)], moved=4e5, smem=(0,))(
         place, slice_, *rotated(slice_, "dp")
     )[0]
+    part = call(local_kernel, [((BLK, BLK), BF)], flops=1.3e8, moved=1.2e6)(recv2, u)[0]
+    mine_y, part = lax.optimization_barrier((mine_y, part))
     halves = [mine_y] + rotated(mine_y, "y")
     others = [swapped(half) for half in halves]
+
+    mixed, dx = call(
+        last_kernel, [(wide, BF), (wide, BF)], scratch=[pltpu.VMEM(wide, F32)],
+        flops=6e8, moved=8e6,
+    )(recv2, x, gain2, act, dgd, w_u, w_v, w_o, local_factor)
+    grad_local = call(
+        ordered_sum_kernel,
+        [((BLK, BLK), F32)],
+        scratch=[pltpu.VMEM((4, BLK, BLK), BF)],
+        moved=8e5,
+        smem=(0,),
+    )(place, part, *rotated(part, "dp"))[0]
+    mixed, dx, grad_local, others = lax.optimization_barrier((mixed, dx, grad_local, others))
+
     shape = (GROUPS, BLK, BLK)
     gu, gv, go, grad_gain, grad_bfly = call(
         place_kernel,
@@ -415,19 +476,6 @@
         moved=5e6,
         smem=(0,),
     )(place, w_u, w_v, gain2, *halves, *others)
-
-    part = call(local_kernel, [((BLK, BLK), BF)], flops=1.3e8, moved=1.2e6)(recv2, u)[0]
-    grad_local = call(
-        functools.partial(ordered_sum_kernel, 0),
-        [((BLK, BLK), F32)],
-        scratch=[pltpu.VMEM((4, BLK, BLK), BF)],
-        moved=8e5,
-        smem=(0,),
-    )(place, part, *rotated(part, "dp"))[0]
-    mixed, dx = call(
-        last_kernel, [(wide, BF), (wide, BF)], scratch=[pltpu.VMEM(wide, F32)],
-        flops=6e8, moved=8e6,
-    )(recv2, x, gain2, act, dgd, w_u, w_v, w_o, local_factor)
 
     return (
         mixed.reshape(tokens.shape),

time: 151 us -> 146 us (0.967)
  waiting for transfers between devices: 53.6 us -> 70 us
  starting transfers between devices: 62.2 us -> 47.1 us
  local copies, waits for them, and re-layouts: 12.4 us -> 3.53 us
  Pallas kernels: 20.5 us -> 23.7 us
    ppermute x5 -> x8, waiting for transfers between devices: 1.3 us -> 24.6 us  [swapped(): lax.ppermute(value, axis, [(s, s ^ bit) for s in range(lax.axis_size(axis...]
    ppermute x19 -> x12, starting transfers between devices: 32.2 us -> 13.3 us  [rotated(): lax.ppermute(value, axis, [(s, (s + k) % n) for s in range(n)])]
    unnamed x49 -> x24, local copies, waits for them, and re-layouts: 10.9 us -> 3.53 us
    ppermute x19 -> x12, waiting for transfers between devices: 16.1 us -> 10.9 us  [rotated(): lax.ppermute(value, axis, [(s, (s + k) % n) for s in range(n)])]
    ppermute x5 -> x8, starting transfers between devices: 9.87 us -> 13.9 us  [swapped(): lax.ppermute(value, axis, [(s, s ^ bit) for s in range(lax.axis_size(axis...]
    pallas_call x11 -> x13, Pallas kernels: 20.5 us -> 23.7 us  [run(): pl.pallas_call(kernel, out_shape=shapes, in_specs=specs, out_specs=[pl.Bl...]
    all_to_all x1, waiting for transfers between devices: 36.2 us -> 34.5 us  [per_device(): recv = lax.all_to_all(send.reshape(BLOCKS, 3 * PL, BLK), SEQ, 0, 0)]
  transfers between devices with their start and end apart: 26 -> 22, of which waited for: 10 -> 12; matrix products, arithmetic and copies ran while one was open for 2% -> 0% of each run, Pallas kernels for 6% -> 6%
where the time goes in v3:
time: 146 us
  waiting for transfers between devices  70 us (48%)
  starting transfers between devices  47.1 us (32%)
  Pallas kernels  23.7 us (16%)
  local copies, waits for them, and re-layouts  3.53 us (2%)
    all_to_all x1, waiting for transfers between devices, per_device(): recv = lax.all_to_all(send.reshape(BLOCKS, 3 * PL, BLK), SEQ, 0, 0)  34.5 us
    ppermute x8, waiting for transfers between devices, swapped(): lax.ppermute(value, axis, [(s, s ^ bit) for s in range(lax.axis_size(axis...  24.6 us
    pallas_call x13, Pallas kernels, run(): pl.pallas_call(kernel, out_shape=shapes, in_specs=specs, out_specs=[pl.Bl...  23.7 us
    ppermute x8, starting transfers between devices, swapped(): lax.ppermute(value, axis, [(s, s ^ bit) for s in range(lax.axis_size(axis...  13.9 us
    ppermute x12, starting transfers between devices, rotated(): lax.ppermute(value, axis, [(s, (s + k) % n) for s in range(n)])  13.3 us
    all_to_all x1, starting transfers between devices, per_device(): recv = lax.all_to_all(send.reshape(BLOCKS, 3 * PL, BLK), SEQ, 0, 0)  13.3 us
    ppermute x12, waiting for transfers between devices, rotated(): lax.ppermute(value, axis, [(s, (s + k) % n) for s in range(n)])  10.9 us
    all_to_all x1, starting transfers between devices, per_device(): recv2 = lax.all_to_all(back, SEQ, 0, 0).reshape(8, 4, 2, 2 * PL, BLK)  6.61 us
  transfers between devices with their start and end apart: 22, of which 12 were waited for; matrix products, arithmetic and copies ran while one was open for 0% of the time, Pallas kernels for 6%

profile of v3, /device:TPU:1, one launch (start us, length us, event | category | flops | bytes accessed | tf_op | source)
XLA Modules:
  0.0 145.8 jit_solution(3760706351489229094)
XLA Ops:
  0.6 3.5 %shard_map.143 = bf16[8,4,2,48,256]{4,3,2,1,0:T(8,128)(2,1)} custom-call(bf16[256,1024]{1,0:T(8,128)(2,1)} %bitcast.14, bf16[256,1024]{1,0:T(8,128)(2,1)} %bitcast.22, f32[1,1024]{1,0:T(1,128)} %bitcast.17, bf16[256,256]{1,0:T(8,128)(2,1)} %local_ref.1), custom_call_target="tpu_custom_call" | custom-call | flops 140000000 | bytes 4000000 | tf_op jit(solution)/shard_map/pallas_call | solution.py:348
  4.1 13.3 %all-to-all-start = ((bf16[64,48,256]{2,1,0:T(8,128)(2,1)}), bf16[64,48,256]{2,1,0:T(8,128)(2,1)}, u32[]{:S(2)}, u32[]{:S(2)}) async-start(bf16[64,48,256]{2,1,0:T(8,128)(2,1)} %bitcast.21), calls=%async_computation | async-start | bytes 3145728 | tf_op jit(solution)/shard_map/all_to_all | solution.py:401
  17.5 3.8 %shard_map.144 = (bf16[256,1024]{1,0:T(8,128)(2,1)}, f32[256,1024]{1,0:T(8,128)}, f32[256,1024]{1,0:T(8,128)}) custom-call(bf16[256,1024]{1,0:T(8,128)(2,1)} %bitcast.15, bf16[256,1024]{1,0:T(8,128)(2,1)} %bitcast.23, f32[1,1024]{1,0:T(1,128)} %bitcast.18, bf16[4,256,256]{2,1,0:T(8,128)(2,1)} %wu_ref.5, bf16[4,256,256]{2,1,0:T(8,128)(2,1)} %wv_ref.5, ...), custom_call_target="tpu_custom_call" | custom-call | flops 400000000 | bytes 8000000 | tf_op jit(solution)/shard_map/pallas_call | solution.py:348
  21.3 0.6 pad_add_fusion.place_ref
  21.9 34.5 %all-to-all-done.recv_hbm = bf16[64,48,256]{2,1,0:T(8,128)(2,1)} async-done(((bf16[64,48,256]{2,1,0:T(8,128)(2,1)}), bf16[64,48,256]{2,1,0:T(8,128)(2,1)}, u32[]{:S(2)}, u32[]{:S(2)}) %all-to-all-start) | async-done | bytes 1572896 | tf_op jit(solution)/shard_map/all_to_all | solution.py:401
  56.4 8.8 %shard_map.145 = (bf16[64,32,256]{2,1,0:T(8,128)(2,1)}, f32[4,25,8,128]{3,2,1,0:T(8,128)}, bf16[4,25,8,128]{3,2,1,0:T(8,128)(2,1)}) custom-call(s32[4]{0:T(128)} %pad_add_fusion.place_ref, bf16[64,48,256]{2,1,0:T(8,128)(2,1)} %all-to-all-done.recv_hbm, f32[6,2,2,1024]{3,2,1,0:T(2,128)} %coef_hbm.1, bf16[4,256,256]{2,1,0:T(8,128)(2,1)} %wu_ref.5, ...), custom_call_target="tpu_custom_call" | custom-call | flops 800000000 | bytes 4000000 | tf_op jit(solution)/shard_map/pallas_call | solution.py:348
  65.3 6.6 %all-to-all-start.1 = ((bf16[64,32,256]{2,1,0:T(8,128)(2,1)}), bf16[64,32,256]{2,1,0:T(8,128)(2,1)S(1)}, u32[]{:S(2)}, u32[]{:S(2)}) async-start(bf16[64,32,256]{2,1,0:T(8,128)(2,1)} %get-tuple-element.42), calls=%async_computation.1 | async-start | bytes 2097152 | tf_op jit(solution)/shard_map/all_to_all | solution.py:441
  71.9 0.5 collective-permute-start
  72.5 1.1 collective-permute-done.got_ref
  73.6 0.6 shard_map.147
  74.2 0.0 copy-start
  74.2 0.0 copy-start.1
  74.2 1.3 collective-permute-start.1
  75.5 2.5 %collective-permute-start.2 = (bf16[25,8,128]{2,1,0:T(8,128)(2,1)S(1)}, bf16[25,8,128]{2,1,0:T(8,128)(2,1)S(1)}, u32[]{:S(2)}, u32[]{:S(2)}) collective-permute-start(bf16[25,8,128]{2,1,0:T(8,128)(2,1)S(1)} %get-tuple-element.51), channel_id=1, source_target_pairs={{0,128},{64,192},{128,0},{192,64},{1,129},{65,193},{129,1},{193,65... | collective-permute-start | bytes 153608 | tf_op jit(solution)/shard_map/ppermute | solution.py:371
  77.9 1.2 collective-permute-start.3
  79.1 1.5 %collective-permute-done.2.refs_1_ = bf16[25,8,128]{2,1,0:T(8,128)(2,1)S(1)} collective-permute-done((bf16[25,8,128]{2,1,0:T(8,128)(2,1)S(1)}, bf16[25,8,128]{2,1,0:T(8,128)(2,1)S(1)}, u32[]{:S(2)}, u32[]{:S(2)}) %collective-permute-start.2) | collective-permute-done | bytes 51232 | tf_op jit(solution)/shard_map/ppermute | solution.py:371
  80.6 0.6 collective-permute-done.3.refs_2_
  81.2 1.4 collective-permute-start.4
  82.6 14.7 %collective-permute-done.4.b_ref = bf16[25,8,128]{2,1,0:T(8,128)(2,1)S(1)} collective-permute-done((bf16[25,8,128]{2,1,0:T(8,128)(2,1)S(1)}, bf16[25,8,128]{2,1,0:T(8,128)(2,1)S(1)}, u32[]{:S(2)}, u32[]{:S(2)}) %collective-permute-start.4) | collective-permute-done | bytes 51232 | tf_op jit(solution)/shard_map/ppermute | solution.py:377
  97.4 0.9 collective-permute-start.5
  98.3 4.8 %collective-permute-done.5.b_ref = bf16[25,8,128]{2,1,0:T(8,128)(2,1)S(1)} collective-permute-done((bf16[25,8,128]{2,1,0:T(8,128)(2,1)S(1)}, bf16[25,8,128]{2,1,0:T(8,128)(2,1)S(1)}, u32[]{:S(2)}, u32[]{:S(2)}) %collective-permute-start.5) | collective-permute-done | bytes 51232 | tf_op jit(solution)/shard_map/ppermute | solution.py:377
  103.1 3.0 %collective-permute-start.6 = (bf16[25,8,128]{2,1,0:T(8,128)(2,1)S(1)}, bf16[25,8,128]{2,1,0:T(8,128)(2,1)S(1)}, u32[]{:S(2)}, u32[]{:S(2)}) collective-permute-start(bf16[25,8,128]{2,1,0:T(8,128)(2,1)S(1)} %shard_map.150.a_ref), channel_id=1, source_target_pairs={{0,32},{8,40},{16,48},{24,56},{32,0},{40,8},{48,16},{56,24},{1,33}... | collective-permute-start | bytes 153608 | tf_op jit(solution)/shard_map/ppermute | solution.py:377
  106.1 4.0 %collective-permute-done.6.b_ref = bf16[25,8,128]{2,1,0:T(8,128)(2,1)S(1)} collective-permute-done((bf16[25,8,128]{2,1,0:T(8,128)(2,1)S(1)}, bf16[25,8,128]{2,1,0:T(8,128)(2,1)S(1)}, u32[]{:S(2)}, u32[]{:S(2)}) %collective-permute-start.6) | collective-permute-done | bytes 51232 | tf_op jit(solution)/shard_map/ppermute | solution.py:377
  110.1 2.6 %collective-permute-start.9 = (bf16[25,8,128]{2,1,0:T(8,128)(2,1)S(1)}, bf16[25,8,128]{2,1,0:T(8,128)(2,1)S(1)}, u32[]{:S(2)}, u32[]{:S(2)}) collective-permute-start(bf16[25,8,128]{2,1,0:T(8,128)(2,1)S(1)} %shard_map.151.refs_0_), channel_id=1, source_target_pairs={{0,192},{64,0},{128,64},{192,128},{1,193},{65,1},{129,65},{193,129... | collective-permute-start | bytes 153608 | tf_op jit(solution)/shard_map/ppermute | solution.py:371
  112.7 0.5 collective-permute-start.8
  113.2 0.6 collective-permute-start.7
  113.8 0.1 collective-permute-done.9.refs_3_
  113.8 3.3 %collective-permute-done.8.refs_2_ = bf16[25,8,128]{2,1,0:T(8,128)(2,1)S(1)} collective-permute-done((bf16[25,8,128]{2,1,0:T(8,128)(2,1)S(1)}, bf16[25,8,128]{2,1,0:T(8,128)(2,1)S(1)}, u32[]{:S(2)}, u32[]{:S(2)}) %collective-permute-start.8) | collective-permute-done | bytes 51232 | tf_op jit(solution)/shard_map/ppermute | solution.py:371
  117.2 0.5 collective-permute-done.7.refs_1_
  117.7 0.6 shard_map.152.refs_0_
  118.2 0.0 copy-start.6
  118.3 1.0 copy-done.6
  119.3 0.3 shard_map.153.refs_0_
  119.6 2.4 %collective-permute-start.18 = (bf16[4,25,8,128]{3,2,1,0:T(8,128)(2,1)S(1)}, bf16[4,25,8,128]{3,2,1,0:T(8,128)(2,1)S(1)}, u32[]{:S(2)}, u32[]{:S(2)}) collective-permute-start(bf16[4,25,8,128]{3,2,1,0:T(8,128)(2,1)S(1)} %shard_map.152.refs_0_), channel_id=1, source_target_pairs={{0,6},{2,0},{4,2},{6,4},{1,7},{3,1},{5,3},{7,5},{8,14},{10,8},{12,... | collective-permute-start | bytes 614408 | tf_op jit(solution)/shard_map/ppermute | solution.py:371
  122.0 0.7 collective-permute-start.16
  122.7 0.5 collective-permute-start.14
  123.2 0.3 collective-permute-start.12
  123.5 0.9 collective-permute-start.11
  124.4 3.0 %collective-permute-done.12.refs_3_ = bf16[256,256]{1,0:T(8,128)(2,1)S(1)} collective-permute-done((bf16[256,256]{1,0:T(8,128)(2,1)S(1)}, bf16[256,256]{1,0:T(8,128)(2,1)S(1)}, u32[]{:S(2)}, u32[]{:S(2)}) %collective-permute-start.12) | collective-permute-done | bytes 131104 | tf_op jit(solution)/shard_map/ppermute | solution.py:371
  127.3 5.2 %collective-permute-start.13 = (bf16[4,25,8,128]{3,2,1,0:T(8,128)(2,1)S(1)}, bf16[4,25,8,128]{3,2,1,0:T(8,128)(2,1)S(1)}, u32[]{:S(2)}, u32[]{:S(2)}) collective-permute-start(bf16[4,25,8,128]{3,2,1,0:T(8,128)(2,1)S(1)} %shard_map.152.refs_0_), channel_id=1, source_target_pairs={{0,1},{1,0},{2,3},{3,2},{4,5},{5,4},{6,7},{7,6},{8,9},{9,8},{10,11... | collective-permute-start | bytes 614408 | tf_op jit(solution)/shard_map/ppermute | solution.py:377
  132.6 0.8 collective-permute-start.17
  133.3 2.1 %collective-permute-start.15 = (bf16[4,25,8,128]{3,2,1,0:T(8,128)(2,1)S(1)}, bf16[4,25,8,128]{3,2,1,0:T(8,128)(2,1)S(1)}, u32[]{:S(2)}, u32[]{:S(2)}) collective-permute-start(bf16[4,25,8,128]{3,2,1,0:T(8,128)(2,1)S(1)} %collective-permute-done.14.refs_1_), channel_id=1, source_target_pairs={{0,1},{1,0},{2,3},{3,2},{4,5},{5,4},{6,7},{7,6},{8,9},{9,8},{10,11... | collective-permute-start | bytes 614408 | tf_op jit(solution)/shard_map/ppermute | solution.py:377
  135.5 1.2 copy-done.4
  136.7 1.2 copy-done.5
  137.9 1.9 %shard_map.146 = (bf16[256,1024]{1,0:T(8,128)(2,1)}, bf16[256,1024]{1,0:T(8,128)(2,1)}) custom-call(bf16[8,4,2,32,256]{4,3,2,1,0:T(8,128)(2,1)S(1)} %bitcast.13, bf16[256,1024]{1,0:T(8,128)(2,1)S(1)} %bitcast.16, f32[1,1024]{1,0:T(1,128)S(1)} %bitcast.19, f32[256,1024]{1,0:T(8,128)S(1)} %copy-done.4, f32[256,1024]{1,0:T(8,128)S(1)} %copy-done.5, ...), custom_call_target="tpu_custom_call" | custom-call | flops 600000000 | bytes 8000000 | tf_op jit(solution)/shard_map/pallas_call | solution.py:348
  139.8 2.0 %collective-permute-done.10.refs_1_ = bf16[256,256]{1,0:T(8,128)(2,1)S(1)} collective-permute-done((bf16[256,256]{1,0:T(8,128)(2,1)S(1)}, bf16[256,256]{1,0:T(8,128)(2,1)S(1)}, u32[]{:S(2)}, u32[]{:S(2)}) %collective-permute-start.10) | collective-permute-done | bytes 131104 | tf_op jit(solution)/shard_map/ppermute | solution.py:371
  141.8 1.4 shard_map.154
  143.2 2.7 %shard_map.155 = (f32[4,256,256]{2,1,0:T(8,128)}, f32[4,256,256]{2,1,0:T(8,128)}, f32[4,256,256]{2,1,0:T(8,128)}, f32[1,1024]{1,0:T(1,128)}, f32[6,2,2,1024]{3,2,1,0:T(2,128)}) custom-call(s32[4]{0:T(128)S(1)} %copy-done.10, bf16[4,256,256]{2,1,0:T(8,128)(2,1)S(1)} %copy-done, bf16[4,256,256]{2,1,0:T(8,128)(2,1)S(1)} %copy-done.1, f32[1,1024]{1,0:T(1,128)S(1)} %bitcast.20, ...), custom_call_target="tpu_custom_call" | custom-call | bytes 5000000 | tf_op jit(solution)/shard_map/pallas_call | solution.py:348
  (34 shorter events, 0.2 us)
Async XLA Ops:
  4.1 52.3 %all-to-all-start = ((bf16[64,48,256]{2,1,0:T(8,128)(2,1)}), bf16[64,48,256]{2,1,0:T(8,128)(2,1)}, u32[]{:S(2)}, u32[]{:S(2)}) async-start(bf16[64,48,256]{2,1,0:T(8,128)(2,1)} %bitcast.21), calls=%async_computation | async-start | bytes 3145728 | tf_op jit(solution)/shard_map/all_to_all | solution.py:401
  65.3 6.7 %copy-start.11 = (bf16[4,25,8,128]{3,2,1,0:T(8,128)(2,1)S(1)}, bf16[4,25,8,128]{3,2,1,0:T(8,128)(2,1)}, u32[]{:S(2)}) copy-start(bf16[4,25,8,128]{3,2,1,0:T(8,128)(2,1)} %get-tuple-element.48) | copy-start | bytes 614404
  65.3 8.3 %copy-start.8 = (f32[4,25,8,128]{3,2,1,0:T(8,128)S(1)}, f32[4,25,8,128]{3,2,1,0:T(8,128)}, u32[]{:S(2)}) copy-start(f32[4,25,8,128]{3,2,1,0:T(8,128)} %get-tuple-element.47.keep_ref) | copy-start | bytes 1228804
  65.3 8.3 %copy-start.10 = (s32[4]{0:T(128)S(1)}, s32[4]{0:T(128)}, u32[]{:S(2)}) copy-start(s32[4]{0:T(128)} %pad_add_fusion.place_ref) | copy-start | bytes 52
  65.3 52.9 %all-to-all-start.1 = ((bf16[64,32,256]{2,1,0:T(8,128)(2,1)}), bf16[64,32,256]{2,1,0:T(8,128)(2,1)S(1)}, u32[]{:S(2)}, u32[]{:S(2)}) async-start(bf16[64,32,256]{2,1,0:T(8,128)(2,1)} %get-tuple-element.42), calls=%async_computation.1 | async-start | bytes 2097152 | tf_op jit(solution)/shard_map/all_to_all | solution.py:441
  71.9 1.6 %collective-permute-start = (bf16[4,25,8,128]{3,2,1,0:T(8,128)(2,1)S(1)}, bf16[4,25,8,128]{3,2,1,0:T(8,128)(2,1)S(1)}, u32[]{:S(2)}, u32[]{:S(2)}) collective-permute-start(bf16[4,25,8,128]{3,2,1,0:T(8,128)(2,1)S(1)} %copy-done.11), channel_id=1, source_target_pairs={{0,1},{1,0},{2,3},{3,2},{4,5},{5,4},{6,7},{7,6},{8,9},{9,8},{10,11... | collective-permute-start | bytes 614408 | tf_op jit(solution)/shard_map/ppermute | solution.py:377
  73.6 61.9 %copy-start.7 = (bf16[256,256]{1,0:T(8,128)(2,1)S(1)}, bf16[256,256]{1,0:T(8,128)(2,1)}, u32[]{:S(2)}) copy-start(bf16[256,256]{1,0:T(8,128)(2,1)} %local_ref.1) | copy-start | bytes 393220
  73.6 61.9 %copy-start.9 = (f32[1024]{0:T(1024)S(1)}, f32[1024]{0:T(1024)}, u32[]{:S(2)}) copy-start(f32[1024]{0:T(1024)} %param.10) | copy-start | bytes 12292
  74.2 61.3 %copy-start = (bf16[4,256,256]{2,1,0:T(8,128)(2,1)S(1)}, bf16[4,256,256]{2,1,0:T(8,128)(2,1)}, u32[]{:S(2)}) copy-start(bf16[4,256,256]{2,1,0:T(8,128)(2,1)} %wu_ref.5) | copy-start | bytes 1572868
  74.2 61.3 %copy-start.1 = (bf16[4,256,256]{2,1,0:T(8,128)(2,1)S(1)}, bf16[4,256,256]{2,1,0:T(8,128)(2,1)}, u32[]{:S(2)}) copy-start(bf16[4,256,256]{2,1,0:T(8,128)(2,1)} %wv_ref.5) | copy-start | bytes 1572868
  74.2 61.3 %copy-start.2 = (bf16[1,256,1024]{2,1,0:T(8,128)(2,1)S(1)}, bf16[1,256,1024]{2,1,0:T(8,128)(2,1)}, u32[]{:S(2)}) copy-start(bf16[1,256,1024]{2,1,0:T(8,128)(2,1)} %param.8) | copy-start | bytes 1572868
  74.2 61.3 %copy-start.3 = (bf16[4,256,256]{2,1,0:T(8,128)(2,1)S(1)}, bf16[4,256,256]{2,1,0:T(8,128)(2,1)}, u32[]{:S(2)}) copy-start(bf16[4,256,256]{2,1,0:T(8,128)(2,1)} %wo_ref.3) | copy-start | bytes 1572868
  74.2 4.9 %collective-permute-start.1 = (bf16[25,8,128]{2,1,0:T(8,128)(2,1)S(1)}, bf16[25,8,128]{2,1,0:T(8,128)(2,1)S(1)}, u32[]{:S(2)}, u32[]{:S(2)}) collective-permute-start(bf16[25,8,128]{2,1,0:T(8,128)(2,1)S(1)} %get-tuple-element.50), channel_id=1, source_target_pairs={{0,64},{64,128},{128,192},{192,0},{1,65},{65,129},{129,193},{193,1... | collective-permute-start | bytes 153608 | tf_op jit(solution)/shard_map/ppermute | solution.py:371
  75.5 5.1 %collective-permute-start.2 = (bf16[25,8,128]{2,1,0:T(8,128)(2,1)S(1)}, bf16[25,8,128]{2,1,0:T(8,128)(2,1)S(1)}, u32[]{:S(2)}, u32[]{:S(2)}) collective-permute-start(bf16[25,8,128]{2,1,0:T(8,128)(2,1)S(1)} %get-tuple-element.51), channel_id=1, source_target_pairs={{0,128},{64,192},{128,0},{192,64},{1,129},{65,193},{129,1},{193,65... | collective-permute-start | bytes 153608 | tf_op jit(solution)/shard_map/ppermute | solution.py:371
  77.9 3.3 %collective-permute-start.3 = (bf16[25,8,128]{2,1,0:T(8,128)(2,1)S(1)}, bf16[25,8,128]{2,1,0:T(8,128)(2,1)S(1)}, u32[]{:S(2)}, u32[]{:S(2)}) collective-permute-start(bf16[25,8,128]{2,1,0:T(8,128)(2,1)S(1)} %get-tuple-element.52), channel_id=1, source_target_pairs={{0,192},{64,0},{128,64},{192,128},{1,193},{65,1},{129,65},{193,129... | collective-permute-start | bytes 153608 | tf_op jit(solution)/shard_map/ppermute | solution.py:371
  81.2 16.1 %collective-permute-start.4 = (bf16[25,8,128]{2,1,0:T(8,128)(2,1)S(1)}, bf16[25,8,128]{2,1,0:T(8,128)(2,1)S(1)}, u32[]{:S(2)}, u32[]{:S(2)}) collective-permute-start(bf16[25,8,128]{2,1,0:T(8,128)(2,1)S(1)} %shard_map.148.a_ref), channel_id=1, source_target_pairs={{0,8},{8,0},{16,24},{24,16},{32,40},{40,32},{48,56},{56,48},{1,9},... | collective-permute-start | bytes 153608 | tf_op jit(solution)/shard_map/ppermute | solution.py:377
  97.4 5.7 %collective-permute-start.5 = (bf16[25,8,128]{2,1,0:T(8,128)(2,1)S(1)}, bf16[25,8,128]{2,1,0:T(8,128)(2,1)S(1)}, u32[]{:S(2)}, u32[]{:S(2)}) collective-permute-start(bf16[25,8,128]{2,1,0:T(8,128)(2,1)S(1)} %shard_map.149.a_ref), channel_id=1, source_target_pairs={{0,16},{8,24},{16,0},{24,8},{32,48},{40,56},{48,32},{56,40},{1,17}... | collective-permute-start | bytes 153608 | tf_op jit(solution)/shard_map/ppermute | solution.py:377
  103.1 7.0 %collective-permute-start.6 = (bf16[25,8,128]{2,1,0:T(8,128)(2,1)S(1)}, bf16[25,8,128]{2,1,0:T(8,128)(2,1)S(1)}, u32[]{:S(2)}, u32[]{:S(2)}) collective-permute-start(bf16[25,8,128]{2,1,0:T(8,128)(2,1)S(1)} %shard_map.150.a_ref), channel_id=1, source_target_pairs={{0,32},{8,40},{16,48},{24,56},{32,0},{40,8},{48,16},{56,24},{1,33}... | collective-permute-start | bytes 153608 | tf_op jit(solution)/shard_map/ppermute | solution.py:377
  110.1 3.8 %collective-permute-start.9 = (bf16[25,8,128]{2,1,0:T(8,128)(2,1)S(1)}, bf16[25,8,128]{2,1,0:T(8,128)(2,1)S(1)}, u32[]{:S(2)}, u32[]{:S(2)}) collective-permute-start(bf16[25,8,128]{2,1,0:T(8,128)(2,1)S(1)} %shard_map.151.refs_0_), channel_id=1, source_target_pairs={{0,192},{64,0},{128,64},{192,128},{1,193},{65,1},{129,65},{193,129... | collective-permute-start | bytes 153608 | tf_op jit(solution)/shard_map/ppermute | solution.py:371
  112.7 4.5 %collective-permute-start.8 = (bf16[25,8,128]{2,1,0:T(8,128)(2,1)S(1)}, bf16[25,8,128]{2,1,0:T(8,128)(2,1)S(1)}, u32[]{:S(2)}, u32[]{:S(2)}) collective-permute-start(bf16[25,8,128]{2,1,0:T(8,128)(2,1)S(1)} %shard_map.151.refs_0_), channel_id=1, source_target_pairs={{0,128},{64,192},{128,0},{192,64},{1,129},{65,193},{129,1},{193,65... | collective-permute-start | bytes 153608 | tf_op jit(solution)/shard_map/ppermute | solution.py:371
  113.2 4.5 %collective-permute-start.7 = (bf16[25,8,128]{2,1,0:T(8,128)(2,1)S(1)}, bf16[25,8,128]{2,1,0:T(8,128)(2,1)S(1)}, u32[]{:S(2)}, u32[]{:S(2)}) collective-permute-start(bf16[25,8,128]{2,1,0:T(8,128)(2,1)S(1)} %shard_map.151.refs_0_), channel_id=1, source_target_pairs={{0,64},{64,128},{128,192},{192,0},{1,65},{65,129},{129,193},{193,1... | collective-permute-start | bytes 153608 | tf_op jit(solution)/shard_map/ppermute | solution.py:371
  118.2 1.0 copy-start.6
  119.6 12.9 %collective-permute-start.18 = (bf16[4,25,8,128]{3,2,1,0:T(8,128)(2,1)S(1)}, bf16[4,25,8,128]{3,2,1,0:T(8,128)(2,1)S(1)}, u32[]{:S(2)}, u32[]{:S(2)}) collective-permute-start(bf16[4,25,8,128]{3,2,1,0:T(8,128)(2,1)S(1)} %shard_map.152.refs_0_), channel_id=1, source_target_pairs={{0,6},{2,0},{4,2},{6,4},{1,7},{3,1},{5,3},{7,5},{8,14},{10,8},{12,... | collective-permute-start | bytes 614408 | tf_op jit(solution)/shard_map/ppermute | solution.py:371
  122.0 10.6 %collective-permute-start.16 = (bf16[4,25,8,128]{3,2,1,0:T(8,128)(2,1)S(1)}, bf16[4,25,8,128]{3,2,1,0:T(8,128)(2,1)S(1)}, u32[]{:S(2)}, u32[]{:S(2)}) collective-permute-start(bf16[4,25,8,128]{3,2,1,0:T(8,128)(2,1)S(1)} %shard_map.152.refs_0_), channel_id=1, source_target_pairs={{0,4},{2,6},{4,0},{6,2},{1,5},{3,7},{5,1},{7,3},{8,12},{10,14},{12... | collective-permute-start | bytes 614408 | tf_op jit(solution)/shard_map/ppermute | solution.py:371
  122.7 10.6 %collective-permute-start.14 = (bf16[4,25,8,128]{3,2,1,0:T(8,128)(2,1)S(1)}, bf16[4,25,8,128]{3,2,1,0:T(8,128)(2,1)S(1)}, u32[]{:S(2)}, u32[]{:S(2)}) collective-permute-start(bf16[4,25,8,128]{3,2,1,0:T(8,128)(2,1)S(1)} %shard_map.152.refs_0_), channel_id=1, source_target_pairs={{0,2},{2,4},{4,6},{6,0},{1,3},{3,5},{5,7},{7,1},{8,10},{10,12},{12... | collective-permute-start | bytes 614408 | tf_op jit(solution)/shard_map/ppermute | solution.py:371
  123.2 4.1 %collective-permute-start.12 = (bf16[256,256]{1,0:T(8,128)(2,1)S(1)}, bf16[256,256]{1,0:T(8,128)(2,1)S(1)}, u32[]{:S(2)}, u32[]{:S(2)}) collective-permute-start(bf16[256,256]{1,0:T(8,128)(2,1)S(1)} %shard_map.153.refs_0_), channel_id=1, source_target_pairs={{0,192},{64,0},{128,64},{192,128},{1,193},{65,1},{129,65},{193,129... | collective-permute-start | bytes 393224 | tf_op jit(solution)/shard_map/ppermute | solution.py:371
  123.5 11.9 %collective-permute-start.11 = (bf16[256,256]{1,0:T(8,128)(2,1)S(1)}, bf16[256,256]{1,0:T(8,128)(2,1)S(1)}, u32[]{:S(2)}, u32[]{:S(2)}) collective-permute-start(bf16[256,256]{1,0:T(8,128)(2,1)S(1)} %shard_map.153.refs_0_), channel_id=1, source_target_pairs={{0,128},{64,192},{128,0},{192,64},{1,129},{65,193},{129,1},{193,65... | collective-permute-start | bytes 393224 | tf_op jit(solution)/shard_map/ppermute | solution.py:371
  127.3 15.8 %collective-permute-start.13 = (bf16[4,25,8,128]{3,2,1,0:T(8,128)(2,1)S(1)}, bf16[4,25,8,128]{3,2,1,0:T(8,128)(2,1)S(1)}, u32[]{:S(2)}, u32[]{:S(2)}) collective-permute-start(bf16[4,25,8,128]{3,2,1,0:T(8,128)(2,1)S(1)} %shard_map.152.refs_0_), channel_id=1, source_target_pairs={{0,1},{1,0},{2,3},{3,2},{4,5},{5,4},{6,7},{7,6},{8,9},{9,8},{10,11... | collective-permute-start | bytes 614408 | tf_op jit(solution)/shard_map/ppermute | solution.py:377
  132.6 10.6 %collective-permute-start.19 = (bf16[4,25,8,128]{3,2,1,0:T(8,128)(2,1)S(1)}, bf16[4,25,8,128]{3,2,1,0:T(8,128)(2,1)S(1)}, u32[]{:S(2)}, u32[]{:S(2)}) collective-permute-start(bf16[4,25,8,128]{3,2,1,0:T(8,128)(2,1)S(1)} %collective-permute-done.18.refs_3_), channel_id=1, source_target_pairs={{0,1},{1,0},{2,3},{3,2},{4,5},{5,4},{6,7},{7,6},{8,9},{9,8},{10,11... | collective-permute-start | bytes 614408 | tf_op jit(solution)/shard_map/ppermute | solution.py:377
  132.6 10.6 %collective-permute-start.17 = (bf16[4,25,8,128]{3,2,1,0:T(8,128)(2,1)S(1)}, bf16[4,25,8,128]{3,2,1,0:T(8,128)(2,1)S(1)}, u32[]{:S(2)}, u32[]{:S(2)}) collective-permute-start(bf16[4,25,8,128]{3,2,1,0:T(8,128)(2,1)S(1)} %collective-permute-done.16.refs_2_), channel_id=1, source_target_pairs={{0,1},{1,0},{2,3},{3,2},{4,5},{5,4},{6,7},{7,6},{8,9},{9,8},{10,11... | collective-permute-start | bytes 614408 | tf_op jit(solution)/shard_map/ppermute | solution.py:377
  133.3 9.8 %collective-permute-start.15 = (bf16[4,25,8,128]{3,2,1,0:T(8,128)(2,1)S(1)}, bf16[4,25,8,128]{3,2,1,0:T(8,128)(2,1)S(1)}, u32[]{:S(2)}, u32[]{:S(2)}) collective-permute-start(bf16[4,25,8,128]{3,2,1,0:T(8,128)(2,1)S(1)} %collective-permute-done.14.refs_1_), channel_id=1, source_target_pairs={{0,1},{1,0},{2,3},{3,2},{4,5},{5,4},{6,7},{7,6},{8,9},{9,8},{10,11... | collective-permute-start | bytes 614408 | tf_op jit(solution)/shard_map/ppermute | solution.py:377
  135.4 6.3 %collective-permute-start.10 = (bf16[256,256]{1,0:T(8,128)(2,1)S(1)}, bf16[256,256]{1,0:T(8,128)(2,1)S(1)}, u32[]{:S(2)}, u32[]{:S(2)}) collective-permute-start(bf16[256,256]{1,0:T(8,128)(2,1)S(1)} %shard_map.153.refs_0_), channel_id=1, source_target_pairs={{0,64},{64,128},{128,192},{192,0},{1,65},{65,129},{129,193},{193,1... | collective-permute-start | bytes 393224 | tf_op jit(solution)/shard_map/ppermute | solution.py:371
  135.5 1.2 copy-start.4
  136.7 1.2 copy-start.5

commit v4 on v3

--- a/solution.py
+++ b/solution.py
@@ -14,7 +14,6 @@
 BLOCKS = 64
 PL = 16
 SEQ = ("z", "y", "c")
-SAME_GROUP = ("dp", "z", "c")
 
 
 def dot(a, b, dims):
@@ -56,7 +55,7 @@
         copy.start()
 
     def put(g, at, value):
-        send_ref[:, g, :, at * PL : (at + 1) * PL, :] = value.reshape(8, 2, PL, BLK)
+        send_ref[g, :, at * PL : (at + 1) * PL, :] = value.reshape(16, PL, BLK)
 
     copies[0].wait()
     r = inv_rms(x_ref)
@@ -99,7 +98,7 @@
     recv_ref, send_ref, coef_ref, wu_ref, wv_ref, wo_ref,
     z0, zs, es, act_s, dgd_s, coef, acc, gsum, in_sems, out_sems, sems,
 ):
-    group = place_ref[2]
+    group = place_ref[1]
 
     def fetch(at):
         here = pl.ds(at * 16, 16)
@@ -220,7 +219,7 @@
         gsum[1] += mm_tn(rows(at, 1), dv)
         gsum[2] += mm_tn(gated, rows(at, 2))
 
-    own = place_ref[3]
+    own = place_ref[2]
     for ref, half in ((keep_ref, own), (give_ref, 1 - own)):
         cut = pl.ds(pl.multiple_of(half * 128, 128), 128)
         for w in range(3):
@@ -270,11 +269,11 @@
 def gather_kernel(place_ref, *refs):
     *parts, out_ref = refs
     for k, ref in enumerate(parts):
-        out_ref[(place_ref[0] + 4 - k) & 3] = ref[...]
+        out_ref[(place_ref[1] + 4 - k) & 3] = ref[...]
 
 
 def group_of(recv_ref, g, which):
-    return recv_ref[:, g, :, which * PL : (which + 1) * PL, :].reshape(BLK, BLK)
+    return recv_ref[g, :, which * PL : (which + 1) * PL, :].reshape(BLK, BLK)
 
 
 def local_kernel(recv_ref, u_ref, out_ref):
@@ -307,22 +306,28 @@
 
 
 def place_kernel(place_ref, wu_ref, wv_ref, gain_ref, *refs):
-    own, other = refs[:GROUPS], refs[GROUPS : 2 * GROUPS]
-    gu_ref, gv_ref, go_ref, gain_out, bfly_ref = refs[2 * GROUPS :]
-    for k in range(GROUPS):
-        g = (place_ref[2] + GROUPS - k) & (GROUPS - 1)
-        for parts, half in ((own, place_ref[3]), (other, 1 - place_ref[3])):
+    own, other = refs[:4], refs[4:8]
+    gu_ref, gv_ref, go_ref, gain_out, bfly_ref = refs[8:]
+    for k in range(4):
+        d = (place_ref[0] + 4 - k) & 3
+        rows = pl.ds(pl.multiple_of(d * 64, 64), 64)
+        for parts, half in ((own, place_ref[2]), (other, 1 - place_ref[2])):
             cut = pl.ds(pl.multiple_of(half * 128, 128), 128)
             for w, out in enumerate((gu_ref, gv_ref, go_ref)):
-                out[g, :, cut] = (
-                    parts[k][:, w * 8 : (w + 1) * 8].astype(F32).reshape(BLK, 128)
+                out[:, rows, cut] = (
+                    parts[k][:, w * 8 : (w + 1) * 8].astype(F32).reshape(GROUPS, 64, 128)
                 )
-            wide = pl.ds(pl.multiple_of(g * BLK + half * 128, 128), 128)
-            for part in range(3):
-                tile = parts[k][part, 24].astype(F32)
-                for s in range(8):
-                    row = part * 8 + s
-                    bfly_ref[row // 4, row // 2 % 2, row % 2 : row % 2 + 1, wide] = tile[s : s + 1]
+
+            @pl.when(d < 3)
+            def _():
+                for g in range(GROUPS):
+                    wide = pl.ds(pl.multiple_of(g * BLK + half * 128, 128), 128)
+                    tile = parts[k][g, 24].astype(F32)
+                    for s in range(8):
+                        bfly_ref[2 * d + s // 4, s // 2 % 2, s % 2 : s % 2 + 1, wide] = (
+                            tile[s : s + 1]
+                        )
+
     ones = jnp.ones((8, BLK), F32)
     for g in range(GROUPS):
         product = gu_ref[g] * wu_ref[g].astype(F32) + gv_ref[g] * wv_ref[g].astype(F32)
@@ -363,12 +368,12 @@
     return run
 
 
-def rotated(values, axis):
+def rotated(values, axis, step=1):
     n = lax.axis_size(axis)
     if not isinstance(values, (list, tuple)):
-        values = [values] * (n - 1)
+        values = [values] * (n // step - 1)
     return [
-        lax.ppermute(value, axis, [(s, (s + k) % n) for s in range(n)])
+        lax.ppermute(value, axis, [(s, (s + k * step) % n) for s in range(n)])
         for k, value in enumerate(values, 1)
     ]
 
@@ -382,11 +387,13 @@
     cot = cotangent.reshape(BLK, -1)
     gain2 = gain.reshape(1, -1)
     wide = (BLK, GROUPS * BLK)
-    place = jnp.stack([lax.axis_index(axis) for axis in ("dp", "z", "y", "c")]).astype(jnp.int32)
+    place = jnp.stack(
+        [lax.axis_index("dp"), lax.axis_index("z") >> 1, lax.axis_index("c")]
+    ).astype(jnp.int32)
 
     send = call(
         first_kernel,
-        [((8, 4, 2, 3 * PL, BLK), BF)],
+        [((GROUPS, 16, 3 * PL, BLK), BF)],
         scratch=[
             pltpu.VMEM(wide, BF),
             pltpu.VMEM(wide, BF),
@@ -438,22 +445,22 @@
         hbm_out=(0,),
     )(place, recv, butterfly, w_u, w_v, w_o)
 
-    recv2 = lax.all_to_all(back, SEQ, 0, 0).reshape(8, 4, 2, 2 * PL, BLK)
+    recv2 = lax.all_to_all(back, SEQ, 0, 0).reshape(GROUPS, 16, 2 * PL, BLK)
 
     own, *gives = call(
         core_sum_kernel, [(quarter, F32)] + [(quarter, BF)] * 3, moved=1e6, smem=(0,)
     )(place, keep, swapped(give))
     slice_ = call(dp_sum_kernel, [(quarter, BF)], moved=3e5)(own, *rotated(gives, "dp"))[0]
-    for bit in (1, 2, 4):
+    for axis, bit in (("y", 1), ("y", 2), ("z", 1)):
         slice_ = call(pair_sum_kernel, [(quarter, BF)], moved=2e5)(
-            slice_, swapped(slice_, "z", bit)
+            slice_, swapped(slice_, axis, bit)
         )[0]
-    mine_y = call(gather_kernel, [((4,) + quarter, BF)], moved=4e5, smem=(0,))(
-        place, slice_, *rotated(slice_, "dp")
+    part = call(local_kernel, [((BLK, BLK), BF)], flops=1.3e8, moved=1.2e6)(recv2, u)[0]
+    slice_, part = lax.optimization_barrier((slice_, part))
+    mine_d = call(gather_kernel, [((4,) + quarter, BF)], moved=4e5, smem=(0,))(
+        place, slice_, *rotated(slice_, "z", 2)
     )[0]
-    part = call(local_kernel, [((BLK, BLK), BF)], flops=1.3e8, moved=1.2e6)(recv2, u)[0]
-    mine_y, part = lax.optimization_barrier((mine_y, part))
-    halves = [mine_y] + rotated(mine_y, "y")
+    halves = [mine_d] + rotated(mine_d, "dp")
     others = [swapped(half) for half in halves]
 
     mixed, dx = call(

time: 146 us -> 143 us (0.979)
  waiting for transfers between devices: 70 us -> 65.2 us
    ppermute x8, waiting for transfers between devices: 24.6 us -> 10.7 us  [swapped(): lax.ppermute(value, axis, [(s, s ^ bit) for s in range(lax.axis_size(axis...]
    ppermute x12, waiting for transfers between devices: 10.9 us -> 17.2 us  [rotated(): lax.ppermute(value, axis, [(s, (s + k * step) % n) for s in range(n)])]
    ppermute x12, starting transfers between devices: 13.3 us -> 17.3 us  [rotated(): lax.ppermute(value, axis, [(s, (s + k * step) % n) for s in range(n)])]
    all_to_all x1, waiting for transfers between devices: 0.01 us -> 2.84 us  [per_device(): recv2 = lax.all_to_all(back, SEQ, 0, 0).reshape(GROUPS, 16, 2 * PL, BLK)]
    ppermute x8, starting transfers between devices: 13.9 us -> 11.1 us  [swapped(): lax.ppermute(value, axis, [(s, s ^ bit) for s in range(lax.axis_size(axis...]
  transfers between devices with their start and end apart: 22 -> 22, of which waited for: 12 -> 12; matrix products, arithmetic and copies ran while one was open for 0% -> 0% of each run, Pallas kernels for 6% -> 5%
where the time goes in v4:
time: 143 us; the launch traced here: 142 us
  waiting for transfers between devices  65.2 us (46%)
  starting transfers between devices  48.4 us (34%)
  Pallas kernels  23.5 us (16%)
  local copies, waits for them, and re-layouts  3.54 us (2%)
    all_to_all x1, waiting for transfers between devices, per_device(): recv = lax.all_to_all(send.reshape(BLOCKS, 3 * PL, BLK), SEQ, 0, 0)  34.5 us
    pallas_call x13, Pallas kernels, run(): pl.pallas_call(kernel, out_shape=shapes, in_specs=specs, out_specs=[pl.Bl...  23.5 us
    ppermute x12, starting transfers between devices, rotated(): lax.ppermute(value, axis, [(s, (s + k * step) % n) for s in range(n)])  17.3 us
    ppermute x12, waiting for transfers between devices, rotated(): lax.ppermute(value, axis, [(s, (s + k * step) % n) for s in range(n)])  17.2 us
    all_to_all x1, starting transfers between devices, per_device(): recv = lax.all_to_all(send.reshape(BLOCKS, 3 * PL, BLK), SEQ, 0, 0)  13.3 us
    ppermute x8, starting transfers between devices, swapped(): lax.ppermute(value, axis, [(s, s ^ bit) for s in range(lax.axis_size(axis...  11.1 us
    ppermute x8, waiting for transfers between devices, swapped(): lax.ppermute(value, axis, [(s, s ^ bit) for s in range(lax.axis_size(axis...  10.7 us
    all_to_all x1, starting transfers between devices, per_device(): recv2 = lax.all_to_all(back, SEQ, 0, 0).reshape(GROUPS, 16, 2 * PL, BLK)  6.6 us
  transfers between devices with their start and end apart: 22, of which 12 were waited for; matrix products, arithmetic and copies ran while one was open for 0% of the time, Pallas kernels for 5%

profile of v4, /device:TPU:1, one launch (start us, length us, event | category | flops | bytes accessed | tf_op | source)
XLA Modules:
  0.0 142.1 jit_solution(4300058781735862495)
XLA Ops:
  0.6 3.5 %shard_map.143 = bf16[4,16,48,256]{3,2,1,0:T(8,128)(2,1)} custom-call(bf16[256,1024]{1,0:T(8,128)(2,1)} %bitcast.13, bf16[256,1024]{1,0:T(8,128)(2,1)} %bitcast.21, f32[1,1024]{1,0:T(1,128)} %bitcast.16, bf16[256,256]{1,0:T(8,128)(2,1)} %local_ref.1), custom_call_target="tpu_custom_call" | custom-call | flops 140000000 | bytes 4000000 | tf_op jit(solution)/shard_map/pallas_call | solution.py:353
  4.1 13.3 %all-to-all-start = ((bf16[64,48,256]{2,1,0:T(8,128)(2,1)}), bf16[64,48,256]{2,1,0:T(8,128)(2,1)}, u32[]{:S(2)}, u32[]{:S(2)}) async-start(bf16[64,48,256]{2,1,0:T(8,128)(2,1)} %bitcast.20), calls=%async_computation | async-start | bytes 3145728 | tf_op jit(solution)/shard_map/all_to_all | solution.py:408
  17.5 3.8 %shard_map.144 = (bf16[256,1024]{1,0:T(8,128)(2,1)}, f32[256,1024]{1,0:T(8,128)}, f32[256,1024]{1,0:T(8,128)}) custom-call(bf16[256,1024]{1,0:T(8,128)(2,1)} %bitcast.14, bf16[256,1024]{1,0:T(8,128)(2,1)} %bitcast.22, f32[1,1024]{1,0:T(1,128)} %bitcast.17, bf16[4,256,256]{2,1,0:T(8,128)(2,1)} %wu_ref.5, bf16[4,256,256]{2,1,0:T(8,128)(2,1)} %wv_ref.5, ...), custom_call_target="tpu_custom_call" | custom-call | flops 400000000 | bytes 8000000 | tf_op jit(solution)/shard_map/pallas_call | solution.py:353
  21.3 0.6 pad_add_fusion.place_ref
  21.9 34.5 %all-to-all-done.recv_hbm = bf16[64,48,256]{2,1,0:T(8,128)(2,1)} async-done(((bf16[64,48,256]{2,1,0:T(8,128)(2,1)}), bf16[64,48,256]{2,1,0:T(8,128)(2,1)}, u32[]{:S(2)}, u32[]{:S(2)}) %all-to-all-start) | async-done | bytes 1572896 | tf_op jit(solution)/shard_map/all_to_all | solution.py:408
  56.4 8.8 %shard_map.145 = (bf16[64,32,256]{2,1,0:T(8,128)(2,1)}, f32[4,25,8,128]{3,2,1,0:T(8,128)}, bf16[4,25,8,128]{3,2,1,0:T(8,128)(2,1)}) custom-call(s32[3]{0:T(128)} %pad_add_fusion.place_ref, bf16[64,48,256]{2,1,0:T(8,128)(2,1)} %all-to-all-done.recv_hbm, f32[6,2,2,1024]{3,2,1,0:T(2,128)} %coef_hbm.1, bf16[4,256,256]{2,1,0:T(8,128)(2,1)} %wu_ref.5, ...), custom_call_target="tpu_custom_call" | custom-call | flops 800000000 | bytes 4000000 | tf_op jit(solution)/shard_map/pallas_call | solution.py:353
  65.3 0.0 copy-start.11
  65.3 6.6 %all-to-all-start.1 = ((bf16[64,32,256]{2,1,0:T(8,128)(2,1)}), bf16[64,32,256]{2,1,0:T(8,128)(2,1)S(1)}, u32[]{:S(2)}, u32[]{:S(2)}) async-start(bf16[64,32,256]{2,1,0:T(8,128)(2,1)} %get-tuple-element.42), calls=%async_computation.1 | async-start | bytes 2097152 | tf_op jit(solution)/shard_map/all_to_all | solution.py:448
  71.9 0.5 collective-permute-start
  72.5 1.1 collective-permute-done.got_ref
  73.6 0.6 shard_map.147
  74.2 0.0 copy-start.1
  74.2 1.3 collective-permute-start.1
  75.5 2.5 %collective-permute-start.2 = (bf16[25,8,128]{2,1,0:T(8,128)(2,1)S(1)}, bf16[25,8,128]{2,1,0:T(8,128)(2,1)S(1)}, u32[]{:S(2)}, u32[]{:S(2)}) collective-permute-start(bf16[25,8,128]{2,1,0:T(8,128)(2,1)S(1)} %get-tuple-element.51), channel_id=1, source_target_pairs={{0,128},{64,192},{128,0},{192,64},{1,129},{65,193},{129,1},{193,65... | collective-permute-start | bytes 153608 | tf_op jit(solution)/shard_map/ppermute | solution.py:376
  77.9 1.2 collective-permute-start.3
  79.1 1.5 %collective-permute-done.2.refs_1_ = bf16[25,8,128]{2,1,0:T(8,128)(2,1)S(1)} collective-permute-done((bf16[25,8,128]{2,1,0:T(8,128)(2,1)S(1)}, bf16[25,8,128]{2,1,0:T(8,128)(2,1)S(1)}, u32[]{:S(2)}, u32[]{:S(2)}) %collective-permute-start.2) | collective-permute-done | bytes 51232 | tf_op jit(solution)/shard_map/ppermute | solution.py:376
  80.6 0.6 collective-permute-done.3.refs_2_
  81.2 1.4 collective-permute-start.4
  82.6 2.2 %collective-permute-done.4.b_ref = bf16[25,8,128]{2,1,0:T(8,128)(2,1)S(1)} collective-permute-done((bf16[25,8,128]{2,1,0:T(8,128)(2,1)S(1)}, bf16[25,8,128]{2,1,0:T(8,128)(2,1)S(1)}, u32[]{:S(2)}, u32[]{:S(2)}) %collective-permute-start.4) | collective-permute-done | bytes 51232 | tf_op jit(solution)/shard_map/ppermute | solution.py:382
  84.9 2.9 %collective-permute-start.5 = (bf16[25,8,128]{2,1,0:T(8,128)(2,1)S(1)}, bf16[25,8,128]{2,1,0:T(8,128)(2,1)S(1)}, u32[]{:S(2)}, u32[]{:S(2)}) collective-permute-start(bf16[25,8,128]{2,1,0:T(8,128)(2,1)S(1)} %shard_map.149.a_ref), channel_id=1, source_target_pairs={{0,4},{2,6},{4,0},{6,2},{1,5},{3,7},{5,1},{7,3},{8,12},{10,14},{12... | collective-permute-start | bytes 153608 | tf_op jit(solution)/shard_map/ppermute | solution.py:382
  87.8 2.5 %collective-permute-done.5.b_ref = bf16[25,8,128]{2,1,0:T(8,128)(2,1)S(1)} collective-permute-done((bf16[25,8,128]{2,1,0:T(8,128)(2,1)S(1)}, bf16[25,8,128]{2,1,0:T(8,128)(2,1)S(1)}, u32[]{:S(2)}, u32[]{:S(2)}) %collective-permute-start.5) | collective-permute-done | bytes 51232 | tf_op jit(solution)/shard_map/ppermute | solution.py:382
  90.3 2.0 %collective-permute-start.6 = (bf16[25,8,128]{2,1,0:T(8,128)(2,1)S(1)}, bf16[25,8,128]{2,1,0:T(8,128)(2,1)S(1)}, u32[]{:S(2)}, u32[]{:S(2)}) collective-permute-start(bf16[25,8,128]{2,1,0:T(8,128)(2,1)S(1)} %shard_map.150.a_ref), channel_id=1, source_target_pairs={{0,8},{8,0},{16,24},{24,16},{32,40},{40,32},{48,56},{56,48},{1,9},... | collective-permute-start | bytes 153608 | tf_op jit(solution)/shard_map/ppermute | solution.py:382
  92.3 5.0 %collective-permute-done.6.b_ref = bf16[25,8,128]{2,1,0:T(8,128)(2,1)S(1)} collective-permute-done((bf16[25,8,128]{2,1,0:T(8,128)(2,1)S(1)}, bf16[25,8,128]{2,1,0:T(8,128)(2,1)S(1)}, u32[]{:S(2)}, u32[]{:S(2)}) %collective-permute-start.6) | collective-permute-done | bytes 51232 | tf_op jit(solution)/shard_map/ppermute | solution.py:382
  97.3 2.8 %all-to-all-done.1 = bf16[64,32,256]{2,1,0:T(8,128)(2,1)S(1)} async-done(((bf16[64,32,256]{2,1,0:T(8,128)(2,1)}), bf16[64,32,256]{2,1,0:T(8,128)(2,1)S(1)}, u32[]{:S(2)}, u32[]{:S(2)}) %all-to-all-start.1) | async-done | bytes 1048608 | tf_op jit(solution)/shard_map/all_to_all | solution.py:448
  100.1 1.0 copy-done.6
  101.2 0.3 shard_map.152.refs_0_
  101.5 2.7 %collective-permute-start.12 = (bf16[25,8,128]{2,1,0:T(8,128)(2,1)S(1)}, bf16[25,8,128]{2,1,0:T(8,128)(2,1)S(1)}, u32[]{:S(2)}, u32[]{:S(2)}) collective-permute-start(bf16[25,8,128]{2,1,0:T(8,128)(2,1)S(1)} %shard_map.151.refs_0_), channel_id=1, source_target_pairs={{0,48},{8,56},{16,0},{24,8},{32,16},{40,24},{48,32},{56,40},{1,49}... | collective-permute-start | bytes 153608 | tf_op jit(solution)/shard_map/ppermute | solution.py:376
  104.2 1.5 %collective-permute-start.11 = (bf16[25,8,128]{2,1,0:T(8,128)(2,1)S(1)}, bf16[25,8,128]{2,1,0:T(8,128)(2,1)S(1)}, u32[]{:S(2)}, u32[]{:S(2)}) collective-permute-start(bf16[25,8,128]{2,1,0:T(8,128)(2,1)S(1)} %shard_map.151.refs_0_), channel_id=1, source_target_pairs={{0,32},{8,40},{16,48},{24,56},{32,0},{40,8},{48,16},{56,24},{1,33}... | collective-permute-start | bytes 153608 | tf_op jit(solution)/shard_map/ppermute | solution.py:376
  105.7 0.7 collective-permute-start.10
  106.4 5.4 %collective-permute-done.11.refs_2_ = bf16[25,8,128]{2,1,0:T(8,128)(2,1)S(1)} collective-permute-done((bf16[25,8,128]{2,1,0:T(8,128)(2,1)S(1)}, bf16[25,8,128]{2,1,0:T(8,128)(2,1)S(1)}, u32[]{:S(2)}, u32[]{:S(2)}) %collective-permute-start.11) | collective-permute-done | bytes 51232 | tf_op jit(solution)/shard_map/ppermute | solution.py:376
  111.8 0.3 collective-permute-done.10.refs_1_
  112.1 0.6 shard_map.154.refs_0_
  112.7 2.7 %collective-permute-start.18 = (bf16[4,25,8,128]{3,2,1,0:T(8,128)(2,1)S(1)}, bf16[4,25,8,128]{3,2,1,0:T(8,128)(2,1)S(1)}, u32[]{:S(2)}, u32[]{:S(2)}) collective-permute-start(bf16[4,25,8,128]{3,2,1,0:T(8,128)(2,1)S(1)} %shard_map.154.refs_0_), channel_id=1, source_target_pairs={{0,192},{64,0},{128,64},{192,128},{1,193},{65,1},{129,65},{193,129... | collective-permute-start | bytes 614408 | tf_op jit(solution)/shard_map/ppermute | solution.py:376
  115.3 0.5 collective-permute-start.16
  115.9 0.6 collective-permute-start.14
  116.4 2.1 %collective-permute-start.9 = (bf16[256,256]{1,0:T(8,128)(2,1)S(1)}, bf16[256,256]{1,0:T(8,128)(2,1)S(1)}, u32[]{:S(2)}, u32[]{:S(2)}) collective-permute-start(bf16[256,256]{1,0:T(8,128)(2,1)S(1)} %shard_map.152.refs_0_), channel_id=1, source_target_pairs={{0,192},{64,0},{128,64},{192,128},{1,193},{65,1},{129,65},{193,129... | collective-permute-start | bytes 393224 | tf_op jit(solution)/shard_map/ppermute | solution.py:376
  118.5 1.2 collective-permute-start.8
  119.8 7.2 %collective-permute-done.9.refs_3_ = bf16[256,256]{1,0:T(8,128)(2,1)S(1)} collective-permute-done((bf16[256,256]{1,0:T(8,128)(2,1)S(1)}, bf16[256,256]{1,0:T(8,128)(2,1)S(1)}, u32[]{:S(2)}, u32[]{:S(2)}) %collective-permute-start.9) | collective-permute-done | bytes 131104 | tf_op jit(solution)/shard_map/ppermute | solution.py:376
  127.0 3.7 %collective-permute-start.13 = (bf16[4,25,8,128]{3,2,1,0:T(8,128)(2,1)S(1)}, bf16[4,25,8,128]{3,2,1,0:T(8,128)(2,1)S(1)}, u32[]{:S(2)}, u32[]{:S(2)}) collective-permute-start(bf16[4,25,8,128]{3,2,1,0:T(8,128)(2,1)S(1)} %shard_map.154.refs_0_), channel_id=1, source_target_pairs={{0,1},{1,0},{2,3},{3,2},{4,5},{5,4},{6,7},{7,6},{8,9},{9,8},{10,11... | collective-permute-start | bytes 614408 | tf_op jit(solution)/shard_map/ppermute | solution.py:382
  130.7 0.5 collective-permute-start.17
  131.2 0.1 collective-permute-start.15
  131.3 0.4 collective-permute-start.7
  131.7 1.2 copy-done.4
  132.9 1.2 copy-done.5
  134.2 1.9 %shard_map.146 = (bf16[256,1024]{1,0:T(8,128)(2,1)}, bf16[256,1024]{1,0:T(8,128)(2,1)}) custom-call(bf16[4,16,32,256]{3,2,1,0:T(8,128)(2,1)S(1)} %bitcast.12, bf16[256,1024]{1,0:T(8,128)(2,1)S(1)} %bitcast.15, f32[1,1024]{1,0:T(1,128)S(1)} %bitcast.18, f32[256,1024]{1,0:T(8,128)S(1)} %copy-done.4, f32[256,1024]{1,0:T(8,128)S(1)} %copy-done.5, ...), custom_call_target="tpu_custom_call" | custom-call | flops 600000000 | bytes 8000000 | tf_op jit(solution)/shard_map/pallas_call | solution.py:353
  136.0 2.1 %collective-permute-done.7.refs_1_ = bf16[256,256]{1,0:T(8,128)(2,1)S(1)} collective-permute-done((bf16[256,256]{1,0:T(8,128)(2,1)S(1)}, bf16[256,256]{1,0:T(8,128)(2,1)S(1)}, u32[]{:S(2)}, u32[]{:S(2)}) %collective-permute-start.7) | collective-permute-done | bytes 131104 | tf_op jit(solution)/shard_map/ppermute | solution.py:376
  138.2 1.4 shard_map.153
  139.6 2.5 %shard_map.155 = (f32[4,256,256]{2,1,0:T(8,128)}, f32[4,256,256]{2,1,0:T(8,128)}, f32[4,256,256]{2,1,0:T(8,128)}, f32[1,1024]{1,0:T(1,128)}, f32[6,2,2,1024]{3,2,1,0:T(2,128)}) custom-call(s32[3]{0:T(128)S(1)} %copy-done.10, bf16[4,256,256]{2,1,0:T(8,128)(2,1)S(1)} %copy-done, bf16[4,256,256]{2,1,0:T(8,128)(2,1)S(1)} %copy-done.1, f32[1,1024]{1,0:T(1,128)S(1)} %bitcast.19, ...), custom_call_target="tpu_custom_call" | custom-call | bytes 5000000 | tf_op jit(solution)/shard_map/pallas_call | solution.py:353
  (34 shorter events, 0.2 us)
Async XLA Ops:
  4.1 52.3 %all-to-all-start = ((bf16[64,48,256]{2,1,0:T(8,128)(2,1)}), bf16[64,48,256]{2,1,0:T(8,128)(2,1)}, u32[]{:S(2)}, u32[]{:S(2)}) async-start(bf16[64,48,256]{2,1,0:T(8,128)(2,1)} %bitcast.20), calls=%async_computation | async-start | bytes 3145728 | tf_op jit(solution)/shard_map/all_to_all | solution.py:408
  65.3 6.6 %copy-start.11 = (bf16[4,25,8,128]{3,2,1,0:T(8,128)(2,1)S(1)}, bf16[4,25,8,128]{3,2,1,0:T(8,128)(2,1)}, u32[]{:S(2)}) copy-start(bf16[4,25,8,128]{3,2,1,0:T(8,128)(2,1)} %get-tuple-element.48) | copy-start | bytes 614404
  65.3 8.3 %copy-start.8 = (f32[4,25,8,128]{3,2,1,0:T(8,128)S(1)}, f32[4,25,8,128]{3,2,1,0:T(8,128)}, u32[]{:S(2)}) copy-start(f32[4,25,8,128]{3,2,1,0:T(8,128)} %get-tuple-element.47.keep_ref) | copy-start | bytes 1228804
  65.3 8.3 %copy-start.10 = (s32[3]{0:T(128)S(1)}, s32[3]{0:T(128)}, u32[]{:S(2)}) copy-start(s32[3]{0:T(128)} %pad_add_fusion.place_ref) | copy-start | bytes 40
  65.3 34.8 %all-to-all-start.1 = ((bf16[64,32,256]{2,1,0:T(8,128)(2,1)}), bf16[64,32,256]{2,1,0:T(8,128)(2,1)S(1)}, u32[]{:S(2)}, u32[]{:S(2)}) async-start(bf16[64,32,256]{2,1,0:T(8,128)(2,1)} %get-tuple-element.42), calls=%async_computation.1 | async-start | bytes 2097152 | tf_op jit(solution)/shard_map/all_to_all | solution.py:448
  71.9 1.6 %collective-permute-start = (bf16[4,25,8,128]{3,2,1,0:T(8,128)(2,1)S(1)}, bf16[4,25,8,128]{3,2,1,0:T(8,128)(2,1)S(1)}, u32[]{:S(2)}, u32[]{:S(2)}) collective-permute-start(bf16[4,25,8,128]{3,2,1,0:T(8,128)(2,1)S(1)} %copy-done.11), channel_id=1, source_target_pairs={{0,1},{1,0},{2,3},{3,2},{4,5},{5,4},{6,7},{7,6},{8,9},{9,8},{10,11... | collective-permute-start | bytes 614408 | tf_op jit(solution)/shard_map/ppermute | solution.py:382
  73.6 58.1 %copy-start.7 = (bf16[256,256]{1,0:T(8,128)(2,1)S(1)}, bf16[256,256]{1,0:T(8,128)(2,1)}, u32[]{:S(2)}) copy-start(bf16[256,256]{1,0:T(8,128)(2,1)} %local_ref.1) | copy-start | bytes 393220
  73.6 58.1 %copy-start.9 = (f32[1024]{0:T(1024)S(1)}, f32[1024]{0:T(1024)}, u32[]{:S(2)}) copy-start(f32[1024]{0:T(1024)} %param.10) | copy-start | bytes 12292
  74.2 57.5 %copy-start = (bf16[4,256,256]{2,1,0:T(8,128)(2,1)S(1)}, bf16[4,256,256]{2,1,0:T(8,128)(2,1)}, u32[]{:S(2)}) copy-start(bf16[4,256,256]{2,1,0:T(8,128)(2,1)} %wu_ref.5) | copy-start | bytes 1572868
  74.2 57.5 %copy-start.1 = (bf16[4,256,256]{2,1,0:T(8,128)(2,1)S(1)}, bf16[4,256,256]{2,1,0:T(8,128)(2,1)}, u32[]{:S(2)}) copy-start(bf16[4,256,256]{2,1,0:T(8,128)(2,1)} %wv_ref.5) | copy-start | bytes 1572868
  74.2 57.5 %copy-start.2 = (bf16[1,256,1024]{2,1,0:T(8,128)(2,1)S(1)}, bf16[1,256,1024]{2,1,0:T(8,128)(2,1)}, u32[]{:S(2)}) copy-start(bf16[1,256,1024]{2,1,0:T(8,128)(2,1)} %param.8) | copy-start | bytes 1572868
  74.2 57.5 %copy-start.3 = (bf16[4,256,256]{2,1,0:T(8,128)(2,1)S(1)}, bf16[4,256,256]{2,1,0:T(8,128)(2,1)}, u32[]{:S(2)}) copy-start(bf16[4,256,256]{2,1,0:T(8,128)(2,1)} %wo_ref.3) | copy-start | bytes 1572868
  74.2 4.9 %collective-permute-start.1 = (bf16[25,8,128]{2,1,0:T(8,128)(2,1)S(1)}, bf16[25,8,128]{2,1,0:T(8,128)(2,1)S(1)}, u32[]{:S(2)}, u32[]{:S(2)}) collective-permute-start(bf16[25,8,128]{2,1,0:T(8,128)(2,1)S(1)} %get-tuple-element.50), channel_id=1, source_target_pairs={{0,64},{64,128},{128,192},{192,0},{1,65},{65,129},{129,193},{193,1... | collective-permute-start | bytes 153608 | tf_op jit(solution)/shard_map/ppermute | solution.py:376
  75.5 5.1 %collective-permute-start.2 = (bf16[25,8,128]{2,1,0:T(8,128)(2,1)S(1)}, bf16[25,8,128]{2,1,0:T(8,128)(2,1)S(1)}, u32[]{:S(2)}, u32[]{:S(2)}) collective-permute-start(bf16[25,8,128]{2,1,0:T(8,128)(2,1)S(1)} %get-tuple-element.51), channel_id=1, source_target_pairs={{0,128},{64,192},{128,0},{192,64},{1,129},{65,193},{129,1},{193,65... | collective-permute-start | bytes 153608 | tf_op jit(solution)/shard_map/ppermute | solution.py:376
  77.9 3.3 %collective-permute-start.3 = (bf16[25,8,128]{2,1,0:T(8,128)(2,1)S(1)}, bf16[25,8,128]{2,1,0:T(8,128)(2,1)S(1)}, u32[]{:S(2)}, u32[]{:S(2)}) collective-permute-start(bf16[25,8,128]{2,1,0:T(8,128)(2,1)S(1)} %get-tuple-element.52), channel_id=1, source_target_pairs={{0,192},{64,0},{128,64},{192,128},{1,193},{65,1},{129,65},{193,129... | collective-permute-start | bytes 153608 | tf_op jit(solution)/shard_map/ppermute | solution.py:376
  81.2 3.6 %collective-permute-start.4 = (bf16[25,8,128]{2,1,0:T(8,128)(2,1)S(1)}, bf16[25,8,128]{2,1,0:T(8,128)(2,1)S(1)}, u32[]{:S(2)}, u32[]{:S(2)}) collective-permute-start(bf16[25,8,128]{2,1,0:T(8,128)(2,1)S(1)} %shard_map.148.a_ref), channel_id=1, source_target_pairs={{0,2},{2,0},{4,6},{6,4},{1,3},{3,1},{5,7},{7,5},{8,10},{10,8},{12,... | collective-permute-start | bytes 153608 | tf_op jit(solution)/shard_map/ppermute | solution.py:382
  84.9 5.4 %collective-permute-start.5 = (bf16[25,8,128]{2,1,0:T(8,128)(2,1)S(1)}, bf16[25,8,128]{2,1,0:T(8,128)(2,1)S(1)}, u32[]{:S(2)}, u32[]{:S(2)}) collective-permute-start(bf16[25,8,128]{2,1,0:T(8,128)(2,1)S(1)} %shard_map.149.a_ref), channel_id=1, source_target_pairs={{0,4},{2,6},{4,0},{6,2},{1,5},{3,7},{5,1},{7,3},{8,12},{10,14},{12... | collective-permute-start | bytes 153608 | tf_op jit(solution)/shard_map/ppermute | solution.py:382
  90.3 7.0 %collective-permute-start.6 = (bf16[25,8,128]{2,1,0:T(8,128)(2,1)S(1)}, bf16[25,8,128]{2,1,0:T(8,128)(2,1)S(1)}, u32[]{:S(2)}, u32[]{:S(2)}) collective-permute-start(bf16[25,8,128]{2,1,0:T(8,128)(2,1)S(1)} %shard_map.150.a_ref), channel_id=1, source_target_pairs={{0,8},{8,0},{16,24},{24,16},{32,40},{40,32},{48,56},{56,48},{1,9},... | collective-permute-start | bytes 153608 | tf_op jit(solution)/shard_map/ppermute | solution.py:382
  100.1 1.0 copy-start.6
  101.5 4.9 %collective-permute-start.12 = (bf16[25,8,128]{2,1,0:T(8,128)(2,1)S(1)}, bf16[25,8,128]{2,1,0:T(8,128)(2,1)S(1)}, u32[]{:S(2)}, u32[]{:S(2)}) collective-permute-start(bf16[25,8,128]{2,1,0:T(8,128)(2,1)S(1)} %shard_map.151.refs_0_), channel_id=1, source_target_pairs={{0,48},{8,56},{16,0},{24,8},{32,16},{40,24},{48,32},{56,40},{1,49}... | collective-permute-start | bytes 153608 | tf_op jit(solution)/shard_map/ppermute | solution.py:376
  104.2 7.6 %collective-permute-start.11 = (bf16[25,8,128]{2,1,0:T(8,128)(2,1)S(1)}, bf16[25,8,128]{2,1,0:T(8,128)(2,1)S(1)}, u32[]{:S(2)}, u32[]{:S(2)}) collective-permute-start(bf16[25,8,128]{2,1,0:T(8,128)(2,1)S(1)} %shard_map.151.refs_0_), channel_id=1, source_target_pairs={{0,32},{8,40},{16,48},{24,56},{32,0},{40,8},{48,16},{56,24},{1,33}... | collective-permute-start | bytes 153608 | tf_op jit(solution)/shard_map/ppermute | solution.py:376
  105.7 6.4 %collective-permute-start.10 = (bf16[25,8,128]{2,1,0:T(8,128)(2,1)S(1)}, bf16[25,8,128]{2,1,0:T(8,128)(2,1)S(1)}, u32[]{:S(2)}, u32[]{:S(2)}) collective-permute-start(bf16[25,8,128]{2,1,0:T(8,128)(2,1)S(1)} %shard_map.151.refs_0_), channel_id=1, source_target_pairs={{0,16},{8,24},{16,32},{24,40},{32,48},{40,56},{48,0},{56,8},{1,17}... | collective-permute-start | bytes 153608 | tf_op jit(solution)/shard_map/ppermute | solution.py:376
  112.7 18.0 %collective-permute-start.18 = (bf16[4,25,8,128]{3,2,1,0:T(8,128)(2,1)S(1)}, bf16[4,25,8,128]{3,2,1,0:T(8,128)(2,1)S(1)}, u32[]{:S(2)}, u32[]{:S(2)}) collective-permute-start(bf16[4,25,8,128]{3,2,1,0:T(8,128)(2,1)S(1)} %shard_map.154.refs_0_), channel_id=1, source_target_pairs={{0,192},{64,0},{128,64},{192,128},{1,193},{65,1},{129,65},{193,129... | collective-permute-start | bytes 614408 | tf_op jit(solution)/shard_map/ppermute | solution.py:376
  115.3 15.3 %collective-permute-start.16 = (bf16[4,25,8,128]{3,2,1,0:T(8,128)(2,1)S(1)}, bf16[4,25,8,128]{3,2,1,0:T(8,128)(2,1)S(1)}, u32[]{:S(2)}, u32[]{:S(2)}) collective-permute-start(bf16[4,25,8,128]{3,2,1,0:T(8,128)(2,1)S(1)} %shard_map.154.refs_0_), channel_id=1, source_target_pairs={{0,128},{64,192},{128,0},{192,64},{1,129},{65,193},{129,1},{193,65... | collective-permute-start | bytes 614408 | tf_op jit(solution)/shard_map/ppermute | solution.py:376
  115.9 15.3 %collective-permute-start.14 = (bf16[4,25,8,128]{3,2,1,0:T(8,128)(2,1)S(1)}, bf16[4,25,8,128]{3,2,1,0:T(8,128)(2,1)S(1)}, u32[]{:S(2)}, u32[]{:S(2)}) collective-permute-start(bf16[4,25,8,128]{3,2,1,0:T(8,128)(2,1)S(1)} %shard_map.154.refs_0_), channel_id=1, source_target_pairs={{0,64},{64,128},{128,192},{192,0},{1,65},{65,129},{129,193},{193,1... | collective-permute-start | bytes 614408 | tf_op jit(solution)/shard_map/ppermute | solution.py:376
  116.4 10.6 %collective-permute-start.9 = (bf16[256,256]{1,0:T(8,128)(2,1)S(1)}, bf16[256,256]{1,0:T(8,128)(2,1)S(1)}, u32[]{:S(2)}, u32[]{:S(2)}) collective-permute-start(bf16[256,256]{1,0:T(8,128)(2,1)S(1)} %shard_map.152.refs_0_), channel_id=1, source_target_pairs={{0,192},{64,0},{128,64},{192,128},{1,193},{65,1},{129,65},{193,129... | collective-permute-start | bytes 393224 | tf_op jit(solution)/shard_map/ppermute | solution.py:376
  118.5 12.7 %collective-permute-start.8 = (bf16[256,256]{1,0:T(8,128)(2,1)S(1)}, bf16[256,256]{1,0:T(8,128)(2,1)S(1)}, u32[]{:S(2)}, u32[]{:S(2)}) collective-permute-start(bf16[256,256]{1,0:T(8,128)(2,1)S(1)} %shard_map.152.refs_0_), channel_id=1, source_target_pairs={{0,128},{64,192},{128,0},{192,64},{1,129},{65,193},{129,1},{193,65... | collective-permute-start | bytes 393224 | tf_op jit(solution)/shard_map/ppermute | solution.py:376
  127.0 12.6 %collective-permute-start.13 = (bf16[4,25,8,128]{3,2,1,0:T(8,128)(2,1)S(1)}, bf16[4,25,8,128]{3,2,1,0:T(8,128)(2,1)S(1)}, u32[]{:S(2)}, u32[]{:S(2)}) collective-permute-start(bf16[4,25,8,128]{3,2,1,0:T(8,128)(2,1)S(1)} %shard_map.154.refs_0_), channel_id=1, source_target_pairs={{0,1},{1,0},{2,3},{3,2},{4,5},{5,4},{6,7},{7,6},{8,9},{9,8},{10,11... | collective-permute-start | bytes 614408 | tf_op jit(solution)/shard_map/ppermute | solution.py:382
  130.7 8.9 %collective-permute-start.19 = (bf16[4,25,8,128]{3,2,1,0:T(8,128)(2,1)S(1)}, bf16[4,25,8,128]{3,2,1,0:T(8,128)(2,1)S(1)}, u32[]{:S(2)}, u32[]{:S(2)}) collective-permute-start(bf16[4,25,8,128]{3,2,1,0:T(8,128)(2,1)S(1)} %collective-permute-done.18.refs_3_), channel_id=1, source_target_pairs={{0,1},{1,0},{2,3},{3,2},{4,5},{5,4},{6,7},{7,6},{8,9},{9,8},{10,11... | collective-permute-start | bytes 614408 | tf_op jit(solution)/shard_map/ppermute | solution.py:382
  130.7 8.9 %collective-permute-start.17 = (bf16[4,25,8,128]{3,2,1,0:T(8,128)(2,1)S(1)}, bf16[4,25,8,128]{3,2,1,0:T(8,128)(2,1)S(1)}, u32[]{:S(2)}, u32[]{:S(2)}) collective-permute-start(bf16[4,25,8,128]{3,2,1,0:T(8,128)(2,1)S(1)} %collective-permute-done.16.refs_2_), channel_id=1, source_target_pairs={{0,1},{1,0},{2,3},{3,2},{4,5},{5,4},{6,7},{7,6},{8,9},{9,8},{10,11... | collective-permute-start | bytes 614408 | tf_op jit(solution)/shard_map/ppermute | solution.py:382
  131.2 8.4 %collective-permute-start.15 = (bf16[4,25,8,128]{3,2,1,0:T(8,128)(2,1)S(1)}, bf16[4,25,8,128]{3,2,1,0:T(8,128)(2,1)S(1)}, u32[]{:S(2)}, u32[]{:S(2)}) collective-permute-start(bf16[4,25,8,128]{3,2,1,0:T(8,128)(2,1)S(1)} %collective-permute-done.14.refs_1_), channel_id=1, source_target_pairs={{0,1},{1,0},{2,3},{3,2},{4,5},{5,4},{6,7},{7,6},{8,9},{9,8},{10,11... | collective-permute-start | bytes 614408 | tf_op jit(solution)/shard_map/ppermute | solution.py:382
  131.3 6.9 %collective-permute-start.7 = (bf16[256,256]{1,0:T(8,128)(2,1)S(1)}, bf16[256,256]{1,0:T(8,128)(2,1)S(1)}, u32[]{:S(2)}, u32[]{:S(2)}) collective-permute-start(bf16[256,256]{1,0:T(8,128)(2,1)S(1)} %shard_map.152.refs_0_), channel_id=1, source_target_pairs={{0,64},{64,128},{128,192},{192,0},{1,65},{65,129},{129,193},{193,1... | collective-permute-start | bytes 393224 | tf_op jit(solution)/shard_map/ppermute | solution.py:376
  131.7 1.2 copy-start.4
  132.9 1.2 copy-start.5

commit v5 on v4

--- a/solution.py
+++ b/solution.py
@@ -455,26 +455,30 @@
         slice_ = call(pair_sum_kernel, [(quarter, BF)], moved=2e5)(
             slice_, swapped(slice_, axis, bit)
         )[0]
+    got_z = rotated(slice_, "z", 2)
+
     part = call(local_kernel, [((BLK, BLK), BF)], flops=1.3e8, moved=1.2e6)(recv2, u)[0]
-    slice_, part = lax.optimization_barrier((slice_, part))
-    mine_d = call(gather_kernel, [((4,) + quarter, BF)], moved=4e5, smem=(0,))(
-        place, slice_, *rotated(slice_, "z", 2)
-    )[0]
-    halves = [mine_d] + rotated(mine_d, "dp")
-    others = [swapped(half) for half in halves]
-
+    parts = rotated(part, "dp")
     mixed, dx = call(
         last_kernel, [(wide, BF), (wide, BF)], scratch=[pltpu.VMEM(wide, F32)],
         flops=6e8, moved=8e6,
     )(recv2, x, gain2, act, dgd, w_u, w_v, w_o, local_factor)
+    got_z, mixed, dx = lax.optimization_barrier((got_z, mixed, dx))
+
+    mine_d = call(gather_kernel, [((4,) + quarter, BF)], moved=4e5, smem=(0,))(
+        place, slice_, *got_z
+    )[0]
+    mine_d, parts = lax.optimization_barrier((mine_d, parts))
+    halves = [mine_d] + rotated(mine_d, "dp")
     grad_local = call(
         ordered_sum_kernel,
         [((BLK, BLK), F32)],
         scratch=[pltpu.VMEM((4, BLK, BLK), BF)],
         moved=8e5,
         smem=(0,),
-    )(place, part, *rotated(part, "dp"))[0]
-    mixed, dx, grad_local, others = lax.optimization_barrier((mixed, dx, grad_local, others))
+    )(place, part, *parts)[0]
+    others = [swapped(half) for half in halves]
+    others, grad_local = lax.optimization_barrier((others, grad_local))
 
     shape = (GROUPS, BLK, BLK)
     gu, gv, go, grad_gain, grad_bfly = call(

time: 143 us -> 137 us (0.958)
  waiting for transfers between devices: 65.2 us -> 50.5 us
  starting transfers between devices: 48.4 us -> 56.4 us
    ppermute x12, waiting for transfers between devices: 17.2 us -> 2.13 us  [rotated(): lax.ppermute(value, axis, [(s, (s + k * step) % n) for s in range(n)])]
    ppermute x8, starting transfers between devices: 11.1 us -> 18.3 us  [swapped(): lax.ppermute(value, axis, [(s, s ^ bit) for s in range(lax.axis_size(axis...]
    all_to_all x1, waiting for transfers between devices: 2.84 us -> 7.11 us  [per_device(): recv2 = lax.all_to_all(back, SEQ, 0, 0).reshape(GROUPS, 16, 2 * PL, BLK)]
    ppermute x8, waiting for transfers between devices: 10.7 us -> 6.79 us  [swapped(): lax.ppermute(value, axis, [(s, s ^ bit) for s in range(lax.axis_size(axis...]
    unnamed x24 -> x22, local copies, waits for them, and re-layouts: 3.54 us -> 4.53 us
  transfers between devices with their start and end apart: 22 -> 22, of which waited for: 12 -> 7; matrix products, arithmetic and copies ran while one was open for 0% -> 0% of each run, Pallas kernels for 5% -> 6%
where the time goes in v5:
time: 137 us; the launch traced here: 136 us
  starting transfers between devices  56.4 us (41%)
  waiting for transfers between devices  50.5 us (37%)
  Pallas kernels  23.5 us (17%)
  local copies, waits for them, and re-layouts  4.53 us (3%)
    all_to_all x1, waiting for transfers between devices, per_device(): recv = lax.all_to_all(send.reshape(BLOCKS, 3 * PL, BLK), SEQ, 0, 0)  34.4 us
    pallas_call x13, Pallas kernels, run(): pl.pallas_call(kernel, out_shape=shapes, in_specs=specs, out_specs=[pl.Bl...  23.5 us
    ppermute x8, starting transfers between devices, swapped(): lax.ppermute(value, axis, [(s, s ^ bit) for s in range(lax.axis_size(axis...  18.3 us
    ppermute x12, starting transfers between devices, rotated(): lax.ppermute(value, axis, [(s, (s + k * step) % n) for s in range(n)])  18.2 us
    all_to_all x1, starting transfers between devices, per_device(): recv = lax.all_to_all(send.reshape(BLOCKS, 3 * PL, BLK), SEQ, 0, 0)  13.3 us
    all_to_all x1, waiting for transfers between devices, per_device(): recv2 = lax.all_to_all(back, SEQ, 0, 0).reshape(GROUPS, 16, 2 * PL, BLK)  7.11 us
    ppermute x8, waiting for transfers between devices, swapped(): lax.ppermute(value, axis, [(s, s ^ bit) for s in range(lax.axis_size(axis...  6.79 us
    all_to_all x1, starting transfers between devices, per_device(): recv2 = lax.all_to_all(back, SEQ, 0, 0).reshape(GROUPS, 16, 2 * PL, BLK)  6.6 us
  transfers between devices with their start and end apart: 22, of which 7 were waited for; matrix products, arithmetic and copies ran while one was open for 0% of the time, Pallas kernels for 6%

profile of v5, /device:TPU:1, one launch (start us, length us, event | category | flops | bytes accessed | tf_op | source)
XLA Modules:
  0.0 136.5 jit_solution(4149407738939450466)
XLA Ops:
  0.6 3.5 %shard_map.143 = bf16[4,16,48,256]{3,2,1,0:T(8,128)(2,1)} custom-call(bf16[256,1024]{1,0:T(8,128)(2,1)} %bitcast.13, bf16[256,1024]{1,0:T(8,128)(2,1)} %bitcast.21, f32[1,1024]{1,0:T(1,128)} %bitcast.16, bf16[256,256]{1,0:T(8,128)(2,1)} %local_ref.1), custom_call_target="tpu_custom_call" | custom-call | flops 140000000 | bytes 4000000 | tf_op jit(solution)/shard_map/pallas_call | solution.py:353
  4.1 13.3 %all-to-all-start = ((bf16[64,48,256]{2,1,0:T(8,128)(2,1)}), bf16[64,48,256]{2,1,0:T(8,128)(2,1)}, u32[]{:S(2)}, u32[]{:S(2)}) async-start(bf16[64,48,256]{2,1,0:T(8,128)(2,1)} %bitcast.20), calls=%async_computation | async-start | bytes 3145728 | tf_op jit(solution)/shard_map/all_to_all | solution.py:408
  17.5 3.8 %shard_map.144 = (bf16[256,1024]{1,0:T(8,128)(2,1)}, f32[256,1024]{1,0:T(8,128)}, f32[256,1024]{1,0:T(8,128)}) custom-call(bf16[256,1024]{1,0:T(8,128)(2,1)} %bitcast.14, bf16[256,1024]{1,0:T(8,128)(2,1)} %bitcast.22, f32[1,1024]{1,0:T(1,128)} %bitcast.17, bf16[4,256,256]{2,1,0:T(8,128)(2,1)} %wu_ref.5, bf16[4,256,256]{2,1,0:T(8,128)(2,1)} %wv_ref.5, ...), custom_call_target="tpu_custom_call" | custom-call | flops 400000000 | bytes 8000000 | tf_op jit(solution)/shard_map/pallas_call | solution.py:353
  21.3 0.6 pad_add_fusion.place_ref
  22.0 34.4 %all-to-all-done.recv_hbm = bf16[64,48,256]{2,1,0:T(8,128)(2,1)} async-done(((bf16[64,48,256]{2,1,0:T(8,128)(2,1)}), bf16[64,48,256]{2,1,0:T(8,128)(2,1)}, u32[]{:S(2)}, u32[]{:S(2)}) %all-to-all-start) | async-done | bytes 1572896 | tf_op jit(solution)/shard_map/all_to_all | solution.py:408
  56.4 8.8 %shard_map.145 = (bf16[64,32,256]{2,1,0:T(8,128)(2,1)}, f32[4,25,8,128]{3,2,1,0:T(8,128)}, bf16[4,25,8,128]{3,2,1,0:T(8,128)(2,1)}) custom-call(s32[3]{0:T(128)} %pad_add_fusion.place_ref, bf16[64,48,256]{2,1,0:T(8,128)(2,1)} %all-to-all-done.recv_hbm, f32[6,2,2,1024]{3,2,1,0:T(2,128)} %coef_hbm.1, bf16[4,256,256]{2,1,0:T(8,128)(2,1)} %wu_ref.5, ...), custom_call_target="tpu_custom_call" | custom-call | flops 800000000 | bytes 4000000 | tf_op jit(solution)/shard_map/pallas_call | solution.py:353
  65.3 0.0 copy-start.7
  65.3 0.0 copy-start.9
  65.3 6.6 %all-to-all-start.1 = ((bf16[64,32,256]{2,1,0:T(8,128)(2,1)}), bf16[64,32,256]{2,1,0:T(8,128)(2,1)S(1)}, u32[]{:S(2)}, u32[]{:S(2)}) async-start(bf16[64,32,256]{2,1,0:T(8,128)(2,1)} %get-tuple-element.53), calls=%async_computation.1 | async-start | bytes 2097152 | tf_op jit(solution)/shard_map/all_to_all | solution.py:448
  71.9 0.0 copy-start
  71.9 0.0 copy-start.1
  71.9 0.0 copy-start.2
  72.0 0.5 collective-permute-start
  72.5 1.3 collective-permute-done.got_ref
  73.8 1.0 copy-done.8
  74.8 0.6 shard_map.146
  75.4 1.3 collective-permute-start.1
  76.7 2.5 %collective-permute-start.2 = (bf16[25,8,128]{2,1,0:T(8,128)(2,1)S(1)}, bf16[25,8,128]{2,1,0:T(8,128)(2,1)S(1)}, u32[]{:S(2)}, u32[]{:S(2)}) collective-permute-start(bf16[25,8,128]{2,1,0:T(8,128)(2,1)S(1)} %get-tuple-element.51), channel_id=1, source_target_pairs={{0,128},{64,192},{128,0},{192,64},{1,129},{65,193},{129,1},{193,65... | collective-permute-start | bytes 153608 | tf_op jit(solution)/shard_map/ppermute | solution.py:376
  79.1 1.1 collective-permute-start.3
  80.3 1.5 %collective-permute-done.2.refs_1_ = bf16[25,8,128]{2,1,0:T(8,128)(2,1)S(1)} collective-permute-done((bf16[25,8,128]{2,1,0:T(8,128)(2,1)S(1)}, bf16[25,8,128]{2,1,0:T(8,128)(2,1)S(1)}, u32[]{:S(2)}, u32[]{:S(2)}) %collective-permute-start.2) | collective-permute-done | bytes 51232 | tf_op jit(solution)/shard_map/ppermute | solution.py:376
  81.8 0.6 collective-permute-done.3.refs_2_
  82.4 1.4 %collective-permute-start.4 = (bf16[25,8,128]{2,1,0:T(8,128)(2,1)S(1)}, bf16[25,8,128]{2,1,0:T(8,128)(2,1)S(1)}, u32[]{:S(2)}, u32[]{:S(2)}) collective-permute-start(bf16[25,8,128]{2,1,0:T(8,128)(2,1)S(1)} %shard_map.147.a_ref), channel_id=1, source_target_pairs={{0,2},{2,0},{4,6},{6,4},{1,3},{3,1},{5,7},{7,5},{8,10},{10,8},{12,... | collective-permute-start | bytes 153608 | tf_op jit(solution)/shard_map/ppermute | solution.py:382
  83.8 2.4 %collective-permute-done.4.b_ref = bf16[25,8,128]{2,1,0:T(8,128)(2,1)S(1)} collective-permute-done((bf16[25,8,128]{2,1,0:T(8,128)(2,1)S(1)}, bf16[25,8,128]{2,1,0:T(8,128)(2,1)S(1)}, u32[]{:S(2)}, u32[]{:S(2)}) %collective-permute-start.4) | collective-permute-done | bytes 51232 | tf_op jit(solution)/shard_map/ppermute | solution.py:382
  86.2 2.6 %collective-permute-start.5 = (bf16[25,8,128]{2,1,0:T(8,128)(2,1)S(1)}, bf16[25,8,128]{2,1,0:T(8,128)(2,1)S(1)}, u32[]{:S(2)}, u32[]{:S(2)}) collective-permute-start(bf16[25,8,128]{2,1,0:T(8,128)(2,1)S(1)} %shard_map.148.a_ref), channel_id=1, source_target_pairs={{0,4},{2,6},{4,0},{6,2},{1,5},{3,7},{5,1},{7,3},{8,12},{10,14},{12... | collective-permute-start | bytes 153608 | tf_op jit(solution)/shard_map/ppermute | solution.py:382
  88.9 3.1 %collective-permute-done.5.b_ref = bf16[25,8,128]{2,1,0:T(8,128)(2,1)S(1)} collective-permute-done((bf16[25,8,128]{2,1,0:T(8,128)(2,1)S(1)}, bf16[25,8,128]{2,1,0:T(8,128)(2,1)S(1)}, u32[]{:S(2)}, u32[]{:S(2)}) %collective-permute-start.5) | collective-permute-done | bytes 51232 | tf_op jit(solution)/shard_map/ppermute | solution.py:382
  92.0 0.8 collective-permute-start.6
  92.8 7.1 %all-to-all-done.1 = bf16[64,32,256]{2,1,0:T(8,128)(2,1)S(1)} async-done(((bf16[64,32,256]{2,1,0:T(8,128)(2,1)}), bf16[64,32,256]{2,1,0:T(8,128)(2,1)S(1)}, u32[]{:S(2)}, u32[]{:S(2)}) %all-to-all-start.1) | async-done | bytes 1048608 | tf_op jit(solution)/shard_map/all_to_all | solution.py:448
  99.9 1.0 copy-done.6
  100.9 0.3 shard_map.153.refs_0_
  101.3 2.6 %collective-permute-start.12 = (bf16[256,256]{1,0:T(8,128)(2,1)S(1)}, bf16[256,256]{1,0:T(8,128)(2,1)S(1)}, u32[]{:S(2)}, u32[]{:S(2)}) collective-permute-start(bf16[256,256]{1,0:T(8,128)(2,1)S(1)} %shard_map.153.refs_0_), channel_id=1, source_target_pairs={{0,192},{64,0},{128,64},{192,128},{1,193},{65,1},{129,65},{193,129... | collective-permute-start | bytes 393224 | tf_op jit(solution)/shard_map/ppermute | solution.py:376
  103.8 0.6 collective-permute-start.11
  104.4 0.8 collective-permute-start.10
  105.2 2.7 %collective-permute-start.9 = (bf16[25,8,128]{2,1,0:T(8,128)(2,1)S(1)}, bf16[25,8,128]{2,1,0:T(8,128)(2,1)S(1)}, u32[]{:S(2)}, u32[]{:S(2)}) collective-permute-start(bf16[25,8,128]{2,1,0:T(8,128)(2,1)S(1)} %shard_map.150.refs_0_), channel_id=1, source_target_pairs={{0,48},{8,56},{16,0},{24,8},{32,16},{40,24},{48,32},{56,40},{1,49}... | collective-permute-start | bytes 153608 | tf_op jit(solution)/shard_map/ppermute | solution.py:376
  107.9 1.5 %collective-permute-start.8 = (bf16[25,8,128]{2,1,0:T(8,128)(2,1)S(1)}, bf16[25,8,128]{2,1,0:T(8,128)(2,1)S(1)}, u32[]{:S(2)}, u32[]{:S(2)}) collective-permute-start(bf16[25,8,128]{2,1,0:T(8,128)(2,1)S(1)} %shard_map.150.refs_0_), channel_id=1, source_target_pairs={{0,32},{8,40},{16,48},{24,56},{32,0},{40,8},{48,16},{56,24},{1,33}... | collective-permute-start | bytes 153608 | tf_op jit(solution)/shard_map/ppermute | solution.py:376
  109.4 1.9 %collective-permute-start.7 = (bf16[25,8,128]{2,1,0:T(8,128)(2,1)S(1)}, bf16[25,8,128]{2,1,0:T(8,128)(2,1)S(1)}, u32[]{:S(2)}, u32[]{:S(2)}) collective-permute-start(bf16[25,8,128]{2,1,0:T(8,128)(2,1)S(1)} %shard_map.150.refs_0_), channel_id=1, source_target_pairs={{0,16},{8,24},{16,32},{24,40},{32,48},{40,56},{48,0},{56,8},{1,17}... | collective-permute-start | bytes 153608 | tf_op jit(solution)/shard_map/ppermute | solution.py:376
  111.3 0.0 copy-start.4
  111.3 1.2 copy-done.4
  112.5 1.2 copy-done.5
  113.7 1.9 %shard_map.151 = (bf16[256,1024]{1,0:T(8,128)(2,1)}, bf16[256,1024]{1,0:T(8,128)(2,1)}) custom-call(bf16[4,16,32,256]{3,2,1,0:T(8,128)(2,1)S(1)} %bitcast.12, bf16[256,1024]{1,0:T(8,128)(2,1)S(1)} %bitcast.15, f32[1,1024]{1,0:T(1,128)S(1)} %bitcast.18, f32[256,1024]{1,0:T(8,128)S(1)} %copy-done.4, f32[256,1024]{1,0:T(8,128)S(1)} %copy-done.5, ...), custom_call_target="tpu_custom_call" | custom-call | flops 600000000 | bytes 8000000 | tf_op jit(solution)/shard_map/pallas_call | solution.py:353
  115.6 0.6 shard_map.152.refs_0_
  116.2 2.3 %collective-permute-start.15 = (bf16[4,25,8,128]{3,2,1,0:T(8,128)(2,1)S(1)}, bf16[4,25,8,128]{3,2,1,0:T(8,128)(2,1)S(1)}, u32[]{:S(2)}, u32[]{:S(2)}) collective-permute-start(bf16[4,25,8,128]{3,2,1,0:T(8,128)(2,1)S(1)} %shard_map.152.refs_0_), channel_id=1, source_target_pairs={{0,192},{64,0},{128,64},{192,128},{1,193},{65,1},{129,65},{193,129... | collective-permute-start | bytes 614408 | tf_op jit(solution)/shard_map/ppermute | solution.py:376
  118.6 1.0 collective-permute-start.14
  119.6 5.0 %collective-permute-start.16 = (bf16[4,25,8,128]{3,2,1,0:T(8,128)(2,1)S(1)}, bf16[4,25,8,128]{3,2,1,0:T(8,128)(2,1)S(1)}, u32[]{:S(2)}, u32[]{:S(2)}) collective-permute-start(bf16[4,25,8,128]{3,2,1,0:T(8,128)(2,1)S(1)} %shard_map.152.refs_0_), channel_id=1, source_target_pairs={{0,1},{1,0},{2,3},{3,2},{4,5},{5,4},{6,7},{7,6},{8,9},{9,8},{10,11... | collective-permute-start | bytes 614408 | tf_op jit(solution)/shard_map/ppermute | solution.py:382
  124.6 4.0 %collective-permute-start.19 = (bf16[4,25,8,128]{3,2,1,0:T(8,128)(2,1)S(1)}, bf16[4,25,8,128]{3,2,1,0:T(8,128)(2,1)S(1)}, u32[]{:S(2)}, u32[]{:S(2)}) collective-permute-start(bf16[4,25,8,128]{3,2,1,0:T(8,128)(2,1)S(1)} %collective-permute-done.15.refs_3_), channel_id=1, source_target_pairs={{0,1},{1,0},{2,3},{3,2},{4,5},{5,4},{6,7},{7,6},{8,9},{9,8},{10,11... | collective-permute-start | bytes 614408 | tf_op jit(solution)/shard_map/ppermute | solution.py:382
  128.6 1.9 %collective-permute-start.18 = (bf16[4,25,8,128]{3,2,1,0:T(8,128)(2,1)S(1)}, bf16[4,25,8,128]{3,2,1,0:T(8,128)(2,1)S(1)}, u32[]{:S(2)}, u32[]{:S(2)}) collective-permute-start(bf16[4,25,8,128]{3,2,1,0:T(8,128)(2,1)S(1)} %collective-permute-done.14.refs_2_), channel_id=1, source_target_pairs={{0,1},{1,0},{2,3},{3,2},{4,5},{5,4},{6,7},{7,6},{8,9},{9,8},{10,11... | collective-permute-start | bytes 614408 | tf_op jit(solution)/shard_map/ppermute | solution.py:382
  130.5 2.1 %collective-permute-start.17 = (bf16[4,25,8,128]{3,2,1,0:T(8,128)(2,1)S(1)}, bf16[4,25,8,128]{3,2,1,0:T(8,128)(2,1)S(1)}, u32[]{:S(2)}, u32[]{:S(2)}) collective-permute-start(bf16[4,25,8,128]{3,2,1,0:T(8,128)(2,1)S(1)} %collective-permute-done.13.refs_1_), channel_id=1, source_target_pairs={{0,1},{1,0},{2,3},{3,2},{4,5},{5,4},{6,7},{7,6},{8,9},{9,8},{10,11... | collective-permute-start | bytes 614408 | tf_op jit(solution)/shard_map/ppermute | solution.py:382
  132.5 1.4 %shard_map.154 = f32[256,256]{1,0:T(8,128)} custom-call(s32[3]{0:T(128)S(1)} %copy-done.10, bf16[256,256]{1,0:T(8,128)(2,1)S(1)} %shard_map.153.refs_0_, bf16[256,256]{1,0:T(8,128)(2,1)S(1)} %collective-permute-done.10.refs_1_, bf16[256,256]{1,0:T(8,128)(2,1)S(1)} %collective-permute-done.11.refs_2_, bf16[256,256]{1,0:T(8,128)(2,1)S(1)} %collective-permute-done.12.refs_3_), custom_call_target="tpu_custom_call" | custom-call | bytes 800000 | tf_op jit(solution)/shard_map/pallas_call | solution.py:353
  133.9 2.5 %shard_map.155 = (f32[4,256,256]{2,1,0:T(8,128)}, f32[4,256,256]{2,1,0:T(8,128)}, f32[4,256,256]{2,1,0:T(8,128)}, f32[1,1024]{1,0:T(1,128)}, f32[6,2,2,1024]{3,2,1,0:T(2,128)}) custom-call(s32[3]{0:T(128)S(1)} %copy-done.10, bf16[4,256,256]{2,1,0:T(8,128)(2,1)S(1)} %copy-done, bf16[4,256,256]{2,1,0:T(8,128)(2,1)S(1)} %copy-done.1, f32[1,1024]{1,0:T(1,128)S(1)} %bitcast.19, ...), custom_call_target="tpu_custom_call" | custom-call | bytes 5000000 | tf_op jit(solution)/shard_map/pallas_call | solution.py:353
  (32 shorter events, 0.1 us)
Async XLA Ops:
  4.1 52.3 %all-to-all-start = ((bf16[64,48,256]{2,1,0:T(8,128)(2,1)}), bf16[64,48,256]{2,1,0:T(8,128)(2,1)}, u32[]{:S(2)}, u32[]{:S(2)}) async-start(bf16[64,48,256]{2,1,0:T(8,128)(2,1)} %bitcast.20), calls=%async_computation | async-start | bytes 3145728 | tf_op jit(solution)/shard_map/all_to_all | solution.py:408
  65.3 8.5 %copy-start.10 = (s32[3]{0:T(128)S(1)}, s32[3]{0:T(128)}, u32[]{:S(2)}) copy-start(s32[3]{0:T(128)} %pad_add_fusion.place_ref) | copy-start | bytes 40
  65.3 46.0 %copy-start.7 = (bf16[256,256]{1,0:T(8,128)(2,1)S(1)}, bf16[256,256]{1,0:T(8,128)(2,1)}, u32[]{:S(2)}) copy-start(bf16[256,256]{1,0:T(8,128)(2,1)} %local_ref.1) | copy-start | bytes 393220
  65.3 46.0 %copy-start.9 = (f32[1024]{0:T(1024)S(1)}, f32[1024]{0:T(1024)}, u32[]{:S(2)}) copy-start(f32[1024]{0:T(1024)} %param.10) | copy-start | bytes 12292
  65.3 34.6 %all-to-all-start.1 = ((bf16[64,32,256]{2,1,0:T(8,128)(2,1)}), bf16[64,32,256]{2,1,0:T(8,128)(2,1)S(1)}, u32[]{:S(2)}, u32[]{:S(2)}) async-start(bf16[64,32,256]{2,1,0:T(8,128)(2,1)} %get-tuple-element.53), calls=%async_computation.1 | async-start | bytes 2097152 | tf_op jit(solution)/shard_map/all_to_all | solution.py:448
  71.9 39.3 %copy-start = (bf16[4,256,256]{2,1,0:T(8,128)(2,1)S(1)}, bf16[4,256,256]{2,1,0:T(8,128)(2,1)}, u32[]{:S(2)}) copy-start(bf16[4,256,256]{2,1,0:T(8,128)(2,1)} %wu_ref.5) | copy-start | bytes 1572868
  71.9 39.3 %copy-start.1 = (bf16[4,256,256]{2,1,0:T(8,128)(2,1)S(1)}, bf16[4,256,256]{2,1,0:T(8,128)(2,1)}, u32[]{:S(2)}) copy-start(bf16[4,256,256]{2,1,0:T(8,128)(2,1)} %wv_ref.5) | copy-start | bytes 1572868
  71.9 39.3 %copy-start.2 = (bf16[1,256,1024]{2,1,0:T(8,128)(2,1)S(1)}, bf16[1,256,1024]{2,1,0:T(8,128)(2,1)}, u32[]{:S(2)}) copy-start(bf16[1,256,1024]{2,1,0:T(8,128)(2,1)} %param.8) | copy-start | bytes 1572868
  72.0 39.3 %copy-start.3 = (bf16[4,256,256]{2,1,0:T(8,128)(2,1)S(1)}, bf16[4,256,256]{2,1,0:T(8,128)(2,1)}, u32[]{:S(2)}) copy-start(bf16[4,256,256]{2,1,0:T(8,128)(2,1)} %wo_ref.3) | copy-start | bytes 1572868
  72.0 1.8 %collective-permute-start = (bf16[4,25,8,128]{3,2,1,0:T(8,128)(2,1)}, bf16[4,25,8,128]{3,2,1,0:T(8,128)(2,1)S(1)}, u32[]{:S(2)}, u32[]{:S(2)}) collective-permute-start(bf16[4,25,8,128]{3,2,1,0:T(8,128)(2,1)} %get-tuple-element.48), channel_id=1, source_target_pairs={{0,1},{1,0},{2,3},{3,2},{4,5},{5,4},{6,7},{7,6},{8,9},{9,8},{10,11... | collective-permute-start | bytes 614408 | tf_op jit(solution)/shard_map/ppermute | solution.py:382
  73.8 1.0 copy-start.8
  75.4 4.9 %collective-permute-start.1 = (bf16[25,8,128]{2,1,0:T(8,128)(2,1)S(1)}, bf16[25,8,128]{2,1,0:T(8,128)(2,1)S(1)}, u32[]{:S(2)}, u32[]{:S(2)}) collective-permute-start(bf16[25,8,128]{2,1,0:T(8,128)(2,1)S(1)} %get-tuple-element.50), channel_id=1, source_target_pairs={{0,64},{64,128},{128,192},{192,0},{1,65},{65,129},{129,193},{193,1... | collective-permute-start | bytes 153608 | tf_op jit(solution)/shard_map/ppermute | solution.py:376
  76.7 5.1 %collective-permute-start.2 = (bf16[25,8,128]{2,1,0:T(8,128)(2,1)S(1)}, bf16[25,8,128]{2,1,0:T(8,128)(2,1)S(1)}, u32[]{:S(2)}, u32[]{:S(2)}) collective-permute-start(bf16[25,8,128]{2,1,0:T(8,128)(2,1)S(1)} %get-tuple-element.51), channel_id=1, source_target_pairs={{0,128},{64,192},{128,0},{192,64},{1,129},{65,193},{129,1},{193,65... | collective-permute-start | bytes 153608 | tf_op jit(solution)/shard_map/ppermute | solution.py:376
  79.1 3.3 %collective-permute-start.3 = (bf16[25,8,128]{2,1,0:T(8,128)(2,1)S(1)}, bf16[25,8,128]{2,1,0:T(8,128)(2,1)S(1)}, u32[]{:S(2)}, u32[]{:S(2)}) collective-permute-start(bf16[25,8,128]{2,1,0:T(8,128)(2,1)S(1)} %get-tuple-element.52), channel_id=1, source_target_pairs={{0,192},{64,0},{128,64},{192,128},{1,193},{65,1},{129,65},{193,129... | collective-permute-start | bytes 153608 | tf_op jit(solution)/shard_map/ppermute | solution.py:376
  82.4 3.8 %collective-permute-start.4 = (bf16[25,8,128]{2,1,0:T(8,128)(2,1)S(1)}, bf16[25,8,128]{2,1,0:T(8,128)(2,1)S(1)}, u32[]{:S(2)}, u32[]{:S(2)}) collective-permute-start(bf16[25,8,128]{2,1,0:T(8,128)(2,1)S(1)} %shard_map.147.a_ref), channel_id=1, source_target_pairs={{0,2},{2,0},{4,6},{6,4},{1,3},{3,1},{5,7},{7,5},{8,10},{10,8},{12,... | collective-permute-start | bytes 153608 | tf_op jit(solution)/shard_map/ppermute | solution.py:382
  86.2 5.7 %collective-permute-start.5 = (bf16[25,8,128]{2,1,0:T(8,128)(2,1)S(1)}, bf16[25,8,128]{2,1,0:T(8,128)(2,1)S(1)}, u32[]{:S(2)}, u32[]{:S(2)}) collective-permute-start(bf16[25,8,128]{2,1,0:T(8,128)(2,1)S(1)} %shard_map.148.a_ref), channel_id=1, source_target_pairs={{0,4},{2,6},{4,0},{6,2},{1,5},{3,7},{5,1},{7,3},{8,12},{10,14},{12... | collective-permute-start | bytes 153608 | tf_op jit(solution)/shard_map/ppermute | solution.py:382
  92.0 13.2 %collective-permute-start.6 = (bf16[25,8,128]{2,1,0:T(8,128)(2,1)S(1)}, bf16[25,8,128]{2,1,0:T(8,128)(2,1)S(1)}, u32[]{:S(2)}, u32[]{:S(2)}) collective-permute-start(bf16[25,8,128]{2,1,0:T(8,128)(2,1)S(1)} %shard_map.149.a_ref), channel_id=1, source_target_pairs={{0,8},{8,0},{16,24},{24,16},{32,40},{40,32},{48,56},{56,48},{1,9},... | collective-permute-start | bytes 153608 | tf_op jit(solution)/shard_map/ppermute | solution.py:382
  99.9 1.0 copy-start.6
  101.3 14.9 %collective-permute-start.12 = (bf16[256,256]{1,0:T(8,128)(2,1)S(1)}, bf16[256,256]{1,0:T(8,128)(2,1)S(1)}, u32[]{:S(2)}, u32[]{:S(2)}) collective-permute-start(bf16[256,256]{1,0:T(8,128)(2,1)S(1)} %shard_map.153.refs_0_), channel_id=1, source_target_pairs={{0,192},{64,0},{128,64},{192,128},{1,193},{65,1},{129,65},{193,129... | collective-permute-start | bytes 393224 | tf_op jit(solution)/shard_map/ppermute | solution.py:376
  103.8 12.4 %collective-permute-start.11 = (bf16[256,256]{1,0:T(8,128)(2,1)S(1)}, bf16[256,256]{1,0:T(8,128)(2,1)S(1)}, u32[]{:S(2)}, u32[]{:S(2)}) collective-permute-start(bf16[256,256]{1,0:T(8,128)(2,1)S(1)} %shard_map.153.refs_0_), channel_id=1, source_target_pairs={{0,128},{64,192},{128,0},{192,64},{1,129},{65,193},{129,1},{193,65... | collective-permute-start | bytes 393224 | tf_op jit(solution)/shard_map/ppermute | solution.py:376
  104.4 11.8 %collective-permute-start.10 = (bf16[256,256]{1,0:T(8,128)(2,1)S(1)}, bf16[256,256]{1,0:T(8,128)(2,1)S(1)}, u32[]{:S(2)}, u32[]{:S(2)}) collective-permute-start(bf16[256,256]{1,0:T(8,128)(2,1)S(1)} %shard_map.153.refs_0_), channel_id=1, source_target_pairs={{0,64},{64,128},{128,192},{192,0},{1,65},{65,129},{129,193},{193,1... | collective-permute-start | bytes 393224 | tf_op jit(solution)/shard_map/ppermute | solution.py:376
  105.2 4.2 %collective-permute-start.9 = (bf16[25,8,128]{2,1,0:T(8,128)(2,1)S(1)}, bf16[25,8,128]{2,1,0:T(8,128)(2,1)S(1)}, u32[]{:S(2)}, u32[]{:S(2)}) collective-permute-start(bf16[25,8,128]{2,1,0:T(8,128)(2,1)S(1)} %shard_map.150.refs_0_), channel_id=1, source_target_pairs={{0,48},{8,56},{16,0},{24,8},{32,16},{40,24},{48,32},{56,40},{1,49}... | collective-permute-start | bytes 153608 | tf_op jit(solution)/shard_map/ppermute | solution.py:376
  107.9 7.7 %collective-permute-start.8 = (bf16[25,8,128]{2,1,0:T(8,128)(2,1)S(1)}, bf16[25,8,128]{2,1,0:T(8,128)(2,1)S(1)}, u32[]{:S(2)}, u32[]{:S(2)}) collective-permute-start(bf16[25,8,128]{2,1,0:T(8,128)(2,1)S(1)} %shard_map.150.refs_0_), channel_id=1, source_target_pairs={{0,32},{8,40},{16,48},{24,56},{32,0},{40,8},{48,16},{56,24},{1,33}... | collective-permute-start | bytes 153608 | tf_op jit(solution)/shard_map/ppermute | solution.py:376
  109.4 6.2 %collective-permute-start.7 = (bf16[25,8,128]{2,1,0:T(8,128)(2,1)S(1)}, bf16[25,8,128]{2,1,0:T(8,128)(2,1)S(1)}, u32[]{:S(2)}, u32[]{:S(2)}) collective-permute-start(bf16[25,8,128]{2,1,0:T(8,128)(2,1)S(1)} %shard_map.150.refs_0_), channel_id=1, source_target_pairs={{0,16},{8,24},{16,32},{24,40},{32,48},{40,56},{48,0},{56,8},{1,17}... | collective-permute-start | bytes 153608 | tf_op jit(solution)/shard_map/ppermute | solution.py:376
  111.3 1.2 copy-start.4
  112.5 1.2 copy-start.5
  116.2 8.4 %collective-permute-start.15 = (bf16[4,25,8,128]{3,2,1,0:T(8,128)(2,1)S(1)}, bf16[4,25,8,128]{3,2,1,0:T(8,128)(2,1)S(1)}, u32[]{:S(2)}, u32[]{:S(2)}) collective-permute-start(bf16[4,25,8,128]{3,2,1,0:T(8,128)(2,1)S(1)} %shard_map.152.refs_0_), channel_id=1, source_target_pairs={{0,192},{64,0},{128,64},{192,128},{1,193},{65,1},{129,65},{193,129... | collective-permute-start | bytes 614408 | tf_op jit(solution)/shard_map/ppermute | solution.py:376
  118.6 10.0 %collective-permute-start.14 = (bf16[4,25,8,128]{3,2,1,0:T(8,128)(2,1)S(1)}, bf16[4,25,8,128]{3,2,1,0:T(8,128)(2,1)S(1)}, u32[]{:S(2)}, u32[]{:S(2)}) collective-permute-start(bf16[4,25,8,128]{3,2,1,0:T(8,128)(2,1)S(1)} %shard_map.152.refs_0_), channel_id=1, source_target_pairs={{0,128},{64,192},{128,0},{192,64},{1,129},{65,193},{129,1},{193,65... | collective-permute-start | bytes 614408 | tf_op jit(solution)/shard_map/ppermute | solution.py:376
  119.6 10.9 %collective-permute-start.13 = (bf16[4,25,8,128]{3,2,1,0:T(8,128)(2,1)S(1)}, bf16[4,25,8,128]{3,2,1,0:T(8,128)(2,1)S(1)}, u32[]{:S(2)}, u32[]{:S(2)}) collective-permute-start(bf16[4,25,8,128]{3,2,1,0:T(8,128)(2,1)S(1)} %shard_map.152.refs_0_), channel_id=1, source_target_pairs={{0,64},{64,128},{128,192},{192,0},{1,65},{65,129},{129,193},{193,1... | collective-permute-start | bytes 614408 | tf_op jit(solution)/shard_map/ppermute | solution.py:376
  119.6 14.3 %collective-permute-start.16 = (bf16[4,25,8,128]{3,2,1,0:T(8,128)(2,1)S(1)}, bf16[4,25,8,128]{3,2,1,0:T(8,128)(2,1)S(1)}, u32[]{:S(2)}, u32[]{:S(2)}) collective-permute-start(bf16[4,25,8,128]{3,2,1,0:T(8,128)(2,1)S(1)} %shard_map.152.refs_0_), channel_id=1, source_target_pairs={{0,1},{1,0},{2,3},{3,2},{4,5},{5,4},{6,7},{7,6},{8,9},{9,8},{10,11... | collective-permute-start | bytes 614408 | tf_op jit(solution)/shard_map/ppermute | solution.py:382
  124.6 9.3 %collective-permute-start.19 = (bf16[4,25,8,128]{3,2,1,0:T(8,128)(2,1)S(1)}, bf16[4,25,8,128]{3,2,1,0:T(8,128)(2,1)S(1)}, u32[]{:S(2)}, u32[]{:S(2)}) collective-permute-start(bf16[4,25,8,128]{3,2,1,0:T(8,128)(2,1)S(1)} %collective-permute-done.15.refs_3_), channel_id=1, source_target_pairs={{0,1},{1,0},{2,3},{3,2},{4,5},{5,4},{6,7},{7,6},{8,9},{9,8},{10,11... | collective-permute-start | bytes 614408 | tf_op jit(solution)/shard_map/ppermute | solution.py:382
  128.6 5.3 %collective-permute-start.18 = (bf16[4,25,8,128]{3,2,1,0:T(8,128)(2,1)S(1)}, bf16[4,25,8,128]{3,2,1,0:T(8,128)(2,1)S(1)}, u32[]{:S(2)}, u32[]{:S(2)}) collective-permute-start(bf16[4,25,8,128]{3,2,1,0:T(8,128)(2,1)S(1)} %collective-permute-done.14.refs_2_), channel_id=1, source_target_pairs={{0,1},{1,0},{2,3},{3,2},{4,5},{5,4},{6,7},{7,6},{8,9},{9,8},{10,11... | collective-permute-start | bytes 614408 | tf_op jit(solution)/shard_map/ppermute | solution.py:382
  130.5 3.5 %collective-permute-start.17 = (bf16[4,25,8,128]{3,2,1,0:T(8,128)(2,1)S(1)}, bf16[4,25,8,128]{3,2,1,0:T(8,128)(2,1)S(1)}, u32[]{:S(2)}, u32[]{:S(2)}) collective-permute-start(bf16[4,25,8,128]{3,2,1,0:T(8,128)(2,1)S(1)} %collective-permute-done.13.refs_1_), channel_id=1, source_target_pairs={{0,1},{1,0},{2,3},{3,2},{4,5},{5,4},{6,7},{7,6},{8,9},{9,8},{10,11... | collective-permute-start | bytes 614408 | tf_op jit(solution)/shard_map/ppermute | solution.py:382

commit v6 on v5

--- a/solution.py
+++ b/solution.py
@@ -44,30 +44,34 @@
     return lax.rsqrt(total * (1.0 / (GROUPS * BLK)) + 1e-06)
 
 
-def first_kernel(x_hbm, cot_hbm, gain_ref, local_hbm, send_ref, x_ref, cot_ref, local_ref, sems):
-    copies = [
-        pltpu.make_async_copy(src, dst, sems.at[at])
-        for at, (src, dst) in enumerate(
-            ((x_hbm, x_ref), (local_hbm, local_ref), (cot_hbm, cot_ref))
+def first_kernel(x_hbm, cot_hbm, gain_ref, local_hbm, send_hbm, x_ref, local_ref, send_ref, sems):
+    fetch_x = pltpu.make_async_copy(x_hbm, x_ref, sems.at[0])
+    fetch_local = pltpu.make_async_copy(local_hbm, local_ref, sems.at[1])
+    passed = [
+        pltpu.make_async_copy(
+            cot_hbm.at[:, :, lanes(g)], send_hbm.at[g, :, 2 * PL :, :], sems.at[2 + g]
         )
+        for g in range(GROUPS)
     ]
-    for copy in copies:
+    made = [
+        pltpu.make_async_copy(
+            send_ref.at[g], send_hbm.at[g, :, : 2 * PL, :], sems.at[6 + g]
+        )
+        for g in range(GROUPS)
+    ]
+    for copy in (fetch_x, fetch_local, *passed):
         copy.start()
-
-    def put(g, at, value):
-        send_ref[g, :, at * PL : (at + 1) * PL, :] = value.reshape(16, PL, BLK)
-
-    copies[0].wait()
+    fetch_x.wait()
     r = inv_rms(x_ref)
-    copies[1].wait()
+    fetch_local.wait()
     local = local_ref[...]
     for g in range(GROUPS):
         xn = (x_ref[:, lanes(g)].astype(F32) * r * gain_ref[:, lanes(g)]).astype(BF)
-        put(g, 1, xn)
-        put(g, 0, mm(local, xn).astype(BF))
-    copies[2].wait()
-    for g in range(GROUPS):
-        put(g, 2, cot_ref[:, lanes(g)])
+        send_ref[g, :, PL:, :] = xn.reshape(16, PL, BLK)
+        send_ref[g, :, :PL, :] = mm(local, xn).astype(BF).reshape(16, PL, BLK)
+        made[g].start()
+    for copy in (*passed, *made):
+        copy.wait()
 
 
 def side_kernel(x_ref, cot_ref, gain_ref, wu_ref, wv_ref, wo_ref, u_ref, act_ref, dgd_ref):
@@ -133,7 +137,7 @@
     def rows(at, which):
         return recv_ref[pl.ds(at * 16, 16), which * PL : (which + 1) * PL, :].reshape(BLK, BLK)
 
-    @pl.loop(0, 4)
+    @pl.loop(0, 4, unroll=True)
     def _(at):
         fetch(at).wait()
         here = pl.ds(at * 16, 16)
@@ -179,14 +183,14 @@
 
     low, high = (0, 1, 2), (3, 4, 5)
 
-    @pl.loop(0, 32)
+    @pl.loop(0, 32, unroll=4)
     def _(t):
         hi, rh, lh = place(t)
         z = forward([z0[hi * 8 + i, rh, lh] for i in range(8)], low, lh)[-1]
         for i in range(8):
             zs[hi * 8 + i, rh, lh] = z[i]
 
-    @pl.loop(0, 32)
+    @pl.loop(0, 32, unroll=4)
     def _(t):
         lo, rh, lh = place(t)
         states = forward([zs[i * 8 + lo, rh, lh] for i in range(8)], high, lh)
@@ -196,7 +200,7 @@
         for i in range(8):
             es[i * 8 + lo, rh, lh] = e[i]
 
-    @pl.loop(0, 32)
+    @pl.loop(0, 32, unroll=4)
     def _(t):
         hi, rh, lh = place(t)
         states = forward([z0[hi * 8 + i, rh, lh] for i in range(8)], low, lh)
@@ -204,7 +208,7 @@
         for i in range(8):
             es[hi * 8 + i, rh, lh] = e[i]
 
-    @pl.loop(0, 4)
+    @pl.loop(0, 4, unroll=True)
     def _(at):
         here = pl.ds(at * 16, 16)
         z = from_tiles(zs, at).astype(BF)
@@ -396,15 +400,16 @@
         [((GROUPS, 16, 3 * PL, BLK), BF)],
         scratch=[
             pltpu.VMEM(wide, BF),
-            pltpu.VMEM(wide, BF),
             pltpu.VMEM((BLK, BLK), BF),
-            pltpu.SemaphoreType.DMA((3,)),
+            pltpu.VMEM((GROUPS, 16, 2 * PL, BLK), BF),
+            pltpu.SemaphoreType.DMA((10,)),
         ],
         flops=1.4e8,
         moved=4e6,
         hbm=(0, 1, 3),
+        hbm_out=(0,),
         vmem=58,
-    )(x, cot, gain2, local_factor)[0]
+    )(x, cot.reshape(16, PL, -1), gain2, local_factor)[0]
     recv = lax.all_to_all(send.reshape(BLOCKS, 3 * PL, BLK), SEQ, 0, 0)
 
     u, act, dgd = call(
@@ -457,19 +462,14 @@
         )[0]
     got_z = rotated(slice_, "z", 2)
 
+    recv2, slice_ = lax.optimization_barrier((recv2, slice_))
     part = call(local_kernel, [((BLK, BLK), BF)], flops=1.3e8, moved=1.2e6)(recv2, u)[0]
     parts = rotated(part, "dp")
-    mixed, dx = call(
-        last_kernel, [(wide, BF), (wide, BF)], scratch=[pltpu.VMEM(wide, F32)],
-        flops=6e8, moved=8e6,
-    )(recv2, x, gain2, act, dgd, w_u, w_v, w_o, local_factor)
-    got_z, mixed, dx = lax.optimization_barrier((got_z, mixed, dx))
-
     mine_d = call(gather_kernel, [((4,) + quarter, BF)], moved=4e5, smem=(0,))(
         place, slice_, *got_z
     )[0]
     mine_d, parts = lax.optimization_barrier((mine_d, parts))
-    halves = [mine_d] + rotated(mine_d, "dp")
+    got_d = rotated(mine_d, "dp")
     grad_local = call(
         ordered_sum_kernel,
         [((BLK, BLK), F32)],
@@ -477,8 +477,13 @@
         moved=8e5,
         smem=(0,),
     )(place, part, *parts)[0]
+    mixed, dx = call(
+        last_kernel, [(wide, BF), (wide, BF)], scratch=[pltpu.VMEM(wide, F32)],
+        flops=6e8, moved=8e6,
+    )(recv2, x, gain2, act, dgd, w_u, w_v, w_o, local_factor)
+    got_d, grad_local, mixed, dx = lax.optimization_barrier((got_d, grad_local, mixed, dx))
+    halves = [mine_d] + got_d
     others = [swapped(half) for half in halves]
-    others, grad_local = lax.optimization_barrier((others, grad_local))
 
     shape = (GROUPS, BLK, BLK)
     gu, gv, go, grad_gain, grad_bfly = call(

time: 137 us -> 151 us (1.10)
  Pallas kernels: 23.5 us -> 37.2 us
  waiting for transfers between devices: 50.5 us -> 55.8 us
  starting transfers between devices: 56.4 us -> 52.4 us
    pallas_call x13, Pallas kernels: 23.5 us -> 37.2 us  [run(): pl.pallas_call(kernel, out_shape=shapes, in_specs=specs, out_specs=[pl.Bl...]
    ppermute x8, waiting for transfers between devices: 6.79 us -> 12 us  [swapped(): lax.ppermute(value, axis, [(s, s ^ bit) for s in range(lax.axis_size(axis...]
    ppermute x12, waiting for transfers between devices: 2.13 us -> 6.47 us  [rotated(): lax.ppermute(value, axis, [(s, (s + k * step) % n) for s in range(n)])]
    all_to_all x1, waiting for transfers between devices: 7.11 us -> 2.84 us  [per_device(): recv2 = lax.all_to_all(back, SEQ, 0, 0).reshape(GROUPS, 16, 2 * PL, BLK)]
    ppermute x8, starting transfers between devices: 18.3 us -> 15 us  [swapped(): lax.ppermute(value, axis, [(s, s ^ bit) for s in range(lax.axis_size(axis...]
    unnamed x22 -> x24, local copies, waits for them, and re-layouts: 4.53 us -> 3.54 us
  transfers between devices with their start and end apart: 22 -> 22, of which waited for: 7 -> 13; matrix products, arithmetic and copies ran while one was open for 0% -> 0% of each run, Pallas kernels for 6% -> 6%
where the time goes in v6:
time: 151 us; the launch traced here: 150 us
  waiting for transfers between devices  55.8 us (37%)
  starting transfers between devices  52.4 us (35%)
  Pallas kernels  37.2 us (25%)
  local copies, waits for them, and re-layouts  3.54 us (2%)
    pallas_call x13, Pallas kernels, run(): pl.pallas_call(kernel, out_shape=shapes, in_specs=specs, out_specs=[pl.Bl...  37.2 us
    all_to_all x1, waiting for transfers between devices, per_device(): recv = lax.all_to_all(send.reshape(BLOCKS, 3 * PL, BLK), SEQ, 0, 0)  34.5 us
    ppermute x12, starting transfers between devices, rotated(): lax.ppermute(value, axis, [(s, (s + k * step) % n) for s in range(n)])  17.5 us
    ppermute x8, starting transfers between devices, swapped(): lax.ppermute(value, axis, [(s, s ^ bit) for s in range(lax.axis_size(axis...  15 us
    all_to_all x1, starting transfers between devices, per_device(): recv = lax.all_to_all(send.reshape(BLOCKS, 3 * PL, BLK), SEQ, 0, 0)  13.3 us
    ppermute x8, waiting for transfers between devices, swapped(): lax.ppermute(value, axis, [(s, s ^ bit) for s in range(lax.axis_size(axis...  12 us
    all_to_all x1, starting transfers between devices, per_device(): recv2 = lax.all_to_all(back, SEQ, 0, 0).reshape(GROUPS, 16, 2 * PL, BLK)  6.61 us
    ppermute x12, waiting for transfers between devices, rotated(): lax.ppermute(value, axis, [(s, (s + k * step) % n) for s in range(n)])  6.47 us
  transfers between devices with their start and end apart: 22, of which 13 were waited for; matrix products, arithmetic and copies ran while one was open for 0% of the time, Pallas kernels for 6%

profile of v6, /device:TPU:1, one launch (start us, length us, event | category | flops | bytes accessed | tf_op | source)
XLA Modules:
  0.0 150.4 jit_solution(1720505978868760916)
XLA Ops:
  0.6 17.8 %shard_map.143 = bf16[4,16,48,256]{3,2,1,0:T(8,128)(2,1)} custom-call(bf16[256,1024]{1,0:T(8,128)(2,1)} %bitcast.14, bf16[16,16,1024]{2,1,0:T(8,128)(2,1)} %bitcast.22, f32[1,1024]{1,0:T(1,128)} %bitcast.17, bf16[256,256]{1,0:T(8,128)(2,1)} %local_ref.1), custom_call_target="tpu_custom_call" | custom-call | flops 140000000 | bytes 4000000 | tf_op jit(solution)/shard_map/pallas_call | solution.py:357
  18.4 13.3 %all-to-all-start = ((bf16[64,48,256]{2,1,0:T(8,128)(2,1)}), bf16[64,48,256]{2,1,0:T(8,128)(2,1)}, u32[]{:S(2)}, u32[]{:S(2)}) async-start(bf16[64,48,256]{2,1,0:T(8,128)(2,1)} %bitcast.21), calls=%async_computation | async-start | bytes 3145728 | tf_op jit(solution)/shard_map/all_to_all | solution.py:413
  31.8 3.8 %shard_map.144 = (bf16[256,1024]{1,0:T(8,128)(2,1)}, f32[256,1024]{1,0:T(8,128)}, f32[256,1024]{1,0:T(8,128)}) custom-call(bf16[256,1024]{1,0:T(8,128)(2,1)} %bitcast.15, bf16[256,1024]{1,0:T(8,128)(2,1)} %bitcast.23, f32[1,1024]{1,0:T(1,128)} %bitcast.18, bf16[4,256,256]{2,1,0:T(8,128)(2,1)} %wu_ref.5, bf16[4,256,256]{2,1,0:T(8,128)(2,1)} %wv_ref.5, ...), custom_call_target="tpu_custom_call" | custom-call | flops 400000000 | bytes 8000000 | tf_op jit(solution)/shard_map/pallas_call | solution.py:357
  35.6 0.6 pad_add_fusion.place_ref
  36.2 34.5 %all-to-all-done.recv_hbm = bf16[64,48,256]{2,1,0:T(8,128)(2,1)} async-done(((bf16[64,48,256]{2,1,0:T(8,128)(2,1)}), bf16[64,48,256]{2,1,0:T(8,128)(2,1)}, u32[]{:S(2)}, u32[]{:S(2)}) %all-to-all-start) | async-done | bytes 1572896 | tf_op jit(solution)/shard_map/all_to_all | solution.py:413
  70.7 8.3 %shard_map.145 = (bf16[64,32,256]{2,1,0:T(8,128)(2,1)}, f32[4,25,8,128]{3,2,1,0:T(8,128)}, bf16[4,25,8,128]{3,2,1,0:T(8,128)(2,1)}) custom-call(s32[3]{0:T(128)} %pad_add_fusion.place_ref, bf16[64,48,256]{2,1,0:T(8,128)(2,1)} %all-to-all-done.recv_hbm, f32[6,2,2,1024]{3,2,1,0:T(2,128)} %coef_hbm.1, bf16[4,256,256]{2,1,0:T(8,128)(2,1)} %wu_ref.5, ...), custom_call_target="tpu_custom_call" | custom-call | flops 800000000 | bytes 4000000 | tf_op jit(solution)/shard_map/pallas_call | solution.py:357
  79.0 0.0 copy-start.11
  79.0 0.0 copy-start.8
  79.0 6.6 %all-to-all-start.1 = ((bf16[64,32,256]{2,1,0:T(8,128)(2,1)}), bf16[64,32,256]{2,1,0:T(8,128)(2,1)S(1)}, u32[]{:S(2)}, u32[]{:S(2)}) async-start(bf16[64,32,256]{2,1,0:T(8,128)(2,1)} %get-tuple-element.45), calls=%async_computation.1 | async-start | bytes 2097152 | tf_op jit(solution)/shard_map/all_to_all | solution.py:453
  85.6 0.5 collective-permute-start
  86.2 1.1 collective-permute-done.got_ref
  87.2 0.6 shard_map.146
  87.9 1.3 collective-permute-start.1
  89.2 2.5 %collective-permute-start.2 = (bf16[25,8,128]{2,1,0:T(8,128)(2,1)S(1)}, bf16[25,8,128]{2,1,0:T(8,128)(2,1)S(1)}, u32[]{:S(2)}, u32[]{:S(2)}) collective-permute-start(bf16[25,8,128]{2,1,0:T(8,128)(2,1)S(1)} %get-tuple-element.50), channel_id=1, source_target_pairs={{0,128},{64,192},{128,0},{192,64},{1,129},{65,193},{129,1},{193,65... | collective-permute-start | bytes 153608 | tf_op jit(solution)/shard_map/ppermute | solution.py:380
  91.6 1.2 collective-permute-start.3
  92.8 1.5 collective-permute-done.2.refs_1_
  94.3 0.6 collective-permute-done.3.refs_2_
  94.9 1.4 collective-permute-start.4
  96.3 2.2 %collective-permute-done.4.b_ref = bf16[25,8,128]{2,1,0:T(8,128)(2,1)S(1)} collective-permute-done((bf16[25,8,128]{2,1,0:T(8,128)(2,1)S(1)}, bf16[25,8,128]{2,1,0:T(8,128)(2,1)S(1)}, u32[]{:S(2)}, u32[]{:S(2)}) %collective-permute-start.4) | collective-permute-done | bytes 51232 | tf_op jit(solution)/shard_map/ppermute | solution.py:386
  98.6 2.9 %collective-permute-start.5 = (bf16[25,8,128]{2,1,0:T(8,128)(2,1)S(1)}, bf16[25,8,128]{2,1,0:T(8,128)(2,1)S(1)}, u32[]{:S(2)}, u32[]{:S(2)}) collective-permute-start(bf16[25,8,128]{2,1,0:T(8,128)(2,1)S(1)} %shard_map.148.a_ref), channel_id=1, source_target_pairs={{0,4},{2,6},{4,0},{6,2},{1,5},{3,7},{5,1},{7,3},{8,12},{10,14},{12... | collective-permute-start | bytes 153608 | tf_op jit(solution)/shard_map/ppermute | solution.py:386
  101.5 2.5 %collective-permute-done.5.b_ref = bf16[25,8,128]{2,1,0:T(8,128)(2,1)S(1)} collective-permute-done((bf16[25,8,128]{2,1,0:T(8,128)(2,1)S(1)}, bf16[25,8,128]{2,1,0:T(8,128)(2,1)S(1)}, u32[]{:S(2)}, u32[]{:S(2)}) %collective-permute-start.5) | collective-permute-done | bytes 51232 | tf_op jit(solution)/shard_map/ppermute | solution.py:386
  104.0 2.0 %collective-permute-start.6 = (bf16[25,8,128]{2,1,0:T(8,128)(2,1)S(1)}, bf16[25,8,128]{2,1,0:T(8,128)(2,1)S(1)}, u32[]{:S(2)}, u32[]{:S(2)}) collective-permute-start(bf16[25,8,128]{2,1,0:T(8,128)(2,1)S(1)} %shard_map.149.a_ref), channel_id=1, source_target_pairs={{0,8},{8,0},{16,24},{24,16},{32,40},{40,32},{48,56},{56,48},{1,9},... | collective-permute-start | bytes 153608 | tf_op jit(solution)/shard_map/ppermute | solution.py:386
  106.0 5.0 %collective-permute-done.6.b_ref = bf16[25,8,128]{2,1,0:T(8,128)(2,1)S(1)} collective-permute-done((bf16[25,8,128]{2,1,0:T(8,128)(2,1)S(1)}, bf16[25,8,128]{2,1,0:T(8,128)(2,1)S(1)}, u32[]{:S(2)}, u32[]{:S(2)}) %collective-permute-start.6) | collective-permute-done | bytes 51232 | tf_op jit(solution)/shard_map/ppermute | solution.py:386
  111.0 2.8 %all-to-all-done.1 = bf16[64,32,256]{2,1,0:T(8,128)(2,1)S(1)} async-done(((bf16[64,32,256]{2,1,0:T(8,128)(2,1)}), bf16[64,32,256]{2,1,0:T(8,128)(2,1)S(1)}, u32[]{:S(2)}, u32[]{:S(2)}) %all-to-all-start.1) | async-done | bytes 1048608 | tf_op jit(solution)/shard_map/all_to_all | solution.py:453
  113.8 1.0 copy-done.6
  114.9 0.3 shard_map.152.refs_0_
  115.2 2.6 %collective-permute-start.12 = (bf16[256,256]{1,0:T(8,128)(2,1)S(1)}, bf16[256,256]{1,0:T(8,128)(2,1)S(1)}, u32[]{:S(2)}, u32[]{:S(2)}) collective-permute-start(bf16[256,256]{1,0:T(8,128)(2,1)S(1)} %shard_map.152.refs_0_), channel_id=1, source_target_pairs={{0,192},{64,0},{128,64},{192,128},{1,193},{65,1},{129,65},{193,129... | collective-permute-start | bytes 393224 | tf_op jit(solution)/shard_map/ppermute | solution.py:380
  117.7 0.6 collective-permute-start.11
  118.3 0.6 collective-permute-start.10
  119.0 2.6 %collective-permute-start.9 = (bf16[25,8,128]{2,1,0:T(8,128)(2,1)S(1)}, bf16[25,8,128]{2,1,0:T(8,128)(2,1)S(1)}, u32[]{:S(2)}, u32[]{:S(2)}) collective-permute-start(bf16[25,8,128]{2,1,0:T(8,128)(2,1)S(1)} %shard_map.150.refs_0_), channel_id=1, source_target_pairs={{0,48},{8,56},{16,0},{24,8},{32,16},{40,24},{48,32},{56,40},{1,49}... | collective-permute-start | bytes 153608 | tf_op jit(solution)/shard_map/ppermute | solution.py:380
  121.5 1.4 collective-permute-start.8
  123.0 1.9 %collective-permute-start.7 = (bf16[25,8,128]{2,1,0:T(8,128)(2,1)S(1)}, bf16[25,8,128]{2,1,0:T(8,128)(2,1)S(1)}, u32[]{:S(2)}, u32[]{:S(2)}) collective-permute-start(bf16[25,8,128]{2,1,0:T(8,128)(2,1)S(1)} %shard_map.150.refs_0_), channel_id=1, source_target_pairs={{0,16},{8,24},{16,32},{24,40},{32,48},{40,56},{48,0},{56,8},{1,17}... | collective-permute-start | bytes 153608 | tf_op jit(solution)/shard_map/ppermute | solution.py:380
  124.8 3.9 %collective-permute-done.8.refs_2_ = bf16[25,8,128]{2,1,0:T(8,128)(2,1)S(1)} collective-permute-done((bf16[25,8,128]{2,1,0:T(8,128)(2,1)S(1)}, bf16[25,8,128]{2,1,0:T(8,128)(2,1)S(1)}, u32[]{:S(2)}, u32[]{:S(2)}) %collective-permute-start.8) | collective-permute-done | bytes 51232 | tf_op jit(solution)/shard_map/ppermute | solution.py:380
  128.8 0.4 collective-permute-done.7.refs_1_
  129.2 0.6 shard_map.151.refs_0_
  129.8 1.7 %collective-permute-start.15 = (bf16[4,25,8,128]{3,2,1,0:T(8,128)(2,1)S(1)}, bf16[4,25,8,128]{3,2,1,0:T(8,128)(2,1)S(1)}, u32[]{:S(2)}, u32[]{:S(2)}) collective-permute-start(bf16[4,25,8,128]{3,2,1,0:T(8,128)(2,1)S(1)} %shard_map.151.refs_0_), channel_id=1, source_target_pairs={{0,192},{64,0},{128,64},{192,128},{1,193},{65,1},{129,65},{193,129... | collective-permute-start | bytes 614408 | tf_op jit(solution)/shard_map/ppermute | solution.py:380
  131.5 1.2 collective-permute-start.14
  132.8 1.2 copy-done.4
  134.0 1.2 copy-done.5
  135.3 1.9 %shard_map.154 = (bf16[256,1024]{1,0:T(8,128)(2,1)}, bf16[256,1024]{1,0:T(8,128)(2,1)}) custom-call(bf16[4,16,32,256]{3,2,1,0:T(8,128)(2,1)S(1)} %bitcast.13, bf16[256,1024]{1,0:T(8,128)(2,1)S(1)} %bitcast.16, f32[1,1024]{1,0:T(1,128)S(1)} %bitcast.19, f32[256,1024]{1,0:T(8,128)S(1)} %copy-done.4, f32[256,1024]{1,0:T(8,128)S(1)} %copy-done.5, ...), custom_call_target="tpu_custom_call" | custom-call | flops 600000000 | bytes 8000000 | tf_op jit(solution)/shard_map/pallas_call | solution.py:357
  137.1 5.4 %collective-permute-start.16 = (bf16[4,25,8,128]{3,2,1,0:T(8,128)(2,1)S(1)}, bf16[4,25,8,128]{3,2,1,0:T(8,128)(2,1)S(1)}, u32[]{:S(2)}, u32[]{:S(2)}) collective-permute-start(bf16[4,25,8,128]{3,2,1,0:T(8,128)(2,1)S(1)} %shard_map.151.refs_0_), channel_id=1, source_target_pairs={{0,1},{1,0},{2,3},{3,2},{4,5},{5,4},{6,7},{7,6},{8,9},{9,8},{10,11... | collective-permute-start | bytes 614408 | tf_op jit(solution)/shard_map/ppermute | solution.py:386
  142.6 1.4 shard_map.153
  144.0 2.2 %collective-permute-start.17 = (bf16[4,25,8,128]{3,2,1,0:T(8,128)(2,1)S(1)}, bf16[4,25,8,128]{3,2,1,0:T(8,128)(2,1)S(1)}, u32[]{:S(2)}, u32[]{:S(2)}) collective-permute-start(bf16[4,25,8,128]{3,2,1,0:T(8,128)(2,1)S(1)} %collective-permute-done.13.refs_1_), channel_id=1, source_target_pairs={{0,1},{1,0},{2,3},{3,2},{4,5},{5,4},{6,7},{7,6},{8,9},{9,8},{10,11... | collective-permute-start | bytes 614408 | tf_op jit(solution)/shard_map/ppermute | solution.py:386
  146.1 0.5 collective-permute-start.19
  146.6 0.6 collective-permute-done.17.refs_5_
  147.2 0.4 collective-permute-done.18.refs_6_
  147.6 0.3 collective-permute-done.19.refs_7_
  147.9 2.5 %shard_map.155 = (f32[4,256,256]{2,1,0:T(8,128)}, f32[4,256,256]{2,1,0:T(8,128)}, f32[4,256,256]{2,1,0:T(8,128)}, f32[1,1024]{1,0:T(1,128)}, f32[6,2,2,1024]{3,2,1,0:T(2,128)}) custom-call(s32[3]{0:T(128)S(1)} %copy-done.10, bf16[4,256,256]{2,1,0:T(8,128)(2,1)S(1)} %copy-done, bf16[4,256,256]{2,1,0:T(8,128)(2,1)S(1)} %copy-done.1, f32[1,1024]{1,0:T(1,128)S(1)} %bitcast.20, ...), custom_call_target="tpu_custom_call" | custom-call | bytes 5000000 | tf_op jit(solution)/shard_map/pallas_call | solution.py:357
  (34 shorter events, 0.2 us)
Async XLA Ops:
  18.4 52.3 %all-to-all-start = ((bf16[64,48,256]{2,1,0:T(8,128)(2,1)}), bf16[64,48,256]{2,1,0:T(8,128)(2,1)}, u32[]{:S(2)}, u32[]{:S(2)}) async-start(bf16[64,48,256]{2,1,0:T(8,128)(2,1)} %bitcast.21), calls=%async_computation | async-start | bytes 3145728 | tf_op jit(solution)/shard_map/all_to_all | solution.py:413
  79.0 6.7 %copy-start.11 = (bf16[4,25,8,128]{3,2,1,0:T(8,128)(2,1)S(1)}, bf16[4,25,8,128]{3,2,1,0:T(8,128)(2,1)}, u32[]{:S(2)}) copy-start(bf16[4,25,8,128]{3,2,1,0:T(8,128)(2,1)} %get-tuple-element.47) | copy-start | bytes 614404
  79.0 8.3 %copy-start.8 = (f32[4,25,8,128]{3,2,1,0:T(8,128)S(1)}, f32[4,25,8,128]{3,2,1,0:T(8,128)}, u32[]{:S(2)}) copy-start(f32[4,25,8,128]{3,2,1,0:T(8,128)} %get-tuple-element.46.keep_ref) | copy-start | bytes 1228804
  79.0 8.3 %copy-start.10 = (s32[3]{0:T(128)S(1)}, s32[3]{0:T(128)}, u32[]{:S(2)}) copy-start(s32[3]{0:T(128)} %pad_add_fusion.place_ref) | copy-start | bytes 40
  79.0 34.8 %all-to-all-start.1 = ((bf16[64,32,256]{2,1,0:T(8,128)(2,1)}), bf16[64,32,256]{2,1,0:T(8,128)(2,1)S(1)}, u32[]{:S(2)}, u32[]{:S(2)}) async-start(bf16[64,32,256]{2,1,0:T(8,128)(2,1)} %get-tuple-element.45), calls=%async_computation.1 | async-start | bytes 2097152 | tf_op jit(solution)/shard_map/all_to_all | solution.py:453
  85.6 1.6 %collective-permute-start = (bf16[4,25,8,128]{3,2,1,0:T(8,128)(2,1)S(1)}, bf16[4,25,8,128]{3,2,1,0:T(8,128)(2,1)S(1)}, u32[]{:S(2)}, u32[]{:S(2)}) collective-permute-start(bf16[4,25,8,128]{3,2,1,0:T(8,128)(2,1)S(1)} %copy-done.11), channel_id=1, source_target_pairs={{0,1},{1,0},{2,3},{3,2},{4,5},{5,4},{6,7},{7,6},{8,9},{9,8},{10,11... | collective-permute-start | bytes 614408 | tf_op jit(solution)/shard_map/ppermute | solution.py:386
  87.2 45.5 %copy-start.7 = (bf16[256,256]{1,0:T(8,128)(2,1)S(1)}, bf16[256,256]{1,0:T(8,128)(2,1)}, u32[]{:S(2)}) copy-start(bf16[256,256]{1,0:T(8,128)(2,1)} %local_ref.1) | copy-start | bytes 393220
  87.2 45.5 %copy-start.9 = (f32[1024]{0:T(1024)S(1)}, f32[1024]{0:T(1024)}, u32[]{:S(2)}) copy-start(f32[1024]{0:T(1024)} %param.10) | copy-start | bytes 12292
  87.8 44.9 %copy-start = (bf16[4,256,256]{2,1,0:T(8,128)(2,1)S(1)}, bf16[4,256,256]{2,1,0:T(8,128)(2,1)}, u32[]{:S(2)}) copy-start(bf16[4,256,256]{2,1,0:T(8,128)(2,1)} %wu_ref.5) | copy-start | bytes 1572868
  87.9 44.9 %copy-start.1 = (bf16[4,256,256]{2,1,0:T(8,128)(2,1)S(1)}, bf16[4,256,256]{2,1,0:T(8,128)(2,1)}, u32[]{:S(2)}) copy-start(bf16[4,256,256]{2,1,0:T(8,128)(2,1)} %wv_ref.5) | copy-start | bytes 1572868
  87.9 44.9 %copy-start.2 = (bf16[1,256,1024]{2,1,0:T(8,128)(2,1)S(1)}, bf16[1,256,1024]{2,1,0:T(8,128)(2,1)}, u32[]{:S(2)}) copy-start(bf16[1,256,1024]{2,1,0:T(8,128)(2,1)} %param.8) | copy-start | bytes 1572868
  87.9 44.9 %copy-start.3 = (bf16[4,256,256]{2,1,0:T(8,128)(2,1)S(1)}, bf16[4,256,256]{2,1,0:T(8,128)(2,1)}, u32[]{:S(2)}) copy-start(bf16[4,256,256]{2,1,0:T(8,128)(2,1)} %wo_ref.3) | copy-start | bytes 1572868
  87.9 4.9 %collective-permute-start.1 = (bf16[25,8,128]{2,1,0:T(8,128)(2,1)S(1)}, bf16[25,8,128]{2,1,0:T(8,128)(2,1)S(1)}, u32[]{:S(2)}, u32[]{:S(2)}) collective-permute-start(bf16[25,8,128]{2,1,0:T(8,128)(2,1)S(1)} %get-tuple-element.49), channel_id=1, source_target_pairs={{0,64},{64,128},{128,192},{192,0},{1,65},{65,129},{129,193},{193,1... | collective-permute-start | bytes 153608 | tf_op jit(solution)/shard_map/ppermute | solution.py:380
  89.2 5.1 %collective-permute-start.2 = (bf16[25,8,128]{2,1,0:T(8,128)(2,1)S(1)}, bf16[25,8,128]{2,1,0:T(8,128)(2,1)S(1)}, u32[]{:S(2)}, u32[]{:S(2)}) collective-permute-start(bf16[25,8,128]{2,1,0:T(8,128)(2,1)S(1)} %get-tuple-element.50), channel_id=1, source_target_pairs={{0,128},{64,192},{128,0},{192,64},{1,129},{65,193},{129,1},{193,65... | collective-permute-start | bytes 153608 | tf_op jit(solution)/shard_map/ppermute | solution.py:380
  91.6 3.3 %collective-permute-start.3 = (bf16[25,8,128]{2,1,0:T(8,128)(2,1)S(1)}, bf16[25,8,128]{2,1,0:T(8,128)(2,1)S(1)}, u32[]{:S(2)}, u32[]{:S(2)}) collective-permute-start(bf16[25,8,128]{2,1,0:T(8,128)(2,1)S(1)} %get-tuple-element.51), channel_id=1, source_target_pairs={{0,192},{64,0},{128,64},{192,128},{1,193},{65,1},{129,65},{193,129... | collective-permute-start | bytes 153608 | tf_op jit(solution)/shard_map/ppermute | solution.py:380
  94.9 3.6 %collective-permute-start.4 = (bf16[25,8,128]{2,1,0:T(8,128)(2,1)S(1)}, bf16[25,8,128]{2,1,0:T(8,128)(2,1)S(1)}, u32[]{:S(2)}, u32[]{:S(2)}) collective-permute-start(bf16[25,8,128]{2,1,0:T(8,128)(2,1)S(1)} %shard_map.147.a_ref), channel_id=1, source_target_pairs={{0,2},{2,0},{4,6},{6,4},{1,3},{3,1},{5,7},{7,5},{8,10},{10,8},{12,... | collective-permute-start | bytes 153608 | tf_op jit(solution)/shard_map/ppermute | solution.py:386
  98.6 5.4 %collective-permute-start.5 = (bf16[25,8,128]{2,1,0:T(8,128)(2,1)S(1)}, bf16[25,8,128]{2,1,0:T(8,128)(2,1)S(1)}, u32[]{:S(2)}, u32[]{:S(2)}) collective-permute-start(bf16[25,8,128]{2,1,0:T(8,128)(2,1)S(1)} %shard_map.148.a_ref), channel_id=1, source_target_pairs={{0,4},{2,6},{4,0},{6,2},{1,5},{3,7},{5,1},{7,3},{8,12},{10,14},{12... | collective-permute-start | bytes 153608 | tf_op jit(solution)/shard_map/ppermute | solution.py:386
  104.0 7.0 %collective-permute-start.6 = (bf16[25,8,128]{2,1,0:T(8,128)(2,1)S(1)}, bf16[25,8,128]{2,1,0:T(8,128)(2,1)S(1)}, u32[]{:S(2)}, u32[]{:S(2)}) collective-permute-start(bf16[25,8,128]{2,1,0:T(8,128)(2,1)S(1)} %shard_map.149.a_ref), channel_id=1, source_target_pairs={{0,8},{8,0},{16,24},{24,16},{32,40},{40,32},{48,56},{56,48},{1,9},... | collective-permute-start | bytes 153608 | tf_op jit(solution)/shard_map/ppermute | solution.py:386
  113.8 1.0 copy-start.6
  115.2 14.6 %collective-permute-start.12 = (bf16[256,256]{1,0:T(8,128)(2,1)S(1)}, bf16[256,256]{1,0:T(8,128)(2,1)S(1)}, u32[]{:S(2)}, u32[]{:S(2)}) collective-permute-start(bf16[256,256]{1,0:T(8,128)(2,1)S(1)} %shard_map.152.refs_0_), channel_id=1, source_target_pairs={{0,192},{64,0},{128,64},{192,128},{1,193},{65,1},{129,65},{193,129... | collective-permute-start | bytes 393224 | tf_op jit(solution)/shard_map/ppermute | solution.py:380
  117.7 12.0 %collective-permute-start.11 = (bf16[256,256]{1,0:T(8,128)(2,1)S(1)}, bf16[256,256]{1,0:T(8,128)(2,1)S(1)}, u32[]{:S(2)}, u32[]{:S(2)}) collective-permute-start(bf16[256,256]{1,0:T(8,128)(2,1)S(1)} %shard_map.152.refs_0_), channel_id=1, source_target_pairs={{0,128},{64,192},{128,0},{192,64},{1,129},{65,193},{129,1},{193,65... | collective-permute-start | bytes 393224 | tf_op jit(solution)/shard_map/ppermute | solution.py:380
  118.3 11.4 %collective-permute-start.10 = (bf16[256,256]{1,0:T(8,128)(2,1)S(1)}, bf16[256,256]{1,0:T(8,128)(2,1)S(1)}, u32[]{:S(2)}, u32[]{:S(2)}) collective-permute-start(bf16[256,256]{1,0:T(8,128)(2,1)S(1)} %shard_map.152.refs_0_), channel_id=1, source_target_pairs={{0,64},{64,128},{128,192},{192,0},{1,65},{65,129},{129,193},{193,1... | collective-permute-start | bytes 393224 | tf_op jit(solution)/shard_map/ppermute | solution.py:380
  119.0 4.0 %collective-permute-start.9 = (bf16[25,8,128]{2,1,0:T(8,128)(2,1)S(1)}, bf16[25,8,128]{2,1,0:T(8,128)(2,1)S(1)}, u32[]{:S(2)}, u32[]{:S(2)}) collective-permute-start(bf16[25,8,128]{2,1,0:T(8,128)(2,1)S(1)} %shard_map.150.refs_0_), channel_id=1, source_target_pairs={{0,48},{8,56},{16,0},{24,8},{32,16},{40,24},{48,32},{56,40},{1,49}... | collective-permute-start | bytes 153608 | tf_op jit(solution)/shard_map/ppermute | solution.py:380
  121.5 7.3 %collective-permute-start.8 = (bf16[25,8,128]{2,1,0:T(8,128)(2,1)S(1)}, bf16[25,8,128]{2,1,0:T(8,128)(2,1)S(1)}, u32[]{:S(2)}, u32[]{:S(2)}) collective-permute-start(bf16[25,8,128]{2,1,0:T(8,128)(2,1)S(1)} %shard_map.150.refs_0_), channel_id=1, source_target_pairs={{0,32},{8,40},{16,48},{24,56},{32,0},{40,8},{48,16},{56,24},{1,33}... | collective-permute-start | bytes 153608 | tf_op jit(solution)/shard_map/ppermute | solution.py:380
  123.0 6.2 %collective-permute-start.7 = (bf16[25,8,128]{2,1,0:T(8,128)(2,1)S(1)}, bf16[25,8,128]{2,1,0:T(8,128)(2,1)S(1)}, u32[]{:S(2)}, u32[]{:S(2)}) collective-permute-start(bf16[25,8,128]{2,1,0:T(8,128)(2,1)S(1)} %shard_map.150.refs_0_), channel_id=1, source_target_pairs={{0,16},{8,24},{16,32},{24,40},{32,48},{40,56},{48,0},{56,8},{1,17}... | collective-permute-start | bytes 153608 | tf_op jit(solution)/shard_map/ppermute | solution.py:380
  129.8 14.1 %collective-permute-start.15 = (bf16[4,25,8,128]{3,2,1,0:T(8,128)(2,1)S(1)}, bf16[4,25,8,128]{3,2,1,0:T(8,128)(2,1)S(1)}, u32[]{:S(2)}, u32[]{:S(2)}) collective-permute-start(bf16[4,25,8,128]{3,2,1,0:T(8,128)(2,1)S(1)} %shard_map.151.refs_0_), channel_id=1, source_target_pairs={{0,192},{64,0},{128,64},{192,128},{1,193},{65,1},{129,65},{193,129... | collective-permute-start | bytes 614408 | tf_op jit(solution)/shard_map/ppermute | solution.py:380
  131.5 12.4 %collective-permute-start.14 = (bf16[4,25,8,128]{3,2,1,0:T(8,128)(2,1)S(1)}, bf16[4,25,8,128]{3,2,1,0:T(8,128)(2,1)S(1)}, u32[]{:S(2)}, u32[]{:S(2)}) collective-permute-start(bf16[4,25,8,128]{3,2,1,0:T(8,128)(2,1)S(1)} %shard_map.151.refs_0_), channel_id=1, source_target_pairs={{0,128},{64,192},{128,0},{192,64},{1,129},{65,193},{129,1},{193,65... | collective-permute-start | bytes 614408 | tf_op jit(solution)/shard_map/ppermute | solution.py:380
  132.8 11.2 %collective-permute-start.13 = (bf16[4,25,8,128]{3,2,1,0:T(8,128)(2,1)S(1)}, bf16[4,25,8,128]{3,2,1,0:T(8,128)(2,1)S(1)}, u32[]{:S(2)}, u32[]{:S(2)}) collective-permute-start(bf16[4,25,8,128]{3,2,1,0:T(8,128)(2,1)S(1)} %shard_map.151.refs_0_), channel_id=1, source_target_pairs={{0,64},{64,128},{128,192},{192,0},{1,65},{65,129},{129,193},{193,1... | collective-permute-start | bytes 614408 | tf_op jit(solution)/shard_map/ppermute | solution.py:380
  132.8 1.2 copy-start.4
  134.0 1.2 copy-start.5
  137.1 9.5 %collective-permute-start.16 = (bf16[4,25,8,128]{3,2,1,0:T(8,128)(2,1)S(1)}, bf16[4,25,8,128]{3,2,1,0:T(8,128)(2,1)S(1)}, u32[]{:S(2)}, u32[]{:S(2)}) collective-permute-start(bf16[4,25,8,128]{3,2,1,0:T(8,128)(2,1)S(1)} %shard_map.151.refs_0_), channel_id=1, source_target_pairs={{0,1},{1,0},{2,3},{3,2},{4,5},{5,4},{6,7},{7,6},{8,9},{9,8},{10,11... | collective-permute-start | bytes 614408 | tf_op jit(solution)/shard_map/ppermute | solution.py:386
  144.0 3.2 %collective-permute-start.17 = (bf16[4,25,8,128]{3,2,1,0:T(8,128)(2,1)S(1)}, bf16[4,25,8,128]{3,2,1,0:T(8,128)(2,1)S(1)}, u32[]{:S(2)}, u32[]{:S(2)}) collective-permute-start(bf16[4,25,8,128]{3,2,1,0:T(8,128)(2,1)S(1)} %collective-permute-done.13.refs_1_), channel_id=1, source_target_pairs={{0,1},{1,0},{2,3},{3,2},{4,5},{5,4},{6,7},{7,6},{8,9},{9,8},{10,11... | collective-permute-start | bytes 614408 | tf_op jit(solution)/shard_map/ppermute | solution.py:386
  146.1 1.5 collective-permute-start.18
  146.1 1.7 %collective-permute-start.19 = (bf16[4,25,8,128]{3,2,1,0:T(8,128)(2,1)S(1)}, bf16[4,25,8,128]{3,2,1,0:T(8,128)(2,1)S(1)}, u32[]{:S(2)}, u32[]{:S(2)}) collective-permute-start(bf16[4,25,8,128]{3,2,1,0:T(8,128)(2,1)S(1)} %collective-permute-done.15.refs_3_), channel_id=1, source_target_pairs={{0,1},{1,0},{2,3},{3,2},{4,5},{5,4},{6,7},{7,6},{8,9},{9,8},{10,11... | collective-permute-start | bytes 614408 | tf_op jit(solution)/shard_map/ppermute | solution.py:386

commit v7 on v6

--- a/solution.py
+++ b/solution.py
@@ -44,33 +44,37 @@
     return lax.rsqrt(total * (1.0 / (GROUPS * BLK)) + 1e-06)
 
 
-def first_kernel(x_hbm, cot_hbm, gain_ref, local_hbm, send_hbm, x_ref, local_ref, send_ref, sems):
-    fetch_x = pltpu.make_async_copy(x_hbm, x_ref, sems.at[0])
-    fetch_local = pltpu.make_async_copy(local_hbm, local_ref, sems.at[1])
-    passed = [
-        pltpu.make_async_copy(
-            cot_hbm.at[:, :, lanes(g)], send_hbm.at[g, :, 2 * PL :, :], sems.at[2 + g]
+def first_kernel(
+    x_hbm, cot_hbm, gain_ref, local_hbm, send_hbm, x_ref, cot_ref, local_ref, send_ref, sems
+):
+    fetches = [
+        pltpu.make_async_copy(src, dst, sems.at[at])
+        for at, (src, dst) in enumerate(
+            ((x_hbm, x_ref), (local_hbm, local_ref), (cot_hbm, cot_ref))
         )
+    ]
+    made = [
+        pltpu.make_async_copy(send_ref.at[g], send_hbm.at[g], sems.at[3 + g])
         for g in range(GROUPS)
     ]
-    made = [
-        pltpu.make_async_copy(
-            send_ref.at[g], send_hbm.at[g, :, : 2 * PL, :], sems.at[6 + g]
-        )
-        for g in range(GROUPS)
-    ]
-    for copy in (fetch_x, fetch_local, *passed):
+    for copy in fetches:
         copy.start()
-    fetch_x.wait()
+
+    def put(g, at, value):
+        send_ref[g, :, at * PL : (at + 1) * PL, :] = value.reshape(16, PL, BLK)
+
+    fetches[0].wait()
     r = inv_rms(x_ref)
-    fetch_local.wait()
+    fetches[1].wait()
+    fetches[2].wait()
     local = local_ref[...]
     for g in range(GROUPS):
         xn = (x_ref[:, lanes(g)].astype(F32) * r * gain_ref[:, lanes(g)]).astype(BF)
-        send_ref[g, :, PL:, :] = xn.reshape(16, PL, BLK)
-        send_ref[g, :, :PL, :] = mm(local, xn).astype(BF).reshape(16, PL, BLK)
+        put(g, 0, mm(local, xn).astype(BF))
+        put(g, 1, xn)
+        put(g, 2, cot_ref[:, lanes(g)])
         made[g].start()
-    for copy in (*passed, *made):
+    for copy in made:
         copy.wait()
 
 
@@ -400,16 +404,17 @@
         [((GROUPS, 16, 3 * PL, BLK), BF)],
         scratch=[
             pltpu.VMEM(wide, BF),
+            pltpu.VMEM(wide, BF),
             pltpu.VMEM((BLK, BLK), BF),
-            pltpu.VMEM((GROUPS, 16, 2 * PL, BLK), BF),
-            pltpu.SemaphoreType.DMA((10,)),
+            pltpu.VMEM((GROUPS, 16, 3 * PL, BLK), BF),
+            pltpu.SemaphoreType.DMA((7,)),
         ],
         flops=1.4e8,
         moved=4e6,
         hbm=(0, 1, 3),
         hbm_out=(0,),
         vmem=58,
-    )(x, cot.reshape(16, PL, -1), gain2, local_factor)[0]
+    )(x, cot, gain2, local_factor)[0]
     recv = lax.all_to_all(send.reshape(BLOCKS, 3 * PL, BLK), SEQ, 0, 0)
 
     u, act, dgd = call(
@@ -462,13 +467,12 @@
         )[0]
     got_z = rotated(slice_, "z", 2)
 
-    recv2, slice_ = lax.optimization_barrier((recv2, slice_))
+    recv2, got_z = lax.optimization_barrier((recv2, got_z))
     part = call(local_kernel, [((BLK, BLK), BF)], flops=1.3e8, moved=1.2e6)(recv2, u)[0]
     parts = rotated(part, "dp")
     mine_d = call(gather_kernel, [((4,) + quarter, BF)], moved=4e5, smem=(0,))(
         place, slice_, *got_z
     )[0]
-    mine_d, parts = lax.optimization_barrier((mine_d, parts))
     got_d = rotated(mine_d, "dp")
     grad_local = call(
         ordered_sum_kernel,

time: 151 us -> 138 us (0.914)
  Pallas kernels: 37.2 us -> 22.9 us
    pallas_call x13, Pallas kernels: 37.2 us -> 22.9 us  [run(): pl.pallas_call(kernel, out_shape=shapes, in_specs=specs, out_specs=[pl.Bl...]
    ppermute x12, waiting for transfers between devices: 6.47 us -> 10.4 us  [rotated(): lax.ppermute(value, axis, [(s, (s + k * step) % n) for s in range(n)])]
    all_to_all x1, waiting for transfers between devices: 2.84 us -> 0.01 us  [per_device(): recv2 = lax.all_to_all(back, SEQ, 0, 0).reshape(GROUPS, 16, 2 * PL, BLK)]
    ppermute x12, starting transfers between devices: 17.5 us -> 19.5 us  [rotated(): lax.ppermute(value, axis, [(s, (s + k * step) % n) for s in range(n)])]
    ppermute x8, starting transfers between devices: 15 us -> 13.4 us  [swapped(): lax.ppermute(value, axis, [(s, s ^ bit) for s in range(lax.axis_size(axis...]
where the time goes in v7:
time: 138 us
  waiting for transfers between devices  56.9 us (41%)
  starting transfers between devices  52.9 us (38%)
  Pallas kernels  22.9 us (17%)
  local copies, waits for them, and re-layouts  3.54 us (3%)
    all_to_all x1, waiting for transfers between devices, per_device(): recv = lax.all_to_all(send.reshape(BLOCKS, 3 * PL, BLK), SEQ, 0, 0)  34.5 us
    pallas_call x13, Pallas kernels, run(): pl.pallas_call(kernel, out_shape=shapes, in_specs=specs, out_specs=[pl.Bl...  22.9 us
    ppermute x12, starting transfers between devices, rotated(): lax.ppermute(value, axis, [(s, (s + k * step) % n) for s in range(n)])  19.5 us
    ppermute x8, starting transfers between devices, swapped(): lax.ppermute(value, axis, [(s, s ^ bit) for s in range(lax.axis_size(axis...  13.4 us
    all_to_all x1, starting transfers between devices, per_device(): recv = lax.all_to_all(send.reshape(BLOCKS, 3 * PL, BLK), SEQ, 0, 0)  13.3 us
    ppermute x8, waiting for transfers between devices, swapped(): lax.ppermute(value, axis, [(s, s ^ bit) for s in range(lax.axis_size(axis...  12 us
    ppermute x12, waiting for transfers between devices, rotated(): lax.ppermute(value, axis, [(s, (s + k * step) % n) for s in range(n)])  10.4 us
    all_to_all x1, starting transfers between devices, per_device(): recv2 = lax.all_to_all(back, SEQ, 0, 0).reshape(GROUPS, 16, 2 * PL, BLK)  6.61 us
  transfers between devices with their start and end apart: 22, of which 13 were waited for; matrix products, arithmetic and copies ran while one was open for 0% of the time, Pallas kernels for 6%

profile of v7, /device:TPU:1, one launch (start us, length us, event | category | flops | bytes accessed | tf_op | source)
XLA Modules:
  0.0 137.6 jit_solution(1649121854326459460)
XLA Ops:
  0.6 3.4 %shard_map.143 = bf16[4,16,48,256]{3,2,1,0:T(8,128)(2,1)} custom-call(bf16[256,1024]{1,0:T(8,128)(2,1)} %bitcast.13, bf16[256,1024]{1,0:T(8,128)(2,1)} %bitcast.21, f32[1,1024]{1,0:T(1,128)} %bitcast.16, bf16[256,256]{1,0:T(8,128)(2,1)} %local_ref.1), custom_call_target="tpu_custom_call" | custom-call | flops 140000000 | bytes 4000000 | tf_op jit(solution)/shard_map/pallas_call | solution.py:361
  4.1 13.3 %all-to-all-start = ((bf16[64,48,256]{2,1,0:T(8,128)(2,1)}), bf16[64,48,256]{2,1,0:T(8,128)(2,1)}, u32[]{:S(2)}, u32[]{:S(2)}) async-start(bf16[64,48,256]{2,1,0:T(8,128)(2,1)} %bitcast.20), calls=%async_computation | async-start | bytes 3145728 | tf_op jit(solution)/shard_map/all_to_all | solution.py:418
  17.4 3.8 %shard_map.144 = (bf16[256,1024]{1,0:T(8,128)(2,1)}, f32[256,1024]{1,0:T(8,128)}, f32[256,1024]{1,0:T(8,128)}) custom-call(bf16[256,1024]{1,0:T(8,128)(2,1)} %bitcast.14, bf16[256,1024]{1,0:T(8,128)(2,1)} %bitcast.22, f32[1,1024]{1,0:T(1,128)} %bitcast.17, bf16[4,256,256]{2,1,0:T(8,128)(2,1)} %wu_ref.5, bf16[4,256,256]{2,1,0:T(8,128)(2,1)} %wv_ref.5, ...), custom_call_target="tpu_custom_call" | custom-call | flops 400000000 | bytes 8000000 | tf_op jit(solution)/shard_map/pallas_call | solution.py:361
  21.3 0.6 pad_add_fusion.place_ref
  21.8 34.5 %all-to-all-done.recv_hbm = bf16[64,48,256]{2,1,0:T(8,128)(2,1)} async-done(((bf16[64,48,256]{2,1,0:T(8,128)(2,1)}), bf16[64,48,256]{2,1,0:T(8,128)(2,1)}, u32[]{:S(2)}, u32[]{:S(2)}) %all-to-all-start) | async-done | bytes 1572896 | tf_op jit(solution)/shard_map/all_to_all | solution.py:418
  56.4 8.3 %shard_map.145 = (bf16[64,32,256]{2,1,0:T(8,128)(2,1)}, f32[4,25,8,128]{3,2,1,0:T(8,128)}, bf16[4,25,8,128]{3,2,1,0:T(8,128)(2,1)}) custom-call(s32[3]{0:T(128)} %pad_add_fusion.place_ref, bf16[64,48,256]{2,1,0:T(8,128)(2,1)} %all-to-all-done.recv_hbm, f32[6,2,2,1024]{3,2,1,0:T(2,128)} %coef_hbm.1, bf16[4,256,256]{2,1,0:T(8,128)(2,1)} %wu_ref.5, ...), custom_call_target="tpu_custom_call" | custom-call | flops 800000000 | bytes 4000000 | tf_op jit(solution)/shard_map/pallas_call | solution.py:361
  64.6 0.0 copy-start.11
  64.7 6.6 %all-to-all-start.1 = ((bf16[64,32,256]{2,1,0:T(8,128)(2,1)}), bf16[64,32,256]{2,1,0:T(8,128)(2,1)S(1)}, u32[]{:S(2)}, u32[]{:S(2)}) async-start(bf16[64,32,256]{2,1,0:T(8,128)(2,1)} %get-tuple-element.49), calls=%async_computation.1 | async-start | bytes 2097152 | tf_op jit(solution)/shard_map/all_to_all | solution.py:458
  71.3 0.5 collective-permute-start
  71.8 1.1 collective-permute-done.got_ref
  72.9 0.6 shard_map.146
  73.5 0.0 copy-start.1
  73.6 1.3 collective-permute-start.1
  74.9 2.4 %collective-permute-start.2 = (bf16[25,8,128]{2,1,0:T(8,128)(2,1)S(1)}, bf16[25,8,128]{2,1,0:T(8,128)(2,1)S(1)}, u32[]{:S(2)}, u32[]{:S(2)}) collective-permute-start(bf16[25,8,128]{2,1,0:T(8,128)(2,1)S(1)} %get-tuple-element.47), channel_id=1, source_target_pairs={{0,128},{64,192},{128,0},{192,64},{1,129},{65,193},{129,1},{193,65... | collective-permute-start | bytes 153608 | tf_op jit(solution)/shard_map/ppermute | solution.py:384
  77.3 1.2 collective-permute-start.3
  78.5 1.5 %collective-permute-done.2.refs_1_ = bf16[25,8,128]{2,1,0:T(8,128)(2,1)S(1)} collective-permute-done((bf16[25,8,128]{2,1,0:T(8,128)(2,1)S(1)}, bf16[25,8,128]{2,1,0:T(8,128)(2,1)S(1)}, u32[]{:S(2)}, u32[]{:S(2)}) %collective-permute-start.2) | collective-permute-done | bytes 51232 | tf_op jit(solution)/shard_map/ppermute | solution.py:384
  79.9 0.6 collective-permute-done.3.refs_2_
  80.6 1.4 %collective-permute-start.4 = (bf16[25,8,128]{2,1,0:T(8,128)(2,1)S(1)}, bf16[25,8,128]{2,1,0:T(8,128)(2,1)S(1)}, u32[]{:S(2)}, u32[]{:S(2)}) collective-permute-start(bf16[25,8,128]{2,1,0:T(8,128)(2,1)S(1)} %shard_map.147.a_ref), channel_id=1, source_target_pairs={{0,2},{2,0},{4,6},{6,4},{1,3},{3,1},{5,7},{7,5},{8,10},{10,8},{12,... | collective-permute-start | bytes 153608 | tf_op jit(solution)/shard_map/ppermute | solution.py:390
  82.0 2.2 %collective-permute-done.4.b_ref = bf16[25,8,128]{2,1,0:T(8,128)(2,1)S(1)} collective-permute-done((bf16[25,8,128]{2,1,0:T(8,128)(2,1)S(1)}, bf16[25,8,128]{2,1,0:T(8,128)(2,1)S(1)}, u32[]{:S(2)}, u32[]{:S(2)}) %collective-permute-start.4) | collective-permute-done | bytes 51232 | tf_op jit(solution)/shard_map/ppermute | solution.py:390
  84.2 2.9 %collective-permute-start.5 = (bf16[25,8,128]{2,1,0:T(8,128)(2,1)S(1)}, bf16[25,8,128]{2,1,0:T(8,128)(2,1)S(1)}, u32[]{:S(2)}, u32[]{:S(2)}) collective-permute-start(bf16[25,8,128]{2,1,0:T(8,128)(2,1)S(1)} %shard_map.148.a_ref), channel_id=1, source_target_pairs={{0,4},{2,6},{4,0},{6,2},{1,5},{3,7},{5,1},{7,3},{8,12},{10,14},{12... | collective-permute-start | bytes 153608 | tf_op jit(solution)/shard_map/ppermute | solution.py:390
  87.1 2.5 %collective-permute-done.5.b_ref = bf16[25,8,128]{2,1,0:T(8,128)(2,1)S(1)} collective-permute-done((bf16[25,8,128]{2,1,0:T(8,128)(2,1)S(1)}, bf16[25,8,128]{2,1,0:T(8,128)(2,1)S(1)}, u32[]{:S(2)}, u32[]{:S(2)}) %collective-permute-start.5) | collective-permute-done | bytes 51232 | tf_op jit(solution)/shard_map/ppermute | solution.py:390
  89.6 2.0 %collective-permute-start.6 = (bf16[25,8,128]{2,1,0:T(8,128)(2,1)S(1)}, bf16[25,8,128]{2,1,0:T(8,128)(2,1)S(1)}, u32[]{:S(2)}, u32[]{:S(2)}) collective-permute-start(bf16[25,8,128]{2,1,0:T(8,128)(2,1)S(1)} %shard_map.149.a_ref), channel_id=1, source_target_pairs={{0,8},{8,0},{16,24},{24,16},{32,40},{40,32},{48,56},{56,48},{1,9},... | collective-permute-start | bytes 153608 | tf_op jit(solution)/shard_map/ppermute | solution.py:390
  91.6 5.0 %collective-permute-done.6.b_ref = bf16[25,8,128]{2,1,0:T(8,128)(2,1)S(1)} collective-permute-done((bf16[25,8,128]{2,1,0:T(8,128)(2,1)S(1)}, bf16[25,8,128]{2,1,0:T(8,128)(2,1)S(1)}, u32[]{:S(2)}, u32[]{:S(2)}) %collective-permute-start.6) | collective-permute-done | bytes 51232 | tf_op jit(solution)/shard_map/ppermute | solution.py:390
  96.6 2.1 %collective-permute-start.9 = (bf16[25,8,128]{2,1,0:T(8,128)(2,1)S(1)}, bf16[25,8,128]{2,1,0:T(8,128)(2,1)S(1)}, u32[]{:S(2)}, u32[]{:S(2)}) collective-permute-start(bf16[25,8,128]{2,1,0:T(8,128)(2,1)S(1)} %shard_map.150.refs_0_), channel_id=1, source_target_pairs={{0,48},{8,56},{16,0},{24,8},{32,16},{40,24},{48,32},{56,40},{1,49}... | collective-permute-start | bytes 153608 | tf_op jit(solution)/shard_map/ppermute | solution.py:384
  98.8 2.5 %collective-permute-start.8 = (bf16[25,8,128]{2,1,0:T(8,128)(2,1)S(1)}, bf16[25,8,128]{2,1,0:T(8,128)(2,1)S(1)}, u32[]{:S(2)}, u32[]{:S(2)}) collective-permute-start(bf16[25,8,128]{2,1,0:T(8,128)(2,1)S(1)} %shard_map.150.refs_0_), channel_id=1, source_target_pairs={{0,32},{8,40},{16,48},{24,56},{32,0},{40,8},{48,16},{56,24},{1,33}... | collective-permute-start | bytes 153608 | tf_op jit(solution)/shard_map/ppermute | solution.py:384
  101.3 2.3 %collective-permute-start.7 = (bf16[25,8,128]{2,1,0:T(8,128)(2,1)S(1)}, bf16[25,8,128]{2,1,0:T(8,128)(2,1)S(1)}, u32[]{:S(2)}, u32[]{:S(2)}) collective-permute-start(bf16[25,8,128]{2,1,0:T(8,128)(2,1)S(1)} %shard_map.150.refs_0_), channel_id=1, source_target_pairs={{0,16},{8,24},{16,32},{24,40},{32,48},{40,56},{48,0},{56,8},{1,17}... | collective-permute-start | bytes 153608 | tf_op jit(solution)/shard_map/ppermute | solution.py:384
  103.6 2.1 %collective-permute-done.8.refs_2_ = bf16[25,8,128]{2,1,0:T(8,128)(2,1)S(1)} collective-permute-done((bf16[25,8,128]{2,1,0:T(8,128)(2,1)S(1)}, bf16[25,8,128]{2,1,0:T(8,128)(2,1)S(1)}, u32[]{:S(2)}, u32[]{:S(2)}) %collective-permute-start.8) | collective-permute-done | bytes 51232 | tf_op jit(solution)/shard_map/ppermute | solution.py:384
  105.7 1.6 %collective-permute-done.7.refs_1_ = bf16[25,8,128]{2,1,0:T(8,128)(2,1)S(1)} collective-permute-done((bf16[25,8,128]{2,1,0:T(8,128)(2,1)S(1)}, bf16[25,8,128]{2,1,0:T(8,128)(2,1)S(1)}, u32[]{:S(2)}, u32[]{:S(2)}) %collective-permute-start.7) | collective-permute-done | bytes 51232 | tf_op jit(solution)/shard_map/ppermute | solution.py:384
  107.3 1.0 copy-done.6
  108.4 0.3 shard_map.152.refs_0_
  108.7 2.6 %collective-permute-start.15 = (bf16[256,256]{1,0:T(8,128)(2,1)S(1)}, bf16[256,256]{1,0:T(8,128)(2,1)S(1)}, u32[]{:S(2)}, u32[]{:S(2)}) collective-permute-start(bf16[256,256]{1,0:T(8,128)(2,1)S(1)} %shard_map.152.refs_0_), channel_id=1, source_target_pairs={{0,192},{64,0},{128,64},{192,128},{1,193},{65,1},{129,65},{193,129... | collective-permute-start | bytes 393224 | tf_op jit(solution)/shard_map/ppermute | solution.py:384
  111.2 0.6 shard_map.151.refs_0_
  111.8 1.3 collective-permute-start.12
  113.1 0.7 collective-permute-start.10
  113.8 3.1 %collective-permute-start.14 = (bf16[256,256]{1,0:T(8,128)(2,1)S(1)}, bf16[256,256]{1,0:T(8,128)(2,1)S(1)}, u32[]{:S(2)}, u32[]{:S(2)}) collective-permute-start(bf16[256,256]{1,0:T(8,128)(2,1)S(1)} %shard_map.152.refs_0_), channel_id=1, source_target_pairs={{0,128},{64,192},{128,0},{192,64},{1,129},{65,193},{129,1},{193,65... | collective-permute-start | bytes 393224 | tf_op jit(solution)/shard_map/ppermute | solution.py:384
  117.0 1.2 copy-done.4
  118.2 1.2 copy-done.5
  119.5 1.9 %shard_map.154 = (bf16[256,1024]{1,0:T(8,128)(2,1)}, bf16[256,1024]{1,0:T(8,128)(2,1)}) custom-call(bf16[4,16,32,256]{3,2,1,0:T(8,128)(2,1)S(1)} %bitcast.12, bf16[256,1024]{1,0:T(8,128)(2,1)S(1)} %bitcast.15, f32[1,1024]{1,0:T(1,128)S(1)} %bitcast.18, f32[256,1024]{1,0:T(8,128)S(1)} %copy-done.4, f32[256,1024]{1,0:T(8,128)S(1)} %copy-done.5, ...), custom_call_target="tpu_custom_call" | custom-call | flops 600000000 | bytes 8000000 | tf_op jit(solution)/shard_map/pallas_call | solution.py:361
  121.3 4.5 %collective-permute-done.14.refs_2_ = bf16[256,256]{1,0:T(8,128)(2,1)S(1)} collective-permute-done((bf16[256,256]{1,0:T(8,128)(2,1)S(1)}, bf16[256,256]{1,0:T(8,128)(2,1)S(1)}, u32[]{:S(2)}, u32[]{:S(2)}) %collective-permute-start.14) | collective-permute-done | bytes 131104 | tf_op jit(solution)/shard_map/ppermute | solution.py:384
  125.9 5.0 %collective-permute-start.16 = (bf16[4,25,8,128]{3,2,1,0:T(8,128)(2,1)S(1)}, bf16[4,25,8,128]{3,2,1,0:T(8,128)(2,1)S(1)}, u32[]{:S(2)}, u32[]{:S(2)}) collective-permute-start(bf16[4,25,8,128]{3,2,1,0:T(8,128)(2,1)S(1)} %shard_map.151.refs_0_), channel_id=1, source_target_pairs={{0,1},{1,0},{2,3},{3,2},{4,5},{5,4},{6,7},{7,6},{8,9},{9,8},{10,11... | collective-permute-start | bytes 614408 | tf_op jit(solution)/shard_map/ppermute | solution.py:390
  130.9 1.4 %shard_map.153 = f32[256,256]{1,0:T(8,128)} custom-call(s32[3]{0:T(128)S(1)} %copy-done.10, bf16[256,256]{1,0:T(8,128)(2,1)S(1)} %shard_map.152.refs_0_, bf16[256,256]{1,0:T(8,128)(2,1)S(1)} %collective-permute-done.13.refs_1_, bf16[256,256]{1,0:T(8,128)(2,1)S(1)} %collective-permute-done.14.refs_2_, bf16[256,256]{1,0:T(8,128)(2,1)S(1)} %collective-permute-done.15.refs_3_), custom_call_target="tpu_custom_call" | custom-call | bytes 800000 | tf_op jit(solution)/shard_map/pallas_call | solution.py:361
  132.3 1.0 collective-permute-start.17
  133.3 0.1 collective-permute-start.18
  133.4 0.4 collective-permute-start.19
  133.8 0.6 collective-permute-done.17.refs_5_
  134.4 0.4 collective-permute-done.18.refs_6_
  134.8 0.3 collective-permute-done.19.refs_7_
  135.1 2.5 %shard_map.155 = (f32[4,256,256]{2,1,0:T(8,128)}, f32[4,256,256]{2,1,0:T(8,128)}, f32[4,256,256]{2,1,0:T(8,128)}, f32[1,1024]{1,0:T(1,128)}, f32[6,2,2,1024]{3,2,1,0:T(2,128)}) custom-call(s32[3]{0:T(128)S(1)} %copy-done.10, bf16[4,256,256]{2,1,0:T(8,128)(2,1)S(1)} %copy-done, bf16[4,256,256]{2,1,0:T(8,128)(2,1)S(1)} %copy-done.1, f32[1,1024]{1,0:T(1,128)S(1)} %bitcast.19, ...), custom_call_target="tpu_custom_call" | custom-call | bytes 5000000 | tf_op jit(solution)/shard_map/pallas_call | solution.py:361
  (34 shorter events, 0.2 us)
Async XLA Ops:
  4.1 52.3 %all-to-all-start = ((bf16[64,48,256]{2,1,0:T(8,128)(2,1)}), bf16[64,48,256]{2,1,0:T(8,128)(2,1)}, u32[]{:S(2)}, u32[]{:S(2)}) async-start(bf16[64,48,256]{2,1,0:T(8,128)(2,1)} %bitcast.20), calls=%async_computation | async-start | bytes 3145728 | tf_op jit(solution)/shard_map/all_to_all | solution.py:418
  64.6 6.7 %copy-start.11 = (bf16[4,25,8,128]{3,2,1,0:T(8,128)(2,1)S(1)}, bf16[4,25,8,128]{3,2,1,0:T(8,128)(2,1)}, u32[]{:S(2)}) copy-start(bf16[4,25,8,128]{3,2,1,0:T(8,128)(2,1)} %get-tuple-element.44) | copy-start | bytes 614404
  64.6 8.3 %copy-start.8 = (f32[4,25,8,128]{3,2,1,0:T(8,128)S(1)}, f32[4,25,8,128]{3,2,1,0:T(8,128)}, u32[]{:S(2)}) copy-start(f32[4,25,8,128]{3,2,1,0:T(8,128)} %get-tuple-element.43.keep_ref) | copy-start | bytes 1228804
  64.6 8.3 %copy-start.10 = (s32[3]{0:T(128)S(1)}, s32[3]{0:T(128)}, u32[]{:S(2)}) copy-start(s32[3]{0:T(128)} %pad_add_fusion.place_ref) | copy-start | bytes 40
  64.7 42.7 %all-to-all-start.1 = ((bf16[64,32,256]{2,1,0:T(8,128)(2,1)}), bf16[64,32,256]{2,1,0:T(8,128)(2,1)S(1)}, u32[]{:S(2)}, u32[]{:S(2)}) async-start(bf16[64,32,256]{2,1,0:T(8,128)(2,1)} %get-tuple-element.49), calls=%async_computation.1 | async-start | bytes 2097152 | tf_op jit(solution)/shard_map/all_to_all | solution.py:458
  71.3 1.6 %collective-permute-start = (bf16[4,25,8,128]{3,2,1,0:T(8,128)(2,1)S(1)}, bf16[4,25,8,128]{3,2,1,0:T(8,128)(2,1)S(1)}, u32[]{:S(2)}, u32[]{:S(2)}) collective-permute-start(bf16[4,25,8,128]{3,2,1,0:T(8,128)(2,1)S(1)} %copy-done.11), channel_id=1, source_target_pairs={{0,1},{1,0},{2,3},{3,2},{4,5},{5,4},{6,7},{7,6},{8,9},{9,8},{10,11... | collective-permute-start | bytes 614408 | tf_op jit(solution)/shard_map/ppermute | solution.py:390
  72.9 44.0 %copy-start.7 = (bf16[256,256]{1,0:T(8,128)(2,1)S(1)}, bf16[256,256]{1,0:T(8,128)(2,1)}, u32[]{:S(2)}) copy-start(bf16[256,256]{1,0:T(8,128)(2,1)} %local_ref.1) | copy-start | bytes 393220
  72.9 44.0 %copy-start.9 = (f32[1024]{0:T(1024)S(1)}, f32[1024]{0:T(1024)}, u32[]{:S(2)}) copy-start(f32[1024]{0:T(1024)} %param.10) | copy-start | bytes 12292
  73.5 43.4 %copy-start = (bf16[4,256,256]{2,1,0:T(8,128)(2,1)S(1)}, bf16[4,256,256]{2,1,0:T(8,128)(2,1)}, u32[]{:S(2)}) copy-start(bf16[4,256,256]{2,1,0:T(8,128)(2,1)} %wu_ref.5) | copy-start | bytes 1572868
  73.5 43.4 %copy-start.1 = (bf16[4,256,256]{2,1,0:T(8,128)(2,1)S(1)}, bf16[4,256,256]{2,1,0:T(8,128)(2,1)}, u32[]{:S(2)}) copy-start(bf16[4,256,256]{2,1,0:T(8,128)(2,1)} %wv_ref.5) | copy-start | bytes 1572868
  73.5 43.4 %copy-start.2 = (bf16[1,256,1024]{2,1,0:T(8,128)(2,1)S(1)}, bf16[1,256,1024]{2,1,0:T(8,128)(2,1)}, u32[]{:S(2)}) copy-start(bf16[1,256,1024]{2,1,0:T(8,128)(2,1)} %param.8) | copy-start | bytes 1572868
  73.5 43.4 %copy-start.3 = (bf16[4,256,256]{2,1,0:T(8,128)(2,1)S(1)}, bf16[4,256,256]{2,1,0:T(8,128)(2,1)}, u32[]{:S(2)}) copy-start(bf16[4,256,256]{2,1,0:T(8,128)(2,1)} %wo_ref.3) | copy-start | bytes 1572868
  73.6 4.9 %collective-permute-start.1 = (bf16[25,8,128]{2,1,0:T(8,128)(2,1)S(1)}, bf16[25,8,128]{2,1,0:T(8,128)(2,1)S(1)}, u32[]{:S(2)}, u32[]{:S(2)}) collective-permute-start(bf16[25,8,128]{2,1,0:T(8,128)(2,1)S(1)} %get-tuple-element.46), channel_id=1, source_target_pairs={{0,64},{64,128},{128,192},{192,0},{1,65},{65,129},{129,193},{193,1... | collective-permute-start | bytes 153608 | tf_op jit(solution)/shard_map/ppermute | solution.py:384
  74.9 5.1 %collective-permute-start.2 = (bf16[25,8,128]{2,1,0:T(8,128)(2,1)S(1)}, bf16[25,8,128]{2,1,0:T(8,128)(2,1)S(1)}, u32[]{:S(2)}, u32[]{:S(2)}) collective-permute-start(bf16[25,8,128]{2,1,0:T(8,128)(2,1)S(1)} %get-tuple-element.47), channel_id=1, source_target_pairs={{0,128},{64,192},{128,0},{192,64},{1,129},{65,193},{129,1},{193,65... | collective-permute-start | bytes 153608 | tf_op jit(solution)/shard_map/ppermute | solution.py:384
  77.3 3.3 %collective-permute-start.3 = (bf16[25,8,128]{2,1,0:T(8,128)(2,1)S(1)}, bf16[25,8,128]{2,1,0:T(8,128)(2,1)S(1)}, u32[]{:S(2)}, u32[]{:S(2)}) collective-permute-start(bf16[25,8,128]{2,1,0:T(8,128)(2,1)S(1)} %get-tuple-element.48), channel_id=1, source_target_pairs={{0,192},{64,0},{128,64},{192,128},{1,193},{65,1},{129,65},{193,129... | collective-permute-start | bytes 153608 | tf_op jit(solution)/shard_map/ppermute | solution.py:384
  80.6 3.6 %collective-permute-start.4 = (bf16[25,8,128]{2,1,0:T(8,128)(2,1)S(1)}, bf16[25,8,128]{2,1,0:T(8,128)(2,1)S(1)}, u32[]{:S(2)}, u32[]{:S(2)}) collective-permute-start(bf16[25,8,128]{2,1,0:T(8,128)(2,1)S(1)} %shard_map.147.a_ref), channel_id=1, source_target_pairs={{0,2},{2,0},{4,6},{6,4},{1,3},{3,1},{5,7},{7,5},{8,10},{10,8},{12,... | collective-permute-start | bytes 153608 | tf_op jit(solution)/shard_map/ppermute | solution.py:390
  84.2 5.4 %collective-permute-start.5 = (bf16[25,8,128]{2,1,0:T(8,128)(2,1)S(1)}, bf16[25,8,128]{2,1,0:T(8,128)(2,1)S(1)}, u32[]{:S(2)}, u32[]{:S(2)}) collective-permute-start(bf16[25,8,128]{2,1,0:T(8,128)(2,1)S(1)} %shard_map.148.a_ref), channel_id=1, source_target_pairs={{0,4},{2,6},{4,0},{6,2},{1,5},{3,7},{5,1},{7,3},{8,12},{10,14},{12... | collective-permute-start | bytes 153608 | tf_op jit(solution)/shard_map/ppermute | solution.py:390
  89.6 7.0 %collective-permute-start.6 = (bf16[25,8,128]{2,1,0:T(8,128)(2,1)S(1)}, bf16[25,8,128]{2,1,0:T(8,128)(2,1)S(1)}, u32[]{:S(2)}, u32[]{:S(2)}) collective-permute-start(bf16[25,8,128]{2,1,0:T(8,128)(2,1)S(1)} %shard_map.149.a_ref), channel_id=1, source_target_pairs={{0,8},{8,0},{16,24},{24,16},{32,40},{40,32},{48,56},{56,48},{1,9},... | collective-permute-start | bytes 153608 | tf_op jit(solution)/shard_map/ppermute | solution.py:390
  96.6 6.9 %collective-permute-start.9 = (bf16[25,8,128]{2,1,0:T(8,128)(2,1)S(1)}, bf16[25,8,128]{2,1,0:T(8,128)(2,1)S(1)}, u32[]{:S(2)}, u32[]{:S(2)}) collective-permute-start(bf16[25,8,128]{2,1,0:T(8,128)(2,1)S(1)} %shard_map.150.refs_0_), channel_id=1, source_target_pairs={{0,48},{8,56},{16,0},{24,8},{32,16},{40,24},{48,32},{56,40},{1,49}... | collective-permute-start | bytes 153608 | tf_op jit(solution)/shard_map/ppermute | solution.py:384
  98.8 6.9 %collective-permute-start.8 = (bf16[25,8,128]{2,1,0:T(8,128)(2,1)S(1)}, bf16[25,8,128]{2,1,0:T(8,128)(2,1)S(1)}, u32[]{:S(2)}, u32[]{:S(2)}) collective-permute-start(bf16[25,8,128]{2,1,0:T(8,128)(2,1)S(1)} %shard_map.150.refs_0_), channel_id=1, source_target_pairs={{0,32},{8,40},{16,48},{24,56},{32,0},{40,8},{48,16},{56,24},{1,33}... | collective-permute-start | bytes 153608 | tf_op jit(solution)/shard_map/ppermute | solution.py:384
  101.3 6.0 %collective-permute-start.7 = (bf16[25,8,128]{2,1,0:T(8,128)(2,1)S(1)}, bf16[25,8,128]{2,1,0:T(8,128)(2,1)S(1)}, u32[]{:S(2)}, u32[]{:S(2)}) collective-permute-start(bf16[25,8,128]{2,1,0:T(8,128)(2,1)S(1)} %shard_map.150.refs_0_), channel_id=1, source_target_pairs={{0,16},{8,24},{16,32},{24,40},{32,48},{40,56},{48,0},{56,8},{1,17}... | collective-permute-start | bytes 153608 | tf_op jit(solution)/shard_map/ppermute | solution.py:384
  107.3 1.0 copy-start.6
  108.7 8.2 %collective-permute-start.15 = (bf16[256,256]{1,0:T(8,128)(2,1)S(1)}, bf16[256,256]{1,0:T(8,128)(2,1)S(1)}, u32[]{:S(2)}, u32[]{:S(2)}) collective-permute-start(bf16[256,256]{1,0:T(8,128)(2,1)S(1)} %shard_map.152.refs_0_), channel_id=1, source_target_pairs={{0,192},{64,0},{128,64},{192,128},{1,193},{65,1},{129,65},{193,129... | collective-permute-start | bytes 393224 | tf_op jit(solution)/shard_map/ppermute | solution.py:384
  111.8 20.5 %collective-permute-start.12 = (bf16[4,25,8,128]{3,2,1,0:T(8,128)(2,1)S(1)}, bf16[4,25,8,128]{3,2,1,0:T(8,128)(2,1)S(1)}, u32[]{:S(2)}, u32[]{:S(2)}) collective-permute-start(bf16[4,25,8,128]{3,2,1,0:T(8,128)(2,1)S(1)} %shard_map.151.refs_0_), channel_id=1, source_target_pairs={{0,192},{64,0},{128,64},{192,128},{1,193},{65,1},{129,65},{193,129... | collective-permute-start | bytes 614408 | tf_op jit(solution)/shard_map/ppermute | solution.py:384
  113.1 19.1 %collective-permute-start.11 = (bf16[4,25,8,128]{3,2,1,0:T(8,128)(2,1)S(1)}, bf16[4,25,8,128]{3,2,1,0:T(8,128)(2,1)S(1)}, u32[]{:S(2)}, u32[]{:S(2)}) collective-permute-start(bf16[4,25,8,128]{3,2,1,0:T(8,128)(2,1)S(1)} %shard_map.151.refs_0_), channel_id=1, source_target_pairs={{0,128},{64,192},{128,0},{192,64},{1,129},{65,193},{129,1},{193,65... | collective-permute-start | bytes 614408 | tf_op jit(solution)/shard_map/ppermute | solution.py:384
  113.1 19.1 %collective-permute-start.10 = (bf16[4,25,8,128]{3,2,1,0:T(8,128)(2,1)S(1)}, bf16[4,25,8,128]{3,2,1,0:T(8,128)(2,1)S(1)}, u32[]{:S(2)}, u32[]{:S(2)}) collective-permute-start(bf16[4,25,8,128]{3,2,1,0:T(8,128)(2,1)S(1)} %shard_map.151.refs_0_), channel_id=1, source_target_pairs={{0,64},{64,128},{128,192},{192,0},{1,65},{65,129},{129,193},{193,1... | collective-permute-start | bytes 614408 | tf_op jit(solution)/shard_map/ppermute | solution.py:384
  113.8 12.1 %collective-permute-start.14 = (bf16[256,256]{1,0:T(8,128)(2,1)S(1)}, bf16[256,256]{1,0:T(8,128)(2,1)S(1)}, u32[]{:S(2)}, u32[]{:S(2)}) collective-permute-start(bf16[256,256]{1,0:T(8,128)(2,1)S(1)} %shard_map.152.refs_0_), channel_id=1, source_target_pairs={{0,128},{64,192},{128,0},{192,64},{1,129},{65,193},{129,1},{193,65... | collective-permute-start | bytes 393224 | tf_op jit(solution)/shard_map/ppermute | solution.py:384
  116.9 13.9 %collective-permute-start.13 = (bf16[256,256]{1,0:T(8,128)(2,1)S(1)}, bf16[256,256]{1,0:T(8,128)(2,1)S(1)}, u32[]{:S(2)}, u32[]{:S(2)}) collective-permute-start(bf16[256,256]{1,0:T(8,128)(2,1)S(1)} %shard_map.152.refs_0_), channel_id=1, source_target_pairs={{0,64},{64,128},{128,192},{192,0},{1,65},{65,129},{129,193},{193,1... | collective-permute-start | bytes 393224 | tf_op jit(solution)/shard_map/ppermute | solution.py:384
  117.0 1.2 copy-start.4
  118.2 1.2 copy-start.5
  125.9 8.0 %collective-permute-start.16 = (bf16[4,25,8,128]{3,2,1,0:T(8,128)(2,1)S(1)}, bf16[4,25,8,128]{3,2,1,0:T(8,128)(2,1)S(1)}, u32[]{:S(2)}, u32[]{:S(2)}) collective-permute-start(bf16[4,25,8,128]{3,2,1,0:T(8,128)(2,1)S(1)} %shard_map.151.refs_0_), channel_id=1, source_target_pairs={{0,1},{1,0},{2,3},{3,2},{4,5},{5,4},{6,7},{7,6},{8,9},{9,8},{10,11... | collective-permute-start | bytes 614408 | tf_op jit(solution)/shard_map/ppermute | solution.py:390
  132.3 2.1 %collective-permute-start.17 = (bf16[4,25,8,128]{3,2,1,0:T(8,128)(2,1)S(1)}, bf16[4,25,8,128]{3,2,1,0:T(8,128)(2,1)S(1)}, u32[]{:S(2)}, u32[]{:S(2)}) collective-permute-start(bf16[4,25,8,128]{3,2,1,0:T(8,128)(2,1)S(1)} %collective-permute-done.10.refs_1_), channel_id=1, source_target_pairs={{0,1},{1,0},{2,3},{3,2},{4,5},{5,4},{6,7},{7,6},{8,9},{9,8},{10,11... | collective-permute-start | bytes 614408 | tf_op jit(solution)/shard_map/ppermute | solution.py:390
  133.3 1.5 %collective-permute-start.18 = (bf16[4,25,8,128]{3,2,1,0:T(8,128)(2,1)S(1)}, bf16[4,25,8,128]{3,2,1,0:T(8,128)(2,1)S(1)}, u32[]{:S(2)}, u32[]{:S(2)}) collective-permute-start(bf16[4,25,8,128]{3,2,1,0:T(8,128)(2,1)S(1)} %collective-permute-done.11.refs_2_), channel_id=1, source_target_pairs={{0,1},{1,0},{2,3},{3,2},{4,5},{5,4},{6,7},{7,6},{8,9},{9,8},{10,11... | collective-permute-start | bytes 614408 | tf_op jit(solution)/shard_map/ppermute | solution.py:390
  133.4 1.6 %collective-permute-start.19 = (bf16[4,25,8,128]{3,2,1,0:T(8,128)(2,1)S(1)}, bf16[4,25,8,128]{3,2,1,0:T(8,128)(2,1)S(1)}, u32[]{:S(2)}, u32[]{:S(2)}) collective-permute-start(bf16[4,25,8,128]{3,2,1,0:T(8,128)(2,1)S(1)} %collective-permute-done.12.refs_3_), channel_id=1, source_target_pairs={{0,1},{1,0},{2,3},{3,2},{4,5},{5,4},{6,7},{7,6},{8,9},{9,8},{10,11... | collective-permute-start | bytes 614408 | tf_op jit(solution)/shard_map/ppermute | solution.py:390

commit v8 on v7

--- a/solution.py
+++ b/solution.py
@@ -106,7 +106,7 @@
     recv_ref, send_ref, coef_ref, wu_ref, wv_ref, wo_ref,
     z0, zs, es, act_s, dgd_s, coef, acc, gsum, in_sems, out_sems, sems,
 ):
-    group = place_ref[1]
+    group = place_ref[1] >> 1
 
     def fetch(at):
         here = pl.ds(at * 16, 16)
@@ -252,7 +252,7 @@
         ref[...] = piece(k).astype(BF)
 
 
-def dp_sum_kernel(own_ref, *refs):
+def quarter_sum_kernel(own_ref, *refs):
     *got, out_ref = refs
     total = own_ref[...]
     for ref in got:
@@ -267,7 +267,7 @@
 def ordered_sum_kernel(place_ref, *refs):
     *parts, out_ref, held = refs
     for k, ref in enumerate(parts):
-        held[(place_ref[0] + 4 - k) & 3] = ref[...]
+        held[(place_ref[3] + 4 - k) & 3] = ref[...]
     total = held[0].astype(F32)
     for at in range(1, 4):
         total = total + held[at].astype(F32)
@@ -277,7 +277,7 @@
 def gather_kernel(place_ref, *refs):
     *parts, out_ref = refs
     for k, ref in enumerate(parts):
-        out_ref[(place_ref[1] + 4 - k) & 3] = ref[...]
+        out_ref[((place_ref[1] >> 1) + 4 - k) & 3] = ref[...]
 
 
 def group_of(recv_ref, g, which):
@@ -396,7 +396,7 @@
     gain2 = gain.reshape(1, -1)
     wide = (BLK, GROUPS * BLK)
     place = jnp.stack(
-        [lax.axis_index("dp"), lax.axis_index("z") >> 1, lax.axis_index("c")]
+        [lax.axis_index(a) for a in ("y", "z", "c", "dp")]
     ).astype(jnp.int32)
 
     send = call(
@@ -460,8 +460,8 @@
     own, *gives = call(
         core_sum_kernel, [(quarter, F32)] + [(quarter, BF)] * 3, moved=1e6, smem=(0,)
     )(place, keep, swapped(give))
-    slice_ = call(dp_sum_kernel, [(quarter, BF)], moved=3e5)(own, *rotated(gives, "dp"))[0]
-    for axis, bit in (("y", 1), ("y", 2), ("z", 1)):
+    slice_ = call(quarter_sum_kernel, [(quarter, BF)], moved=3e5)(own, *rotated(gives, "y"))[0]
+    for axis, bit in (("dp", 1), ("dp", 2), ("z", 1)):
         slice_ = call(pair_sum_kernel, [(quarter, BF)], moved=2e5)(
             slice_, swapped(slice_, axis, bit)
         )[0]
@@ -470,10 +470,10 @@
     recv2, got_z = lax.optimization_barrier((recv2, got_z))
     part = call(local_kernel, [((BLK, BLK), BF)], flops=1.3e8, moved=1.2e6)(recv2, u)[0]
     parts = rotated(part, "dp")
-    mine_d = call(gather_kernel, [((4,) + quarter, BF)], moved=4e5, smem=(0,))(
+    mine_y = call(gather_kernel, [((4,) + quarter, BF)], moved=4e5, smem=(0,))(
         place, slice_, *got_z
     )[0]
-    got_d = rotated(mine_d, "dp")
+    got_y = rotated(mine_y, "y")
     grad_local = call(
         ordered_sum_kernel,
         [((BLK, BLK), F32)],
@@ -485,9 +485,10 @@
         last_kernel, [(wide, BF), (wide, BF)], scratch=[pltpu.VMEM(wide, F32)],
         flops=6e8, moved=8e6,
     )(recv2, x, gain2, act, dgd, w_u, w_v, w_o, local_factor)
-    got_d, grad_local, mixed, dx = lax.optimization_barrier((got_d, grad_local, mixed, dx))
-    halves = [mine_d] + got_d
+    got_y, mixed, dx = lax.optimization_barrier((got_y, mixed, dx))
+    halves = [mine_y] + got_y
     others = [swapped(half) for half in halves]
+    others, grad_local = lax.optimization_barrier((others, grad_local))
 
     shape = (GROUPS, BLK, BLK)
     gu, gv, go, grad_gain, grad_bfly = call(

time: 138 us -> 135 us (0.978)
  starting transfers between devices: 52.9 us -> 49.7 us
    ppermute x8, starting transfers between devices: 13.4 us -> 10.4 us  [swapped(): lax.ppermute(value, axis, [(s, s ^ bit) for s in range(lax.axis_size(axis...]
  transfers between devices with their start and end apart: 22 -> 22, of which waited for: 13 -> 10; matrix products, arithmetic and copies ran while one was open for 0% -> 0% of each run, Pallas kernels for 6% -> 6%
where the time goes in v8:
time: 135 us
  waiting for transfers between devices  57 us (42%)
  starting transfers between devices  49.7 us (37%)
  Pallas kernels  22.9 us (17%)
  local copies, waits for them, and re-layouts  3.54 us (3%)
    all_to_all x1, waiting for transfers between devices, per_device(): recv = lax.all_to_all(send.reshape(BLOCKS, 3 * PL, BLK), SEQ, 0, 0)  34.5 us
    pallas_call x13, Pallas kernels, run(): pl.pallas_call(kernel, out_shape=shapes, in_specs=specs, out_specs=[pl.Bl...  22.9 us
    ppermute x12, starting transfers between devices, rotated(): lax.ppermute(value, axis, [(s, (s + k * step) % n) for s in range(n)])  19.3 us
    all_to_all x1, starting transfers between devices, per_device(): recv = lax.all_to_all(send.reshape(BLOCKS, 3 * PL, BLK), SEQ, 0, 0)  13.3 us
    ppermute x12, waiting for transfers between devices, rotated(): lax.ppermute(value, axis, [(s, (s + k * step) % n) for s in range(n)])  11.8 us
    ppermute x8, waiting for transfers between devices, swapped(): lax.ppermute(value, axis, [(s, s ^ bit) for s in range(lax.axis_size(axis...  10.7 us
    ppermute x8, starting transfers between devices, swapped(): lax.ppermute(value, axis, [(s, s ^ bit) for s in range(lax.axis_size(axis...  10.4 us
    all_to_all x1, starting transfers between devices, per_device(): recv2 = lax.all_to_all(back, SEQ, 0, 0).reshape(GROUPS, 16, 2 * PL, BLK)  6.62 us
  transfers between devices with their start and end apart: 22, of which 10 were waited for; matrix products, arithmetic and copies ran while one was open for 0% of the time, Pallas kernels for 6%

profile of v8, /device:TPU:1, one launch (start us, length us, event | category | flops | bytes accessed | tf_op | source)
XLA Modules:
  0.0 134.5 jit_solution(10584310744502295019)
XLA Ops:
  0.6 3.4 %shard_map.143 = bf16[4,16,48,256]{3,2,1,0:T(8,128)(2,1)} custom-call(bf16[256,1024]{1,0:T(8,128)(2,1)} %bitcast.14, bf16[256,1024]{1,0:T(8,128)(2,1)} %bitcast.22, f32[1,1024]{1,0:T(1,128)} %bitcast.17, bf16[256,256]{1,0:T(8,128)(2,1)} %local_ref.1), custom_call_target="tpu_custom_call" | custom-call | flops 140000000 | bytes 4000000 | tf_op jit(solution)/shard_map/pallas_call | solution.py:361
  4.1 13.3 %all-to-all-start = ((bf16[64,48,256]{2,1,0:T(8,128)(2,1)}), bf16[64,48,256]{2,1,0:T(8,128)(2,1)}, u32[]{:S(2)}, u32[]{:S(2)}) async-start(bf16[64,48,256]{2,1,0:T(8,128)(2,1)} %bitcast.21), calls=%async_computation | async-start | bytes 3145728 | tf_op jit(solution)/shard_map/all_to_all | solution.py:418
  17.4 3.8 %shard_map.144 = (bf16[256,1024]{1,0:T(8,128)(2,1)}, f32[256,1024]{1,0:T(8,128)}, f32[256,1024]{1,0:T(8,128)}) custom-call(bf16[256,1024]{1,0:T(8,128)(2,1)} %bitcast.15, bf16[256,1024]{1,0:T(8,128)(2,1)} %bitcast.23, f32[1,1024]{1,0:T(1,128)} %bitcast.18, bf16[4,256,256]{2,1,0:T(8,128)(2,1)} %wu_ref.5, bf16[4,256,256]{2,1,0:T(8,128)(2,1)} %wv_ref.5, ...), custom_call_target="tpu_custom_call" | custom-call | flops 400000000 | bytes 8000000 | tf_op jit(solution)/shard_map/pallas_call | solution.py:361
  21.3 0.6 pad_add_fusion.place_ref
  21.8 34.5 %all-to-all-done.recv_hbm = bf16[64,48,256]{2,1,0:T(8,128)(2,1)} async-done(((bf16[64,48,256]{2,1,0:T(8,128)(2,1)}), bf16[64,48,256]{2,1,0:T(8,128)(2,1)}, u32[]{:S(2)}, u32[]{:S(2)}) %all-to-all-start) | async-done | bytes 1572896 | tf_op jit(solution)/shard_map/all_to_all | solution.py:418
  56.4 8.3 %shard_map.145 = (bf16[64,32,256]{2,1,0:T(8,128)(2,1)}, f32[4,25,8,128]{3,2,1,0:T(8,128)}, bf16[4,25,8,128]{3,2,1,0:T(8,128)(2,1)}) custom-call(s32[4]{0:T(128)} %pad_add_fusion.place_ref, bf16[64,48,256]{2,1,0:T(8,128)(2,1)} %all-to-all-done.recv_hbm, f32[6,2,2,1024]{3,2,1,0:T(2,128)} %coef_hbm.1, bf16[4,256,256]{2,1,0:T(8,128)(2,1)} %wu_ref.5, ...), custom_call_target="tpu_custom_call" | custom-call | flops 800000000 | bytes 4000000 | tf_op jit(solution)/shard_map/pallas_call | solution.py:361
  64.6 0.0 copy-start.8
  64.7 6.6 %all-to-all-start.1 = ((bf16[64,32,256]{2,1,0:T(8,128)(2,1)}), bf16[64,32,256]{2,1,0:T(8,128)(2,1)S(1)}, u32[]{:S(2)}, u32[]{:S(2)}) async-start(bf16[64,32,256]{2,1,0:T(8,128)(2,1)} %get-tuple-element.53), calls=%async_computation.1 | async-start | bytes 2097152 | tf_op jit(solution)/shard_map/all_to_all | solution.py:458
  71.3 0.5 collective-permute-start
  71.8 1.1 collective-permute-done.got_ref
  72.9 0.6 shard_map.146
  73.5 0.0 copy-start.1
  73.5 0.0 copy-start.2
  73.6 1.4 %collective-permute-start.1 = (bf16[25,8,128]{2,1,0:T(8,128)(2,1)S(1)}, bf16[25,8,128]{2,1,0:T(8,128)(2,1)S(1)}, u32[]{:S(2)}, u32[]{:S(2)}) collective-permute-start(bf16[25,8,128]{2,1,0:T(8,128)(2,1)S(1)} %get-tuple-element.50), channel_id=1, source_target_pairs={{0,2},{2,4},{4,6},{6,0},{1,3},{3,5},{5,7},{7,1},{8,10},{10,12},{12... | collective-permute-start | bytes 153608 | tf_op jit(solution)/shard_map/ppermute | solution.py:384
  75.0 2.4 %collective-permute-start.2 = (bf16[25,8,128]{2,1,0:T(8,128)(2,1)S(1)}, bf16[25,8,128]{2,1,0:T(8,128)(2,1)S(1)}, u32[]{:S(2)}, u32[]{:S(2)}) collective-permute-start(bf16[25,8,128]{2,1,0:T(8,128)(2,1)S(1)} %get-tuple-element.51), channel_id=1, source_target_pairs={{0,4},{2,6},{4,0},{6,2},{1,5},{3,7},{5,1},{7,3},{8,12},{10,14},{12... | collective-permute-start | bytes 153608 | tf_op jit(solution)/shard_map/ppermute | solution.py:384
  77.3 1.2 collective-permute-start.3
  78.5 0.2 collective-permute-done.1.refs_0_
  78.7 2.9 %collective-permute-done.2.refs_1_ = bf16[25,8,128]{2,1,0:T(8,128)(2,1)S(1)} collective-permute-done((bf16[25,8,128]{2,1,0:T(8,128)(2,1)S(1)}, bf16[25,8,128]{2,1,0:T(8,128)(2,1)S(1)}, u32[]{:S(2)}, u32[]{:S(2)}) %collective-permute-start.2) | collective-permute-done | bytes 51232 | tf_op jit(solution)/shard_map/ppermute | solution.py:384
  81.6 1.3 collective-permute-start.4
  82.9 2.0 %collective-permute-done.4.b_ref = bf16[25,8,128]{2,1,0:T(8,128)(2,1)S(1)} collective-permute-done((bf16[25,8,128]{2,1,0:T(8,128)(2,1)S(1)}, bf16[25,8,128]{2,1,0:T(8,128)(2,1)S(1)}, u32[]{:S(2)}, u32[]{:S(2)}) %collective-permute-start.4) | collective-permute-done | bytes 51232 | tf_op jit(solution)/shard_map/ppermute | solution.py:390
  85.0 2.8 %collective-permute-start.5 = (bf16[25,8,128]{2,1,0:T(8,128)(2,1)S(1)}, bf16[25,8,128]{2,1,0:T(8,128)(2,1)S(1)}, u32[]{:S(2)}, u32[]{:S(2)}) collective-permute-start(bf16[25,8,128]{2,1,0:T(8,128)(2,1)S(1)} %shard_map.148.a_ref), channel_id=1, source_target_pairs={{0,128},{64,192},{128,0},{192,64},{1,129},{65,193},{129,1},{193,65... | collective-permute-start | bytes 153608 | tf_op jit(solution)/shard_map/ppermute | solution.py:390
  87.8 2.0 %collective-permute-done.5.b_ref = bf16[25,8,128]{2,1,0:T(8,128)(2,1)S(1)} collective-permute-done((bf16[25,8,128]{2,1,0:T(8,128)(2,1)S(1)}, bf16[25,8,128]{2,1,0:T(8,128)(2,1)S(1)}, u32[]{:S(2)}, u32[]{:S(2)}) %collective-permute-start.5) | collective-permute-done | bytes 51232 | tf_op jit(solution)/shard_map/ppermute | solution.py:390
  89.9 1.4 %collective-permute-start.6 = (bf16[25,8,128]{2,1,0:T(8,128)(2,1)S(1)}, bf16[25,8,128]{2,1,0:T(8,128)(2,1)S(1)}, u32[]{:S(2)}, u32[]{:S(2)}) collective-permute-start(bf16[25,8,128]{2,1,0:T(8,128)(2,1)S(1)} %shard_map.149.a_ref), channel_id=1, source_target_pairs={{0,8},{8,0},{16,24},{24,16},{32,40},{40,32},{48,56},{56,48},{1,9},... | collective-permute-start | bytes 153608 | tf_op jit(solution)/shard_map/ppermute | solution.py:390
  91.3 5.6 %collective-permute-done.6.b_ref = bf16[25,8,128]{2,1,0:T(8,128)(2,1)S(1)} collective-permute-done((bf16[25,8,128]{2,1,0:T(8,128)(2,1)S(1)}, bf16[25,8,128]{2,1,0:T(8,128)(2,1)S(1)}, u32[]{:S(2)}, u32[]{:S(2)}) %collective-permute-start.6) | collective-permute-done | bytes 51232 | tf_op jit(solution)/shard_map/ppermute | solution.py:390
  96.9 1.9 %collective-permute-start.9 = (bf16[25,8,128]{2,1,0:T(8,128)(2,1)S(1)}, bf16[25,8,128]{2,1,0:T(8,128)(2,1)S(1)}, u32[]{:S(2)}, u32[]{:S(2)}) collective-permute-start(bf16[25,8,128]{2,1,0:T(8,128)(2,1)S(1)} %shard_map.150.refs_0_), channel_id=1, source_target_pairs={{0,48},{8,56},{16,0},{24,8},{32,16},{40,24},{48,32},{56,40},{1,49}... | collective-permute-start | bytes 153608 | tf_op jit(solution)/shard_map/ppermute | solution.py:384
  98.8 2.5 %collective-permute-start.8 = (bf16[25,8,128]{2,1,0:T(8,128)(2,1)S(1)}, bf16[25,8,128]{2,1,0:T(8,128)(2,1)S(1)}, u32[]{:S(2)}, u32[]{:S(2)}) collective-permute-start(bf16[25,8,128]{2,1,0:T(8,128)(2,1)S(1)} %shard_map.150.refs_0_), channel_id=1, source_target_pairs={{0,32},{8,40},{16,48},{24,56},{32,0},{40,8},{48,16},{56,24},{1,33}... | collective-permute-start | bytes 153608 | tf_op jit(solution)/shard_map/ppermute | solution.py:384
  101.3 2.3 %collective-permute-start.7 = (bf16[25,8,128]{2,1,0:T(8,128)(2,1)S(1)}, bf16[25,8,128]{2,1,0:T(8,128)(2,1)S(1)}, u32[]{:S(2)}, u32[]{:S(2)}) collective-permute-start(bf16[25,8,128]{2,1,0:T(8,128)(2,1)S(1)} %shard_map.150.refs_0_), channel_id=1, source_target_pairs={{0,16},{8,24},{16,32},{24,40},{32,48},{40,56},{48,0},{56,8},{1,17}... | collective-permute-start | bytes 153608 | tf_op jit(solution)/shard_map/ppermute | solution.py:384
  103.6 2.2 %collective-permute-done.8.refs_2_ = bf16[25,8,128]{2,1,0:T(8,128)(2,1)S(1)} collective-permute-done((bf16[25,8,128]{2,1,0:T(8,128)(2,1)S(1)}, bf16[25,8,128]{2,1,0:T(8,128)(2,1)S(1)}, u32[]{:S(2)}, u32[]{:S(2)}) %collective-permute-start.8) | collective-permute-done | bytes 51232 | tf_op jit(solution)/shard_map/ppermute | solution.py:384
  105.7 1.6 %collective-permute-done.7.refs_1_ = bf16[25,8,128]{2,1,0:T(8,128)(2,1)S(1)} collective-permute-done((bf16[25,8,128]{2,1,0:T(8,128)(2,1)S(1)}, bf16[25,8,128]{2,1,0:T(8,128)(2,1)S(1)}, u32[]{:S(2)}, u32[]{:S(2)}) %collective-permute-start.7) | collective-permute-done | bytes 51232 | tf_op jit(solution)/shard_map/ppermute | solution.py:384
  107.3 0.6 shard_map.151.refs_0_
  107.9 2.5 %collective-permute-start.12 = (bf16[4,25,8,128]{3,2,1,0:T(8,128)(2,1)S(1)}, bf16[4,25,8,128]{3,2,1,0:T(8,128)(2,1)S(1)}, u32[]{:S(2)}, u32[]{:S(2)}) collective-permute-start(bf16[4,25,8,128]{3,2,1,0:T(8,128)(2,1)S(1)} %shard_map.151.refs_0_), channel_id=1, source_target_pairs={{0,6},{2,0},{4,2},{6,4},{1,7},{3,1},{5,3},{7,5},{8,14},{10,8},{12,... | collective-permute-start | bytes 614408 | tf_op jit(solution)/shard_map/ppermute | solution.py:384
  110.4 1.4 %collective-permute-start.11 = (bf16[4,25,8,128]{3,2,1,0:T(8,128)(2,1)S(1)}, bf16[4,25,8,128]{3,2,1,0:T(8,128)(2,1)S(1)}, u32[]{:S(2)}, u32[]{:S(2)}) collective-permute-start(bf16[4,25,8,128]{3,2,1,0:T(8,128)(2,1)S(1)} %shard_map.151.refs_0_), channel_id=1, source_target_pairs={{0,4},{2,6},{4,0},{6,2},{1,5},{3,7},{5,1},{7,3},{8,12},{10,14},{12... | collective-permute-start | bytes 614408 | tf_op jit(solution)/shard_map/ppermute | solution.py:384
  111.8 1.0 copy-done.6
  112.9 0.3 shard_map.153.refs_0_
  113.2 2.6 %collective-permute-start.19 = (bf16[256,256]{1,0:T(8,128)(2,1)S(1)}, bf16[256,256]{1,0:T(8,128)(2,1)S(1)}, u32[]{:S(2)}, u32[]{:S(2)}) collective-permute-start(bf16[256,256]{1,0:T(8,128)(2,1)S(1)} %shard_map.153.refs_0_), channel_id=1, source_target_pairs={{0,192},{64,0},{128,64},{192,128},{1,193},{65,1},{129,65},{193,129... | collective-permute-start | bytes 393224 | tf_op jit(solution)/shard_map/ppermute | solution.py:384
  115.8 0.5 collective-permute-start.18
  116.3 0.0 copy-start.4
  116.3 1.2 copy-done.4
  117.6 1.2 copy-done.5
  118.8 1.9 %shard_map.152 = (bf16[256,1024]{1,0:T(8,128)(2,1)}, bf16[256,1024]{1,0:T(8,128)(2,1)}) custom-call(bf16[4,16,32,256]{3,2,1,0:T(8,128)(2,1)S(1)} %bitcast.13, bf16[256,1024]{1,0:T(8,128)(2,1)S(1)} %bitcast.16, f32[1,1024]{1,0:T(1,128)S(1)} %bitcast.19, f32[256,1024]{1,0:T(8,128)S(1)} %copy-done.4, f32[256,1024]{1,0:T(8,128)S(1)} %copy-done.5, ...), custom_call_target="tpu_custom_call" | custom-call | flops 600000000 | bytes 8000000 | tf_op jit(solution)/shard_map/pallas_call | solution.py:361
  120.7 3.8 %collective-permute-start.13 = (bf16[4,25,8,128]{3,2,1,0:T(8,128)(2,1)S(1)}, bf16[4,25,8,128]{3,2,1,0:T(8,128)(2,1)S(1)}, u32[]{:S(2)}, u32[]{:S(2)}) collective-permute-start(bf16[4,25,8,128]{3,2,1,0:T(8,128)(2,1)S(1)} %shard_map.151.refs_0_), channel_id=1, source_target_pairs={{0,1},{1,0},{2,3},{3,2},{4,5},{5,4},{6,7},{7,6},{8,9},{9,8},{10,11... | collective-permute-start | bytes 614408 | tf_op jit(solution)/shard_map/ppermute | solution.py:390
  124.4 0.1 collective-permute-start.14
  124.5 0.4 collective-permute-start.15
  124.9 0.1 collective-permute-start.16
  125.0 0.6 collective-permute-start.17
  125.6 5.0 %collective-permute-done.17.refs_1_ = bf16[256,256]{1,0:T(8,128)(2,1)S(1)} collective-permute-done((bf16[256,256]{1,0:T(8,128)(2,1)S(1)}, bf16[256,256]{1,0:T(8,128)(2,1)S(1)}, u32[]{:S(2)}, u32[]{:S(2)}) %collective-permute-start.17) | collective-permute-done | bytes 131104 | tf_op jit(solution)/shard_map/ppermute | solution.py:384
  130.6 1.4 %shard_map.154 = f32[256,256]{1,0:T(8,128)} custom-call(s32[4]{0:T(128)S(1)} %copy-done.10, bf16[256,256]{1,0:T(8,128)(2,1)S(1)} %shard_map.153.refs_0_, bf16[256,256]{1,0:T(8,128)(2,1)S(1)} %collective-permute-done.17.refs_1_, bf16[256,256]{1,0:T(8,128)(2,1)S(1)} %collective-permute-done.18.refs_2_, bf16[256,256]{1,0:T(8,128)(2,1)S(1)} %collective-permute-done.19.refs_3_), custom_call_target="tpu_custom_call" | custom-call | bytes 800000 | tf_op jit(solution)/shard_map/pallas_call | solution.py:361
  132.0 2.5 %shard_map.155 = (f32[4,256,256]{2,1,0:T(8,128)}, f32[4,256,256]{2,1,0:T(8,128)}, f32[4,256,256]{2,1,0:T(8,128)}, f32[1,1024]{1,0:T(1,128)}, f32[6,2,2,1024]{3,2,1,0:T(2,128)}) custom-call(s32[4]{0:T(128)S(1)} %copy-done.10, bf16[4,256,256]{2,1,0:T(8,128)(2,1)S(1)} %copy-done, bf16[4,256,256]{2,1,0:T(8,128)(2,1)S(1)} %copy-done.1, f32[1,1024]{1,0:T(1,128)S(1)} %bitcast.20, ...), custom_call_target="tpu_custom_call" | custom-call | bytes 5000000 | tf_op jit(solution)/shard_map/pallas_call | solution.py:361
  (34 shorter events, 0.2 us)
Async XLA Ops:
  4.1 52.3 %all-to-all-start = ((bf16[64,48,256]{2,1,0:T(8,128)(2,1)}), bf16[64,48,256]{2,1,0:T(8,128)(2,1)}, u32[]{:S(2)}, u32[]{:S(2)}) async-start(bf16[64,48,256]{2,1,0:T(8,128)(2,1)} %bitcast.21), calls=%async_computation | async-start | bytes 3145728 | tf_op jit(solution)/shard_map/all_to_all | solution.py:418
  64.6 6.7 %copy-start.11 = (bf16[4,25,8,128]{3,2,1,0:T(8,128)(2,1)S(1)}, bf16[4,25,8,128]{3,2,1,0:T(8,128)(2,1)}, u32[]{:S(2)}) copy-start(bf16[4,25,8,128]{3,2,1,0:T(8,128)(2,1)} %get-tuple-element.48) | copy-start | bytes 614404
  64.6 8.3 %copy-start.8 = (f32[4,25,8,128]{3,2,1,0:T(8,128)S(1)}, f32[4,25,8,128]{3,2,1,0:T(8,128)}, u32[]{:S(2)}) copy-start(f32[4,25,8,128]{3,2,1,0:T(8,128)} %get-tuple-element.47.keep_ref) | copy-start | bytes 1228804
  64.6 8.3 %copy-start.10 = (s32[4]{0:T(128)S(1)}, s32[4]{0:T(128)}, u32[]{:S(2)}) copy-start(s32[4]{0:T(128)} %pad_add_fusion.place_ref) | copy-start | bytes 52
  64.7 42.7 %all-to-all-start.1 = ((bf16[64,32,256]{2,1,0:T(8,128)(2,1)}), bf16[64,32,256]{2,1,0:T(8,128)(2,1)S(1)}, u32[]{:S(2)}, u32[]{:S(2)}) async-start(bf16[64,32,256]{2,1,0:T(8,128)(2,1)} %get-tuple-element.53), calls=%async_computation.1 | async-start | bytes 2097152 | tf_op jit(solution)/shard_map/all_to_all | solution.py:458
  71.3 1.6 %collective-permute-start = (bf16[4,25,8,128]{3,2,1,0:T(8,128)(2,1)S(1)}, bf16[4,25,8,128]{3,2,1,0:T(8,128)(2,1)S(1)}, u32[]{:S(2)}, u32[]{:S(2)}) collective-permute-start(bf16[4,25,8,128]{3,2,1,0:T(8,128)(2,1)S(1)} %copy-done.11), channel_id=1, source_target_pairs={{0,1},{1,0},{2,3},{3,2},{4,5},{5,4},{6,7},{7,6},{8,9},{9,8},{10,11... | collective-permute-start | bytes 614408 | tf_op jit(solution)/shard_map/ppermute | solution.py:390
  72.9 43.4 %copy-start.7 = (bf16[256,256]{1,0:T(8,128)(2,1)S(1)}, bf16[256,256]{1,0:T(8,128)(2,1)}, u32[]{:S(2)}) copy-start(bf16[256,256]{1,0:T(8,128)(2,1)} %local_ref.1) | copy-start | bytes 393220
  72.9 43.4 %copy-start.9 = (f32[1024]{0:T(1024)S(1)}, f32[1024]{0:T(1024)}, u32[]{:S(2)}) copy-start(f32[1024]{0:T(1024)} %param.10) | copy-start | bytes 12292
  73.5 42.8 %copy-start = (bf16[4,256,256]{2,1,0:T(8,128)(2,1)S(1)}, bf16[4,256,256]{2,1,0:T(8,128)(2,1)}, u32[]{:S(2)}) copy-start(bf16[4,256,256]{2,1,0:T(8,128)(2,1)} %wu_ref.5) | copy-start | bytes 1572868
  73.5 42.8 %copy-start.1 = (bf16[4,256,256]{2,1,0:T(8,128)(2,1)S(1)}, bf16[4,256,256]{2,1,0:T(8,128)(2,1)}, u32[]{:S(2)}) copy-start(bf16[4,256,256]{2,1,0:T(8,128)(2,1)} %wv_ref.5) | copy-start | bytes 1572868
  73.5 42.8 %copy-start.2 = (bf16[1,256,1024]{2,1,0:T(8,128)(2,1)S(1)}, bf16[1,256,1024]{2,1,0:T(8,128)(2,1)}, u32[]{:S(2)}) copy-start(bf16[1,256,1024]{2,1,0:T(8,128)(2,1)} %param.8) | copy-start | bytes 1572868
  73.6 42.8 %copy-start.3 = (bf16[4,256,256]{2,1,0:T(8,128)(2,1)S(1)}, bf16[4,256,256]{2,1,0:T(8,128)(2,1)}, u32[]{:S(2)}) copy-start(bf16[4,256,256]{2,1,0:T(8,128)(2,1)} %wo_ref.3) | copy-start | bytes 1572868
  73.6 5.1 %collective-permute-start.1 = (bf16[25,8,128]{2,1,0:T(8,128)(2,1)S(1)}, bf16[25,8,128]{2,1,0:T(8,128)(2,1)S(1)}, u32[]{:S(2)}, u32[]{:S(2)}) collective-permute-start(bf16[25,8,128]{2,1,0:T(8,128)(2,1)S(1)} %get-tuple-element.50), channel_id=1, source_target_pairs={{0,2},{2,4},{4,6},{6,0},{1,3},{3,5},{5,7},{7,1},{8,10},{10,12},{12... | collective-permute-start | bytes 153608 | tf_op jit(solution)/shard_map/ppermute | solution.py:384
  75.0 6.6 %collective-permute-start.2 = (bf16[25,8,128]{2,1,0:T(8,128)(2,1)S(1)}, bf16[25,8,128]{2,1,0:T(8,128)(2,1)S(1)}, u32[]{:S(2)}, u32[]{:S(2)}) collective-permute-start(bf16[25,8,128]{2,1,0:T(8,128)(2,1)S(1)} %get-tuple-element.51), channel_id=1, source_target_pairs={{0,4},{2,6},{4,0},{6,2},{1,5},{3,7},{5,1},{7,3},{8,12},{10,14},{12... | collective-permute-start | bytes 153608 | tf_op jit(solution)/shard_map/ppermute | solution.py:384
  77.3 4.2 %collective-permute-start.3 = (bf16[25,8,128]{2,1,0:T(8,128)(2,1)S(1)}, bf16[25,8,128]{2,1,0:T(8,128)(2,1)S(1)}, u32[]{:S(2)}, u32[]{:S(2)}) collective-permute-start(bf16[25,8,128]{2,1,0:T(8,128)(2,1)S(1)} %get-tuple-element.52), channel_id=1, source_target_pairs={{0,6},{2,0},{4,2},{6,4},{1,7},{3,1},{5,3},{7,5},{8,14},{10,8},{12,... | collective-permute-start | bytes 153608 | tf_op jit(solution)/shard_map/ppermute | solution.py:384
  81.6 3.3 %collective-permute-start.4 = (bf16[25,8,128]{2,1,0:T(8,128)(2,1)S(1)}, bf16[25,8,128]{2,1,0:T(8,128)(2,1)S(1)}, u32[]{:S(2)}, u32[]{:S(2)}) collective-permute-start(bf16[25,8,128]{2,1,0:T(8,128)(2,1)S(1)} %shard_map.147.a_ref), channel_id=1, source_target_pairs={{0,64},{64,0},{128,192},{192,128},{1,65},{65,1},{129,193},{193,129... | collective-permute-start | bytes 153608 | tf_op jit(solution)/shard_map/ppermute | solution.py:390
  85.0 4.8 %collective-permute-start.5 = (bf16[25,8,128]{2,1,0:T(8,128)(2,1)S(1)}, bf16[25,8,128]{2,1,0:T(8,128)(2,1)S(1)}, u32[]{:S(2)}, u32[]{:S(2)}) collective-permute-start(bf16[25,8,128]{2,1,0:T(8,128)(2,1)S(1)} %shard_map.148.a_ref), channel_id=1, source_target_pairs={{0,128},{64,192},{128,0},{192,64},{1,129},{65,193},{129,1},{193,65... | collective-permute-start | bytes 153608 | tf_op jit(solution)/shard_map/ppermute | solution.py:390
  89.9 7.0 %collective-permute-start.6 = (bf16[25,8,128]{2,1,0:T(8,128)(2,1)S(1)}, bf16[25,8,128]{2,1,0:T(8,128)(2,1)S(1)}, u32[]{:S(2)}, u32[]{:S(2)}) collective-permute-start(bf16[25,8,128]{2,1,0:T(8,128)(2,1)S(1)} %shard_map.149.a_ref), channel_id=1, source_target_pairs={{0,8},{8,0},{16,24},{24,16},{32,40},{40,32},{48,56},{56,48},{1,9},... | collective-permute-start | bytes 153608 | tf_op jit(solution)/shard_map/ppermute | solution.py:390
  96.9 6.7 %collective-permute-start.9 = (bf16[25,8,128]{2,1,0:T(8,128)(2,1)S(1)}, bf16[25,8,128]{2,1,0:T(8,128)(2,1)S(1)}, u32[]{:S(2)}, u32[]{:S(2)}) collective-permute-start(bf16[25,8,128]{2,1,0:T(8,128)(2,1)S(1)} %shard_map.150.refs_0_), channel_id=1, source_target_pairs={{0,48},{8,56},{16,0},{24,8},{32,16},{40,24},{48,32},{56,40},{1,49}... | collective-permute-start | bytes 153608 | tf_op jit(solution)/shard_map/ppermute | solution.py:384
  98.8 6.9 %collective-permute-start.8 = (bf16[25,8,128]{2,1,0:T(8,128)(2,1)S(1)}, bf16[25,8,128]{2,1,0:T(8,128)(2,1)S(1)}, u32[]{:S(2)}, u32[]{:S(2)}) collective-permute-start(bf16[25,8,128]{2,1,0:T(8,128)(2,1)S(1)} %shard_map.150.refs_0_), channel_id=1, source_target_pairs={{0,32},{8,40},{16,48},{24,56},{32,0},{40,8},{48,16},{56,24},{1,33}... | collective-permute-start | bytes 153608 | tf_op jit(solution)/shard_map/ppermute | solution.py:384
  101.3 6.0 %collective-permute-start.7 = (bf16[25,8,128]{2,1,0:T(8,128)(2,1)S(1)}, bf16[25,8,128]{2,1,0:T(8,128)(2,1)S(1)}, u32[]{:S(2)}, u32[]{:S(2)}) collective-permute-start(bf16[25,8,128]{2,1,0:T(8,128)(2,1)S(1)} %shard_map.150.refs_0_), channel_id=1, source_target_pairs={{0,16},{8,24},{16,32},{24,40},{32,48},{40,56},{48,0},{56,8},{1,17}... | collective-permute-start | bytes 153608 | tf_op jit(solution)/shard_map/ppermute | solution.py:384
  107.9 12.8 %collective-permute-start.12 = (bf16[4,25,8,128]{3,2,1,0:T(8,128)(2,1)S(1)}, bf16[4,25,8,128]{3,2,1,0:T(8,128)(2,1)S(1)}, u32[]{:S(2)}, u32[]{:S(2)}) collective-permute-start(bf16[4,25,8,128]{3,2,1,0:T(8,128)(2,1)S(1)} %shard_map.151.refs_0_), channel_id=1, source_target_pairs={{0,6},{2,0},{4,2},{6,4},{1,7},{3,1},{5,3},{7,5},{8,14},{10,8},{12,... | collective-permute-start | bytes 614408 | tf_op jit(solution)/shard_map/ppermute | solution.py:384
  110.4 14.0 %collective-permute-start.11 = (bf16[4,25,8,128]{3,2,1,0:T(8,128)(2,1)S(1)}, bf16[4,25,8,128]{3,2,1,0:T(8,128)(2,1)S(1)}, u32[]{:S(2)}, u32[]{:S(2)}) collective-permute-start(bf16[4,25,8,128]{3,2,1,0:T(8,128)(2,1)S(1)} %shard_map.151.refs_0_), channel_id=1, source_target_pairs={{0,4},{2,6},{4,0},{6,2},{1,5},{3,7},{5,1},{7,3},{8,12},{10,14},{12... | collective-permute-start | bytes 614408 | tf_op jit(solution)/shard_map/ppermute | solution.py:384
  111.8 12.6 %collective-permute-start.10 = (bf16[4,25,8,128]{3,2,1,0:T(8,128)(2,1)S(1)}, bf16[4,25,8,128]{3,2,1,0:T(8,128)(2,1)S(1)}, u32[]{:S(2)}, u32[]{:S(2)}) collective-permute-start(bf16[4,25,8,128]{3,2,1,0:T(8,128)(2,1)S(1)} %shard_map.151.refs_0_), channel_id=1, source_target_pairs={{0,2},{2,4},{4,6},{6,0},{1,3},{3,5},{5,7},{7,1},{8,10},{10,12},{12... | collective-permute-start | bytes 614408 | tf_op jit(solution)/shard_map/ppermute | solution.py:384
  111.8 1.0 copy-start.6
  113.2 11.7 %collective-permute-start.19 = (bf16[256,256]{1,0:T(8,128)(2,1)S(1)}, bf16[256,256]{1,0:T(8,128)(2,1)S(1)}, u32[]{:S(2)}, u32[]{:S(2)}) collective-permute-start(bf16[256,256]{1,0:T(8,128)(2,1)S(1)} %shard_map.153.refs_0_), channel_id=1, source_target_pairs={{0,192},{64,0},{128,64},{192,128},{1,193},{65,1},{129,65},{193,129... | collective-permute-start | bytes 393224 | tf_op jit(solution)/shard_map/ppermute | solution.py:384
  115.8 9.3 %collective-permute-start.18 = (bf16[256,256]{1,0:T(8,128)(2,1)S(1)}, bf16[256,256]{1,0:T(8,128)(2,1)S(1)}, u32[]{:S(2)}, u32[]{:S(2)}) collective-permute-start(bf16[256,256]{1,0:T(8,128)(2,1)S(1)} %shard_map.153.refs_0_), channel_id=1, source_target_pairs={{0,128},{64,192},{128,0},{192,64},{1,129},{65,193},{129,1},{193,65... | collective-permute-start | bytes 393224 | tf_op jit(solution)/shard_map/ppermute | solution.py:384
  116.3 1.2 copy-start.4
  117.5 1.2 copy-start.5
  120.7 11.3 %collective-permute-start.13 = (bf16[4,25,8,128]{3,2,1,0:T(8,128)(2,1)S(1)}, bf16[4,25,8,128]{3,2,1,0:T(8,128)(2,1)S(1)}, u32[]{:S(2)}, u32[]{:S(2)}) collective-permute-start(bf16[4,25,8,128]{3,2,1,0:T(8,128)(2,1)S(1)} %shard_map.151.refs_0_), channel_id=1, source_target_pairs={{0,1},{1,0},{2,3},{3,2},{4,5},{5,4},{6,7},{7,6},{8,9},{9,8},{10,11... | collective-permute-start | bytes 614408 | tf_op jit(solution)/shard_map/ppermute | solution.py:390
  124.4 7.6 %collective-permute-start.14 = (bf16[4,25,8,128]{3,2,1,0:T(8,128)(2,1)S(1)}, bf16[4,25,8,128]{3,2,1,0:T(8,128)(2,1)S(1)}, u32[]{:S(2)}, u32[]{:S(2)}) collective-permute-start(bf16[4,25,8,128]{3,2,1,0:T(8,128)(2,1)S(1)} %collective-permute-done.10.refs_1_), channel_id=1, source_target_pairs={{0,1},{1,0},{2,3},{3,2},{4,5},{5,4},{6,7},{7,6},{8,9},{9,8},{10,11... | collective-permute-start | bytes 614408 | tf_op jit(solution)/shard_map/ppermute | solution.py:390
  124.5 7.5 %collective-permute-start.15 = (bf16[4,25,8,128]{3,2,1,0:T(8,128)(2,1)S(1)}, bf16[4,25,8,128]{3,2,1,0:T(8,128)(2,1)S(1)}, u32[]{:S(2)}, u32[]{:S(2)}) collective-permute-start(bf16[4,25,8,128]{3,2,1,0:T(8,128)(2,1)S(1)} %collective-permute-done.11.refs_2_), channel_id=1, source_target_pairs={{0,1},{1,0},{2,3},{3,2},{4,5},{5,4},{6,7},{7,6},{8,9},{9,8},{10,11... | collective-permute-start | bytes 614408 | tf_op jit(solution)/shard_map/ppermute | solution.py:390
  124.9 7.1 %collective-permute-start.16 = (bf16[4,25,8,128]{3,2,1,0:T(8,128)(2,1)S(1)}, bf16[4,25,8,128]{3,2,1,0:T(8,128)(2,1)S(1)}, u32[]{:S(2)}, u32[]{:S(2)}) collective-permute-start(bf16[4,25,8,128]{3,2,1,0:T(8,128)(2,1)S(1)} %collective-permute-done.12.refs_3_), channel_id=1, source_target_pairs={{0,1},{1,0},{2,3},{3,2},{4,5},{5,4},{6,7},{7,6},{8,9},{9,8},{10,11... | collective-permute-start | bytes 614408 | tf_op jit(solution)/shard_map/ppermute | solution.py:390
  125.0 5.6 %collective-permute-start.17 = (bf16[256,256]{1,0:T(8,128)(2,1)S(1)}, bf16[256,256]{1,0:T(8,128)(2,1)S(1)}, u32[]{:S(2)}, u32[]{:S(2)}) collective-permute-start(bf16[256,256]{1,0:T(8,128)(2,1)S(1)} %shard_map.153.refs_0_), channel_id=1, source_target_pairs={{0,64},{64,128},{128,192},{192,0},{1,65},{65,129},{129,193},{193,1... | collective-permute-start | bytes 393224 | tf_op jit(solution)/shard_map/ppermute | solution.py:384

commit v9 on v8

--- a/solution.py
+++ b/solution.py
@@ -264,16 +264,6 @@
     out_ref[...] = (a_ref[...].astype(F32) + b_ref[...].astype(F32)).astype(out_ref.dtype)
 
 
-def ordered_sum_kernel(place_ref, *refs):
-    *parts, out_ref, held = refs
-    for k, ref in enumerate(parts):
-        held[(place_ref[3] + 4 - k) & 3] = ref[...]
-    total = held[0].astype(F32)
-    for at in range(1, 4):
-        total = total + held[at].astype(F32)
-    out_ref[...] = total
-
-
 def gather_kernel(place_ref, *refs):
     *parts, out_ref = refs
     for k, ref in enumerate(parts):
@@ -315,26 +305,33 @@
 
 def place_kernel(place_ref, wu_ref, wv_ref, gain_ref, *refs):
     own, other = refs[:4], refs[4:8]
-    gu_ref, gv_ref, go_ref, gain_out, bfly_ref = refs[8:]
-    for k in range(4):
-        d = (place_ref[0] + 4 - k) & 3
-        rows = pl.ds(pl.multiple_of(d * 64, 64), 64)
-        for parts, half in ((own, place_ref[2]), (other, 1 - place_ref[2])):
+    *grads_hbm, gain_out, bfly_ref, gu_ref, gv_ref, go_ref, sems = refs[8:]
+    outs = [
+        pltpu.make_async_copy(src, dst, sems.at[at])
+        for at, (src, dst) in enumerate(zip((gu_ref, gv_ref, go_ref), grads_hbm))
+    ]
+    pieces = [
+        (parts[k], (place_ref[0] + 4 - k) & 3, half)
+        for k in range(4)
+        for parts, half in ((own, place_ref[2]), (other, 1 - place_ref[2]))
+    ]
+    for w, out in enumerate((gu_ref, gv_ref, go_ref)):
+        for part, d, half in pieces:
+            rows = pl.ds(pl.multiple_of(d * 64, 64), 64)
             cut = pl.ds(pl.multiple_of(half * 128, 128), 128)
-            for w, out in enumerate((gu_ref, gv_ref, go_ref)):
-                out[:, rows, cut] = (
-                    parts[k][:, w * 8 : (w + 1) * 8].astype(F32).reshape(GROUPS, 64, 128)
-                )
-
-            @pl.when(d < 3)
-            def _():
-                for g in range(GROUPS):
-                    wide = pl.ds(pl.multiple_of(g * BLK + half * 128, 128), 128)
-                    tile = parts[k][g, 24].astype(F32)
-                    for s in range(8):
-                        bfly_ref[2 * d + s // 4, s // 2 % 2, s % 2 : s % 2 + 1, wide] = (
-                            tile[s : s + 1]
-                        )
+            out[:, rows, cut] = (
+                part[:, w * 8 : (w + 1) * 8].astype(F32).reshape(GROUPS, 64, 128)
+            )
+        outs[w].start()
+    for part, d, half in pieces:
+
+        @pl.when(d < 3)
+        def _(part=part, d=d, half=half):
+            for g in range(GROUPS):
+                wide = pl.ds(pl.multiple_of(g * BLK + half * 128, 128), 128)
+                tile = part[g, 24].astype(F32)
+                for s in range(8):
+                    bfly_ref[2 * d + s // 4, s // 2 % 2, s % 2 : s % 2 + 1, wide] = tile[s : s + 1]
 
     ones = jnp.ones((8, BLK), F32)
     for g in range(GROUPS):
@@ -344,6 +341,8 @@
             precision=lax.Precision.HIGHEST, preferred_element_type=F32,
         )
         gain_out[:, lanes(g)] = sums[:1] / gain_ref[:, lanes(g)]
+    for copy in outs:
+        copy.wait()
 
 
 def call(kernel, outs, scratch=(), flops=0, moved=0, vmem=24, smem=(), hbm=(), hbm_out=(), free=()):
@@ -396,7 +395,7 @@
     gain2 = gain.reshape(1, -1)
     wide = (BLK, GROUPS * BLK)
     place = jnp.stack(
-        [lax.axis_index(a) for a in ("y", "z", "c", "dp")]
+        [lax.axis_index(a) for a in ("y", "z", "c")]
     ).astype(jnp.int32)
 
     send = call(
@@ -467,25 +466,21 @@
         )[0]
     got_z = rotated(slice_, "z", 2)
 
-    recv2, got_z = lax.optimization_barrier((recv2, got_z))
+    recv2, slice_ = lax.optimization_barrier((recv2, slice_))
     part = call(local_kernel, [((BLK, BLK), BF)], flops=1.3e8, moved=1.2e6)(recv2, u)[0]
-    parts = rotated(part, "dp")
+    got_z, part = lax.optimization_barrier((got_z, part))
+    pair = call(pair_sum_kernel, [((BLK, BLK), BF)], moved=4e5)(part, swapped(part, "dp", 1))[0]
+    other_pair = swapped(pair, "dp", 2)
     mine_y = call(gather_kernel, [((4,) + quarter, BF)], moved=4e5, smem=(0,))(
         place, slice_, *got_z
     )[0]
     got_y = rotated(mine_y, "y")
-    grad_local = call(
-        ordered_sum_kernel,
-        [((BLK, BLK), F32)],
-        scratch=[pltpu.VMEM((4, BLK, BLK), BF)],
-        moved=8e5,
-        smem=(0,),
-    )(place, part, *parts)[0]
+    grad_local = call(pair_sum_kernel, [((BLK, BLK), F32)], moved=5e5)(pair, other_pair)[0]
     mixed, dx = call(
         last_kernel, [(wide, BF), (wide, BF)], scratch=[pltpu.VMEM(wide, F32)],
         flops=6e8, moved=8e6,
     )(recv2, x, gain2, act, dgd, w_u, w_v, w_o, local_factor)
-    got_y, mixed, dx = lax.optimization_barrier((got_y, mixed, dx))
+    got_y, mixed, dx, pair = lax.optimization_barrier((got_y, mixed, dx, pair))
     halves = [mine_y] + got_y
     others = [swapped(half) for half in halves]
     others, grad_local = lax.optimization_barrier((others, grad_local))
@@ -494,8 +489,10 @@
     gu, gv, go, grad_gain, grad_bfly = call(
         place_kernel,
         [(shape, F32)] * 3 + [(gain2.shape, F32), (butterfly.shape, F32)],
+        scratch=[pltpu.VMEM(shape, F32)] * 3 + [pltpu.SemaphoreType.DMA((3,))],
         moved=5e6,
         smem=(0,),
+        hbm_out=(0, 1, 2),
     )(place, w_u, w_v, gain2, *halves, *others)
 
     return (

time: 135 us -> 135 us (level)
  starting transfers between devices: 49.7 us -> 51.8 us
  waiting for transfers between devices: 57 us -> 55.1 us
    ppermute x8 -> x10, starting transfers between devices: 10.4 us -> 16.2 us  [swapped(): lax.ppermute(value, axis, [(s, s ^ bit) for s in range(lax.axis_size(axis...]
    ppermute x12 -> x9, waiting for transfers between devices: 11.8 us -> 6.06 us  [rotated(): lax.ppermute(value, axis, [(s, (s + k * step) % n) for s in range(n)])]
    ppermute x8 -> x10, waiting for transfers between devices: 10.7 us -> 14.6 us  [swapped(): lax.ppermute(value, axis, [(s, s ^ bit) for s in range(lax.axis_size(axis...]
    ppermute x12 -> x9, starting transfers between devices: 19.3 us -> 15.6 us  [rotated(): lax.ppermute(value, axis, [(s, (s + k * step) % n) for s in range(n)])]
    pallas_call x13 -> x14, Pallas kernels: 22.9 us -> 22.8 us  [run(): pl.pallas_call(kernel, out_shape=shapes, in_specs=specs, out_specs=[pl.Bl...]
  transfers between devices with their start and end apart: 22 -> 21, of which waited for: 10 -> 11; matrix products, arithmetic and copies ran while one was open for 0% -> 0% of each run, Pallas kernels for 6% -> 6%
where the time goes in v9:
time: 135 us
  waiting for transfers between devices  55.1 us (41%)
  starting transfers between devices  51.8 us (38%)
  Pallas kernels  22.8 us (17%)
  local copies, waits for them, and re-layouts  3.54 us (3%)
    all_to_all x1, waiting for transfers between devices, per_device(): recv = lax.all_to_all(send.reshape(BLOCKS, 3 * PL, BLK), SEQ, 0, 0)  34.4 us
    pallas_call x14, Pallas kernels, run(): pl.pallas_call(kernel, out_shape=shapes, in_specs=specs, out_specs=[pl.Bl...  22.8 us
    ppermute x10, starting transfers between devices, swapped(): lax.ppermute(value, axis, [(s, s ^ bit) for s in range(lax.axis_size(axis...  16.2 us
    ppermute x9, starting transfers between devices, rotated(): lax.ppermute(value, axis, [(s, (s + k * step) % n) for s in range(n)])  15.6 us
    ppermute x10, waiting for transfers between devices, swapped(): lax.ppermute(value, axis, [(s, s ^ bit) for s in range(lax.axis_size(axis...  14.6 us
    all_to_all x1, starting transfers between devices, per_device(): recv = lax.all_to_all(send.reshape(BLOCKS, 3 * PL, BLK), SEQ, 0, 0)  13.3 us
    all_to_all x1, starting transfers between devices, per_device(): recv2 = lax.all_to_all(back, SEQ, 0, 0).reshape(GROUPS, 16, 2 * PL, BLK)  6.61 us
    ppermute x9, waiting for transfers between devices, rotated(): lax.ppermute(value, axis, [(s, (s + k * step) % n) for s in range(n)])  6.06 us
  transfers between devices with their start and end apart: 21, of which 11 were waited for; matrix products, arithmetic and copies ran while one was open for 0% of the time, Pallas kernels for 6%

profile of v9, /device:TPU:1, one launch (start us, length us, event | category | flops | bytes accessed | tf_op | source)
XLA Modules:
  0.0 134.9 jit_solution(10781611281423964677)
XLA Ops:
  0.6 3.4 %shard_map.143 = bf16[4,16,48,256]{3,2,1,0:T(8,128)(2,1)} custom-call(bf16[256,1024]{1,0:T(8,128)(2,1)} %bitcast.13, bf16[256,1024]{1,0:T(8,128)(2,1)} %bitcast.21, f32[1,1024]{1,0:T(1,128)} %bitcast.16, bf16[256,256]{1,0:T(8,128)(2,1)} %local_ref.1), custom_call_target="tpu_custom_call" | custom-call | flops 140000000 | bytes 4000000 | tf_op jit(solution)/shard_map/pallas_call | solution.py:360
  4.1 13.3 %all-to-all-start = ((bf16[64,48,256]{2,1,0:T(8,128)(2,1)}), bf16[64,48,256]{2,1,0:T(8,128)(2,1)}, u32[]{:S(2)}, u32[]{:S(2)}) async-start(bf16[64,48,256]{2,1,0:T(8,128)(2,1)} %bitcast.20), calls=%async_computation | async-start | bytes 3145728 | tf_op jit(solution)/shard_map/all_to_all | solution.py:417
  17.4 3.8 %shard_map.144 = (bf16[256,1024]{1,0:T(8,128)(2,1)}, f32[256,1024]{1,0:T(8,128)}, f32[256,1024]{1,0:T(8,128)}) custom-call(bf16[256,1024]{1,0:T(8,128)(2,1)} %bitcast.14, bf16[256,1024]{1,0:T(8,128)(2,1)} %bitcast.22, f32[1,1024]{1,0:T(1,128)} %bitcast.17, bf16[4,256,256]{2,1,0:T(8,128)(2,1)} %wu_ref.5, bf16[4,256,256]{2,1,0:T(8,128)(2,1)} %wv_ref.5, ...), custom_call_target="tpu_custom_call" | custom-call | flops 400000000 | bytes 8000000 | tf_op jit(solution)/shard_map/pallas_call | solution.py:360
  21.3 0.6 pad_add_fusion.place_ref
  21.9 34.4 %all-to-all-done.recv_hbm = bf16[64,48,256]{2,1,0:T(8,128)(2,1)} async-done(((bf16[64,48,256]{2,1,0:T(8,128)(2,1)}), bf16[64,48,256]{2,1,0:T(8,128)(2,1)}, u32[]{:S(2)}, u32[]{:S(2)}) %all-to-all-start) | async-done | bytes 1572896 | tf_op jit(solution)/shard_map/all_to_all | solution.py:417
  56.4 8.3 %shard_map.145 = (bf16[64,32,256]{2,1,0:T(8,128)(2,1)}, f32[4,25,8,128]{3,2,1,0:T(8,128)}, bf16[4,25,8,128]{3,2,1,0:T(8,128)(2,1)}) custom-call(s32[3]{0:T(128)} %pad_add_fusion.place_ref, bf16[64,48,256]{2,1,0:T(8,128)(2,1)} %all-to-all-done.recv_hbm, f32[6,2,2,1024]{3,2,1,0:T(2,128)} %coef_hbm.1, bf16[4,256,256]{2,1,0:T(8,128)(2,1)} %wu_ref.5, ...), custom_call_target="tpu_custom_call" | custom-call | flops 800000000 | bytes 4000000 | tf_op jit(solution)/shard_map/pallas_call | solution.py:360
  64.6 0.0 copy-start.11
  64.6 0.0 copy-start.8
  64.7 6.6 %all-to-all-start.1 = ((bf16[64,32,256]{2,1,0:T(8,128)(2,1)}), bf16[64,32,256]{2,1,0:T(8,128)(2,1)S(1)}, u32[]{:S(2)}, u32[]{:S(2)}) async-start(bf16[64,32,256]{2,1,0:T(8,128)(2,1)} %get-tuple-element.49), calls=%async_computation.1 | async-start | bytes 2097152 | tf_op jit(solution)/shard_map/all_to_all | solution.py:457
  71.3 0.5 collective-permute-start
  71.8 1.1 collective-permute-done.got_ref
  72.9 0.6 shard_map.146
  73.5 0.0 copy-start.2
  73.6 0.0 copy-start.3
  73.6 1.4 %collective-permute-start.1 = (bf16[25,8,128]{2,1,0:T(8,128)(2,1)S(1)}, bf16[25,8,128]{2,1,0:T(8,128)(2,1)S(1)}, u32[]{:S(2)}, u32[]{:S(2)}) collective-permute-start(bf16[25,8,128]{2,1,0:T(8,128)(2,1)S(1)} %get-tuple-element.53), channel_id=1, source_target_pairs={{0,2},{2,4},{4,6},{6,0},{1,3},{3,5},{5,7},{7,1},{8,10},{10,12},{12... | collective-permute-start | bytes 153608 | tf_op jit(solution)/shard_map/ppermute | solution.py:383
  75.0 2.4 %collective-permute-start.2 = (bf16[25,8,128]{2,1,0:T(8,128)(2,1)S(1)}, bf16[25,8,128]{2,1,0:T(8,128)(2,1)S(1)}, u32[]{:S(2)}, u32[]{:S(2)}) collective-permute-start(bf16[25,8,128]{2,1,0:T(8,128)(2,1)S(1)} %get-tuple-element.54), channel_id=1, source_target_pairs={{0,4},{2,6},{4,0},{6,2},{1,5},{3,7},{5,1},{7,3},{8,12},{10,14},{12... | collective-permute-start | bytes 153608 | tf_op jit(solution)/shard_map/ppermute | solution.py:383
  77.3 1.2 collective-permute-start.3
  78.5 0.2 collective-permute-done.1.refs_0_
  78.7 2.9 %collective-permute-done.2.refs_1_ = bf16[25,8,128]{2,1,0:T(8,128)(2,1)S(1)} collective-permute-done((bf16[25,8,128]{2,1,0:T(8,128)(2,1)S(1)}, bf16[25,8,128]{2,1,0:T(8,128)(2,1)S(1)}, u32[]{:S(2)}, u32[]{:S(2)}) %collective-permute-start.2) | collective-permute-done | bytes 51232 | tf_op jit(solution)/shard_map/ppermute | solution.py:383
  81.6 1.3 collective-permute-start.4
  82.9 2.0 %collective-permute-done.4.b_ref = bf16[25,8,128]{2,1,0:T(8,128)(2,1)S(1)} collective-permute-done((bf16[25,8,128]{2,1,0:T(8,128)(2,1)S(1)}, bf16[25,8,128]{2,1,0:T(8,128)(2,1)S(1)}, u32[]{:S(2)}, u32[]{:S(2)}) %collective-permute-start.4) | collective-permute-done | bytes 51232 | tf_op jit(solution)/shard_map/ppermute | solution.py:389
  85.0 2.8 %collective-permute-start.5 = (bf16[25,8,128]{2,1,0:T(8,128)(2,1)S(1)}, bf16[25,8,128]{2,1,0:T(8,128)(2,1)S(1)}, u32[]{:S(2)}, u32[]{:S(2)}) collective-permute-start(bf16[25,8,128]{2,1,0:T(8,128)(2,1)S(1)} %shard_map.148.a_ref), channel_id=1, source_target_pairs={{0,128},{64,192},{128,0},{192,64},{1,129},{65,193},{129,1},{193,65... | collective-permute-start | bytes 153608 | tf_op jit(solution)/shard_map/ppermute | solution.py:389
  87.8 2.0 %collective-permute-done.5.b_ref = bf16[25,8,128]{2,1,0:T(8,128)(2,1)S(1)} collective-permute-done((bf16[25,8,128]{2,1,0:T(8,128)(2,1)S(1)}, bf16[25,8,128]{2,1,0:T(8,128)(2,1)S(1)}, u32[]{:S(2)}, u32[]{:S(2)}) %collective-permute-start.5) | collective-permute-done | bytes 51232 | tf_op jit(solution)/shard_map/ppermute | solution.py:389
  89.9 1.4 %collective-permute-start.6 = (bf16[25,8,128]{2,1,0:T(8,128)(2,1)S(1)}, bf16[25,8,128]{2,1,0:T(8,128)(2,1)S(1)}, u32[]{:S(2)}, u32[]{:S(2)}) collective-permute-start(bf16[25,8,128]{2,1,0:T(8,128)(2,1)S(1)} %shard_map.149.a_ref), channel_id=1, source_target_pairs={{0,8},{8,0},{16,24},{24,16},{32,40},{40,32},{48,56},{56,48},{1,9},... | collective-permute-start | bytes 153608 | tf_op jit(solution)/shard_map/ppermute | solution.py:389
  91.3 5.6 %collective-permute-done.6.b_ref = bf16[25,8,128]{2,1,0:T(8,128)(2,1)S(1)} collective-permute-done((bf16[25,8,128]{2,1,0:T(8,128)(2,1)S(1)}, bf16[25,8,128]{2,1,0:T(8,128)(2,1)S(1)}, u32[]{:S(2)}, u32[]{:S(2)}) %collective-permute-start.6) | collective-permute-done | bytes 51232 | tf_op jit(solution)/shard_map/ppermute | solution.py:389
  96.9 1.9 %collective-permute-start.9 = (bf16[25,8,128]{2,1,0:T(8,128)(2,1)S(1)}, bf16[25,8,128]{2,1,0:T(8,128)(2,1)S(1)}, u32[]{:S(2)}, u32[]{:S(2)}) collective-permute-start(bf16[25,8,128]{2,1,0:T(8,128)(2,1)S(1)} %shard_map.150.refs_0_), channel_id=1, source_target_pairs={{0,48},{8,56},{16,0},{24,8},{32,16},{40,24},{48,32},{56,40},{1,49}... | collective-permute-start | bytes 153608 | tf_op jit(solution)/shard_map/ppermute | solution.py:383
  98.8 2.5 %collective-permute-start.8 = (bf16[25,8,128]{2,1,0:T(8,128)(2,1)S(1)}, bf16[25,8,128]{2,1,0:T(8,128)(2,1)S(1)}, u32[]{:S(2)}, u32[]{:S(2)}) collective-permute-start(bf16[25,8,128]{2,1,0:T(8,128)(2,1)S(1)} %shard_map.150.refs_0_), channel_id=1, source_target_pairs={{0,32},{8,40},{16,48},{24,56},{32,0},{40,8},{48,16},{56,24},{1,33}... | collective-permute-start | bytes 153608 | tf_op jit(solution)/shard_map/ppermute | solution.py:383
  101.3 2.3 %collective-permute-start.7 = (bf16[25,8,128]{2,1,0:T(8,128)(2,1)S(1)}, bf16[25,8,128]{2,1,0:T(8,128)(2,1)S(1)}, u32[]{:S(2)}, u32[]{:S(2)}) collective-permute-start(bf16[25,8,128]{2,1,0:T(8,128)(2,1)S(1)} %shard_map.150.refs_0_), channel_id=1, source_target_pairs={{0,16},{8,24},{16,32},{24,40},{32,48},{40,56},{48,0},{56,8},{1,17}... | collective-permute-start | bytes 153608 | tf_op jit(solution)/shard_map/ppermute | solution.py:383
  103.6 1.0 copy-done.6
  104.6 0.3 shard_map.151.a_ref
  105.0 0.8 collective-permute-done.8.refs_2_
  105.7 1.6 %collective-permute-done.7.refs_1_ = bf16[25,8,128]{2,1,0:T(8,128)(2,1)S(1)} collective-permute-done((bf16[25,8,128]{2,1,0:T(8,128)(2,1)S(1)}, bf16[25,8,128]{2,1,0:T(8,128)(2,1)S(1)}, u32[]{:S(2)}, u32[]{:S(2)}) %collective-permute-start.7) | collective-permute-done | bytes 51232 | tf_op jit(solution)/shard_map/ppermute | solution.py:383
  107.3 0.6 shard_map.152.refs_0_
  107.9 2.5 %collective-permute-start.12 = (bf16[4,25,8,128]{3,2,1,0:T(8,128)(2,1)S(1)}, bf16[4,25,8,128]{3,2,1,0:T(8,128)(2,1)S(1)}, u32[]{:S(2)}, u32[]{:S(2)}) collective-permute-start(bf16[4,25,8,128]{3,2,1,0:T(8,128)(2,1)S(1)} %shard_map.152.refs_0_), channel_id=1, source_target_pairs={{0,6},{2,0},{4,2},{6,4},{1,7},{3,1},{5,3},{7,5},{8,14},{10,8},{12,... | collective-permute-start | bytes 614408 | tf_op jit(solution)/shard_map/ppermute | solution.py:383
  110.4 1.4 %collective-permute-start.11 = (bf16[4,25,8,128]{3,2,1,0:T(8,128)(2,1)S(1)}, bf16[4,25,8,128]{3,2,1,0:T(8,128)(2,1)S(1)}, u32[]{:S(2)}, u32[]{:S(2)}) collective-permute-start(bf16[4,25,8,128]{3,2,1,0:T(8,128)(2,1)S(1)} %shard_map.152.refs_0_), channel_id=1, source_target_pairs={{0,4},{2,6},{4,0},{6,2},{1,5},{3,7},{5,1},{7,3},{8,12},{10,14},{12... | collective-permute-start | bytes 614408 | tf_op jit(solution)/shard_map/ppermute | solution.py:383
  111.8 1.2 collective-permute-start.13
  113.0 3.5 %collective-permute-start.14 = (bf16[4,25,8,128]{3,2,1,0:T(8,128)(2,1)S(1)}, bf16[4,25,8,128]{3,2,1,0:T(8,128)(2,1)S(1)}, u32[]{:S(2)}, u32[]{:S(2)}) collective-permute-start(bf16[4,25,8,128]{3,2,1,0:T(8,128)(2,1)S(1)} %shard_map.152.refs_0_), channel_id=1, source_target_pairs={{0,1},{1,0},{2,3},{3,2},{4,5},{5,4},{6,7},{7,6},{8,9},{9,8},{10,11... | collective-permute-start | bytes 614408 | tf_op jit(solution)/shard_map/ppermute | solution.py:389
  116.6 0.0 copy-start.4
  116.6 1.2 copy-done.4
  117.8 1.2 copy-done.5
  119.0 1.9 %shard_map.153 = (bf16[256,1024]{1,0:T(8,128)(2,1)}, bf16[256,1024]{1,0:T(8,128)(2,1)}) custom-call(bf16[4,16,32,256]{3,2,1,0:T(8,128)(2,1)S(1)} %bitcast.12, bf16[256,1024]{1,0:T(8,128)(2,1)S(1)} %bitcast.15, f32[1,1024]{1,0:T(1,128)S(1)} %bitcast.18, f32[256,1024]{1,0:T(8,128)S(1)} %copy-done.4, f32[256,1024]{1,0:T(8,128)S(1)} %copy-done.5, ...), custom_call_target="tpu_custom_call" | custom-call | flops 600000000 | bytes 8000000 | tf_op jit(solution)/shard_map/pallas_call | solution.py:360
  121.0 0.6 collective-permute-done.10.refs_1_
  121.6 2.2 %collective-permute-start.15 = (bf16[4,25,8,128]{3,2,1,0:T(8,128)(2,1)S(1)}, bf16[4,25,8,128]{3,2,1,0:T(8,128)(2,1)S(1)}, u32[]{:S(2)}, u32[]{:S(2)}) collective-permute-start(bf16[4,25,8,128]{3,2,1,0:T(8,128)(2,1)S(1)} %collective-permute-done.10.refs_1_), channel_id=1, source_target_pairs={{0,1},{1,0},{2,3},{3,2},{4,5},{5,4},{6,7},{7,6},{8,9},{9,8},{10,11... | collective-permute-start | bytes 614408 | tf_op jit(solution)/shard_map/ppermute | solution.py:389
  123.8 0.5 collective-permute-start.17
  124.3 2.7 %collective-permute-start.18 = (bf16[256,256]{1,0:T(8,128)(2,1)S(1)}, bf16[256,256]{1,0:T(8,128)(2,1)S(1)}, u32[]{:S(2)}, u32[]{:S(2)}) collective-permute-start(bf16[256,256]{1,0:T(8,128)(2,1)S(1)} %shard_map.154.a_ref), channel_id=1, source_target_pairs={{0,128},{64,192},{128,0},{192,64},{1,129},{65,193},{129,1},{193,65... | collective-permute-start | bytes 393224 | tf_op jit(solution)/shard_map/ppermute | solution.py:389
  127.1 3.9 %collective-permute-done.18.b_ref = bf16[256,256]{1,0:T(8,128)(2,1)S(1)} collective-permute-done((bf16[256,256]{1,0:T(8,128)(2,1)S(1)}, bf16[256,256]{1,0:T(8,128)(2,1)S(1)}, u32[]{:S(2)}, u32[]{:S(2)}) %collective-permute-start.18) | collective-permute-done | bytes 131104 | tf_op jit(solution)/shard_map/ppermute | solution.py:389
  131.0 0.7 shard_map.155
  131.7 3.1 %shard_map.156 = (f32[4,256,256]{2,1,0:T(8,128)}, f32[4,256,256]{2,1,0:T(8,128)}, f32[4,256,256]{2,1,0:T(8,128)}, f32[1,1024]{1,0:T(1,128)}, f32[6,2,2,1024]{3,2,1,0:T(2,128)}) custom-call(s32[3]{0:T(128)S(1)} %copy-done.10, bf16[4,256,256]{2,1,0:T(8,128)(2,1)S(1)} %copy-done, bf16[4,256,256]{2,1,0:T(8,128)(2,1)S(1)} %copy-done.1, f32[1,1024]{1,0:T(1,128)S(1)} %bitcast.19, ...), custom_call_target="tpu_custom_call" | custom-call | bytes 5000000 | tf_op jit(solution)/shard_map/pallas_call | solution.py:360
  (33 shorter events, 0.2 us)
Async XLA Ops:
  4.1 52.3 %all-to-all-start = ((bf16[64,48,256]{2,1,0:T(8,128)(2,1)}), bf16[64,48,256]{2,1,0:T(8,128)(2,1)}, u32[]{:S(2)}, u32[]{:S(2)}) async-start(bf16[64,48,256]{2,1,0:T(8,128)(2,1)} %bitcast.20), calls=%async_computation | async-start | bytes 3145728 | tf_op jit(solution)/shard_map/all_to_all | solution.py:417
  64.6 6.7 %copy-start.11 = (bf16[4,25,8,128]{3,2,1,0:T(8,128)(2,1)S(1)}, bf16[4,25,8,128]{3,2,1,0:T(8,128)(2,1)}, u32[]{:S(2)}) copy-start(bf16[4,25,8,128]{3,2,1,0:T(8,128)(2,1)} %get-tuple-element.51) | copy-start | bytes 614404
  64.6 8.3 %copy-start.8 = (f32[4,25,8,128]{3,2,1,0:T(8,128)S(1)}, f32[4,25,8,128]{3,2,1,0:T(8,128)}, u32[]{:S(2)}) copy-start(f32[4,25,8,128]{3,2,1,0:T(8,128)} %get-tuple-element.50.keep_ref) | copy-start | bytes 1228804
  64.7 8.3 %copy-start.10 = (s32[3]{0:T(128)S(1)}, s32[3]{0:T(128)}, u32[]{:S(2)}) copy-start(s32[3]{0:T(128)} %pad_add_fusion.place_ref) | copy-start | bytes 40
  64.7 38.9 %all-to-all-start.1 = ((bf16[64,32,256]{2,1,0:T(8,128)(2,1)}), bf16[64,32,256]{2,1,0:T(8,128)(2,1)S(1)}, u32[]{:S(2)}, u32[]{:S(2)}) async-start(bf16[64,32,256]{2,1,0:T(8,128)(2,1)} %get-tuple-element.49), calls=%async_computation.1 | async-start | bytes 2097152 | tf_op jit(solution)/shard_map/all_to_all | solution.py:457
  71.3 1.6 %collective-permute-start = (bf16[4,25,8,128]{3,2,1,0:T(8,128)(2,1)S(1)}, bf16[4,25,8,128]{3,2,1,0:T(8,128)(2,1)S(1)}, u32[]{:S(2)}, u32[]{:S(2)}) collective-permute-start(bf16[4,25,8,128]{3,2,1,0:T(8,128)(2,1)S(1)} %copy-done.11), channel_id=1, source_target_pairs={{0,1},{1,0},{2,3},{3,2},{4,5},{5,4},{6,7},{7,6},{8,9},{9,8},{10,11... | collective-permute-start | bytes 614408 | tf_op jit(solution)/shard_map/ppermute | solution.py:389
  72.9 43.6 %copy-start.7 = (bf16[256,256]{1,0:T(8,128)(2,1)S(1)}, bf16[256,256]{1,0:T(8,128)(2,1)}, u32[]{:S(2)}) copy-start(bf16[256,256]{1,0:T(8,128)(2,1)} %local_ref.1) | copy-start | bytes 393220
  72.9 43.6 %copy-start.9 = (f32[1024]{0:T(1024)S(1)}, f32[1024]{0:T(1024)}, u32[]{:S(2)}) copy-start(f32[1024]{0:T(1024)} %param.10) | copy-start | bytes 12292
  73.5 43.0 %copy-start = (bf16[4,256,256]{2,1,0:T(8,128)(2,1)S(1)}, bf16[4,256,256]{2,1,0:T(8,128)(2,1)}, u32[]{:S(2)}) copy-start(bf16[4,256,256]{2,1,0:T(8,128)(2,1)} %wu_ref.5) | copy-start | bytes 1572868
  73.5 43.0 %copy-start.1 = (bf16[4,256,256]{2,1,0:T(8,128)(2,1)S(1)}, bf16[4,256,256]{2,1,0:T(8,128)(2,1)}, u32[]{:S(2)}) copy-start(bf16[4,256,256]{2,1,0:T(8,128)(2,1)} %wv_ref.5) | copy-start | bytes 1572868
  73.5 43.0 %copy-start.2 = (bf16[1,256,1024]{2,1,0:T(8,128)(2,1)S(1)}, bf16[1,256,1024]{2,1,0:T(8,128)(2,1)}, u32[]{:S(2)}) copy-start(bf16[1,256,1024]{2,1,0:T(8,128)(2,1)} %param.8) | copy-start | bytes 1572868
  73.6 43.0 %copy-start.3 = (bf16[4,256,256]{2,1,0:T(8,128)(2,1)S(1)}, bf16[4,256,256]{2,1,0:T(8,128)(2,1)}, u32[]{:S(2)}) copy-start(bf16[4,256,256]{2,1,0:T(8,128)(2,1)} %wo_ref.3) | copy-start | bytes 1572868
  73.6 5.1 %collective-permute-start.1 = (bf16[25,8,128]{2,1,0:T(8,128)(2,1)S(1)}, bf16[25,8,128]{2,1,0:T(8,128)(2,1)S(1)}, u32[]{:S(2)}, u32[]{:S(2)}) collective-permute-start(bf16[25,8,128]{2,1,0:T(8,128)(2,1)S(1)} %get-tuple-element.53), channel_id=1, source_target_pairs={{0,2},{2,4},{4,6},{6,0},{1,3},{3,5},{5,7},{7,1},{8,10},{10,12},{12... | collective-permute-start | bytes 153608 | tf_op jit(solution)/shard_map/ppermute | solution.py:383
  75.0 6.6 %collective-permute-start.2 = (bf16[25,8,128]{2,1,0:T(8,128)(2,1)S(1)}, bf16[25,8,128]{2,1,0:T(8,128)(2,1)S(1)}, u32[]{:S(2)}, u32[]{:S(2)}) collective-permute-start(bf16[25,8,128]{2,1,0:T(8,128)(2,1)S(1)} %get-tuple-element.54), channel_id=1, source_target_pairs={{0,4},{2,6},{4,0},{6,2},{1,5},{3,7},{5,1},{7,3},{8,12},{10,14},{12... | collective-permute-start | bytes 153608 | tf_op jit(solution)/shard_map/ppermute | solution.py:383
  77.3 4.2 %collective-permute-start.3 = (bf16[25,8,128]{2,1,0:T(8,128)(2,1)S(1)}, bf16[25,8,128]{2,1,0:T(8,128)(2,1)S(1)}, u32[]{:S(2)}, u32[]{:S(2)}) collective-permute-start(bf16[25,8,128]{2,1,0:T(8,128)(2,1)S(1)} %get-tuple-element.55), channel_id=1, source_target_pairs={{0,6},{2,0},{4,2},{6,4},{1,7},{3,1},{5,3},{7,5},{8,14},{10,8},{12,... | collective-permute-start | bytes 153608 | tf_op jit(solution)/shard_map/ppermute | solution.py:383
  81.6 3.3 %collective-permute-start.4 = (bf16[25,8,128]{2,1,0:T(8,128)(2,1)S(1)}, bf16[25,8,128]{2,1,0:T(8,128)(2,1)S(1)}, u32[]{:S(2)}, u32[]{:S(2)}) collective-permute-start(bf16[25,8,128]{2,1,0:T(8,128)(2,1)S(1)} %shard_map.147.a_ref), channel_id=1, source_target_pairs={{0,64},{64,0},{128,192},{192,128},{1,65},{65,1},{129,193},{193,129... | collective-permute-start | bytes 153608 | tf_op jit(solution)/shard_map/ppermute | solution.py:389
  85.0 4.8 %collective-permute-start.5 = (bf16[25,8,128]{2,1,0:T(8,128)(2,1)S(1)}, bf16[25,8,128]{2,1,0:T(8,128)(2,1)S(1)}, u32[]{:S(2)}, u32[]{:S(2)}) collective-permute-start(bf16[25,8,128]{2,1,0:T(8,128)(2,1)S(1)} %shard_map.148.a_ref), channel_id=1, source_target_pairs={{0,128},{64,192},{128,0},{192,64},{1,129},{65,193},{129,1},{193,65... | collective-permute-start | bytes 153608 | tf_op jit(solution)/shard_map/ppermute | solution.py:389
  89.9 7.0 %collective-permute-start.6 = (bf16[25,8,128]{2,1,0:T(8,128)(2,1)S(1)}, bf16[25,8,128]{2,1,0:T(8,128)(2,1)S(1)}, u32[]{:S(2)}, u32[]{:S(2)}) collective-permute-start(bf16[25,8,128]{2,1,0:T(8,128)(2,1)S(1)} %shard_map.149.a_ref), channel_id=1, source_target_pairs={{0,8},{8,0},{16,24},{24,16},{32,40},{40,32},{48,56},{56,48},{1,9},... | collective-permute-start | bytes 153608 | tf_op jit(solution)/shard_map/ppermute | solution.py:389
  96.9 8.1 %collective-permute-start.9 = (bf16[25,8,128]{2,1,0:T(8,128)(2,1)S(1)}, bf16[25,8,128]{2,1,0:T(8,128)(2,1)S(1)}, u32[]{:S(2)}, u32[]{:S(2)}) collective-permute-start(bf16[25,8,128]{2,1,0:T(8,128)(2,1)S(1)} %shard_map.150.refs_0_), channel_id=1, source_target_pairs={{0,48},{8,56},{16,0},{24,8},{32,16},{40,24},{48,32},{56,40},{1,49}... | collective-permute-start | bytes 153608 | tf_op jit(solution)/shard_map/ppermute | solution.py:383
  98.8 6.9 %collective-permute-start.8 = (bf16[25,8,128]{2,1,0:T(8,128)(2,1)S(1)}, bf16[25,8,128]{2,1,0:T(8,128)(2,1)S(1)}, u32[]{:S(2)}, u32[]{:S(2)}) collective-permute-start(bf16[25,8,128]{2,1,0:T(8,128)(2,1)S(1)} %shard_map.150.refs_0_), channel_id=1, source_target_pairs={{0,32},{8,40},{16,48},{24,56},{32,0},{40,8},{48,16},{56,24},{1,33}... | collective-permute-start | bytes 153608 | tf_op jit(solution)/shard_map/ppermute | solution.py:383
  101.3 6.0 %collective-permute-start.7 = (bf16[25,8,128]{2,1,0:T(8,128)(2,1)S(1)}, bf16[25,8,128]{2,1,0:T(8,128)(2,1)S(1)}, u32[]{:S(2)}, u32[]{:S(2)}) collective-permute-start(bf16[25,8,128]{2,1,0:T(8,128)(2,1)S(1)} %shard_map.150.refs_0_), channel_id=1, source_target_pairs={{0,16},{8,24},{16,32},{24,40},{32,48},{40,56},{48,0},{56,8},{1,17}... | collective-permute-start | bytes 153608 | tf_op jit(solution)/shard_map/ppermute | solution.py:383
  103.6 1.0 copy-start.6
  107.9 13.1 %collective-permute-start.12 = (bf16[4,25,8,128]{3,2,1,0:T(8,128)(2,1)S(1)}, bf16[4,25,8,128]{3,2,1,0:T(8,128)(2,1)S(1)}, u32[]{:S(2)}, u32[]{:S(2)}) collective-permute-start(bf16[4,25,8,128]{3,2,1,0:T(8,128)(2,1)S(1)} %shard_map.152.refs_0_), channel_id=1, source_target_pairs={{0,6},{2,0},{4,2},{6,4},{1,7},{3,1},{5,3},{7,5},{8,14},{10,8},{12,... | collective-permute-start | bytes 614408 | tf_op jit(solution)/shard_map/ppermute | solution.py:383
  110.4 10.5 %collective-permute-start.11 = (bf16[4,25,8,128]{3,2,1,0:T(8,128)(2,1)S(1)}, bf16[4,25,8,128]{3,2,1,0:T(8,128)(2,1)S(1)}, u32[]{:S(2)}, u32[]{:S(2)}) collective-permute-start(bf16[4,25,8,128]{3,2,1,0:T(8,128)(2,1)S(1)} %shard_map.152.refs_0_), channel_id=1, source_target_pairs={{0,4},{2,6},{4,0},{6,2},{1,5},{3,7},{5,1},{7,3},{8,12},{10,14},{12... | collective-permute-start | bytes 614408 | tf_op jit(solution)/shard_map/ppermute | solution.py:383
  111.8 9.8 %collective-permute-start.10 = (bf16[4,25,8,128]{3,2,1,0:T(8,128)(2,1)S(1)}, bf16[4,25,8,128]{3,2,1,0:T(8,128)(2,1)S(1)}, u32[]{:S(2)}, u32[]{:S(2)}) collective-permute-start(bf16[4,25,8,128]{3,2,1,0:T(8,128)(2,1)S(1)} %shard_map.152.refs_0_), channel_id=1, source_target_pairs={{0,2},{2,4},{4,6},{6,0},{1,3},{3,5},{5,7},{7,1},{8,10},{10,12},{12... | collective-permute-start | bytes 614408 | tf_op jit(solution)/shard_map/ppermute | solution.py:383
  111.8 9.1 %collective-permute-start.13 = (bf16[256,256]{1,0:T(8,128)(2,1)S(1)}, bf16[256,256]{1,0:T(8,128)(2,1)S(1)}, u32[]{:S(2)}, u32[]{:S(2)}) collective-permute-start(bf16[256,256]{1,0:T(8,128)(2,1)S(1)} %shard_map.151.a_ref), channel_id=1, source_target_pairs={{0,64},{64,0},{128,192},{192,128},{1,65},{65,1},{129,193},{193,129... | collective-permute-start | bytes 393224 | tf_op jit(solution)/shard_map/ppermute | solution.py:389
  113.0 18.6 %collective-permute-start.14 = (bf16[4,25,8,128]{3,2,1,0:T(8,128)(2,1)S(1)}, bf16[4,25,8,128]{3,2,1,0:T(8,128)(2,1)S(1)}, u32[]{:S(2)}, u32[]{:S(2)}) collective-permute-start(bf16[4,25,8,128]{3,2,1,0:T(8,128)(2,1)S(1)} %shard_map.152.refs_0_), channel_id=1, source_target_pairs={{0,1},{1,0},{2,3},{3,2},{4,5},{5,4},{6,7},{7,6},{8,9},{9,8},{10,11... | collective-permute-start | bytes 614408 | tf_op jit(solution)/shard_map/ppermute | solution.py:389
  116.6 1.2 copy-start.4
  117.8 1.2 copy-start.5
  121.6 10.1 %collective-permute-start.15 = (bf16[4,25,8,128]{3,2,1,0:T(8,128)(2,1)S(1)}, bf16[4,25,8,128]{3,2,1,0:T(8,128)(2,1)S(1)}, u32[]{:S(2)}, u32[]{:S(2)}) collective-permute-start(bf16[4,25,8,128]{3,2,1,0:T(8,128)(2,1)S(1)} %collective-permute-done.10.refs_1_), channel_id=1, source_target_pairs={{0,1},{1,0},{2,3},{3,2},{4,5},{5,4},{6,7},{7,6},{8,9},{9,8},{10,11... | collective-permute-start | bytes 614408 | tf_op jit(solution)/shard_map/ppermute | solution.py:389
  123.8 7.9 %collective-permute-start.16 = (bf16[4,25,8,128]{3,2,1,0:T(8,128)(2,1)S(1)}, bf16[4,25,8,128]{3,2,1,0:T(8,128)(2,1)S(1)}, u32[]{:S(2)}, u32[]{:S(2)}) collective-permute-start(bf16[4,25,8,128]{3,2,1,0:T(8,128)(2,1)S(1)} %collective-permute-done.11.refs_2_), channel_id=1, source_target_pairs={{0,1},{1,0},{2,3},{3,2},{4,5},{5,4},{6,7},{7,6},{8,9},{9,8},{10,11... | collective-permute-start | bytes 614408 | tf_op jit(solution)/shard_map/ppermute | solution.py:389
  123.8 7.9 %collective-permute-start.17 = (bf16[4,25,8,128]{3,2,1,0:T(8,128)(2,1)S(1)}, bf16[4,25,8,128]{3,2,1,0:T(8,128)(2,1)S(1)}, u32[]{:S(2)}, u32[]{:S(2)}) collective-permute-start(bf16[4,25,8,128]{3,2,1,0:T(8,128)(2,1)S(1)} %collective-permute-done.12.refs_3_), channel_id=1, source_target_pairs={{0,1},{1,0},{2,3},{3,2},{4,5},{5,4},{6,7},{7,6},{8,9},{9,8},{10,11... | collective-permute-start | bytes 614408 | tf_op jit(solution)/shard_map/ppermute | solution.py:389
  124.3 6.6 %collective-permute-start.18 = (bf16[256,256]{1,0:T(8,128)(2,1)S(1)}, bf16[256,256]{1,0:T(8,128)(2,1)S(1)}, u32[]{:S(2)}, u32[]{:S(2)}) collective-permute-start(bf16[256,256]{1,0:T(8,128)(2,1)S(1)} %shard_map.154.a_ref), channel_id=1, source_target_pairs={{0,128},{64,192},{128,0},{192,64},{1,129},{65,193},{129,1},{193,65... | collective-permute-start | bytes 393224 | tf_op jit(solution)/shard_map/ppermute | solution.py:389

commit v10 on v9

--- a/solution.py
+++ b/solution.py
@@ -305,24 +305,19 @@
 
 def place_kernel(place_ref, wu_ref, wv_ref, gain_ref, *refs):
     own, other = refs[:4], refs[4:8]
-    *grads_hbm, gain_out, bfly_ref, gu_ref, gv_ref, go_ref, sems = refs[8:]
-    outs = [
-        pltpu.make_async_copy(src, dst, sems.at[at])
-        for at, (src, dst) in enumerate(zip((gu_ref, gv_ref, go_ref), grads_hbm))
-    ]
+    gu_ref, gv_ref, go_ref, gain_out, bfly_ref = refs[8:]
     pieces = [
         (parts[k], (place_ref[0] + 4 - k) & 3, half)
         for k in range(4)
         for parts, half in ((own, place_ref[2]), (other, 1 - place_ref[2]))
     ]
-    for w, out in enumerate((gu_ref, gv_ref, go_ref)):
-        for part, d, half in pieces:
+    for part, d, half in pieces:
+        for w, out in enumerate((gu_ref, gv_ref, go_ref)):
             rows = pl.ds(pl.multiple_of(d * 64, 64), 64)
             cut = pl.ds(pl.multiple_of(half * 128, 128), 128)
             out[:, rows, cut] = (
                 part[:, w * 8 : (w + 1) * 8].astype(F32).reshape(GROUPS, 64, 128)
             )
-        outs[w].start()
     for part, d, half in pieces:
 
         @pl.when(d < 3)
@@ -341,8 +336,6 @@
             precision=lax.Precision.HIGHEST, preferred_element_type=F32,
         )
         gain_out[:, lanes(g)] = sums[:1] / gain_ref[:, lanes(g)]
-    for copy in outs:
-        copy.wait()
 
 
 def call(kernel, outs, scratch=(), flops=0, moved=0, vmem=24, smem=(), hbm=(), hbm_out=(), free=()):
@@ -475,7 +468,6 @@
         place, slice_, *got_z
     )[0]
     got_y = rotated(mine_y, "y")
-    grad_local = call(pair_sum_kernel, [((BLK, BLK), F32)], moved=5e5)(pair, other_pair)[0]
     mixed, dx = call(
         last_kernel, [(wide, BF), (wide, BF)], scratch=[pltpu.VMEM(wide, F32)],
         flops=6e8, moved=8e6,
@@ -483,17 +475,16 @@
     got_y, mixed, dx, pair = lax.optimization_barrier((got_y, mixed, dx, pair))
     halves = [mine_y] + got_y
     others = [swapped(half) for half in halves]
-    others, grad_local = lax.optimization_barrier((others, grad_local))
 
     shape = (GROUPS, BLK, BLK)
     gu, gv, go, grad_gain, grad_bfly = call(
         place_kernel,
         [(shape, F32)] * 3 + [(gain2.shape, F32), (butterfly.shape, F32)],
-        scratch=[pltpu.VMEM(shape, F32)] * 3 + [pltpu.SemaphoreType.DMA((3,))],
         moved=5e6,
         smem=(0,),
-        hbm_out=(0, 1, 2),
     )(place, w_u, w_v, gain2, *halves, *others)
+    other_pair, grad_gain = lax.optimization_barrier((other_pair, grad_gain))
+    grad_local = call(pair_sum_kernel, [((BLK, BLK), F32)], moved=5e5)(pair, other_pair)[0]
 
     return (
         mixed.reshape(tokens.shape),

time: 135 us -> 130 us (0.963)
  waiting for transfers between devices: 55.1 us -> 49.4 us
    ppermute x9, waiting for transfers between devices: 6.06 us -> 3.08 us  [rotated(): lax.ppermute(value, axis, [(s, (s + k * step) % n) for s in range(n)])]
    ppermute x9, starting transfers between devices: 15.6 us -> 18.6 us  [rotated(): lax.ppermute(value, axis, [(s, (s + k * step) % n) for s in range(n)])]
    ppermute x10, waiting for transfers between devices: 14.6 us -> 11.9 us  [swapped(): lax.ppermute(value, axis, [(s, s ^ bit) for s in range(lax.axis_size(axis...]
    ppermute x10, starting transfers between devices: 16.2 us -> 14 us  [swapped(): lax.ppermute(value, axis, [(s, s ^ bit) for s in range(lax.axis_size(axis...]
  transfers between devices with their start and end apart: 21 -> 21, of which waited for: 11 -> 8; matrix products, arithmetic and copies ran while one was open for 0% -> 0% of each run, Pallas kernels for 6% -> 7%
where the time goes in v10:
time: 130 us; the launch traced here: 129 us
  starting transfers between devices  52.5 us (40%)
  waiting for transfers between devices  49.4 us (38%)
  Pallas kernels  22.3 us (17%)
  local copies, waits for them, and re-layouts  3.54 us (3%)
    all_to_all x1, waiting for transfers between devices, per_device(): recv = lax.all_to_all(send.reshape(BLOCKS, 3 * PL, BLK), SEQ, 0, 0)  34.4 us
    pallas_call x14, Pallas kernels, run(): pl.pallas_call(kernel, out_shape=shapes, in_specs=specs, out_specs=[pl.Bl...  22.3 us
    ppermute x9, starting transfers between devices, rotated(): lax.ppermute(value, axis, [(s, (s + k * step) % n) for s in range(n)])  18.6 us
    ppermute x10, starting transfers between devices, swapped(): lax.ppermute(value, axis, [(s, s ^ bit) for s in range(lax.axis_size(axis...  14 us
    all_to_all x1, starting transfers between devices, per_device(): recv = lax.all_to_all(send.reshape(BLOCKS, 3 * PL, BLK), SEQ, 0, 0)  13.3 us
    ppermute x10, waiting for transfers between devices, swapped(): lax.ppermute(value, axis, [(s, s ^ bit) for s in range(lax.axis_size(axis...  11.9 us
    all_to_all x1, starting transfers between devices, per_device(): recv2 = lax.all_to_all(back, SEQ, 0, 0).reshape(GROUPS, 16, 2 * PL, BLK)  6.61 us
    unnamed x24, local copies, waits for them, and re-layouts  3.54 us
  transfers between devices with their start and end apart: 21, of which 8 were waited for; matrix products, arithmetic and copies ran while one was open for 0% of the time, Pallas kernels for 7%

profile of v10, /device:TPU:1, one launch (start us, length us, event | category | flops | bytes accessed | tf_op | source)
XLA Modules:
  0.0 129.3 jit_solution(14071661674569726681)
XLA Ops:
  0.6 3.4 %shard_map.143 = bf16[4,16,48,256]{3,2,1,0:T(8,128)(2,1)} custom-call(bf16[256,1024]{1,0:T(8,128)(2,1)} %bitcast.13, bf16[256,1024]{1,0:T(8,128)(2,1)} %bitcast.21, f32[1,1024]{1,0:T(1,128)} %bitcast.16, bf16[256,256]{1,0:T(8,128)(2,1)} %local_ref.1), custom_call_target="tpu_custom_call" | custom-call | flops 140000000 | bytes 4000000 | tf_op jit(solution)/shard_map/pallas_call | solution.py:353
  4.1 13.3 %all-to-all-start = ((bf16[64,48,256]{2,1,0:T(8,128)(2,1)}), bf16[64,48,256]{2,1,0:T(8,128)(2,1)}, u32[]{:S(2)}, u32[]{:S(2)}) async-start(bf16[64,48,256]{2,1,0:T(8,128)(2,1)} %bitcast.20), calls=%async_computation | async-start | bytes 3145728 | tf_op jit(solution)/shard_map/all_to_all | solution.py:410
  17.4 3.8 %shard_map.144 = (bf16[256,1024]{1,0:T(8,128)(2,1)}, f32[256,1024]{1,0:T(8,128)}, f32[256,1024]{1,0:T(8,128)}) custom-call(bf16[256,1024]{1,0:T(8,128)(2,1)} %bitcast.14, bf16[256,1024]{1,0:T(8,128)(2,1)} %bitcast.22, f32[1,1024]{1,0:T(1,128)} %bitcast.17, bf16[4,256,256]{2,1,0:T(8,128)(2,1)} %wu_ref.5, bf16[4,256,256]{2,1,0:T(8,128)(2,1)} %wv_ref.5, ...), custom_call_target="tpu_custom_call" | custom-call | flops 400000000 | bytes 8000000 | tf_op jit(solution)/shard_map/pallas_call | solution.py:353
  21.3 0.6 pad_add_fusion.place_ref
  21.9 34.4 %all-to-all-done.recv_hbm = bf16[64,48,256]{2,1,0:T(8,128)(2,1)} async-done(((bf16[64,48,256]{2,1,0:T(8,128)(2,1)}), bf16[64,48,256]{2,1,0:T(8,128)(2,1)}, u32[]{:S(2)}, u32[]{:S(2)}) %all-to-all-start) | async-done | bytes 1572896 | tf_op jit(solution)/shard_map/all_to_all | solution.py:410
  56.4 8.3 %shard_map.145 = (bf16[64,32,256]{2,1,0:T(8,128)(2,1)}, f32[4,25,8,128]{3,2,1,0:T(8,128)}, bf16[4,25,8,128]{3,2,1,0:T(8,128)(2,1)}) custom-call(s32[3]{0:T(128)} %pad_add_fusion.place_ref, bf16[64,48,256]{2,1,0:T(8,128)(2,1)} %all-to-all-done.recv_hbm, f32[6,2,2,1024]{3,2,1,0:T(2,128)} %coef_hbm.1, bf16[4,256,256]{2,1,0:T(8,128)(2,1)} %wu_ref.5, ...), custom_call_target="tpu_custom_call" | custom-call | flops 800000000 | bytes 4000000 | tf_op jit(solution)/shard_map/pallas_call | solution.py:353
  64.6 0.0 copy-start.11
  64.6 0.0 copy-start.8
  64.7 6.6 %all-to-all-start.1 = ((bf16[64,32,256]{2,1,0:T(8,128)(2,1)}), bf16[64,32,256]{2,1,0:T(8,128)(2,1)S(1)}, u32[]{:S(2)}, u32[]{:S(2)}) async-start(bf16[64,32,256]{2,1,0:T(8,128)(2,1)} %get-tuple-element.47), calls=%async_computation.1 | async-start | bytes 2097152 | tf_op jit(solution)/shard_map/all_to_all | solution.py:450
  71.3 0.5 collective-permute-start
  71.8 1.1 collective-permute-done.got_ref
  72.9 0.6 shard_map.146
  73.5 0.0 copy-start
  73.5 0.0 copy-start.1
  73.5 0.0 copy-start.2
  73.6 0.0 copy-start.3
  73.6 1.4 %collective-permute-start.1 = (bf16[25,8,128]{2,1,0:T(8,128)(2,1)S(1)}, bf16[25,8,128]{2,1,0:T(8,128)(2,1)S(1)}, u32[]{:S(2)}, u32[]{:S(2)}) collective-permute-start(bf16[25,8,128]{2,1,0:T(8,128)(2,1)S(1)} %get-tuple-element.51), channel_id=1, source_target_pairs={{0,2},{2,4},{4,6},{6,0},{1,3},{3,5},{5,7},{7,1},{8,10},{10,12},{12... | collective-permute-start | bytes 153608 | tf_op jit(solution)/shard_map/ppermute | solution.py:376
  75.0 2.4 %collective-permute-start.2 = (bf16[25,8,128]{2,1,0:T(8,128)(2,1)S(1)}, bf16[25,8,128]{2,1,0:T(8,128)(2,1)S(1)}, u32[]{:S(2)}, u32[]{:S(2)}) collective-permute-start(bf16[25,8,128]{2,1,0:T(8,128)(2,1)S(1)} %get-tuple-element.52), channel_id=1, source_target_pairs={{0,4},{2,6},{4,0},{6,2},{1,5},{3,7},{5,1},{7,3},{8,12},{10,14},{12... | collective-permute-start | bytes 153608 | tf_op jit(solution)/shard_map/ppermute | solution.py:376
  77.3 1.2 collective-permute-start.3
  78.5 0.2 collective-permute-done.1.refs_0_
  78.7 2.9 %collective-permute-done.2.refs_1_ = bf16[25,8,128]{2,1,0:T(8,128)(2,1)S(1)} collective-permute-done((bf16[25,8,128]{2,1,0:T(8,128)(2,1)S(1)}, bf16[25,8,128]{2,1,0:T(8,128)(2,1)S(1)}, u32[]{:S(2)}, u32[]{:S(2)}) %collective-permute-start.2) | collective-permute-done | bytes 51232 | tf_op jit(solution)/shard_map/ppermute | solution.py:376
  81.6 1.3 %collective-permute-start.4 = (bf16[25,8,128]{2,1,0:T(8,128)(2,1)S(1)}, bf16[25,8,128]{2,1,0:T(8,128)(2,1)S(1)}, u32[]{:S(2)}, u32[]{:S(2)}) collective-permute-start(bf16[25,8,128]{2,1,0:T(8,128)(2,1)S(1)} %shard_map.147.a_ref), channel_id=1, source_target_pairs={{0,64},{64,0},{128,192},{192,128},{1,65},{65,1},{129,193},{193,129... | collective-permute-start | bytes 153608 | tf_op jit(solution)/shard_map/ppermute | solution.py:382
  82.9 2.0 %collective-permute-done.4.b_ref = bf16[25,8,128]{2,1,0:T(8,128)(2,1)S(1)} collective-permute-done((bf16[25,8,128]{2,1,0:T(8,128)(2,1)S(1)}, bf16[25,8,128]{2,1,0:T(8,128)(2,1)S(1)}, u32[]{:S(2)}, u32[]{:S(2)}) %collective-permute-start.4) | collective-permute-done | bytes 51232 | tf_op jit(solution)/shard_map/ppermute | solution.py:382
  85.0 2.8 %collective-permute-start.5 = (bf16[25,8,128]{2,1,0:T(8,128)(2,1)S(1)}, bf16[25,8,128]{2,1,0:T(8,128)(2,1)S(1)}, u32[]{:S(2)}, u32[]{:S(2)}) collective-permute-start(bf16[25,8,128]{2,1,0:T(8,128)(2,1)S(1)} %shard_map.148.a_ref), channel_id=1, source_target_pairs={{0,128},{64,192},{128,0},{192,64},{1,129},{65,193},{129,1},{193,65... | collective-permute-start | bytes 153608 | tf_op jit(solution)/shard_map/ppermute | solution.py:382
  87.8 2.0 %collective-permute-done.5.b_ref = bf16[25,8,128]{2,1,0:T(8,128)(2,1)S(1)} collective-permute-done((bf16[25,8,128]{2,1,0:T(8,128)(2,1)S(1)}, bf16[25,8,128]{2,1,0:T(8,128)(2,1)S(1)}, u32[]{:S(2)}, u32[]{:S(2)}) %collective-permute-start.5) | collective-permute-done | bytes 51232 | tf_op jit(solution)/shard_map/ppermute | solution.py:382
  89.9 1.4 %collective-permute-start.6 = (bf16[25,8,128]{2,1,0:T(8,128)(2,1)S(1)}, bf16[25,8,128]{2,1,0:T(8,128)(2,1)S(1)}, u32[]{:S(2)}, u32[]{:S(2)}) collective-permute-start(bf16[25,8,128]{2,1,0:T(8,128)(2,1)S(1)} %shard_map.149.a_ref), channel_id=1, source_target_pairs={{0,8},{8,0},{16,24},{24,16},{32,40},{40,32},{48,56},{56,48},{1,9},... | collective-permute-start | bytes 153608 | tf_op jit(solution)/shard_map/ppermute | solution.py:382
  91.3 5.6 %collective-permute-done.6.b_ref = bf16[25,8,128]{2,1,0:T(8,128)(2,1)S(1)} collective-permute-done((bf16[25,8,128]{2,1,0:T(8,128)(2,1)S(1)}, bf16[25,8,128]{2,1,0:T(8,128)(2,1)S(1)}, u32[]{:S(2)}, u32[]{:S(2)}) %collective-permute-start.6) | collective-permute-done | bytes 51232 | tf_op jit(solution)/shard_map/ppermute | solution.py:382
  96.9 0.7 collective-permute-start.7
  97.5 3.8 %collective-permute-start.8 = (bf16[25,8,128]{2,1,0:T(8,128)(2,1)S(1)}, bf16[25,8,128]{2,1,0:T(8,128)(2,1)S(1)}, u32[]{:S(2)}, u32[]{:S(2)}) collective-permute-start(bf16[25,8,128]{2,1,0:T(8,128)(2,1)S(1)} %shard_map.150.refs_0_), channel_id=1, source_target_pairs={{0,32},{8,40},{16,48},{24,56},{32,0},{40,8},{48,16},{56,24},{1,33}... | collective-permute-start | bytes 153608 | tf_op jit(solution)/shard_map/ppermute | solution.py:376
  101.3 3.5 %collective-permute-start.9 = (bf16[25,8,128]{2,1,0:T(8,128)(2,1)S(1)}, bf16[25,8,128]{2,1,0:T(8,128)(2,1)S(1)}, u32[]{:S(2)}, u32[]{:S(2)}) collective-permute-start(bf16[25,8,128]{2,1,0:T(8,128)(2,1)S(1)} %shard_map.150.refs_0_), channel_id=1, source_target_pairs={{0,48},{8,56},{16,0},{24,8},{32,16},{40,24},{48,32},{56,40},{1,49}... | collective-permute-start | bytes 153608 | tf_op jit(solution)/shard_map/ppermute | solution.py:376
  104.8 1.0 copy-done.6
  105.8 0.3 shard_map.151.a_ref
  106.2 0.6 shard_map.152.refs_0_
  106.8 2.7 %collective-permute-start.10 = (bf16[4,25,8,128]{3,2,1,0:T(8,128)(2,1)S(1)}, bf16[4,25,8,128]{3,2,1,0:T(8,128)(2,1)S(1)}, u32[]{:S(2)}, u32[]{:S(2)}) collective-permute-start(bf16[4,25,8,128]{3,2,1,0:T(8,128)(2,1)S(1)} %shard_map.152.refs_0_), channel_id=1, source_target_pairs={{0,2},{2,4},{4,6},{6,0},{1,3},{3,5},{5,7},{7,1},{8,10},{10,12},{12... | collective-permute-start | bytes 614408 | tf_op jit(solution)/shard_map/ppermute | solution.py:376
  109.5 1.0 collective-permute-start.11
  110.5 2.0 %collective-permute-start.12 = (bf16[4,25,8,128]{3,2,1,0:T(8,128)(2,1)S(1)}, bf16[4,25,8,128]{3,2,1,0:T(8,128)(2,1)S(1)}, u32[]{:S(2)}, u32[]{:S(2)}) collective-permute-start(bf16[4,25,8,128]{3,2,1,0:T(8,128)(2,1)S(1)} %shard_map.152.refs_0_), channel_id=1, source_target_pairs={{0,6},{2,0},{4,2},{6,4},{1,7},{3,1},{5,3},{7,5},{8,14},{10,8},{12,... | collective-permute-start | bytes 614408 | tf_op jit(solution)/shard_map/ppermute | solution.py:376
  112.5 1.2 collective-permute-start.13
  113.7 3.5 %collective-permute-start.14 = (bf16[4,25,8,128]{3,2,1,0:T(8,128)(2,1)S(1)}, bf16[4,25,8,128]{3,2,1,0:T(8,128)(2,1)S(1)}, u32[]{:S(2)}, u32[]{:S(2)}) collective-permute-start(bf16[4,25,8,128]{3,2,1,0:T(8,128)(2,1)S(1)} %shard_map.152.refs_0_), channel_id=1, source_target_pairs={{0,1},{1,0},{2,3},{3,2},{4,5},{5,4},{6,7},{7,6},{8,9},{9,8},{10,11... | collective-permute-start | bytes 614408 | tf_op jit(solution)/shard_map/ppermute | solution.py:382
  117.3 1.2 copy-done.4
  118.5 1.2 copy-done.5
  119.7 1.9 %shard_map.153 = (bf16[256,1024]{1,0:T(8,128)(2,1)}, bf16[256,1024]{1,0:T(8,128)(2,1)}) custom-call(bf16[4,16,32,256]{3,2,1,0:T(8,128)(2,1)S(1)} %bitcast.12, bf16[256,1024]{1,0:T(8,128)(2,1)S(1)} %bitcast.15, f32[1,1024]{1,0:T(1,128)S(1)} %bitcast.18, f32[256,1024]{1,0:T(8,128)S(1)} %copy-done.4, f32[256,1024]{1,0:T(8,128)S(1)} %copy-done.5, ...), custom_call_target="tpu_custom_call" | custom-call | flops 600000000 | bytes 8000000 | tf_op jit(solution)/shard_map/pallas_call | solution.py:353
  121.7 0.1 collective-permute-start.15
  121.8 0.5 collective-permute-start.16
  122.3 0.1 collective-permute-start.17
  122.4 2.5 %collective-permute-start.18 = (bf16[256,256]{1,0:T(8,128)(2,1)S(1)}, bf16[256,256]{1,0:T(8,128)(2,1)S(1)}, u32[]{:S(2)}, u32[]{:S(2)}) collective-permute-start(bf16[256,256]{1,0:T(8,128)(2,1)S(1)} %shard_map.154.a_ref), channel_id=1, source_target_pairs={{0,128},{64,192},{128,0},{192,64},{1,129},{65,193},{129,1},{193,65... | collective-permute-start | bytes 393224 | tf_op jit(solution)/shard_map/ppermute | solution.py:382
  124.8 2.5 %shard_map.155 = (f32[4,256,256]{2,1,0:T(8,128)}, f32[4,256,256]{2,1,0:T(8,128)}, f32[4,256,256]{2,1,0:T(8,128)}, f32[1,1024]{1,0:T(1,128)}, f32[6,2,2,1024]{3,2,1,0:T(2,128)}) custom-call(s32[3]{0:T(128)S(1)} %copy-done.10, bf16[4,256,256]{2,1,0:T(8,128)(2,1)S(1)} %copy-done, bf16[4,256,256]{2,1,0:T(8,128)(2,1)S(1)} %copy-done.1, f32[1,1024]{1,0:T(1,128)S(1)} %bitcast.19, ...), custom_call_target="tpu_custom_call" | custom-call | bytes 5000000 | tf_op jit(solution)/shard_map/pallas_call | solution.py:353
  127.4 1.2 collective-permute-done.18.b_ref
  128.5 0.7 shard_map.156
  (33 shorter events, 0.2 us)
Async XLA Ops:
  4.1 52.3 %all-to-all-start = ((bf16[64,48,256]{2,1,0:T(8,128)(2,1)}), bf16[64,48,256]{2,1,0:T(8,128)(2,1)}, u32[]{:S(2)}, u32[]{:S(2)}) async-start(bf16[64,48,256]{2,1,0:T(8,128)(2,1)} %bitcast.20), calls=%async_computation | async-start | bytes 3145728 | tf_op jit(solution)/shard_map/all_to_all | solution.py:410
  64.6 6.7 %copy-start.11 = (bf16[4,25,8,128]{3,2,1,0:T(8,128)(2,1)S(1)}, bf16[4,25,8,128]{3,2,1,0:T(8,128)(2,1)}, u32[]{:S(2)}) copy-start(bf16[4,25,8,128]{3,2,1,0:T(8,128)(2,1)} %get-tuple-element.49) | copy-start | bytes 614404
  64.6 8.3 %copy-start.8 = (f32[4,25,8,128]{3,2,1,0:T(8,128)S(1)}, f32[4,25,8,128]{3,2,1,0:T(8,128)}, u32[]{:S(2)}) copy-start(f32[4,25,8,128]{3,2,1,0:T(8,128)} %get-tuple-element.48.keep_ref) | copy-start | bytes 1228804
  64.7 8.3 %copy-start.10 = (s32[3]{0:T(128)S(1)}, s32[3]{0:T(128)}, u32[]{:S(2)}) copy-start(s32[3]{0:T(128)} %pad_add_fusion.place_ref) | copy-start | bytes 40
  64.7 40.1 %all-to-all-start.1 = ((bf16[64,32,256]{2,1,0:T(8,128)(2,1)}), bf16[64,32,256]{2,1,0:T(8,128)(2,1)S(1)}, u32[]{:S(2)}, u32[]{:S(2)}) async-start(bf16[64,32,256]{2,1,0:T(8,128)(2,1)} %get-tuple-element.47), calls=%async_computation.1 | async-start | bytes 2097152 | tf_op jit(solution)/shard_map/all_to_all | solution.py:450
  71.3 1.6 %collective-permute-start = (bf16[4,25,8,128]{3,2,1,0:T(8,128)(2,1)S(1)}, bf16[4,25,8,128]{3,2,1,0:T(8,128)(2,1)S(1)}, u32[]{:S(2)}, u32[]{:S(2)}) collective-permute-start(bf16[4,25,8,128]{3,2,1,0:T(8,128)(2,1)S(1)} %copy-done.11), channel_id=1, source_target_pairs={{0,1},{1,0},{2,3},{3,2},{4,5},{5,4},{6,7},{7,6},{8,9},{9,8},{10,11... | collective-permute-start | bytes 614408 | tf_op jit(solution)/shard_map/ppermute | solution.py:382
  72.9 44.3 %copy-start.7 = (bf16[256,256]{1,0:T(8,128)(2,1)S(1)}, bf16[256,256]{1,0:T(8,128)(2,1)}, u32[]{:S(2)}) copy-start(bf16[256,256]{1,0:T(8,128)(2,1)} %local_ref.1) | copy-start | bytes 393220
  72.9 44.3 %copy-start.9 = (f32[1024]{0:T(1024)S(1)}, f32[1024]{0:T(1024)}, u32[]{:S(2)}) copy-start(f32[1024]{0:T(1024)} %param.10) | copy-start | bytes 12292
  73.5 43.7 %copy-start = (bf16[4,256,256]{2,1,0:T(8,128)(2,1)S(1)}, bf16[4,256,256]{2,1,0:T(8,128)(2,1)}, u32[]{:S(2)}) copy-start(bf16[4,256,256]{2,1,0:T(8,128)(2,1)} %wu_ref.5) | copy-start | bytes 1572868
  73.5 43.7 %copy-start.1 = (bf16[4,256,256]{2,1,0:T(8,128)(2,1)S(1)}, bf16[4,256,256]{2,1,0:T(8,128)(2,1)}, u32[]{:S(2)}) copy-start(bf16[4,256,256]{2,1,0:T(8,128)(2,1)} %wv_ref.5) | copy-start | bytes 1572868
  73.5 43.7 %copy-start.2 = (bf16[1,256,1024]{2,1,0:T(8,128)(2,1)S(1)}, bf16[1,256,1024]{2,1,0:T(8,128)(2,1)}, u32[]{:S(2)}) copy-start(bf16[1,256,1024]{2,1,0:T(8,128)(2,1)} %param.8) | copy-start | bytes 1572868
  73.6 43.7 %copy-start.3 = (bf16[4,256,256]{2,1,0:T(8,128)(2,1)S(1)}, bf16[4,256,256]{2,1,0:T(8,128)(2,1)}, u32[]{:S(2)}) copy-start(bf16[4,256,256]{2,1,0:T(8,128)(2,1)} %wo_ref.3) | copy-start | bytes 1572868
  73.6 5.1 %collective-permute-start.1 = (bf16[25,8,128]{2,1,0:T(8,128)(2,1)S(1)}, bf16[25,8,128]{2,1,0:T(8,128)(2,1)S(1)}, u32[]{:S(2)}, u32[]{:S(2)}) collective-permute-start(bf16[25,8,128]{2,1,0:T(8,128)(2,1)S(1)} %get-tuple-element.51), channel_id=1, source_target_pairs={{0,2},{2,4},{4,6},{6,0},{1,3},{3,5},{5,7},{7,1},{8,10},{10,12},{12... | collective-permute-start | bytes 153608 | tf_op jit(solution)/shard_map/ppermute | solution.py:376
  75.0 6.6 %collective-permute-start.2 = (bf16[25,8,128]{2,1,0:T(8,128)(2,1)S(1)}, bf16[25,8,128]{2,1,0:T(8,128)(2,1)S(1)}, u32[]{:S(2)}, u32[]{:S(2)}) collective-permute-start(bf16[25,8,128]{2,1,0:T(8,128)(2,1)S(1)} %get-tuple-element.52), channel_id=1, source_target_pairs={{0,4},{2,6},{4,0},{6,2},{1,5},{3,7},{5,1},{7,3},{8,12},{10,14},{12... | collective-permute-start | bytes 153608 | tf_op jit(solution)/shard_map/ppermute | solution.py:376
  77.3 4.2 %collective-permute-start.3 = (bf16[25,8,128]{2,1,0:T(8,128)(2,1)S(1)}, bf16[25,8,128]{2,1,0:T(8,128)(2,1)S(1)}, u32[]{:S(2)}, u32[]{:S(2)}) collective-permute-start(bf16[25,8,128]{2,1,0:T(8,128)(2,1)S(1)} %get-tuple-element.53), channel_id=1, source_target_pairs={{0,6},{2,0},{4,2},{6,4},{1,7},{3,1},{5,3},{7,5},{8,14},{10,8},{12,... | collective-permute-start | bytes 153608 | tf_op jit(solution)/shard_map/ppermute | solution.py:376
  81.6 3.3 %collective-permute-start.4 = (bf16[25,8,128]{2,1,0:T(8,128)(2,1)S(1)}, bf16[25,8,128]{2,1,0:T(8,128)(2,1)S(1)}, u32[]{:S(2)}, u32[]{:S(2)}) collective-permute-start(bf16[25,8,128]{2,1,0:T(8,128)(2,1)S(1)} %shard_map.147.a_ref), channel_id=1, source_target_pairs={{0,64},{64,0},{128,192},{192,128},{1,65},{65,1},{129,193},{193,129... | collective-permute-start | bytes 153608 | tf_op jit(solution)/shard_map/ppermute | solution.py:382
  85.0 4.8 %collective-permute-start.5 = (bf16[25,8,128]{2,1,0:T(8,128)(2,1)S(1)}, bf16[25,8,128]{2,1,0:T(8,128)(2,1)S(1)}, u32[]{:S(2)}, u32[]{:S(2)}) collective-permute-start(bf16[25,8,128]{2,1,0:T(8,128)(2,1)S(1)} %shard_map.148.a_ref), channel_id=1, source_target_pairs={{0,128},{64,192},{128,0},{192,64},{1,129},{65,193},{129,1},{193,65... | collective-permute-start | bytes 153608 | tf_op jit(solution)/shard_map/ppermute | solution.py:382
  89.9 7.0 %collective-permute-start.6 = (bf16[25,8,128]{2,1,0:T(8,128)(2,1)S(1)}, bf16[25,8,128]{2,1,0:T(8,128)(2,1)S(1)}, u32[]{:S(2)}, u32[]{:S(2)}) collective-permute-start(bf16[25,8,128]{2,1,0:T(8,128)(2,1)S(1)} %shard_map.149.a_ref), channel_id=1, source_target_pairs={{0,8},{8,0},{16,24},{24,16},{32,40},{40,32},{48,56},{56,48},{1,9},... | collective-permute-start | bytes 153608 | tf_op jit(solution)/shard_map/ppermute | solution.py:382
  96.9 9.3 %collective-permute-start.7 = (bf16[25,8,128]{2,1,0:T(8,128)(2,1)S(1)}, bf16[25,8,128]{2,1,0:T(8,128)(2,1)S(1)}, u32[]{:S(2)}, u32[]{:S(2)}) collective-permute-start(bf16[25,8,128]{2,1,0:T(8,128)(2,1)S(1)} %shard_map.150.refs_0_), channel_id=1, source_target_pairs={{0,16},{8,24},{16,32},{24,40},{32,48},{40,56},{48,0},{56,8},{1,17}... | collective-permute-start | bytes 153608 | tf_op jit(solution)/shard_map/ppermute | solution.py:376
  97.5 8.7 %collective-permute-start.8 = (bf16[25,8,128]{2,1,0:T(8,128)(2,1)S(1)}, bf16[25,8,128]{2,1,0:T(8,128)(2,1)S(1)}, u32[]{:S(2)}, u32[]{:S(2)}) collective-permute-start(bf16[25,8,128]{2,1,0:T(8,128)(2,1)S(1)} %shard_map.150.refs_0_), channel_id=1, source_target_pairs={{0,32},{8,40},{16,48},{24,56},{32,0},{40,8},{48,16},{56,24},{1,33}... | collective-permute-start | bytes 153608 | tf_op jit(solution)/shard_map/ppermute | solution.py:376
  101.3 4.9 %collective-permute-start.9 = (bf16[25,8,128]{2,1,0:T(8,128)(2,1)S(1)}, bf16[25,8,128]{2,1,0:T(8,128)(2,1)S(1)}, u32[]{:S(2)}, u32[]{:S(2)}) collective-permute-start(bf16[25,8,128]{2,1,0:T(8,128)(2,1)S(1)} %shard_map.150.refs_0_), channel_id=1, source_target_pairs={{0,48},{8,56},{16,0},{24,8},{32,16},{40,24},{48,32},{56,40},{1,49}... | collective-permute-start | bytes 153608 | tf_op jit(solution)/shard_map/ppermute | solution.py:376
  104.8 1.0 copy-start.6
  106.8 14.9 %collective-permute-start.10 = (bf16[4,25,8,128]{3,2,1,0:T(8,128)(2,1)S(1)}, bf16[4,25,8,128]{3,2,1,0:T(8,128)(2,1)S(1)}, u32[]{:S(2)}, u32[]{:S(2)}) collective-permute-start(bf16[4,25,8,128]{3,2,1,0:T(8,128)(2,1)S(1)} %shard_map.152.refs_0_), channel_id=1, source_target_pairs={{0,2},{2,4},{4,6},{6,0},{1,3},{3,5},{5,7},{7,1},{8,10},{10,12},{12... | collective-permute-start | bytes 614408 | tf_op jit(solution)/shard_map/ppermute | solution.py:376
  109.5 12.1 %collective-permute-start.11 = (bf16[4,25,8,128]{3,2,1,0:T(8,128)(2,1)S(1)}, bf16[4,25,8,128]{3,2,1,0:T(8,128)(2,1)S(1)}, u32[]{:S(2)}, u32[]{:S(2)}) collective-permute-start(bf16[4,25,8,128]{3,2,1,0:T(8,128)(2,1)S(1)} %shard_map.152.refs_0_), channel_id=1, source_target_pairs={{0,4},{2,6},{4,0},{6,2},{1,5},{3,7},{5,1},{7,3},{8,12},{10,14},{12... | collective-permute-start | bytes 614408 | tf_op jit(solution)/shard_map/ppermute | solution.py:376
  110.5 11.1 %collective-permute-start.12 = (bf16[4,25,8,128]{3,2,1,0:T(8,128)(2,1)S(1)}, bf16[4,25,8,128]{3,2,1,0:T(8,128)(2,1)S(1)}, u32[]{:S(2)}, u32[]{:S(2)}) collective-permute-start(bf16[4,25,8,128]{3,2,1,0:T(8,128)(2,1)S(1)} %shard_map.152.refs_0_), channel_id=1, source_target_pairs={{0,6},{2,0},{4,2},{6,4},{1,7},{3,1},{5,3},{7,5},{8,14},{10,8},{12,... | collective-permute-start | bytes 614408 | tf_op jit(solution)/shard_map/ppermute | solution.py:376
  112.5 9.1 %collective-permute-start.13 = (bf16[256,256]{1,0:T(8,128)(2,1)S(1)}, bf16[256,256]{1,0:T(8,128)(2,1)S(1)}, u32[]{:S(2)}, u32[]{:S(2)}) collective-permute-start(bf16[256,256]{1,0:T(8,128)(2,1)S(1)} %shard_map.151.a_ref), channel_id=1, source_target_pairs={{0,64},{64,0},{128,192},{192,128},{1,65},{65,1},{129,193},{193,129... | collective-permute-start | bytes 393224 | tf_op jit(solution)/shard_map/ppermute | solution.py:382
  113.7 11.1 %collective-permute-start.14 = (bf16[4,25,8,128]{3,2,1,0:T(8,128)(2,1)S(1)}, bf16[4,25,8,128]{3,2,1,0:T(8,128)(2,1)S(1)}, u32[]{:S(2)}, u32[]{:S(2)}) collective-permute-start(bf16[4,25,8,128]{3,2,1,0:T(8,128)(2,1)S(1)} %shard_map.152.refs_0_), channel_id=1, source_target_pairs={{0,1},{1,0},{2,3},{3,2},{4,5},{5,4},{6,7},{7,6},{8,9},{9,8},{10,11... | collective-permute-start | bytes 614408 | tf_op jit(solution)/shard_map/ppermute | solution.py:382
  117.3 1.2 copy-start.4
  118.5 1.2 copy-start.5
  121.7 3.2 %collective-permute-start.15 = (bf16[4,25,8,128]{3,2,1,0:T(8,128)(2,1)S(1)}, bf16[4,25,8,128]{3,2,1,0:T(8,128)(2,1)S(1)}, u32[]{:S(2)}, u32[]{:S(2)}) collective-permute-start(bf16[4,25,8,128]{3,2,1,0:T(8,128)(2,1)S(1)} %collective-permute-done.10.refs_1_), channel_id=1, source_target_pairs={{0,1},{1,0},{2,3},{3,2},{4,5},{5,4},{6,7},{7,6},{8,9},{9,8},{10,11... | collective-permute-start | bytes 614408 | tf_op jit(solution)/shard_map/ppermute | solution.py:382
  121.8 3.1 %collective-permute-start.16 = (bf16[4,25,8,128]{3,2,1,0:T(8,128)(2,1)S(1)}, bf16[4,25,8,128]{3,2,1,0:T(8,128)(2,1)S(1)}, u32[]{:S(2)}, u32[]{:S(2)}) collective-permute-start(bf16[4,25,8,128]{3,2,1,0:T(8,128)(2,1)S(1)} %collective-permute-done.11.refs_2_), channel_id=1, source_target_pairs={{0,1},{1,0},{2,3},{3,2},{4,5},{5,4},{6,7},{7,6},{8,9},{9,8},{10,11... | collective-permute-start | bytes 614408 | tf_op jit(solution)/shard_map/ppermute | solution.py:382
  122.3 2.6 %collective-permute-start.17 = (bf16[4,25,8,128]{3,2,1,0:T(8,128)(2,1)S(1)}, bf16[4,25,8,128]{3,2,1,0:T(8,128)(2,1)S(1)}, u32[]{:S(2)}, u32[]{:S(2)}) collective-permute-start(bf16[4,25,8,128]{3,2,1,0:T(8,128)(2,1)S(1)} %collective-permute-done.12.refs_3_), channel_id=1, source_target_pairs={{0,1},{1,0},{2,3},{3,2},{4,5},{5,4},{6,7},{7,6},{8,9},{9,8},{10,11... | collective-permute-start | bytes 614408 | tf_op jit(solution)/shard_map/ppermute | solution.py:382
  122.4 6.2 %collective-permute-start.18 = (bf16[256,256]{1,0:T(8,128)(2,1)S(1)}, bf16[256,256]{1,0:T(8,128)(2,1)S(1)}, u32[]{:S(2)}, u32[]{:S(2)}) collective-permute-start(bf16[256,256]{1,0:T(8,128)(2,1)S(1)} %shard_map.154.a_ref), channel_id=1, source_target_pairs={{0,128},{64,192},{128,0},{192,64},{1,129},{65,193},{129,1},{193,65... | collective-permute-start | bytes 393224 | tf_op jit(solution)/shard_map/ppermute | solution.py:382

commit v11 on v10

--- a/solution.py
+++ b/solution.py
@@ -76,18 +76,6 @@
         made[g].start()
     for copy in made:
         copy.wait()
-
-
-def side_kernel(x_ref, cot_ref, gain_ref, wu_ref, wv_ref, wo_ref, u_ref, act_ref, dgd_ref):
-    r = inv_rms(x_ref)
-    for g in range(GROUPS):
-        xn = (x_ref[:, lanes(g)].astype(F32) * r * gain_ref[:, lanes(g)]).astype(BF)
-        u_ref[:, lanes(g)] = mm(xn, wu_ref[g]).astype(BF)
-        v = mm(xn, wv_ref[g])
-        sig = jax.nn.sigmoid(v)
-        act_ref[:, lanes(g)] = v * sig
-        dg = mm_nt(cot_ref[:, lanes(g)], wo_ref[g])
-        dgd_ref[:, lanes(g)] = dg * (sig * (1.0 + v * (1.0 - sig)))
 
 
 def tiles_of(value):
@@ -274,25 +262,32 @@
     return recv_ref[g, :, which * PL : (which + 1) * PL, :].reshape(BLK, BLK)
 
 
-def local_kernel(recv_ref, u_ref, out_ref):
+def local_kernel(recv_ref, x_ref, gain_ref, wu_ref, out_ref):
+    r = inv_rms(x_ref)
     total = jnp.zeros((BLK, BLK), F32)
     for g in range(GROUPS):
-        total = total + mm_nt(group_of(recv_ref, g, 1), u_ref[:, lanes(g)])
+        xn = (x_ref[:, lanes(g)].astype(F32) * r * gain_ref[:, lanes(g)]).astype(BF)
+        u = mm(xn, wu_ref[g]).astype(BF)
+        total = total + mm_nt(group_of(recv_ref, g, 1), u)
     out_ref[...] = total.astype(BF)
 
 
 def last_kernel(
-    recv_ref, x_ref, gain_ref, act_ref, dgd_ref, wu_ref, wv_ref, wo_ref, local_ref,
+    recv_ref, x_ref, cot_ref, gain_ref, wu_ref, wv_ref, wo_ref, local_ref,
     mixed_ref, dx_ref, scaled_ref,
 ):
     r = inv_rms(x_ref)
     local = local_ref[...]
     inner = jnp.zeros((BLK, 1), F32)
     for g in range(GROUPS):
+        xn = (x_ref[:, lanes(g)].astype(F32) * r * gain_ref[:, lanes(g)]).astype(BF)
+        v = mm(xn, wv_ref[g])
+        sig = jax.nn.sigmoid(v)
         z = group_of(recv_ref, g, 0).astype(F32)
-        gated = (z * act_ref[:, lanes(g)]).astype(BF)
+        gated = (z * (v * sig)).astype(BF)
         mixed_ref[:, lanes(g)] = mm(gated, wo_ref[g]).astype(BF)
-        dv = (z * dgd_ref[:, lanes(g)]).astype(BF)
+        dg = mm_nt(cot_ref[:, lanes(g)], wo_ref[g])
+        dv = (z * (dg * (sig * (1.0 + v * (1.0 - sig))))).astype(BF)
         du = mm_tn(local, group_of(recv_ref, g, 1)).astype(BF)
         scaled = (mm_nt(du, wu_ref[g]) + mm_nt(dv, wv_ref[g])) * gain_ref[:, lanes(g)]
         scaled_ref[:, lanes(g)] = scaled
@@ -408,11 +403,6 @@
         vmem=58,
     )(x, cot, gain2, local_factor)[0]
     recv = lax.all_to_all(send.reshape(BLOCKS, 3 * PL, BLK), SEQ, 0, 0)
-
-    u, act, dgd = call(
-        side_kernel, [(wide, BF), (wide, F32), (wide, F32)], flops=4e8, moved=8e6, vmem=63
-    )(x, cot, gain2, w_u, w_v, w_o)
-    recv, u, act, dgd = lax.optimization_barrier((recv, u, act, dgd))
 
     tiled = (BLOCKS, 2, 2, 8, 128)
     quarter = (25, 8, 128)
@@ -460,7 +450,9 @@
     got_z = rotated(slice_, "z", 2)
 
     recv2, slice_ = lax.optimization_barrier((recv2, slice_))
-    part = call(local_kernel, [((BLK, BLK), BF)], flops=1.3e8, moved=1.2e6)(recv2, u)[0]
+    part = call(local_kernel, [((BLK, BLK), BF)], flops=1.3e8, moved=1.2e6)(
+        recv2, x, gain2, w_u
+    )[0]
     got_z, part = lax.optimization_barrier((got_z, part))
     pair = call(pair_sum_kernel, [((BLK, BLK), BF)], moved=4e5)(part, swapped(part, "dp", 1))[0]
     other_pair = swapped(pair, "dp", 2)
@@ -471,7 +463,7 @@
     mixed, dx = call(
         last_kernel, [(wide, BF), (wide, BF)], scratch=[pltpu.VMEM(wide, F32)],
         flops=6e8, moved=8e6,
-    )(recv2, x, gain2, act, dgd, w_u, w_v, w_o, local_factor)
+    )(recv2, x, cot, gain2, w_u, w_v, w_o, local_factor)
     got_y, mixed, dx, pair = lax.optimization_barrier((got_y, mixed, dx, pair))
     halves = [mine_y] + got_y
     others = [swapped(half) for half in halves]

time: 130 us -> 129 us (level)
  waiting for transfers between devices: 49.4 us -> 54 us
  local copies, waits for them, and re-layouts: 3.54 us -> 0.06 us
  Pallas kernels: 22.3 us -> 19.7 us
    all_to_all x1, waiting for transfers between devices: 34.4 us -> 38.3 us  [per_device(): recv = lax.all_to_all(send.reshape(BLOCKS, 3 * PL, BLK), SEQ, 0, 0)]
    unnamed x24 -> x20, local copies, waits for them, and re-layouts: 3.54 us -> 0.06 us
    pallas_call x14 -> x13, Pallas kernels: 22.3 us -> 19.7 us  [run(): pl.pallas_call(kernel, out_shape=shapes, in_specs=specs, out_specs=[pl.Bl...]
  transfers between devices with their start and end apart: 21 -> 21, of which waited for: 8 -> 9; matrix products, arithmetic and copies ran while one was open for 0% -> 0% of each run, Pallas kernels for 7% -> 5%
where the time goes in v11:
time: 129 us
  waiting for transfers between devices  54 us (42%)
  starting transfers between devices  53.5 us (41%)
  Pallas kernels  19.7 us (15%)
    all_to_all x1, waiting for transfers between devices, per_device(): recv = lax.all_to_all(send.reshape(BLOCKS, 3 * PL, BLK), SEQ, 0, 0)  38.3 us
    pallas_call x13, Pallas kernels, run(): pl.pallas_call(kernel, out_shape=shapes, in_specs=specs, out_specs=[pl.Bl...  19.7 us
    ppermute x9, starting transfers between devices, rotated(): lax.ppermute(value, axis, [(s, (s + k * step) % n) for s in range(n)])  18.6 us
    ppermute x10, starting transfers between devices, swapped(): lax.ppermute(value, axis, [(s, s ^ bit) for s in range(lax.axis_size(axis...  14.9 us
    all_to_all x1, starting transfers between devices, per_device(): recv = lax.all_to_all(send.reshape(BLOCKS, 3 * PL, BLK), SEQ, 0, 0)  13.3 us
    ppermute x10, waiting for transfers between devices, swapped(): lax.ppermute(value, axis, [(s, s ^ bit) for s in range(lax.axis_size(axis...  12.1 us
    all_to_all x1, starting transfers between devices, per_device(): recv2 = lax.all_to_all(back, SEQ, 0, 0).reshape(GROUPS, 16, 2 * PL, BLK)  6.61 us
    ppermute x9, waiting for transfers between devices, rotated(): lax.ppermute(value, axis, [(s, (s + k * step) % n) for s in range(n)])  3.57 us
  transfers between devices with their start and end apart: 21, of which 9 were waited for; matrix products, arithmetic and copies ran while one was open for 0% of the time, Pallas kernels for 5%

profile of v11, /device:TPU:1, one launch (start us, length us, event | category | flops | bytes accessed | tf_op | source)
XLA Modules:
  0.0 128.7 jit_solution(5996797714539470172)
XLA Ops:
  0.6 3.4 %shard_map.143 = bf16[4,16,48,256]{3,2,1,0:T(8,128)(2,1)} custom-call(bf16[256,1024]{1,0:T(8,128)(2,1)} %bitcast.13, bf16[256,1024]{1,0:T(8,128)(2,1)} %bitcast.16, f32[1,1024]{1,0:T(1,128)} %bitcast.18, bf16[256,256]{1,0:T(8,128)(2,1)} %local_ref.1), custom_call_target="tpu_custom_call" | custom-call | flops 140000000 | bytes 4000000 | tf_op jit(solution)/shard_map/pallas_call | solution.py:348
  4.1 13.3 %all-to-all-start = ((bf16[64,48,256]{2,1,0:T(8,128)(2,1)}), bf16[64,48,256]{2,1,0:T(8,128)(2,1)}, u32[]{:S(2)}, u32[]{:S(2)}) async-start(bf16[64,48,256]{2,1,0:T(8,128)(2,1)} %bitcast.22), calls=%async_computation | async-start | bytes 3145728 | tf_op jit(solution)/shard_map/all_to_all | solution.py:405
  17.4 0.6 pad_add_fusion.place_ref
  18.0 38.3 %all-to-all-done.recv_hbm = bf16[64,48,256]{2,1,0:T(8,128)(2,1)} async-done(((bf16[64,48,256]{2,1,0:T(8,128)(2,1)}), bf16[64,48,256]{2,1,0:T(8,128)(2,1)}, u32[]{:S(2)}, u32[]{:S(2)}) %all-to-all-start) | async-done | bytes 1572896 | tf_op jit(solution)/shard_map/all_to_all | solution.py:405
  56.4 8.2 %shard_map.144 = (bf16[64,32,256]{2,1,0:T(8,128)(2,1)}, f32[4,25,8,128]{3,2,1,0:T(8,128)}, bf16[4,25,8,128]{3,2,1,0:T(8,128)(2,1)}) custom-call(s32[3]{0:T(128)} %pad_add_fusion.place_ref, bf16[64,48,256]{2,1,0:T(8,128)(2,1)} %all-to-all-done.recv_hbm, f32[6,2,2,1024]{3,2,1,0:T(2,128)} %coef_hbm.1, bf16[4,256,256]{2,1,0:T(8,128)(2,1)} %wu_ref.5, ...), custom_call_target="tpu_custom_call" | custom-call | flops 800000000 | bytes 4000000 | tf_op jit(solution)/shard_map/pallas_call | solution.py:348
  64.6 0.0 copy-start.9
  64.6 0.0 copy-start.6
  64.6 0.0 copy-start.8
  64.6 0.0 copy-start
  64.6 0.0 copy-start.1
  64.7 0.0 copy-start.7
  64.7 6.6 %all-to-all-start.1 = ((bf16[64,32,256]{2,1,0:T(8,128)(2,1)}), bf16[64,32,256]{2,1,0:T(8,128)(2,1)S(1)}, u32[]{:S(2)}, u32[]{:S(2)}) async-start(bf16[64,32,256]{2,1,0:T(8,128)(2,1)} %get-tuple-element.36), calls=%async_computation.1 | async-start | bytes 2097152 | tf_op jit(solution)/shard_map/all_to_all | solution.py:440
  71.3 0.5 collective-permute-start
  71.8 1.1 collective-permute-done.got_ref
  72.9 0.6 shard_map.145
  73.5 1.4 %collective-permute-start.1 = (bf16[25,8,128]{2,1,0:T(8,128)(2,1)S(1)}, bf16[25,8,128]{2,1,0:T(8,128)(2,1)S(1)}, u32[]{:S(2)}, u32[]{:S(2)}) collective-permute-start(bf16[25,8,128]{2,1,0:T(8,128)(2,1)S(1)} %get-tuple-element.40), channel_id=1, source_target_pairs={{0,2},{2,4},{4,6},{6,0},{1,3},{3,5},{5,7},{7,1},{8,10},{10,12},{12... | collective-permute-start | bytes 153608 | tf_op jit(solution)/shard_map/ppermute | solution.py:371
  74.9 2.4 %collective-permute-start.2 = (bf16[25,8,128]{2,1,0:T(8,128)(2,1)S(1)}, bf16[25,8,128]{2,1,0:T(8,128)(2,1)S(1)}, u32[]{:S(2)}, u32[]{:S(2)}) collective-permute-start(bf16[25,8,128]{2,1,0:T(8,128)(2,1)S(1)} %get-tuple-element.41), channel_id=1, source_target_pairs={{0,4},{2,6},{4,0},{6,2},{1,5},{3,7},{5,1},{7,3},{8,12},{10,14},{12... | collective-permute-start | bytes 153608 | tf_op jit(solution)/shard_map/ppermute | solution.py:371
  77.3 1.2 collective-permute-start.3
  78.5 0.1 collective-permute-done.1.refs_0_
  78.6 3.0 %collective-permute-done.2.refs_1_ = bf16[25,8,128]{2,1,0:T(8,128)(2,1)S(1)} collective-permute-done((bf16[25,8,128]{2,1,0:T(8,128)(2,1)S(1)}, bf16[25,8,128]{2,1,0:T(8,128)(2,1)S(1)}, u32[]{:S(2)}, u32[]{:S(2)}) %collective-permute-start.2) | collective-permute-done | bytes 51232 | tf_op jit(solution)/shard_map/ppermute | solution.py:371
  81.6 0.0 copy-start.2
  81.6 0.0 copy-start.3
  81.6 0.0 copy-start.5
  81.6 1.3 %collective-permute-start.4 = (bf16[25,8,128]{2,1,0:T(8,128)(2,1)S(1)}, bf16[25,8,128]{2,1,0:T(8,128)(2,1)S(1)}, u32[]{:S(2)}, u32[]{:S(2)}) collective-permute-start(bf16[25,8,128]{2,1,0:T(8,128)(2,1)S(1)} %shard_map.146.a_ref), channel_id=1, source_target_pairs={{0,64},{64,0},{128,192},{192,128},{1,65},{65,1},{129,193},{193,129... | collective-permute-start | bytes 153608 | tf_op jit(solution)/shard_map/ppermute | solution.py:377
  82.9 2.0 %collective-permute-done.4.b_ref = bf16[25,8,128]{2,1,0:T(8,128)(2,1)S(1)} collective-permute-done((bf16[25,8,128]{2,1,0:T(8,128)(2,1)S(1)}, bf16[25,8,128]{2,1,0:T(8,128)(2,1)S(1)}, u32[]{:S(2)}, u32[]{:S(2)}) %collective-permute-start.4) | collective-permute-done | bytes 51232 | tf_op jit(solution)/shard_map/ppermute | solution.py:377
  85.0 2.8 %collective-permute-start.5 = (bf16[25,8,128]{2,1,0:T(8,128)(2,1)S(1)}, bf16[25,8,128]{2,1,0:T(8,128)(2,1)S(1)}, u32[]{:S(2)}, u32[]{:S(2)}) collective-permute-start(bf16[25,8,128]{2,1,0:T(8,128)(2,1)S(1)} %shard_map.147.a_ref), channel_id=1, source_target_pairs={{0,128},{64,192},{128,0},{192,64},{1,129},{65,193},{129,1},{193,65... | collective-permute-start | bytes 153608 | tf_op jit(solution)/shard_map/ppermute | solution.py:377
  87.8 2.0 %collective-permute-done.5.b_ref = bf16[25,8,128]{2,1,0:T(8,128)(2,1)S(1)} collective-permute-done((bf16[25,8,128]{2,1,0:T(8,128)(2,1)S(1)}, bf16[25,8,128]{2,1,0:T(8,128)(2,1)S(1)}, u32[]{:S(2)}, u32[]{:S(2)}) %collective-permute-start.5) | collective-permute-done | bytes 51232 | tf_op jit(solution)/shard_map/ppermute | solution.py:377
  89.8 1.4 %collective-permute-start.6 = (bf16[25,8,128]{2,1,0:T(8,128)(2,1)S(1)}, bf16[25,8,128]{2,1,0:T(8,128)(2,1)S(1)}, u32[]{:S(2)}, u32[]{:S(2)}) collective-permute-start(bf16[25,8,128]{2,1,0:T(8,128)(2,1)S(1)} %shard_map.148.a_ref), channel_id=1, source_target_pairs={{0,8},{8,0},{16,24},{24,16},{32,40},{40,32},{48,56},{56,48},{1,9},... | collective-permute-start | bytes 153608 | tf_op jit(solution)/shard_map/ppermute | solution.py:377
  91.2 5.6 %collective-permute-done.6.b_ref = bf16[25,8,128]{2,1,0:T(8,128)(2,1)S(1)} collective-permute-done((bf16[25,8,128]{2,1,0:T(8,128)(2,1)S(1)}, bf16[25,8,128]{2,1,0:T(8,128)(2,1)S(1)}, u32[]{:S(2)}, u32[]{:S(2)}) %collective-permute-start.6) | collective-permute-done | bytes 51232 | tf_op jit(solution)/shard_map/ppermute | solution.py:377
  96.9 0.7 collective-permute-start.7
  97.5 3.8 %collective-permute-start.8 = (bf16[25,8,128]{2,1,0:T(8,128)(2,1)S(1)}, bf16[25,8,128]{2,1,0:T(8,128)(2,1)S(1)}, u32[]{:S(2)}, u32[]{:S(2)}) collective-permute-start(bf16[25,8,128]{2,1,0:T(8,128)(2,1)S(1)} %shard_map.149.refs_0_), channel_id=1, source_target_pairs={{0,32},{8,40},{16,48},{24,56},{32,0},{40,8},{48,16},{56,24},{1,33}... | collective-permute-start | bytes 153608 | tf_op jit(solution)/shard_map/ppermute | solution.py:371
  101.3 3.5 %collective-permute-start.9 = (bf16[25,8,128]{2,1,0:T(8,128)(2,1)S(1)}, bf16[25,8,128]{2,1,0:T(8,128)(2,1)S(1)}, u32[]{:S(2)}, u32[]{:S(2)}) collective-permute-start(bf16[25,8,128]{2,1,0:T(8,128)(2,1)S(1)} %shard_map.149.refs_0_), channel_id=1, source_target_pairs={{0,48},{8,56},{16,0},{24,8},{32,16},{40,24},{48,32},{56,40},{1,49}... | collective-permute-start | bytes 153608 | tf_op jit(solution)/shard_map/ppermute | solution.py:371
  104.8 0.9 shard_map.150.a_ref
  105.7 0.5 collective-permute-done.9.refs_3_
  106.2 0.6 shard_map.151.refs_0_
  106.8 2.8 %collective-permute-start.10 = (bf16[4,25,8,128]{3,2,1,0:T(8,128)(2,1)S(1)}, bf16[4,25,8,128]{3,2,1,0:T(8,128)(2,1)S(1)}, u32[]{:S(2)}, u32[]{:S(2)}) collective-permute-start(bf16[4,25,8,128]{3,2,1,0:T(8,128)(2,1)S(1)} %shard_map.151.refs_0_), channel_id=1, source_target_pairs={{0,2},{2,4},{4,6},{6,0},{1,3},{3,5},{5,7},{7,1},{8,10},{10,12},{12... | collective-permute-start | bytes 614408 | tf_op jit(solution)/shard_map/ppermute | solution.py:371
  109.6 0.9 collective-permute-start.11
  110.5 2.0 %collective-permute-start.12 = (bf16[4,25,8,128]{3,2,1,0:T(8,128)(2,1)S(1)}, bf16[4,25,8,128]{3,2,1,0:T(8,128)(2,1)S(1)}, u32[]{:S(2)}, u32[]{:S(2)}) collective-permute-start(bf16[4,25,8,128]{3,2,1,0:T(8,128)(2,1)S(1)} %shard_map.151.refs_0_), channel_id=1, source_target_pairs={{0,6},{2,0},{4,2},{6,4},{1,7},{3,1},{5,3},{7,5},{8,14},{10,8},{12,... | collective-permute-start | bytes 614408 | tf_op jit(solution)/shard_map/ppermute | solution.py:371
  112.5 1.2 collective-permute-start.13
  113.7 3.5 %collective-permute-start.14 = (bf16[4,25,8,128]{3,2,1,0:T(8,128)(2,1)S(1)}, bf16[4,25,8,128]{3,2,1,0:T(8,128)(2,1)S(1)}, u32[]{:S(2)}, u32[]{:S(2)}) collective-permute-start(bf16[4,25,8,128]{3,2,1,0:T(8,128)(2,1)S(1)} %shard_map.151.refs_0_), channel_id=1, source_target_pairs={{0,1},{1,0},{2,3},{3,2},{4,5},{5,4},{6,7},{7,6},{8,9},{9,8},{10,11... | collective-permute-start | bytes 614408 | tf_op jit(solution)/shard_map/ppermute | solution.py:377
  117.2 2.6 %shard_map.152 = (bf16[256,1024]{1,0:T(8,128)(2,1)}, bf16[256,1024]{1,0:T(8,128)(2,1)}) custom-call(bf16[4,16,32,256]{3,2,1,0:T(8,128)(2,1)S(1)} %bitcast.12, bf16[256,1024]{1,0:T(8,128)(2,1)S(1)} %bitcast.15, bf16[256,1024]{1,0:T(8,128)(2,1)S(1)} %bitcast.17, f32[1,1024]{1,0:T(1,128)S(1)} %bitcast.20, bf16[4,256,256]{2,1,0:T(8,128)(2,1)S(1)} %copy-done, ...), custom_call_target="tpu_custom_call" | custom-call | flops 600000000 | bytes 8000000 | tf_op jit(solution)/shard_map/pallas_call | solution.py:348
  119.9 0.9 collective-permute-start.15
  120.8 0.1 collective-permute-start.16
  120.9 0.4 collective-permute-start.17
  121.4 2.8 %collective-permute-start.18 = (bf16[256,256]{1,0:T(8,128)(2,1)S(1)}, bf16[256,256]{1,0:T(8,128)(2,1)S(1)}, u32[]{:S(2)}, u32[]{:S(2)}) collective-permute-start(bf16[256,256]{1,0:T(8,128)(2,1)S(1)} %shard_map.153.a_ref), channel_id=1, source_target_pairs={{0,128},{64,192},{128,0},{192,64},{1,129},{65,193},{129,1},{193,65... | collective-permute-start | bytes 393224 | tf_op jit(solution)/shard_map/ppermute | solution.py:377
  124.1 2.5 %shard_map.154 = (f32[4,256,256]{2,1,0:T(8,128)}, f32[4,256,256]{2,1,0:T(8,128)}, f32[4,256,256]{2,1,0:T(8,128)}, f32[1,1024]{1,0:T(1,128)}, f32[6,2,2,1024]{3,2,1,0:T(2,128)}) custom-call(s32[3]{0:T(128)S(1)} %copy-done.8, bf16[4,256,256]{2,1,0:T(8,128)(2,1)S(1)} %copy-done, bf16[4,256,256]{2,1,0:T(8,128)(2,1)S(1)} %copy-done.2, f32[1,1024]{1,0:T(1,128)S(1)} %bitcast.21, ...), custom_call_target="tpu_custom_call" | custom-call | bytes 5000000 | tf_op jit(solution)/shard_map/pallas_call | solution.py:348
  126.7 1.3 collective-permute-done.18.b_ref
  127.9 0.7 shard_map.155
  (28 shorter events, 0.2 us)
Async XLA Ops:
  4.1 52.3 %all-to-all-start = ((bf16[64,48,256]{2,1,0:T(8,128)(2,1)}), bf16[64,48,256]{2,1,0:T(8,128)(2,1)}, u32[]{:S(2)}, u32[]{:S(2)}) async-start(bf16[64,48,256]{2,1,0:T(8,128)(2,1)} %bitcast.22), calls=%async_computation | async-start | bytes 3145728 | tf_op jit(solution)/shard_map/all_to_all | solution.py:405
  64.6 6.7 %copy-start.9 = (bf16[4,25,8,128]{3,2,1,0:T(8,128)(2,1)S(1)}, bf16[4,25,8,128]{3,2,1,0:T(8,128)(2,1)}, u32[]{:S(2)}) copy-start(bf16[4,25,8,128]{3,2,1,0:T(8,128)(2,1)} %get-tuple-element.38) | copy-start | bytes 614404
  64.6 8.3 %copy-start.6 = (f32[4,25,8,128]{3,2,1,0:T(8,128)S(1)}, f32[4,25,8,128]{3,2,1,0:T(8,128)}, u32[]{:S(2)}) copy-start(f32[4,25,8,128]{3,2,1,0:T(8,128)} %get-tuple-element.37.keep_ref) | copy-start | bytes 1228804
  64.6 8.3 %copy-start.8 = (s32[3]{0:T(128)S(1)}, s32[3]{0:T(128)}, u32[]{:S(2)}) copy-start(s32[3]{0:T(128)} %pad_add_fusion.place_ref) | copy-start | bytes 40
  64.6 40.2 %copy-start = (bf16[4,256,256]{2,1,0:T(8,128)(2,1)S(1)}, bf16[4,256,256]{2,1,0:T(8,128)(2,1)}, u32[]{:S(2)}) copy-start(bf16[4,256,256]{2,1,0:T(8,128)(2,1)} %wu_ref.5) | copy-start | bytes 1572868
  64.6 40.2 %copy-start.1 = (bf16[1,256,1024]{2,1,0:T(8,128)(2,1)S(1)}, bf16[1,256,1024]{2,1,0:T(8,128)(2,1)}, u32[]{:S(2)}) copy-start(bf16[1,256,1024]{2,1,0:T(8,128)(2,1)} %param.8) | copy-start | bytes 1572868
  64.7 40.2 %copy-start.7 = (f32[1024]{0:T(1024)S(1)}, f32[1024]{0:T(1024)}, u32[]{:S(2)}) copy-start(f32[1024]{0:T(1024)} %param.10) | copy-start | bytes 12292
  64.7 40.1 %all-to-all-start.1 = ((bf16[64,32,256]{2,1,0:T(8,128)(2,1)}), bf16[64,32,256]{2,1,0:T(8,128)(2,1)S(1)}, u32[]{:S(2)}, u32[]{:S(2)}) async-start(bf16[64,32,256]{2,1,0:T(8,128)(2,1)} %get-tuple-element.36), calls=%async_computation.1 | async-start | bytes 2097152 | tf_op jit(solution)/shard_map/all_to_all | solution.py:440
  71.3 1.6 %collective-permute-start = (bf16[4,25,8,128]{3,2,1,0:T(8,128)(2,1)S(1)}, bf16[4,25,8,128]{3,2,1,0:T(8,128)(2,1)S(1)}, u32[]{:S(2)}, u32[]{:S(2)}) collective-permute-start(bf16[4,25,8,128]{3,2,1,0:T(8,128)(2,1)S(1)} %copy-done.9), channel_id=1, source_target_pairs={{0,1},{1,0},{2,3},{3,2},{4,5},{5,4},{6,7},{7,6},{8,9},{9,8},{10,11... | collective-permute-start | bytes 614408 | tf_op jit(solution)/shard_map/ppermute | solution.py:377
  73.5 5.1 %collective-permute-start.1 = (bf16[25,8,128]{2,1,0:T(8,128)(2,1)S(1)}, bf16[25,8,128]{2,1,0:T(8,128)(2,1)S(1)}, u32[]{:S(2)}, u32[]{:S(2)}) collective-permute-start(bf16[25,8,128]{2,1,0:T(8,128)(2,1)S(1)} %get-tuple-element.40), channel_id=1, source_target_pairs={{0,2},{2,4},{4,6},{6,0},{1,3},{3,5},{5,7},{7,1},{8,10},{10,12},{12... | collective-permute-start | bytes 153608 | tf_op jit(solution)/shard_map/ppermute | solution.py:371
  74.9 6.6 %collective-permute-start.2 = (bf16[25,8,128]{2,1,0:T(8,128)(2,1)S(1)}, bf16[25,8,128]{2,1,0:T(8,128)(2,1)S(1)}, u32[]{:S(2)}, u32[]{:S(2)}) collective-permute-start(bf16[25,8,128]{2,1,0:T(8,128)(2,1)S(1)} %get-tuple-element.41), channel_id=1, source_target_pairs={{0,4},{2,6},{4,0},{6,2},{1,5},{3,7},{5,1},{7,3},{8,12},{10,14},{12... | collective-permute-start | bytes 153608 | tf_op jit(solution)/shard_map/ppermute | solution.py:371
  77.3 4.2 %collective-permute-start.3 = (bf16[25,8,128]{2,1,0:T(8,128)(2,1)S(1)}, bf16[25,8,128]{2,1,0:T(8,128)(2,1)S(1)}, u32[]{:S(2)}, u32[]{:S(2)}) collective-permute-start(bf16[25,8,128]{2,1,0:T(8,128)(2,1)S(1)} %get-tuple-element.42), channel_id=1, source_target_pairs={{0,6},{2,0},{4,2},{6,4},{1,7},{3,1},{5,3},{7,5},{8,14},{10,8},{12,... | collective-permute-start | bytes 153608 | tf_op jit(solution)/shard_map/ppermute | solution.py:371
  81.6 35.6 %copy-start.2 = (bf16[4,256,256]{2,1,0:T(8,128)(2,1)S(1)}, bf16[4,256,256]{2,1,0:T(8,128)(2,1)}, u32[]{:S(2)}) copy-start(bf16[4,256,256]{2,1,0:T(8,128)(2,1)} %wv_ref.3) | copy-start | bytes 1572868
  81.6 35.6 %copy-start.3 = (bf16[1,256,1024]{2,1,0:T(8,128)(2,1)S(1)}, bf16[1,256,1024]{2,1,0:T(8,128)(2,1)}, u32[]{:S(2)}) copy-start(bf16[1,256,1024]{2,1,0:T(8,128)(2,1)} %param.9) | copy-start | bytes 1572868
  81.6 35.6 %copy-start.5 = (bf16[256,256]{1,0:T(8,128)(2,1)S(1)}, bf16[256,256]{1,0:T(8,128)(2,1)}, u32[]{:S(2)}) copy-start(bf16[256,256]{1,0:T(8,128)(2,1)} %local_ref.1) | copy-start | bytes 393220
  81.6 3.3 %collective-permute-start.4 = (bf16[25,8,128]{2,1,0:T(8,128)(2,1)S(1)}, bf16[25,8,128]{2,1,0:T(8,128)(2,1)S(1)}, u32[]{:S(2)}, u32[]{:S(2)}) collective-permute-start(bf16[25,8,128]{2,1,0:T(8,128)(2,1)S(1)} %shard_map.146.a_ref), channel_id=1, source_target_pairs={{0,64},{64,0},{128,192},{192,128},{1,65},{65,1},{129,193},{193,129... | collective-permute-start | bytes 153608 | tf_op jit(solution)/shard_map/ppermute | solution.py:377
  85.0 4.8 %collective-permute-start.5 = (bf16[25,8,128]{2,1,0:T(8,128)(2,1)S(1)}, bf16[25,8,128]{2,1,0:T(8,128)(2,1)S(1)}, u32[]{:S(2)}, u32[]{:S(2)}) collective-permute-start(bf16[25,8,128]{2,1,0:T(8,128)(2,1)S(1)} %shard_map.147.a_ref), channel_id=1, source_target_pairs={{0,128},{64,192},{128,0},{192,64},{1,129},{65,193},{129,1},{193,65... | collective-permute-start | bytes 153608 | tf_op jit(solution)/shard_map/ppermute | solution.py:377
  89.8 7.0 %collective-permute-start.6 = (bf16[25,8,128]{2,1,0:T(8,128)(2,1)S(1)}, bf16[25,8,128]{2,1,0:T(8,128)(2,1)S(1)}, u32[]{:S(2)}, u32[]{:S(2)}) collective-permute-start(bf16[25,8,128]{2,1,0:T(8,128)(2,1)S(1)} %shard_map.148.a_ref), channel_id=1, source_target_pairs={{0,8},{8,0},{16,24},{24,16},{32,40},{40,32},{48,56},{56,48},{1,9},... | collective-permute-start | bytes 153608 | tf_op jit(solution)/shard_map/ppermute | solution.py:377
  96.9 8.8 %collective-permute-start.7 = (bf16[25,8,128]{2,1,0:T(8,128)(2,1)S(1)}, bf16[25,8,128]{2,1,0:T(8,128)(2,1)S(1)}, u32[]{:S(2)}, u32[]{:S(2)}) collective-permute-start(bf16[25,8,128]{2,1,0:T(8,128)(2,1)S(1)} %shard_map.149.refs_0_), channel_id=1, source_target_pairs={{0,16},{8,24},{16,32},{24,40},{32,48},{40,56},{48,0},{56,8},{1,17}... | collective-permute-start | bytes 153608 | tf_op jit(solution)/shard_map/ppermute | solution.py:371
  97.5 8.2 %collective-permute-start.8 = (bf16[25,8,128]{2,1,0:T(8,128)(2,1)S(1)}, bf16[25,8,128]{2,1,0:T(8,128)(2,1)S(1)}, u32[]{:S(2)}, u32[]{:S(2)}) collective-permute-start(bf16[25,8,128]{2,1,0:T(8,128)(2,1)S(1)} %shard_map.149.refs_0_), channel_id=1, source_target_pairs={{0,32},{8,40},{16,48},{24,56},{32,0},{40,8},{48,16},{56,24},{1,33}... | collective-permute-start | bytes 153608 | tf_op jit(solution)/shard_map/ppermute | solution.py:371
  101.3 4.9 %collective-permute-start.9 = (bf16[25,8,128]{2,1,0:T(8,128)(2,1)S(1)}, bf16[25,8,128]{2,1,0:T(8,128)(2,1)S(1)}, u32[]{:S(2)}, u32[]{:S(2)}) collective-permute-start(bf16[25,8,128]{2,1,0:T(8,128)(2,1)S(1)} %shard_map.149.refs_0_), channel_id=1, source_target_pairs={{0,48},{8,56},{16,0},{24,8},{32,16},{40,24},{48,32},{56,40},{1,49}... | collective-permute-start | bytes 153608 | tf_op jit(solution)/shard_map/ppermute | solution.py:371
  104.8 12.4 %copy-start.4 = (bf16[4,256,256]{2,1,0:T(8,128)(2,1)S(1)}, bf16[4,256,256]{2,1,0:T(8,128)(2,1)}, u32[]{:S(2)}) copy-start(bf16[4,256,256]{2,1,0:T(8,128)(2,1)} %wo_ref.1) | copy-start | bytes 1572868
  106.8 13.1 %collective-permute-start.10 = (bf16[4,25,8,128]{3,2,1,0:T(8,128)(2,1)S(1)}, bf16[4,25,8,128]{3,2,1,0:T(8,128)(2,1)S(1)}, u32[]{:S(2)}, u32[]{:S(2)}) collective-permute-start(bf16[4,25,8,128]{3,2,1,0:T(8,128)(2,1)S(1)} %shard_map.151.refs_0_), channel_id=1, source_target_pairs={{0,2},{2,4},{4,6},{6,0},{1,3},{3,5},{5,7},{7,1},{8,10},{10,12},{12... | collective-permute-start | bytes 614408 | tf_op jit(solution)/shard_map/ppermute | solution.py:371
  109.6 10.3 %collective-permute-start.11 = (bf16[4,25,8,128]{3,2,1,0:T(8,128)(2,1)S(1)}, bf16[4,25,8,128]{3,2,1,0:T(8,128)(2,1)S(1)}, u32[]{:S(2)}, u32[]{:S(2)}) collective-permute-start(bf16[4,25,8,128]{3,2,1,0:T(8,128)(2,1)S(1)} %shard_map.151.refs_0_), channel_id=1, source_target_pairs={{0,4},{2,6},{4,0},{6,2},{1,5},{3,7},{5,1},{7,3},{8,12},{10,14},{12... | collective-permute-start | bytes 614408 | tf_op jit(solution)/shard_map/ppermute | solution.py:371
  110.5 9.4 %collective-permute-start.12 = (bf16[4,25,8,128]{3,2,1,0:T(8,128)(2,1)S(1)}, bf16[4,25,8,128]{3,2,1,0:T(8,128)(2,1)S(1)}, u32[]{:S(2)}, u32[]{:S(2)}) collective-permute-start(bf16[4,25,8,128]{3,2,1,0:T(8,128)(2,1)S(1)} %shard_map.151.refs_0_), channel_id=1, source_target_pairs={{0,6},{2,0},{4,2},{6,4},{1,7},{3,1},{5,3},{7,5},{8,14},{10,8},{12,... | collective-permute-start | bytes 614408 | tf_op jit(solution)/shard_map/ppermute | solution.py:371
  112.5 7.3 %collective-permute-start.13 = (bf16[256,256]{1,0:T(8,128)(2,1)S(1)}, bf16[256,256]{1,0:T(8,128)(2,1)S(1)}, u32[]{:S(2)}, u32[]{:S(2)}) collective-permute-start(bf16[256,256]{1,0:T(8,128)(2,1)S(1)} %shard_map.150.a_ref), channel_id=1, source_target_pairs={{0,64},{64,0},{128,192},{192,128},{1,65},{65,1},{129,193},{193,129... | collective-permute-start | bytes 393224 | tf_op jit(solution)/shard_map/ppermute | solution.py:377
  113.7 10.4 %collective-permute-start.14 = (bf16[4,25,8,128]{3,2,1,0:T(8,128)(2,1)S(1)}, bf16[4,25,8,128]{3,2,1,0:T(8,128)(2,1)S(1)}, u32[]{:S(2)}, u32[]{:S(2)}) collective-permute-start(bf16[4,25,8,128]{3,2,1,0:T(8,128)(2,1)S(1)} %shard_map.151.refs_0_), channel_id=1, source_target_pairs={{0,1},{1,0},{2,3},{3,2},{4,5},{5,4},{6,7},{7,6},{8,9},{9,8},{10,11... | collective-permute-start | bytes 614408 | tf_op jit(solution)/shard_map/ppermute | solution.py:377
  119.9 4.2 %collective-permute-start.15 = (bf16[4,25,8,128]{3,2,1,0:T(8,128)(2,1)S(1)}, bf16[4,25,8,128]{3,2,1,0:T(8,128)(2,1)S(1)}, u32[]{:S(2)}, u32[]{:S(2)}) collective-permute-start(bf16[4,25,8,128]{3,2,1,0:T(8,128)(2,1)S(1)} %collective-permute-done.10.refs_1_), channel_id=1, source_target_pairs={{0,1},{1,0},{2,3},{3,2},{4,5},{5,4},{6,7},{7,6},{8,9},{9,8},{10,11... | collective-permute-start | bytes 614408 | tf_op jit(solution)/shard_map/ppermute | solution.py:377
  120.8 3.3 %collective-permute-start.16 = (bf16[4,25,8,128]{3,2,1,0:T(8,128)(2,1)S(1)}, bf16[4,25,8,128]{3,2,1,0:T(8,128)(2,1)S(1)}, u32[]{:S(2)}, u32[]{:S(2)}) collective-permute-start(bf16[4,25,8,128]{3,2,1,0:T(8,128)(2,1)S(1)} %collective-permute-done.11.refs_2_), channel_id=1, source_target_pairs={{0,1},{1,0},{2,3},{3,2},{4,5},{5,4},{6,7},{7,6},{8,9},{9,8},{10,11... | collective-permute-start | bytes 614408 | tf_op jit(solution)/shard_map/ppermute | solution.py:377
  120.9 3.2 %collective-permute-start.17 = (bf16[4,25,8,128]{3,2,1,0:T(8,128)(2,1)S(1)}, bf16[4,25,8,128]{3,2,1,0:T(8,128)(2,1)S(1)}, u32[]{:S(2)}, u32[]{:S(2)}) collective-permute-start(bf16[4,25,8,128]{3,2,1,0:T(8,128)(2,1)S(1)} %collective-permute-done.12.refs_3_), channel_id=1, source_target_pairs={{0,1},{1,0},{2,3},{3,2},{4,5},{5,4},{6,7},{7,6},{8,9},{9,8},{10,11... | collective-permute-start | bytes 614408 | tf_op jit(solution)/shard_map/ppermute | solution.py:377
  121.4 6.6 %collective-permute-start.18 = (bf16[256,256]{1,0:T(8,128)(2,1)S(1)}, bf16[256,256]{1,0:T(8,128)(2,1)S(1)}, u32[]{:S(2)}, u32[]{:S(2)}) collective-permute-start(bf16[256,256]{1,0:T(8,128)(2,1)S(1)} %shard_map.153.a_ref), channel_id=1, source_target_pairs={{0,128},{64,192},{128,0},{192,64},{1,129},{65,193},{129,1},{193,65... | collective-permute-start | bytes 393224 | tf_op jit(solution)/shard_map/ppermute | solution.py:377

commit v12 on v11

--- a/solution.py
+++ b/solution.py
@@ -453,8 +453,8 @@
     part = call(local_kernel, [((BLK, BLK), BF)], flops=1.3e8, moved=1.2e6)(
         recv2, x, gain2, w_u
     )[0]
-    got_z, part = lax.optimization_barrier((got_z, part))
-    pair = call(pair_sum_kernel, [((BLK, BLK), BF)], moved=4e5)(part, swapped(part, "dp", 1))[0]
+    got_z, part, got_part = lax.optimization_barrier((got_z, part, swapped(part, "dp", 1)))
+    pair = call(pair_sum_kernel, [((BLK, BLK), BF)], moved=4e5)(part, got_part)[0]
     other_pair = swapped(pair, "dp", 2)
     mine_y = call(gather_kernel, [((4,) + quarter, BF)], moved=4e5, smem=(0,))(
         place, slice_, *got_z

time: 129 us -> 137 us (1.062)
  waiting for transfers between devices: 54 us -> 68.4 us
  starting transfers between devices: 53.5 us -> 46.7 us
    ppermute x9, waiting for transfers between devices: 3.57 us -> 15 us  [rotated(): lax.ppermute(value, axis, [(s, (s + k * step) % n) for s in range(n)])]
    ppermute x9, starting transfers between devices: 18.6 us -> 13 us  [rotated(): lax.ppermute(value, axis, [(s, (s + k * step) % n) for s in range(n)])]
    all_to_all x1, waiting for transfers between devices: 0.01 us -> 2.7 us  [per_device(): recv2 = lax.all_to_all(back, SEQ, 0, 0).reshape(GROUPS, 16, 2 * PL, BLK)]
  transfers between devices with their start and end apart: 21 -> 21, of which waited for: 9 -> 12; matrix products, arithmetic and copies ran while one was open for 0% -> 0% of each run, Pallas kernels for 5% -> 4%
where the time goes in v12:
time: 137 us; the launch traced here: 136 us
  waiting for transfers between devices  68.4 us (50%)
  starting transfers between devices  46.7 us (34%)
  Pallas kernels  19.7 us (14%)
    all_to_all x1, waiting for transfers between devices, per_device(): recv = lax.all_to_all(send.reshape(BLOCKS, 3 * PL, BLK), SEQ, 0, 0)  38.3 us
    pallas_call x13, Pallas kernels, run(): pl.pallas_call(kernel, out_shape=shapes, in_specs=specs, out_specs=[pl.Bl...  19.7 us
    ppermute x9, waiting for transfers between devices, rotated(): lax.ppermute(value, axis, [(s, (s + k * step) % n) for s in range(n)])  15 us
    ppermute x10, starting transfers between devices, swapped(): lax.ppermute(value, axis, [(s, s ^ bit) for s in range(lax.axis_size(axis...  13.8 us
    all_to_all x1, starting transfers between devices, per_device(): recv = lax.all_to_all(send.reshape(BLOCKS, 3 * PL, BLK), SEQ, 0, 0)  13.3 us
    ppermute x9, starting transfers between devices, rotated(): lax.ppermute(value, axis, [(s, (s + k * step) % n) for s in range(n)])  13 us
    ppermute x10, waiting for transfers between devices, swapped(): lax.ppermute(value, axis, [(s, s ^ bit) for s in range(lax.axis_size(axis...  12.4 us
    all_to_all x1, starting transfers between devices, per_device(): recv2 = lax.all_to_all(back, SEQ, 0, 0).reshape(GROUPS, 16, 2 * PL, BLK)  6.61 us
  transfers between devices with their start and end apart: 21, of which 12 were waited for; matrix products, arithmetic and copies ran while one was open for 0% of the time, Pallas kernels for 4%

profile of v12, /device:TPU:1, one launch (start us, length us, event | category | flops | bytes accessed | tf_op | source)
XLA Modules:
  0.0 136.3 jit_solution(10264575646770371277)
XLA Ops:
  0.6 3.4 %shard_map.143 = bf16[4,16,48,256]{3,2,1,0:T(8,128)(2,1)} custom-call(bf16[256,1024]{1,0:T(8,128)(2,1)} %bitcast.13, bf16[256,1024]{1,0:T(8,128)(2,1)} %bitcast.16, f32[1,1024]{1,0:T(1,128)} %bitcast.18, bf16[256,256]{1,0:T(8,128)(2,1)} %local_ref.1), custom_call_target="tpu_custom_call" | custom-call | flops 140000000 | bytes 4000000 | tf_op jit(solution)/shard_map/pallas_call | solution.py:348
  4.1 13.3 %all-to-all-start = ((bf16[64,48,256]{2,1,0:T(8,128)(2,1)}), bf16[64,48,256]{2,1,0:T(8,128)(2,1)}, u32[]{:S(2)}, u32[]{:S(2)}) async-start(bf16[64,48,256]{2,1,0:T(8,128)(2,1)} %bitcast.22), calls=%async_computation | async-start | bytes 3145728 | tf_op jit(solution)/shard_map/all_to_all | solution.py:405
  17.4 0.6 pad_add_fusion.place_ref
  18.0 38.3 %all-to-all-done.recv_hbm = bf16[64,48,256]{2,1,0:T(8,128)(2,1)} async-done(((bf16[64,48,256]{2,1,0:T(8,128)(2,1)}), bf16[64,48,256]{2,1,0:T(8,128)(2,1)}, u32[]{:S(2)}, u32[]{:S(2)}) %all-to-all-start) | async-done | bytes 1572896 | tf_op jit(solution)/shard_map/all_to_all | solution.py:405
  56.4 8.2 %shard_map.144 = (bf16[64,32,256]{2,1,0:T(8,128)(2,1)}, f32[4,25,8,128]{3,2,1,0:T(8,128)}, bf16[4,25,8,128]{3,2,1,0:T(8,128)(2,1)}) custom-call(s32[3]{0:T(128)} %pad_add_fusion.place_ref, bf16[64,48,256]{2,1,0:T(8,128)(2,1)} %all-to-all-done.recv_hbm, f32[6,2,2,1024]{3,2,1,0:T(2,128)} %coef_hbm.1, bf16[4,256,256]{2,1,0:T(8,128)(2,1)} %wu_ref.5, ...), custom_call_target="tpu_custom_call" | custom-call | flops 800000000 | bytes 4000000 | tf_op jit(solution)/shard_map/pallas_call | solution.py:348
  64.6 0.0 copy-start.9
  64.6 0.0 copy-start.6
  64.6 0.0 copy-start.8
  64.6 0.0 copy-start
  64.7 0.0 copy-start.7
  64.7 6.6 %all-to-all-start.1 = ((bf16[64,32,256]{2,1,0:T(8,128)(2,1)}), bf16[64,32,256]{2,1,0:T(8,128)(2,1)S(1)}, u32[]{:S(2)}, u32[]{:S(2)}) async-start(bf16[64,32,256]{2,1,0:T(8,128)(2,1)} %get-tuple-element.37), calls=%async_computation.1 | async-start | bytes 2097152 | tf_op jit(solution)/shard_map/all_to_all | solution.py:440
  71.3 0.5 collective-permute-start
  71.8 1.1 collective-permute-done.got_ref
  72.9 0.6 shard_map.145
  73.5 1.4 %collective-permute-start.1 = (bf16[25,8,128]{2,1,0:T(8,128)(2,1)S(1)}, bf16[25,8,128]{2,1,0:T(8,128)(2,1)S(1)}, u32[]{:S(2)}, u32[]{:S(2)}) collective-permute-start(bf16[25,8,128]{2,1,0:T(8,128)(2,1)S(1)} %get-tuple-element.41), channel_id=1, source_target_pairs={{0,2},{2,4},{4,6},{6,0},{1,3},{3,5},{5,7},{7,1},{8,10},{10,12},{12... | collective-permute-start | bytes 153608 | tf_op jit(solution)/shard_map/ppermute | solution.py:371
  74.9 2.4 %collective-permute-start.2 = (bf16[25,8,128]{2,1,0:T(8,128)(2,1)S(1)}, bf16[25,8,128]{2,1,0:T(8,128)(2,1)S(1)}, u32[]{:S(2)}, u32[]{:S(2)}) collective-permute-start(bf16[25,8,128]{2,1,0:T(8,128)(2,1)S(1)} %get-tuple-element.42), channel_id=1, source_target_pairs={{0,4},{2,6},{4,0},{6,2},{1,5},{3,7},{5,1},{7,3},{8,12},{10,14},{12... | collective-permute-start | bytes 153608 | tf_op jit(solution)/shard_map/ppermute | solution.py:371
  77.3 1.2 collective-permute-start.3
  78.5 0.1 collective-permute-done.1.refs_0_
  78.6 3.0 %collective-permute-done.2.refs_1_ = bf16[25,8,128]{2,1,0:T(8,128)(2,1)S(1)} collective-permute-done((bf16[25,8,128]{2,1,0:T(8,128)(2,1)S(1)}, bf16[25,8,128]{2,1,0:T(8,128)(2,1)S(1)}, u32[]{:S(2)}, u32[]{:S(2)}) %collective-permute-start.2) | collective-permute-done | bytes 51232 | tf_op jit(solution)/shard_map/ppermute | solution.py:371
  81.6 0.0 copy-start.2
  81.6 0.0 copy-start.3
  81.6 1.3 collective-permute-start.4
  82.9 2.0 %collective-permute-done.4.b_ref = bf16[25,8,128]{2,1,0:T(8,128)(2,1)S(1)} collective-permute-done((bf16[25,8,128]{2,1,0:T(8,128)(2,1)S(1)}, bf16[25,8,128]{2,1,0:T(8,128)(2,1)S(1)}, u32[]{:S(2)}, u32[]{:S(2)}) %collective-permute-start.4) | collective-permute-done | bytes 51232 | tf_op jit(solution)/shard_map/ppermute | solution.py:377
  85.0 2.8 %collective-permute-start.5 = (bf16[25,8,128]{2,1,0:T(8,128)(2,1)S(1)}, bf16[25,8,128]{2,1,0:T(8,128)(2,1)S(1)}, u32[]{:S(2)}, u32[]{:S(2)}) collective-permute-start(bf16[25,8,128]{2,1,0:T(8,128)(2,1)S(1)} %shard_map.147.a_ref), channel_id=1, source_target_pairs={{0,128},{64,192},{128,0},{192,64},{1,129},{65,193},{129,1},{193,65... | collective-permute-start | bytes 153608 | tf_op jit(solution)/shard_map/ppermute | solution.py:377
  87.8 2.0 %collective-permute-done.5.b_ref = bf16[25,8,128]{2,1,0:T(8,128)(2,1)S(1)} collective-permute-done((bf16[25,8,128]{2,1,0:T(8,128)(2,1)S(1)}, bf16[25,8,128]{2,1,0:T(8,128)(2,1)S(1)}, u32[]{:S(2)}, u32[]{:S(2)}) %collective-permute-start.5) | collective-permute-done | bytes 51232 | tf_op jit(solution)/shard_map/ppermute | solution.py:377
  89.8 1.4 collective-permute-start.6
  91.2 5.6 %collective-permute-done.6.b_ref = bf16[25,8,128]{2,1,0:T(8,128)(2,1)S(1)} collective-permute-done((bf16[25,8,128]{2,1,0:T(8,128)(2,1)S(1)}, bf16[25,8,128]{2,1,0:T(8,128)(2,1)S(1)}, u32[]{:S(2)}, u32[]{:S(2)}) %collective-permute-start.6) | collective-permute-done | bytes 51232 | tf_op jit(solution)/shard_map/ppermute | solution.py:377
  96.9 2.7 %all-to-all-done.1 = bf16[64,32,256]{2,1,0:T(8,128)(2,1)S(1)} async-done(((bf16[64,32,256]{2,1,0:T(8,128)(2,1)}), bf16[64,32,256]{2,1,0:T(8,128)(2,1)S(1)}, u32[]{:S(2)}, u32[]{:S(2)}) %all-to-all-start.1) | async-done | bytes 1048608 | tf_op jit(solution)/shard_map/all_to_all | solution.py:440
  99.6 0.9 shard_map.150.a_ref
  100.5 1.3 collective-permute-start.10
  101.7 0.7 collective-permute-start.7
  102.5 3.9 %collective-permute-start.8 = (bf16[25,8,128]{2,1,0:T(8,128)(2,1)S(1)}, bf16[25,8,128]{2,1,0:T(8,128)(2,1)S(1)}, u32[]{:S(2)}, u32[]{:S(2)}) collective-permute-start(bf16[25,8,128]{2,1,0:T(8,128)(2,1)S(1)} %shard_map.149.refs_0_), channel_id=1, source_target_pairs={{0,32},{8,40},{16,48},{24,56},{32,0},{40,8},{48,16},{56,24},{1,33}... | collective-permute-start | bytes 153608 | tf_op jit(solution)/shard_map/ppermute | solution.py:371
  106.4 0.7 collective-permute-start.9
  107.0 2.8 %collective-permute-done.8.refs_2_ = bf16[25,8,128]{2,1,0:T(8,128)(2,1)S(1)} collective-permute-done((bf16[25,8,128]{2,1,0:T(8,128)(2,1)S(1)}, bf16[25,8,128]{2,1,0:T(8,128)(2,1)S(1)}, u32[]{:S(2)}, u32[]{:S(2)}) %collective-permute-start.8) | collective-permute-done | bytes 51232 | tf_op jit(solution)/shard_map/ppermute | solution.py:371
  109.8 4.3 %collective-permute-done.9.refs_3_ = bf16[25,8,128]{2,1,0:T(8,128)(2,1)S(1)} collective-permute-done((bf16[25,8,128]{2,1,0:T(8,128)(2,1)S(1)}, bf16[25,8,128]{2,1,0:T(8,128)(2,1)S(1)}, u32[]{:S(2)}, u32[]{:S(2)}) %collective-permute-start.9) | collective-permute-done | bytes 51232 | tf_op jit(solution)/shard_map/ppermute | solution.py:371
  114.1 0.6 shard_map.151.refs_0_
  114.7 0.1 collective-permute-start.11
  114.8 0.1 collective-permute-start.12
  114.9 2.6 %collective-permute-start.13 = (bf16[4,25,8,128]{3,2,1,0:T(8,128)(2,1)S(1)}, bf16[4,25,8,128]{3,2,1,0:T(8,128)(2,1)S(1)}, u32[]{:S(2)}, u32[]{:S(2)}) collective-permute-start(bf16[4,25,8,128]{3,2,1,0:T(8,128)(2,1)S(1)} %shard_map.151.refs_0_), channel_id=1, source_target_pairs={{0,6},{2,0},{4,2},{6,4},{1,7},{3,1},{5,3},{7,5},{8,14},{10,8},{12,... | collective-permute-start | bytes 614408 | tf_op jit(solution)/shard_map/ppermute | solution.py:371
  117.4 2.6 %shard_map.152 = (bf16[256,1024]{1,0:T(8,128)(2,1)}, bf16[256,1024]{1,0:T(8,128)(2,1)}) custom-call(bf16[4,16,32,256]{3,2,1,0:T(8,128)(2,1)S(1)} %bitcast.12, bf16[256,1024]{1,0:T(8,128)(2,1)S(1)} %bitcast.15, bf16[256,1024]{1,0:T(8,128)(2,1)S(1)} %bitcast.17, f32[1,1024]{1,0:T(1,128)S(1)} %bitcast.20, bf16[4,256,256]{2,1,0:T(8,128)(2,1)S(1)} %copy-done, ...), custom_call_target="tpu_custom_call" | custom-call | flops 600000000 | bytes 8000000 | tf_op jit(solution)/shard_map/pallas_call | solution.py:348
  120.1 2.0 %collective-permute-start.14 = (bf16[4,25,8,128]{3,2,1,0:T(8,128)(2,1)S(1)}, bf16[4,25,8,128]{3,2,1,0:T(8,128)(2,1)S(1)}, u32[]{:S(2)}, u32[]{:S(2)}) collective-permute-start(bf16[4,25,8,128]{3,2,1,0:T(8,128)(2,1)S(1)} %shard_map.151.refs_0_), channel_id=1, source_target_pairs={{0,1},{1,0},{2,3},{3,2},{4,5},{5,4},{6,7},{7,6},{8,9},{9,8},{10,11... | collective-permute-start | bytes 614408 | tf_op jit(solution)/shard_map/ppermute | solution.py:377
  122.1 4.8 %collective-permute-done.11.refs_1_ = bf16[4,25,8,128]{3,2,1,0:T(8,128)(2,1)S(1)} collective-permute-done((bf16[4,25,8,128]{3,2,1,0:T(8,128)(2,1)S(1)}, bf16[4,25,8,128]{3,2,1,0:T(8,128)(2,1)S(1)}, u32[]{:S(2)}, u32[]{:S(2)}) %collective-permute-start.11) | collective-permute-done | bytes 204832 | tf_op jit(solution)/shard_map/ppermute | solution.py:371
  127.0 1.5 %collective-permute-start.15 = (bf16[4,25,8,128]{3,2,1,0:T(8,128)(2,1)S(1)}, bf16[4,25,8,128]{3,2,1,0:T(8,128)(2,1)S(1)}, u32[]{:S(2)}, u32[]{:S(2)}) collective-permute-start(bf16[4,25,8,128]{3,2,1,0:T(8,128)(2,1)S(1)} %collective-permute-done.11.refs_1_), channel_id=1, source_target_pairs={{0,1},{1,0},{2,3},{3,2},{4,5},{5,4},{6,7},{7,6},{8,9},{9,8},{10,11... | collective-permute-start | bytes 614408 | tf_op jit(solution)/shard_map/ppermute | solution.py:377
  128.5 0.5 collective-permute-start.17
  129.0 2.5 %collective-permute-start.18 = (bf16[256,256]{1,0:T(8,128)(2,1)S(1)}, bf16[256,256]{1,0:T(8,128)(2,1)S(1)}, u32[]{:S(2)}, u32[]{:S(2)}) collective-permute-start(bf16[256,256]{1,0:T(8,128)(2,1)S(1)} %shard_map.153.a_ref), channel_id=1, source_target_pairs={{0,128},{64,192},{128,0},{192,64},{1,129},{65,193},{129,1},{193,65... | collective-permute-start | bytes 393224 | tf_op jit(solution)/shard_map/ppermute | solution.py:377
  131.5 2.5 %shard_map.154 = (f32[4,256,256]{2,1,0:T(8,128)}, f32[4,256,256]{2,1,0:T(8,128)}, f32[4,256,256]{2,1,0:T(8,128)}, f32[1,1024]{1,0:T(1,128)}, f32[6,2,2,1024]{3,2,1,0:T(2,128)}) custom-call(s32[3]{0:T(128)S(1)} %copy-done.8, bf16[4,256,256]{2,1,0:T(8,128)(2,1)S(1)} %copy-done, bf16[4,256,256]{2,1,0:T(8,128)(2,1)S(1)} %copy-done.2, f32[1,1024]{1,0:T(1,128)S(1)} %bitcast.21, ...), custom_call_target="tpu_custom_call" | custom-call | bytes 5000000 | tf_op jit(solution)/shard_map/pallas_call | solution.py:348
  134.0 1.6 %collective-permute-done.18.b_ref = bf16[256,256]{1,0:T(8,128)(2,1)S(1)} collective-permute-done((bf16[256,256]{1,0:T(8,128)(2,1)S(1)}, bf16[256,256]{1,0:T(8,128)(2,1)S(1)}, u32[]{:S(2)}, u32[]{:S(2)}) %collective-permute-start.18) | collective-permute-done | bytes 131104 | tf_op jit(solution)/shard_map/ppermute | solution.py:377
  135.6 0.7 shard_map.155
  (28 shorter events, 0.2 us)
Async XLA Ops:
  4.1 52.3 %all-to-all-start = ((bf16[64,48,256]{2,1,0:T(8,128)(2,1)}), bf16[64,48,256]{2,1,0:T(8,128)(2,1)}, u32[]{:S(2)}, u32[]{:S(2)}) async-start(bf16[64,48,256]{2,1,0:T(8,128)(2,1)} %bitcast.22), calls=%async_computation | async-start | bytes 3145728 | tf_op jit(solution)/shard_map/all_to_all | solution.py:405
  64.6 6.7 %copy-start.9 = (bf16[4,25,8,128]{3,2,1,0:T(8,128)(2,1)S(1)}, bf16[4,25,8,128]{3,2,1,0:T(8,128)(2,1)}, u32[]{:S(2)}) copy-start(bf16[4,25,8,128]{3,2,1,0:T(8,128)(2,1)} %get-tuple-element.39) | copy-start | bytes 614404
  64.6 8.3 %copy-start.6 = (f32[4,25,8,128]{3,2,1,0:T(8,128)S(1)}, f32[4,25,8,128]{3,2,1,0:T(8,128)}, u32[]{:S(2)}) copy-start(f32[4,25,8,128]{3,2,1,0:T(8,128)} %get-tuple-element.38.keep_ref) | copy-start | bytes 1228804
  64.6 8.3 %copy-start.8 = (s32[3]{0:T(128)S(1)}, s32[3]{0:T(128)}, u32[]{:S(2)}) copy-start(s32[3]{0:T(128)} %pad_add_fusion.place_ref) | copy-start | bytes 40
  64.6 34.9 %copy-start = (bf16[4,256,256]{2,1,0:T(8,128)(2,1)S(1)}, bf16[4,256,256]{2,1,0:T(8,128)(2,1)}, u32[]{:S(2)}) copy-start(bf16[4,256,256]{2,1,0:T(8,128)(2,1)} %wu_ref.5) | copy-start | bytes 1572868
  64.6 34.9 %copy-start.1 = (bf16[1,256,1024]{2,1,0:T(8,128)(2,1)S(1)}, bf16[1,256,1024]{2,1,0:T(8,128)(2,1)}, u32[]{:S(2)}) copy-start(bf16[1,256,1024]{2,1,0:T(8,128)(2,1)} %param.8) | copy-start | bytes 1572868
  64.7 34.9 %copy-start.7 = (f32[1024]{0:T(1024)S(1)}, f32[1024]{0:T(1024)}, u32[]{:S(2)}) copy-start(f32[1024]{0:T(1024)} %param.10) | copy-start | bytes 12292
  64.7 34.9 %all-to-all-start.1 = ((bf16[64,32,256]{2,1,0:T(8,128)(2,1)}), bf16[64,32,256]{2,1,0:T(8,128)(2,1)S(1)}, u32[]{:S(2)}, u32[]{:S(2)}) async-start(bf16[64,32,256]{2,1,0:T(8,128)(2,1)} %get-tuple-element.37), calls=%async_computation.1 | async-start | bytes 2097152 | tf_op jit(solution)/shard_map/all_to_all | solution.py:440
  71.3 1.6 %collective-permute-start = (bf16[4,25,8,128]{3,2,1,0:T(8,128)(2,1)S(1)}, bf16[4,25,8,128]{3,2,1,0:T(8,128)(2,1)S(1)}, u32[]{:S(2)}, u32[]{:S(2)}) collective-permute-start(bf16[4,25,8,128]{3,2,1,0:T(8,128)(2,1)S(1)} %copy-done.9), channel_id=1, source_target_pairs={{0,1},{1,0},{2,3},{3,2},{4,5},{5,4},{6,7},{7,6},{8,9},{9,8},{10,11... | collective-permute-start | bytes 614408 | tf_op jit(solution)/shard_map/ppermute | solution.py:377
  73.5 5.1 %collective-permute-start.1 = (bf16[25,8,128]{2,1,0:T(8,128)(2,1)S(1)}, bf16[25,8,128]{2,1,0:T(8,128)(2,1)S(1)}, u32[]{:S(2)}, u32[]{:S(2)}) collective-permute-start(bf16[25,8,128]{2,1,0:T(8,128)(2,1)S(1)} %get-tuple-element.41), channel_id=1, source_target_pairs={{0,2},{2,4},{4,6},{6,0},{1,3},{3,5},{5,7},{7,1},{8,10},{10,12},{12... | collective-permute-start | bytes 153608 | tf_op jit(solution)/shard_map/ppermute | solution.py:371
  74.9 6.6 %collective-permute-start.2 = (bf16[25,8,128]{2,1,0:T(8,128)(2,1)S(1)}, bf16[25,8,128]{2,1,0:T(8,128)(2,1)S(1)}, u32[]{:S(2)}, u32[]{:S(2)}) collective-permute-start(bf16[25,8,128]{2,1,0:T(8,128)(2,1)S(1)} %get-tuple-element.42), channel_id=1, source_target_pairs={{0,4},{2,6},{4,0},{6,2},{1,5},{3,7},{5,1},{7,3},{8,12},{10,14},{12... | collective-permute-start | bytes 153608 | tf_op jit(solution)/shard_map/ppermute | solution.py:371
  77.3 4.2 %collective-permute-start.3 = (bf16[25,8,128]{2,1,0:T(8,128)(2,1)S(1)}, bf16[25,8,128]{2,1,0:T(8,128)(2,1)S(1)}, u32[]{:S(2)}, u32[]{:S(2)}) collective-permute-start(bf16[25,8,128]{2,1,0:T(8,128)(2,1)S(1)} %get-tuple-element.43), channel_id=1, source_target_pairs={{0,6},{2,0},{4,2},{6,4},{1,7},{3,1},{5,3},{7,5},{8,14},{10,8},{12,... | collective-permute-start | bytes 153608 | tf_op jit(solution)/shard_map/ppermute | solution.py:371
  81.6 35.9 %copy-start.2 = (bf16[4,256,256]{2,1,0:T(8,128)(2,1)S(1)}, bf16[4,256,256]{2,1,0:T(8,128)(2,1)}, u32[]{:S(2)}) copy-start(bf16[4,256,256]{2,1,0:T(8,128)(2,1)} %wv_ref.3) | copy-start | bytes 1572868
  81.6 35.8 %copy-start.3 = (bf16[1,256,1024]{2,1,0:T(8,128)(2,1)S(1)}, bf16[1,256,1024]{2,1,0:T(8,128)(2,1)}, u32[]{:S(2)}) copy-start(bf16[1,256,1024]{2,1,0:T(8,128)(2,1)} %param.9) | copy-start | bytes 1572868
  81.6 35.8 %copy-start.5 = (bf16[256,256]{1,0:T(8,128)(2,1)S(1)}, bf16[256,256]{1,0:T(8,128)(2,1)}, u32[]{:S(2)}) copy-start(bf16[256,256]{1,0:T(8,128)(2,1)} %local_ref.1) | copy-start | bytes 393220
  81.6 3.3 %collective-permute-start.4 = (bf16[25,8,128]{2,1,0:T(8,128)(2,1)S(1)}, bf16[25,8,128]{2,1,0:T(8,128)(2,1)S(1)}, u32[]{:S(2)}, u32[]{:S(2)}) collective-permute-start(bf16[25,8,128]{2,1,0:T(8,128)(2,1)S(1)} %shard_map.146.a_ref), channel_id=1, source_target_pairs={{0,64},{64,0},{128,192},{192,128},{1,65},{65,1},{129,193},{193,129... | collective-permute-start | bytes 153608 | tf_op jit(solution)/shard_map/ppermute | solution.py:377
  85.0 4.8 %collective-permute-start.5 = (bf16[25,8,128]{2,1,0:T(8,128)(2,1)S(1)}, bf16[25,8,128]{2,1,0:T(8,128)(2,1)S(1)}, u32[]{:S(2)}, u32[]{:S(2)}) collective-permute-start(bf16[25,8,128]{2,1,0:T(8,128)(2,1)S(1)} %shard_map.147.a_ref), channel_id=1, source_target_pairs={{0,128},{64,192},{128,0},{192,64},{1,129},{65,193},{129,1},{193,65... | collective-permute-start | bytes 153608 | tf_op jit(solution)/shard_map/ppermute | solution.py:377
  89.8 7.0 %collective-permute-start.6 = (bf16[25,8,128]{2,1,0:T(8,128)(2,1)S(1)}, bf16[25,8,128]{2,1,0:T(8,128)(2,1)S(1)}, u32[]{:S(2)}, u32[]{:S(2)}) collective-permute-start(bf16[25,8,128]{2,1,0:T(8,128)(2,1)S(1)} %shard_map.148.a_ref), channel_id=1, source_target_pairs={{0,8},{8,0},{16,24},{24,16},{32,40},{40,32},{48,56},{56,48},{1,9},... | collective-permute-start | bytes 153608 | tf_op jit(solution)/shard_map/ppermute | solution.py:377
  99.6 17.9 %copy-start.4 = (bf16[4,256,256]{2,1,0:T(8,128)(2,1)S(1)}, bf16[4,256,256]{2,1,0:T(8,128)(2,1)}, u32[]{:S(2)}) copy-start(bf16[4,256,256]{2,1,0:T(8,128)(2,1)} %wo_ref.1) | copy-start | bytes 1572868
  100.5 13.6 %collective-permute-start.10 = (bf16[256,256]{1,0:T(8,128)(2,1)S(1)}, bf16[256,256]{1,0:T(8,128)(2,1)S(1)}, u32[]{:S(2)}, u32[]{:S(2)}) collective-permute-start(bf16[256,256]{1,0:T(8,128)(2,1)S(1)} %shard_map.150.a_ref), channel_id=1, source_target_pairs={{0,64},{64,0},{128,192},{192,128},{1,65},{65,1},{129,193},{193,129... | collective-permute-start | bytes 393224 | tf_op jit(solution)/shard_map/ppermute | solution.py:377
  101.7 5.3 %collective-permute-start.7 = (bf16[25,8,128]{2,1,0:T(8,128)(2,1)S(1)}, bf16[25,8,128]{2,1,0:T(8,128)(2,1)S(1)}, u32[]{:S(2)}, u32[]{:S(2)}) collective-permute-start(bf16[25,8,128]{2,1,0:T(8,128)(2,1)S(1)} %shard_map.149.refs_0_), channel_id=1, source_target_pairs={{0,16},{8,24},{16,32},{24,40},{32,48},{40,56},{48,0},{56,8},{1,17}... | collective-permute-start | bytes 153608 | tf_op jit(solution)/shard_map/ppermute | solution.py:371
  102.5 7.4 %collective-permute-start.8 = (bf16[25,8,128]{2,1,0:T(8,128)(2,1)S(1)}, bf16[25,8,128]{2,1,0:T(8,128)(2,1)S(1)}, u32[]{:S(2)}, u32[]{:S(2)}) collective-permute-start(bf16[25,8,128]{2,1,0:T(8,128)(2,1)S(1)} %shard_map.149.refs_0_), channel_id=1, source_target_pairs={{0,32},{8,40},{16,48},{24,56},{32,0},{40,8},{48,16},{56,24},{1,33}... | collective-permute-start | bytes 153608 | tf_op jit(solution)/shard_map/ppermute | solution.py:371
  106.4 7.7 %collective-permute-start.9 = (bf16[25,8,128]{2,1,0:T(8,128)(2,1)S(1)}, bf16[25,8,128]{2,1,0:T(8,128)(2,1)S(1)}, u32[]{:S(2)}, u32[]{:S(2)}) collective-permute-start(bf16[25,8,128]{2,1,0:T(8,128)(2,1)S(1)} %shard_map.149.refs_0_), channel_id=1, source_target_pairs={{0,48},{8,56},{16,0},{24,8},{32,16},{40,24},{48,32},{56,40},{1,49}... | collective-permute-start | bytes 153608 | tf_op jit(solution)/shard_map/ppermute | solution.py:371
  114.7 12.3 %collective-permute-start.11 = (bf16[4,25,8,128]{3,2,1,0:T(8,128)(2,1)S(1)}, bf16[4,25,8,128]{3,2,1,0:T(8,128)(2,1)S(1)}, u32[]{:S(2)}, u32[]{:S(2)}) collective-permute-start(bf16[4,25,8,128]{3,2,1,0:T(8,128)(2,1)S(1)} %shard_map.151.refs_0_), channel_id=1, source_target_pairs={{0,2},{2,4},{4,6},{6,0},{1,3},{3,5},{5,7},{7,1},{8,10},{10,12},{12... | collective-permute-start | bytes 614408 | tf_op jit(solution)/shard_map/ppermute | solution.py:371
  114.8 12.2 %collective-permute-start.12 = (bf16[4,25,8,128]{3,2,1,0:T(8,128)(2,1)S(1)}, bf16[4,25,8,128]{3,2,1,0:T(8,128)(2,1)S(1)}, u32[]{:S(2)}, u32[]{:S(2)}) collective-permute-start(bf16[4,25,8,128]{3,2,1,0:T(8,128)(2,1)S(1)} %shard_map.151.refs_0_), channel_id=1, source_target_pairs={{0,4},{2,6},{4,0},{6,2},{1,5},{3,7},{5,1},{7,3},{8,12},{10,14},{12... | collective-permute-start | bytes 614408 | tf_op jit(solution)/shard_map/ppermute | solution.py:371
  114.9 12.1 %collective-permute-start.13 = (bf16[4,25,8,128]{3,2,1,0:T(8,128)(2,1)S(1)}, bf16[4,25,8,128]{3,2,1,0:T(8,128)(2,1)S(1)}, u32[]{:S(2)}, u32[]{:S(2)}) collective-permute-start(bf16[4,25,8,128]{3,2,1,0:T(8,128)(2,1)S(1)} %shard_map.151.refs_0_), channel_id=1, source_target_pairs={{0,6},{2,0},{4,2},{6,4},{1,7},{3,1},{5,3},{7,5},{8,14},{10,8},{12,... | collective-permute-start | bytes 614408 | tf_op jit(solution)/shard_map/ppermute | solution.py:371
  120.1 11.4 %collective-permute-start.14 = (bf16[4,25,8,128]{3,2,1,0:T(8,128)(2,1)S(1)}, bf16[4,25,8,128]{3,2,1,0:T(8,128)(2,1)S(1)}, u32[]{:S(2)}, u32[]{:S(2)}) collective-permute-start(bf16[4,25,8,128]{3,2,1,0:T(8,128)(2,1)S(1)} %shard_map.151.refs_0_), channel_id=1, source_target_pairs={{0,1},{1,0},{2,3},{3,2},{4,5},{5,4},{6,7},{7,6},{8,9},{9,8},{10,11... | collective-permute-start | bytes 614408 | tf_op jit(solution)/shard_map/ppermute | solution.py:377
  127.0 4.5 %collective-permute-start.15 = (bf16[4,25,8,128]{3,2,1,0:T(8,128)(2,1)S(1)}, bf16[4,25,8,128]{3,2,1,0:T(8,128)(2,1)S(1)}, u32[]{:S(2)}, u32[]{:S(2)}) collective-permute-start(bf16[4,25,8,128]{3,2,1,0:T(8,128)(2,1)S(1)} %collective-permute-done.11.refs_1_), channel_id=1, source_target_pairs={{0,1},{1,0},{2,3},{3,2},{4,5},{5,4},{6,7},{7,6},{8,9},{9,8},{10,11... | collective-permute-start | bytes 614408 | tf_op jit(solution)/shard_map/ppermute | solution.py:377
  128.5 3.0 %collective-permute-start.16 = (bf16[4,25,8,128]{3,2,1,0:T(8,128)(2,1)S(1)}, bf16[4,25,8,128]{3,2,1,0:T(8,128)(2,1)S(1)}, u32[]{:S(2)}, u32[]{:S(2)}) collective-permute-start(bf16[4,25,8,128]{3,2,1,0:T(8,128)(2,1)S(1)} %collective-permute-done.12.refs_2_), channel_id=1, source_target_pairs={{0,1},{1,0},{2,3},{3,2},{4,5},{5,4},{6,7},{7,6},{8,9},{9,8},{10,11... | collective-permute-start | bytes 614408 | tf_op jit(solution)/shard_map/ppermute | solution.py:377
  128.5 3.0 %collective-permute-start.17 = (bf16[4,25,8,128]{3,2,1,0:T(8,128)(2,1)S(1)}, bf16[4,25,8,128]{3,2,1,0:T(8,128)(2,1)S(1)}, u32[]{:S(2)}, u32[]{:S(2)}) collective-permute-start(bf16[4,25,8,128]{3,2,1,0:T(8,128)(2,1)S(1)} %collective-permute-done.13.refs_3_), channel_id=1, source_target_pairs={{0,1},{1,0},{2,3},{3,2},{4,5},{5,4},{6,7},{7,6},{8,9},{9,8},{10,11... | collective-permute-start | bytes 614408 | tf_op jit(solution)/shard_map/ppermute | solution.py:377
  129.0 6.6 %collective-permute-start.18 = (bf16[256,256]{1,0:T(8,128)(2,1)S(1)}, bf16[256,256]{1,0:T(8,128)(2,1)S(1)}, u32[]{:S(2)}, u32[]{:S(2)}) collective-permute-start(bf16[256,256]{1,0:T(8,128)(2,1)S(1)} %shard_map.153.a_ref), channel_id=1, source_target_pairs={{0,128},{64,192},{128,0},{192,64},{1,129},{65,193},{129,1},{193,65... | collective-permute-start | bytes 393224 | tf_op jit(solution)/shard_map/ppermute | solution.py:377
